TPU v7x, 32 devices: a whole 2x2x4 slice. The times are simulated.
32 devices in a mesh: grp: 2 (over x), tok: 16 (over z, y, core).
Axes of the slice: x: 2, y: 2, z: 4, core: 2. Of those that a mesh axis runs over, the one named last changes fastest.
Arguments:
- tokens: bfloat16 [4096, 3584], P(('grp', 'tok')), parts along dimension 0, may hold values from -6 to 6
- route_ids: int32 [4096, 8], P(('grp', 'tok')), parts along dimension 0, may hold values from 0 to 255, as said below
- route_weights: float32 [4096, 8], P(('grp', 'tok')), parts along dimension 0, may hold values from 0.05 to 2.5
Outputs:
- expert_hessian: float32 [57344, 3584], P(('grp', 'tok')), parts along dimension 0
- shared_hessian: float32 [32, 896, 896], P(('grp', 'tok')), parts along dimension 0
There are 2 independent parts, one for each index of `grp`. A program takes and returns all parts, laid end to end along the dimension named above; each array names one. Nothing has to cross between parts.
Inputs may be any that keep to these rules, and one draw needn't show every extreme that they name: `route_ids`: ids below 8 name the window experts. Each token names 8 different ids. Among the tokens of one device at most 32 name any one window expert, and in every draw some window expert is named by exactly 32 tokens of every device.
All inputs are finite; a program needn't handle non-finite values.
Results may differ from a plain program's by a relative error of at most 0.004.
Values may be sent and summed in bfloat16 or wider, within the bound.
No kernel may reach another device: no remote copies, remote signals or barrier semaphores. Data moves between devices by JAX's collectives and lax.ppermute only.
A program may use at most 128 MiB of HBM per device.

v0:
```python
import math

import jax
import jax.numpy as jnp
from jax import lax
from jax.sharding import PartitionSpec as P

EXP = 8
CAP = 32


def pack_rows(tokens, route_ids, route_weights):
    hits = route_ids[:, :, None] == jnp.arange(EXP, dtype=jnp.int32)[None, None, :]
    member = jnp.any(hits, axis=1)
    weight_table = jnp.sum(
        jnp.where(hits, route_weights[:, :, None], jnp.zeros_like(route_weights)[:, :, None]),
        axis=1,
    )
    places = jnp.cumsum(member.astype(jnp.int32), axis=0) - 1
    slots = jnp.arange(CAP, dtype=jnp.int32)
    select = jnp.logical_and(member.T[:, None, :], places.T[:, None, :] == slots[None, :, None])
    packed = jnp.einsum(
        "ect,td->ecd", select.astype(jnp.bfloat16), tokens, preferred_element_type=jnp.float32
    )
    roots = jnp.sqrt(jnp.sum(jnp.where(select, weight_table.T[:, None, :], 0.0), axis=2))
    return (packed * roots[:, :, None]).astype(jnp.bfloat16)


def on_device(tokens, route_ids, route_weights):
    devices = lax.axis_size("tok")
    position = lax.axis_index("tok")
    tok_rows, width = tokens.shape
    grid = math.isqrt(devices)
    edge = width // grid
    group = devices // EXP
    slab_rows = width // group
    scaled = pack_rows(tokens, route_ids, route_weights)
    outgoing = jnp.repeat(scaled, group, axis=0)
    arrived = lax.all_to_all(outgoing, "tok", split_axis=0, concat_axis=0, tiled=True)
    all_rows = arrived.reshape(-1, width)
    slab_index = position % group
    left_rows = lax.dynamic_slice_in_dim(all_rows, slab_index * slab_rows, slab_rows, 1)
    expert_part = lax.dot_general(
        left_rows, all_rows, (((0,), (0,)), ((), ())), preferred_element_type=jnp.float32
    ) / (16.0 * CAP)
    pieces = tokens.reshape(tok_rows, grid, edge).transpose(1, 0, 2)
    row_side = jnp.repeat(pieces, grid, axis=0)
    col_side = jnp.tile(pieces, (grid, 1, 1))
    left_in, right_in = (
        lax.all_to_all(row_side, "tok", split_axis=0, concat_axis=0, tiled=True),
        lax.all_to_all(col_side, "tok", split_axis=0, concat_axis=0, tiled=True),
    )
    total_rows = devices * tok_rows
    tile = lax.dot_general(
        left_in.reshape(total_rows, edge),
        right_in.reshape(total_rows, edge),
        (((0,), (0,)), ((), ())),
        preferred_element_type=jnp.float32,
    ) / float(total_rows)
    return (expert_part, tile[None])


def solution(mesh):
    in_specs = (P(("grp", "tok"), None), P(("grp", "tok"), None), P(("grp", "tok"), None))
    out_specs = (P(("grp", "tok"), None), P(("grp", "tok"), None, None))
    return jax.shard_map(
        on_device, mesh=mesh, in_specs=in_specs, out_specs=out_specs, check_vma=False
    )
```

profile of v0, /device:TPU:13, one launch (start us, length us, event | category | flops | bytes accessed | tf_op | source)
XLA Modules:
  0.0 279.6 jit_solution(10718706945456986820)
XLA Ops:
  0.6 0.7 fusion.8
  1.3 0.7 select_reduce_fusion.1
  2.1 0.1 copy.11
  2.2 0.2 reduce_window_sum.11
  2.4 0.1 select_reduce_fusion
  2.5 1.8 fusion
  4.3 2.2 broadcast_in_dim.49
  6.6 0.0 copy-start
  6.6 6.7 %all-to-all-start = ((bf16[16,32,3584]{2,1,0:T(8,128)(2,1)}), bf16[16,32,3584]{2,1,0:T(8,128)(2,1)}, u32[]{:S(2)}, u32[]{:S(2)}) async-start(bf16[16,32,3584]{2,1,0:T(8,128)(2,1)} %bitcast.22), calls=%async_computation | async-start | bytes 7340032 | tf_op jit(solution)/shard_map/all_to_all | solution.py:39
  13.3 0.0 copy-done
  13.3 0.2 reshape.32
  13.5 1.2 copy.13
  14.7 79.8 %all-to-all-done = bf16[16,32,3584]{2,1,0:T(8,128)(2,1)} async-done(((bf16[16,32,3584]{2,1,0:T(8,128)(2,1)}), bf16[16,32,3584]{2,1,0:T(8,128)(2,1)}, u32[]{:S(2)}, u32[]{:S(2)}) %all-to-all-start) | async-done | bytes 3670048 | tf_op jit(solution)/shard_map/all_to_all | solution.py:39
  94.5 2.5 broadcast_in_dim.50
  97.0 4.9 %all-to-all-start.1 = ((bf16[16,128,896]{1,2,0:T(8,128)(2,1)}), bf16[16,128,896]{1,2,0:T(8,128)(2,1)}, u32[]{:S(2)}, u32[]{:S(2)}) async-start(bf16[16,128,896]{1,2,0:T(8,128)(2,1)} %bitcast.23), calls=%async_computation.1 | async-start | bytes 7340032 | tf_op jit(solution)/shard_map/all_to_all | solution.py:50
  101.9 0.1 copy.14
  102.0 81.1 %all-to-all-done.1 = bf16[16,128,896]{1,2,0:T(8,128)(2,1)} async-done(((bf16[16,128,896]{1,2,0:T(8,128)(2,1)}), bf16[16,128,896]{1,2,0:T(8,128)(2,1)}, u32[]{:S(2)}, u32[]{:S(2)}) %all-to-all-start.1) | async-done | bytes 3670048 | tf_op jit(solution)/shard_map/all_to_all | solution.py:50
  183.2 2.4 tile.4
  185.6 4.9 %all-to-all-start.2 = ((bf16[16,128,896]{2,1,0:T(8,128)(2,1)}), bf16[16,128,896]{2,1,0:T(8,128)(2,1)}, u32[]{:S(2)}, u32[]{:S(2)}) async-start(bf16[16,128,896]{2,1,0:T(8,128)(2,1)} %bitcast.21), calls=%async_computation.2 | async-start | bytes 7340032 | tf_op jit(solution)/shard_map/all_to_all | solution.py:51
  190.5 15.0 %convolution_multiply_fusion = f32[1792,3584]{1,0:T(8,128)} fusion(bf16[512,3584]{1,0:T(8,128)(2,1)} %bitcast.5, s32[]{:T(128)S(6)} %select_n.21), kind=kOutput, calls=%fused_computation | convolution fusion | flops 6583091200 | bytes 31195140 | tf_op jit(solution)/shard_map/dot_general | solution.py:43
  205.5 66.3 %all-to-all-done.2 = bf16[16,128,896]{2,1,0:T(8,128)(2,1)} async-done(((bf16[16,128,896]{2,1,0:T(8,128)(2,1)}), bf16[16,128,896]{2,1,0:T(8,128)(2,1)}, u32[]{:S(2)}, u32[]{:S(2)}) %all-to-all-start.2) | async-done | bytes 3670048 | tf_op jit(solution)/shard_map/all_to_all | solution.py:51
  271.7 7.9 %fusion.1 = f32[1,896,896]{2,1,0:T(8,128)} fusion(bf16[16,128,896]{1,2,0:T(8,128)(2,1)} %all-to-all-done.1, bf16[16,128,896]{2,1,0:T(8,128)(2,1)} %all-to-all-done.2), kind=kOutput, calls=%fused_computation.4 | convolution fusion | flops 3289137152 | bytes 10551296 | tf_op jit(solution)/shard_map/dot_general | solution.py:54
  (4 shorter events, 0.1 us)
Async XLA Ops:
  6.6 6.7 %copy-start = (bf16[128,3584]{1,0:T(8,128)(2,1)S(1)}, bf16[128,3584]{1,0:T(8,128)(2,1)}, u32[]{:S(2)}) copy-start(bf16[128,3584]{1,0:T(8,128)(2,1)} %param.3) | copy-start | bytes 2752516
  6.6 87.9 %all-to-all-start = ((bf16[16,32,3584]{2,1,0:T(8,128)(2,1)}), bf16[16,32,3584]{2,1,0:T(8,128)(2,1)}, u32[]{:S(2)}, u32[]{:S(2)}) async-start(bf16[16,32,3584]{2,1,0:T(8,128)(2,1)} %bitcast.22), calls=%async_computation | async-start | bytes 7340032 | tf_op jit(solution)/shard_map/all_to_all | solution.py:39
  97.0 86.1 %all-to-all-start.1 = ((bf16[16,128,896]{1,2,0:T(8,128)(2,1)}), bf16[16,128,896]{1,2,0:T(8,128)(2,1)}, u32[]{:S(2)}, u32[]{:S(2)}) async-start(bf16[16,128,896]{1,2,0:T(8,128)(2,1)} %bitcast.23), calls=%async_computation.1 | async-start | bytes 7340032 | tf_op jit(solution)/shard_map/all_to_all | solution.py:50
  185.6 86.1 %all-to-all-start.2 = ((bf16[16,128,896]{2,1,0:T(8,128)(2,1)}), bf16[16,128,896]{2,1,0:T(8,128)(2,1)}, u32[]{:S(2)}, u32[]{:S(2)}) async-start(bf16[16,128,896]{2,1,0:T(8,128)(2,1)} %bitcast.21), calls=%async_computation.2 | async-start | bytes 7340032 | tf_op jit(solution)/shard_map/all_to_all | solution.py:51
where the time goes:
time: 280 us
  waiting for transfers between devices  227 us (81%)
  matrix products  24.7 us (9%)
  starting transfers between devices  16.5 us (6%)
  local copies, waits for them, and re-layouts  8.84 us (3%)
    all_to_all x1, waiting for transfers between devices, on_device(): lax.all_to_all(row_side, 'tok', split_axis=0, concat_axis=0, tiled=True)  81.1 us
    all_to_all x1, waiting for transfers between devices, on_device(): lax.all_to_all(outgoing, 'tok', split_axis=0, concat_axis=0, tiled=True)  79.8 us
    all_to_all x1, waiting for transfers between devices, on_device(): lax.all_to_all(col_side, 'tok', split_axis=0, concat_axis=0, tiled=True)  66.3 us
    dot_general x1, matrix products, on_device(): lax.dot_general(left_rows, all_rows, (((0,), (0,)), ((), ())), preferred_...  15 us
    dot_general x1, matrix products, on_device(): lax.dot_general(left_in.reshape(total_rows, edge), right_in.reshape(total...  7.88 us
    all_to_all x1, starting transfers between devices, on_device(): lax.all_to_all(outgoing, 'tok', split_axis=0, concat_axis=0, tiled=True)  6.69 us
  transfers between devices with their start and end apart: 3, of which 3 were waited for; matrix products, arithmetic and copies ran while one was open for 6% of the time, Pallas kernels for 0%

commit v1 on v0

v1 whole, which is shorter than its diff:
```python
import math

import jax
import jax.numpy as jnp
from jax import lax
from jax.sharding import PartitionSpec as P

EXP = 8
CAP = 32


def weight_table(route_ids, route_weights):
    hits = route_ids[:, :, None] == jnp.arange(EXP, dtype=jnp.int32)[None, None, :]
    return jnp.sum(
        jnp.where(hits, route_weights[:, :, None], jnp.zeros_like(route_weights)[:, :, None]),
        axis=1,
    )


def pack_rows(rows, weights):
    member = weights > 0
    places = jnp.cumsum(member.astype(jnp.int32), axis=1) - 1
    slots = jnp.arange(CAP, dtype=jnp.int32)
    select = jnp.logical_and(member[:, None, :], places[:, None, :] == slots[None, :, None])
    packed = jnp.einsum(
        "bct,btd->bcd", select.astype(jnp.bfloat16), rows, preferred_element_type=jnp.float32
    )
    roots = jnp.sqrt(jnp.sum(jnp.where(select, weights[:, None, :], 0.0), axis=2))
    return (packed * roots[:, :, None]).astype(jnp.bfloat16)


def on_device(tokens, route_ids, route_weights):
    devices = lax.axis_size("tok")
    position = lax.axis_index("tok")
    tok_rows, width = tokens.shape
    grid = math.isqrt(devices)
    edge = width // grid
    group = devices // EXP
    slab_rows = width // group
    table = lax.all_gather(weight_table(route_ids, route_weights), "tok", tiled=True)
    everyone = lax.all_gather(tokens, "tok", tiled=True)
    own = lax.dynamic_slice_in_dim(table, position // group, 1, 1).reshape(devices, tok_rows)
    all_rows = pack_rows(everyone.reshape(devices, tok_rows, width), own).reshape(-1, width)
    left_rows = lax.dynamic_slice_in_dim(all_rows, (position % group) * slab_rows, slab_rows, 1)
    expert_part = lax.dot_general(
        left_rows, all_rows, (((0,), (0,)), ((), ())), preferred_element_type=jnp.float32
    ) / (16.0 * CAP)
    left = lax.dynamic_slice_in_dim(everyone, (position // grid) * edge, edge, 1)
    right = lax.dynamic_slice_in_dim(everyone, (position % grid) * edge, edge, 1)
    tile = lax.dot_general(
        left, right, (((0,), (0,)), ((), ())), preferred_element_type=jnp.float32
    ) / float(devices * tok_rows)
    return (expert_part, tile[None])


def solution(mesh):
    in_specs = (P(("grp", "tok"), None), P(("grp", "tok"), None), P(("grp", "tok"), None))
    out_specs = (P(("grp", "tok"), None), P(("grp", "tok"), None, None))
    return jax.shard_map(
        on_device, mesh=mesh, in_specs=in_specs, out_specs=out_specs, check_vma=False
    )
```

time: 280 us -> 160 us (0.57)
  the two profiles are of different devices: /device:TPU:13 before, /device:TPU:0 now
where the time goes in v1:
time: 160 us
  waiting for transfers between devices  94.8 us (59%)
  matrix products  25.9 us (16%)
  blocking collectives  23.7 us (15%)
  between operations  14.2 us (9%)
    all_gather x1, waiting for transfers between devices, on_device(): everyone = lax.all_gather(tokens, 'tok', tiled=True)  94.1 us
    all_gather x1, blocking collectives, on_device(): lax.all_gather(weight_table(route_ids, route_weights), 'tok', tiled=True)  23.7 us
    dot_general x1, matrix products, on_device(): lax.dot_general(left_rows, all_rows, (((0,), (0,)), ((), ())), preferred_...  12.7 us
    dot_general x1, matrix products, pack_rows(): jnp.einsum('bct,btd->bcd', select.astype(jnp.bfloat16), rows, preferred_e...  7.35 us
    dot_general x1, matrix products, on_device(): lax.dot_general(left, right, (((0,), (0,)), ((), ())), preferred_element_...  5.84 us
  transfers between devices with their start and end apart: 1, of which 1 were waited for; matrix products, arithmetic and copies ran while one was open for 1% of the time, Pallas kernels for 0%

profile of v1, /device:TPU:0, one launch (start us, length us, event | category | flops | bytes accessed | tf_op | source)
XLA Modules:
  0.0 159.7 jit_solution(5476527144575701592)
XLA Ops:
  7.2 0.0 all-gather.2.cloned.1.call-start
  7.2 0.7 all-gather.2.cloned.1.call-update
  7.9 0.7 select_reduce_fusion.1
  8.7 23.7 %all_gather.6 = f32[2048,8]{0,1:T(8,128)S(1)} all-gather(f32[128,8]{0,1:T(8,128)S(1)} %select_reduce_fusion.1), channel_id=1, replica_groups=mesh['grp'=2,'tok'=16] {'tok'}, dimensions={0}, use_global_device_ids=true | all-gather | bytes 69632 | tf_op jit(solution)/shard_map/all_gather | solution.py:40
  32.4 0.3 reduce_window_sum.11
  32.7 0.1 select_reduce_fusion
  32.8 94.1 %all-gather.2.cloned.1.call-done = bf16[2048,3584]{1,0:T(8,128)(2,1)} async-done(((bf16[128,3584]{1,0:T(8,128)(2,1)}), bf16[2048,3584]{1,0:T(8,128)(2,1)}) %all-gather.2.cloned.1.call-update) | async-done | bytes 14680080 | tf_op jit(solution)/shard_map/all_gather | solution.py:41
  127.0 0.0 slice-start
  127.0 0.0 slice-start.1
  127.0 7.4 %multiply_convert_fusion = bf16[16,32,3584]{2,1,0:T(8,128)(2,1)S(1)} fusion(bf16[16,128,3584]{2,1,0:T(8,128)(2,1)} %bitcast.7, f32[16,32]{1,0:T(8,128)S(1)} %sqrt.7, s32[16,128]{1,0:T(8,128)S(1)} %broadcast_add_fusion, pred[16,128]{1,0:T(8,128)(4,1)S(1)} %get-tuple-element.3), kind=kOutput, calls=%fused_computation.1 | convolution fusion | flops 473563136 | bytes 18362368 | tf_op jit(solution)/shard_map/bct,btd->bcd/dot_general | solution.py:25
  134.3 0.0 slice-start.2
  134.3 0.0 slice-start.3
  134.4 12.7 %convolution_multiply_fusion = f32[1792,3584]{1,0:T(8,128)} fusion(bf16[512,3584]{1,0:T(8,128)(2,1)S(1)} %bitcast.10, s32[]{:T(128)S(6)} %select_n.43), kind=kOutput, calls=%fused_computation | convolution fusion | flops 6583091200 | bytes 31195140 | tf_op jit(solution)/shard_map/dot_general | solution.py:45
  147.0 0.0 slice-done
  147.0 0.0 slice-done.1
  147.0 0.0 slice-done.2
  147.0 0.0 slice-done.3
  147.1 5.8 %multiply_bitcast_fusion = f32[1,896,896]{2,1,0:T(8,128)} fusion(bf16[2048,3584]{1,0:T(8,128)(2,1)S(1)} %bitcast.9, s32[]{:T(128)S(6)} %select_n.47, s32[]{:T(128)S(6)} %select_n.45), kind=kOutput, calls=%fused_computation.5 | convolution fusion | flops 3289137152 | bytes 10551304 | tf_op jit(solution)/shard_map/dot_general | solution.py:50
  (5 shorter events, 0.0 us)
Async XLA Ops:
  7.2 119.8 %all-gather.2.cloned.1.call-start = ((), (), s32[]{:S(2)}) async-start(), calls=%async_computation | async-start | bytes 15597568 | tf_op jit(solution)/shard_map/all_gather | solution.py:41
  127.0 20.1 %slice-start = ((s8[14680064]{0:T(1024)(128)(4,1)}), s8[4194304]{0:T(1024)(128)(4,1)S(1)}, s32[]{:S(2)}) async-start(s8[14680064]{0:T(1024)(128)(4,1)} %bitcast.8), calls=%async_computation.1 | async-start | bytes 8388608
  127.0 20.1 %slice-start.1 = ((s8[14680064]{0:T(1024)(128)(4,1)}), s8[4194304]{0:T(1024)(128)(4,1)S(1)}, s32[]{:S(2)}) async-start(s8[14680064]{0:T(1024)(128)(4,1)} %bitcast.8), calls=%async_computation.2 | async-start | bytes 8388608
  134.3 12.7 %slice-start.2 = ((s8[14680064]{0:T(1024)(128)(4,1)}), s8[4194304]{0:T(1024)(128)(4,1)S(1)}, s32[]{:S(2)}) async-start(s8[14680064]{0:T(1024)(128)(4,1)} %bitcast.8), calls=%async_computation.3 | async-start | bytes 8388608
  134.3 12.7 %slice-start.3 = ((s8[14680064]{0:T(1024)(128)(4,1)}), s8[2097152]{0:T(1024)(128)(4,1)S(1)}, s32[]{:S(2)}) async-start(s8[14680064]{0:T(1024)(128)(4,1)} %bitcast.8), calls=%async_computation.4 | async-start | bytes 4194304
Sparse Core Ops, SparseCore 0:
  10.3 116.6 all-gather.1

commit v2 on v1

v2 whole, which is shorter than its diff:
```python
import math

import jax
import jax.numpy as jnp
from jax import lax
from jax.sharding import PartitionSpec as P

EXP = 8
CAP = 32
CORES = 2
PARTS = 2


def weight_table(route_ids, route_weights):
    hits = route_ids[:, :, None] == jnp.arange(EXP, dtype=jnp.int32)[None, None, :]
    return jnp.sum(
        jnp.where(hits, route_weights[:, :, None], jnp.zeros_like(route_weights)[:, :, None]),
        axis=1,
    )


def selection(weights):
    member = weights > 0
    places = jnp.cumsum(member.astype(jnp.int32), axis=1) - 1
    slots = jnp.arange(CAP, dtype=jnp.int32)
    select = jnp.logical_and(member[:, None, :], places[:, None, :] == slots[None, :, None])
    roots = jnp.sqrt(jnp.sum(jnp.where(select, weights[:, None, :], 0.0), axis=2))
    return select.astype(jnp.bfloat16), roots


def ring_of(chips):
    return list(range(0, chips, 2)) + list(range(chips - 1, 0, -2))


def gather_tokens(tokens, devices):
    chips = devices // CORES
    ring = ring_of(chips)
    ahead = [
        (ring[i] * CORES + c, ring[(i + 1) % chips] * CORES + c)
        for i in range(chips)
        for c in range(CORES)
    ]
    back = [(b, a) for a, b in ahead]
    pair = [(d, d ^ 1) for d in range(devices)]
    position = lax.axis_index("tok")
    core = position % CORES
    place = jnp.array([ring.index(q) for q in range(chips)], jnp.int32)[position // CORES]
    ring_at = jnp.array(ring, jnp.int32)
    width = tokens.shape[1] // PARTS
    own = [tokens[:, h * width : (h + 1) * width] for h in range(PARTS)]
    pieces = [[rows] for rows in own]
    distances = [0]
    going, coming = list(own), list(own)
    for step in range(1, chips // 2):
        for h in range(PARTS):
            going[h] = lax.ppermute(going[h], "tok", ahead)
            coming[h] = lax.ppermute(coming[h], "tok", back)
            pieces[h] += [going[h], coming[h]]
        distances += [-step, step]
    for h in range(PARTS):
        pieces[h].append(
            lax.ppermute(going[h], "tok", ahead) if h % 2 == 0 else lax.ppermute(coming[h], "tok", back)
        )
    distances.append(chips // 2)
    pieces = [p + [lax.ppermute(rows, "tok", pair) for rows in p] for p in pieces]
    chip_ids = ring_at[(place + chips + jnp.array(distances, jnp.int32)) % chips]
    senders = jnp.concatenate([chip_ids * CORES + core, chip_ids * CORES + 1 - core])
    return pieces, senders


def on_device(tokens, route_ids, route_weights):
    devices = lax.axis_size("tok")
    position = lax.axis_index("tok")
    tok_rows, width = tokens.shape
    grid = math.isqrt(devices)
    edge = width // grid
    group = devices // EXP
    slab_rows = width // group
    pieces, senders = gather_tokens(tokens, devices)
    table = lax.all_gather(weight_table(route_ids, route_weights), "tok", tiled=True)
    own = lax.dynamic_slice_in_dim(table, position // group, 1, 1).reshape(devices, tok_rows)
    select, roots = selection(own[senders])
    everyone = [jnp.stack(p) for p in pieces]
    packed = [
        jnp.einsum("bct,btd->bcd", select, rows, preferred_element_type=jnp.float32)
        for rows in everyone
    ]
    all_rows = jnp.concatenate(
        [(rows * roots[:, :, None]).astype(jnp.bfloat16) for rows in packed], axis=2
    ).reshape(-1, width)
    left_rows = lax.dynamic_slice_in_dim(all_rows, (position % group) * slab_rows, slab_rows, 1)
    expert_part = lax.dot_general(
        left_rows, all_rows, (((0,), (0,)), ((), ())), preferred_element_type=jnp.float32
    ) / (16.0 * CAP)
    in_part = grid // PARTS

    def block(index):
        cuts = [
            lax.dynamic_slice_in_dim(rows.reshape(-1, width // PARTS), (index % in_part) * edge, edge, 1)
            for rows in everyone
        ]
        return jnp.where(index // in_part == 0, cuts[0], cuts[1])

    tile = lax.dot_general(
        block(position // grid), block(position % grid), (((0,), (0,)), ((), ())),
        preferred_element_type=jnp.float32,
    ) / float(devices * tok_rows)
    return (expert_part, tile[None])


def solution(mesh):
    in_specs = (P(("grp", "tok"), None), P(("grp", "tok"), None), P(("grp", "tok"), None))
    out_specs = (P(("grp", "tok"), None), P(("grp", "tok"), None, None))
    return jax.shard_map(
        on_device, mesh=mesh, in_specs=in_specs, out_specs=out_specs, check_vma=False
    )
```

time: 160 us -> 174 us (1.087)
  starting transfers between devices: 0.04 us -> 13.3 us
  between operations: 14.2 us -> 1.6 us
  local copies, waits for them, and re-layouts: 0.03 us -> 6.48 us
  waiting for transfers between devices: 94.8 us -> 101 us
  matrix products: 25.9 us -> 20.7 us
  blocking collectives: 23.7 us -> 28.8 us
    ppermute x0 -> x30, waiting for transfers between devices: none -> 101 us  [the longest x6 42.9 us: gather_tokens(): going[h] = lax.ppermute(going[h], 'tok', ahead)]
    all_gather x1 -> x0, waiting for transfers between devices: 94.1 us -> none  [on_device(): everyone = lax.all_gather(tokens, 'tok', tiled=True)]
    ppermute x0 -> x30, starting transfers between devices: none -> 13.3 us  [the longest x6 6.06 us: gather_tokens(): going[h] = lax.ppermute(going[h], 'tok', ahead)]
    dot_general x2 -> x3, matrix products: 13.2 us -> 8.05 us  [the longest x1 5.88 us: on_device(): lax.dot_general(block(position // grid), block(position % grid), (((0,),...]
    all_gather x1, blocking collectives: 23.7 us -> 28.8 us  [on_device(): lax.all_gather(weight_table(route_ids, route_weights), 'tok', tiled=True)]
    unnamed x8 -> x29, local copies, waits for them, and re-layouts: 0.02 us -> 2.08 us
    gather x0 -> x2, local copies, waits for them, and re-layouts: none -> 1.86 us  [the longest x1 1.3 us: gather_tokens(): ring_at[(place + chips + jnp.array(distances, jnp.int32)) % chips]]
  transfers between devices with their start and end apart: 1 -> 30, of which waited for: 1 -> 18; matrix products, arithmetic and copies ran while one was open for 1% -> 5% of each run, Pallas kernels for 0% -> 0%
where the time goes in v2:
time: 174 us
  waiting for transfers between devices  101 us (58%)
  blocking collectives  28.8 us (17%)
  matrix products  20.7 us (12%)
  starting transfers between devices  13.3 us (8%)
  local copies, waits for them, and re-layouts  6.48 us (4%)
  other arithmetic  2.22 us (1%)
    ppermute x6, waiting for transfers between devices, gather_tokens(): going[h] = lax.ppermute(going[h], 'tok', ahead)  42.9 us
    ppermute x6, waiting for transfers between devices, gather_tokens(): coming[h] = lax.ppermute(coming[h], 'tok', back)  30 us
    all_gather x1, blocking collectives, on_device(): lax.all_gather(weight_table(route_ids, route_weights), 'tok', tiled=True)  28.8 us
    dot_general x1, matrix products, on_device(): lax.dot_general(left_rows, all_rows, (((0,), (0,)), ((), ())), preferred_...  12.7 us
    ppermute x1, waiting for transfers between devices, gather_tokens(): lax.ppermute(coming[h], 'tok', back)  12.1 us
    ppermute x1, waiting for transfers between devices, gather_tokens(): lax.ppermute(going[h], 'tok', ahead)  8.08 us
    ppermute x16, waiting for transfers between devices, gather_tokens(): lax.ppermute(rows, 'tok', pair)  7.71 us
    ppermute x6, starting transfers between devices, gather_tokens(): going[h] = lax.ppermute(going[h], 'tok', ahead)  6.06 us
  transfers between devices with their start and end apart: 30, of which 18 were waited for; matrix products, arithmetic and copies ran while one was open for 5% of the time, Pallas kernels for 0%

profile of v2, /device:TPU:0, one launch (start us, length us, event | category | flops | bytes accessed | tf_op | source)
XLA Modules:
  0.0 173.9 jit_solution(6704797941588665261)
XLA Ops:
  0.6 1.2 fusion.26
  1.9 3.1 %collective-permute-start = (bf16[128,1792]{1,0:T(8,128)(2,1)S(1)}, bf16[128,1792]{1,0:T(8,128)(2,1)S(1)}, u32[]{:S(2)}, u32[]{:S(2)}) collective-permute-start(bf16[128,1792]{1,0:T(8,128)(2,1)S(1)} %get-tuple-element.4), channel_id=1, source_target_pairs={{0,4},{1,5},{4,8},{5,9},{8,12},{9,13},{12,14},{13,15},{14,10},{15,... | collective-permute-start | bytes 1376264 | tf_op jit(solution)/shard_map/ppermute | solution.py:56
  4.9 0.0 collective-permute-start.1
  4.9 0.0 collective-permute-start.7
  4.9 2.0 %collective-permute-start.15 = (bf16[128,1792]{1,0:T(8,128)(2,1)S(1)}, bf16[128,1792]{1,0:T(8,128)(2,1)S(1)}, u32[]{:S(2)}, u32[]{:S(2)}) collective-permute-start(bf16[128,1792]{1,0:T(8,128)(2,1)S(1)} %get-tuple-element.5), channel_id=1, source_target_pairs={{0,4},{1,5},{4,8},{5,9},{8,12},{9,13},{12,14},{13,15},{14,10},{15,... | collective-permute-start | bytes 1376264 | tf_op jit(solution)/shard_map/ppermute | solution.py:56
  7.0 0.0 collective-permute-start.16
  7.0 1.2 dynamic_slice.22
  8.9 0.7 compare_select_fusion.1
  9.5 1.3 gather_fusion
  10.9 0.1 fusion.24
  10.9 0.7 select_reduce_fusion.1
  11.7 28.8 %all_gather.3 = f32[2048,8]{0,1:T(8,128)S(1)} all-gather(f32[128,8]{0,1:T(8,128)S(1)} %select_reduce_fusion.1), channel_id=1, replica_groups=mesh['grp'=2,'tok'=16] {'tok'}, dimensions={0}, use_global_device_ids=true | all-gather | bytes 69632 | tf_op jit(solution)/shard_map/all_gather | solution.py:80
  40.5 0.6 gather_fusion.1
  41.1 0.3 reduce_window_sum.11
  41.4 0.1 select_reduce_fusion
  41.5 1.2 bitcast_dynamic-update-slice_fusion.31
  42.8 0.0 collective-permute-done
  42.8 0.4 collective-permute-start.22
  43.2 0.0 collective-permute-done.1
  43.2 0.1 collective-permute-start.2
  43.3 0.0 collective-permute-done.15
  43.4 2.1 %collective-permute-start.3 = (bf16[128,1792]{1,0:T(8,128)(2,1)S(1)}, bf16[128,1792]{1,0:T(8,128)(2,1)S(1)}, u32[]{:S(2)}, u32[]{:S(2)}) collective-permute-start(bf16[128,1792]{1,0:T(8,128)(2,1)S(1)} %collective-permute-done.1), channel_id=1, source_target_pairs={{4,0},{5,1},{8,4},{9,5},{12,8},{13,9},{14,12},{15,13},{10,14},{11,... | collective-permute-start | bytes 1376264 | tf_op jit(solution)/shard_map/ppermute | solution.py:57
  45.5 0.1 collective-permute-start.8
  45.6 10.3 %collective-permute-done.2 = bf16[128,1792]{1,0:T(8,128)(2,1)S(1)} collective-permute-done((bf16[128,1792]{1,0:T(8,128)(2,1)S(1)}, bf16[128,1792]{1,0:T(8,128)(2,1)S(1)}, u32[]{:S(2)}, u32[]{:S(2)}) %collective-permute-start.2) | collective-permute-done | bytes 458784 | tf_op jit(solution)/shard_map/ppermute | solution.py:56
  55.9 0.1 collective-permute-done.3
  56.0 0.3 collective-permute-start.17
  56.3 12.6 %collective-permute-done.17 = bf16[128,1792]{1,0:T(8,128)(2,1)S(1)} collective-permute-done((bf16[128,1792]{1,0:T(8,128)(2,1)S(1)}, bf16[128,1792]{1,0:T(8,128)(2,1)S(1)}, u32[]{:S(2)}, u32[]{:S(2)}) %collective-permute-start.17) | collective-permute-done | bytes 458784 | tf_op jit(solution)/shard_map/ppermute | solution.py:56
  68.9 0.4 collective-permute-start.18
  69.3 11.7 %collective-permute-done.18 = bf16[128,1792]{1,0:T(8,128)(2,1)S(1)} collective-permute-done((bf16[128,1792]{1,0:T(8,128)(2,1)S(1)}, bf16[128,1792]{1,0:T(8,128)(2,1)S(1)}, u32[]{:S(2)}, u32[]{:S(2)}) %collective-permute-start.18) | collective-permute-done | bytes 458784 | tf_op jit(solution)/shard_map/ppermute | solution.py:57
  81.0 0.3 collective-permute-start.4
  81.4 10.9 %collective-permute-done.4 = bf16[128,1792]{1,0:T(8,128)(2,1)S(1)} collective-permute-done((bf16[128,1792]{1,0:T(8,128)(2,1)S(1)}, bf16[128,1792]{1,0:T(8,128)(2,1)S(1)}, u32[]{:S(2)}, u32[]{:S(2)}) %collective-permute-start.4) | collective-permute-done | bytes 458784 | tf_op jit(solution)/shard_map/ppermute | solution.py:56
  92.3 0.2 collective-permute-start.5
  92.5 10.1 %collective-permute-done.5 = bf16[128,1792]{1,0:T(8,128)(2,1)S(1)} collective-permute-done((bf16[128,1792]{1,0:T(8,128)(2,1)S(1)}, bf16[128,1792]{1,0:T(8,128)(2,1)S(1)}, u32[]{:S(2)}, u32[]{:S(2)}) %collective-permute-start.5) | collective-permute-done | bytes 458784 | tf_op jit(solution)/shard_map/ppermute | solution.py:57
  102.6 0.3 collective-permute-start.19
  103.0 9.0 %collective-permute-done.19 = bf16[128,1792]{1,0:T(8,128)(2,1)S(1)} collective-permute-done((bf16[128,1792]{1,0:T(8,128)(2,1)S(1)}, bf16[128,1792]{1,0:T(8,128)(2,1)S(1)}, u32[]{:S(2)}, u32[]{:S(2)}) %collective-permute-start.19) | collective-permute-done | bytes 458784 | tf_op jit(solution)/shard_map/ppermute | solution.py:56
  112.0 0.4 collective-permute-start.20
  112.4 8.1 %collective-permute-done.20 = bf16[128,1792]{1,0:T(8,128)(2,1)S(1)} collective-permute-done((bf16[128,1792]{1,0:T(8,128)(2,1)S(1)}, bf16[128,1792]{1,0:T(8,128)(2,1)S(1)}, u32[]{:S(2)}, u32[]{:S(2)}) %collective-permute-start.20) | collective-permute-done | bytes 458784 | tf_op jit(solution)/shard_map/ppermute | solution.py:57
  120.5 0.4 collective-permute-start.6
  120.9 8.1 %collective-permute-done.6 = bf16[128,1792]{1,0:T(8,128)(2,1)S(1)} collective-permute-done((bf16[128,1792]{1,0:T(8,128)(2,1)S(1)}, bf16[128,1792]{1,0:T(8,128)(2,1)S(1)}, u32[]{:S(2)}, u32[]{:S(2)}) %collective-permute-start.6) | collective-permute-done | bytes 458784 | tf_op jit(solution)/shard_map/ppermute | solution.py:62
  129.0 0.6 collective-permute-start.24
  129.6 0.1 collective-permute-start.10
  129.8 0.6 collective-permute-start.11
  130.4 1.7 %collective-permute-done.10 = bf16[128,1792]{1,0:T(8,128)(2,1)S(1)} collective-permute-done((bf16[128,1792]{1,0:T(8,128)(2,1)S(1)}, bf16[128,1792]{1,0:T(8,128)(2,1)S(1)}, u32[]{:S(2)}, u32[]{:S(2)}) %collective-permute-start.10) | collective-permute-done | bytes 458784 | tf_op jit(solution)/shard_map/ppermute | solution.py:65
  132.1 0.1 collective-permute-start.25
  132.3 0.5 collective-permute-done.11
  132.8 0.1 collective-permute-start.12
  132.9 1.6 collective-permute-done.12
  134.6 0.1 collective-permute-start.13
  134.7 1.6 collective-permute-done.13
  136.4 0.5 collective-permute-start.21
  136.9 12.1 %collective-permute-done.21 = bf16[128,1792]{1,0:T(8,128)(2,1)S(1)} collective-permute-done((bf16[128,1792]{1,0:T(8,128)(2,1)S(1)}, bf16[128,1792]{1,0:T(8,128)(2,1)S(1)}, u32[]{:S(2)}, u32[]{:S(2)}) %collective-permute-start.21) | collective-permute-done | bytes 458784 | tf_op jit(solution)/shard_map/ppermute | solution.py:62
  149.0 0.6 collective-permute-start.27
  149.6 0.1 collective-permute-start.28
  149.8 0.6 collective-permute-start.14
  150.4 0.1 collective-permute-start.29
  150.5 0.3 collective-permute-done.26
  150.8 0.6 collective-permute-done.27
  151.5 0.6 collective-permute-done.28
  152.1 0.6 collective-permute-done.14
  152.8 1.1 multiply_convert_fusion.1
  153.9 1.1 multiply_convert_fusion
  155.0 0.3 pad_maximum_fusion
  155.3 12.7 %convolution_multiply_fusion = f32[1792,3584]{1,0:T(8,128)} fusion(bf16[512,3584]{1,0:T(8,128)(2,1)S(1)} %bitcast.82, s32[]{:T(128)S(6)} %select_n.103), kind=kOutput, calls=%fused_computation.2 | convolution fusion | flops 6583091200 | bytes 31195140 | tf_op jit(solution)/shard_map/dot_general | solution.py:92
  168.0 5.9 %multiply_bitcast_fusion = f32[1,896,896]{2,1,0:T(8,128)} fusion(bf16[2048,1792]{1,0:T(8,128)(2,1)S(1)} %bitcast.80, s32[]{:T(128)S(6)} %select_n.114, bf16[2048,1792]{1,0:T(8,128)(2,1)S(1)} %bitcast.81, pred[]{:T(512)S(6)} %eq.49, s32[]{:T(128)S(6)} %select_n.108, pred[]{:T(512)S(6)} %eq.48), kind=kOutput, calls=%fused_computation.15 | convolution fusion | flops 3292807168 | bytes 17891338 | tf_op jit(solution)/shard_map/dot_general | solution.py:104
  (49 shorter events, 1.0 us)
Async XLA Ops:
  1.9 40.9 %collective-permute-start = (bf16[128,1792]{1,0:T(8,128)(2,1)S(1)}, bf16[128,1792]{1,0:T(8,128)(2,1)S(1)}, u32[]{:S(2)}, u32[]{:S(2)}) collective-permute-start(bf16[128,1792]{1,0:T(8,128)(2,1)S(1)} %get-tuple-element.4), channel_id=1, source_target_pairs={{0,4},{1,5},{4,8},{5,9},{8,12},{9,13},{12,14},{13,15},{14,10},{15,... | collective-permute-start | bytes 1376264 | tf_op jit(solution)/shard_map/ppermute | solution.py:56
  4.9 38.3 %collective-permute-start.1 = (bf16[128,1792]{1,0:T(8,128)(2,1)S(1)}, bf16[128,1792]{1,0:T(8,128)(2,1)S(1)}, u32[]{:S(2)}, u32[]{:S(2)}) collective-permute-start(bf16[128,1792]{1,0:T(8,128)(2,1)S(1)} %get-tuple-element.4), channel_id=1, source_target_pairs={{4,0},{5,1},{8,4},{9,5},{12,8},{13,9},{14,12},{15,13},{10,14},{11,... | collective-permute-start | bytes 1376264 | tf_op jit(solution)/shard_map/ppermute | solution.py:57
  4.9 124.1 %collective-permute-start.7 = (bf16[128,1792]{1,0:T(8,128)(2,1)S(1)}, bf16[128,1792]{1,0:T(8,128)(2,1)S(1)}, u32[]{:S(2)}, u32[]{:S(2)}) collective-permute-start(bf16[128,1792]{1,0:T(8,128)(2,1)S(1)} %get-tuple-element.4), channel_id=1, source_target_pairs={{0,1},{1,0},{2,3},{3,2},{4,5},{5,4},{6,7},{7,6},{8,9},{9,8},{10,11... | collective-permute-start | bytes 1376264 | tf_op jit(solution)/shard_map/ppermute | solution.py:65
  4.9 38.4 %collective-permute-start.15 = (bf16[128,1792]{1,0:T(8,128)(2,1)S(1)}, bf16[128,1792]{1,0:T(8,128)(2,1)S(1)}, u32[]{:S(2)}, u32[]{:S(2)}) collective-permute-start(bf16[128,1792]{1,0:T(8,128)(2,1)S(1)} %get-tuple-element.5), channel_id=1, source_target_pairs={{0,4},{1,5},{4,8},{5,9},{8,12},{9,13},{12,14},{13,15},{14,10},{15,... | collective-permute-start | bytes 1376264 | tf_op jit(solution)/shard_map/ppermute | solution.py:56
  7.0 38.5 %collective-permute-start.16 = (bf16[128,1792]{1,0:T(8,128)(2,1)S(1)}, bf16[128,1792]{1,0:T(8,128)(2,1)S(1)}, u32[]{:S(2)}, u32[]{:S(2)}) collective-permute-start(bf16[128,1792]{1,0:T(8,128)(2,1)S(1)} %get-tuple-element.5), channel_id=1, source_target_pairs={{4,0},{5,1},{8,4},{9,5},{12,8},{13,9},{14,12},{15,13},{10,14},{11,... | collective-permute-start | bytes 1376264 | tf_op jit(solution)/shard_map/ppermute | solution.py:57
  42.8 106.2 %collective-permute-start.22 = (bf16[128,1792]{1,0:T(8,128)(2,1)S(1)}, bf16[128,1792]{1,0:T(8,128)(2,1)S(1)}, u32[]{:S(2)}, u32[]{:S(2)}) collective-permute-start(bf16[128,1792]{1,0:T(8,128)(2,1)S(1)} %get-tuple-element.5), channel_id=1, source_target_pairs={{0,1},{1,0},{2,3},{3,2},{4,5},{5,4},{6,7},{7,6},{8,9},{9,8},{10,11... | collective-permute-start | bytes 1376264 | tf_op jit(solution)/shard_map/ppermute | solution.py:65
  43.2 12.6 %collective-permute-start.2 = (bf16[128,1792]{1,0:T(8,128)(2,1)S(1)}, bf16[128,1792]{1,0:T(8,128)(2,1)S(1)}, u32[]{:S(2)}, u32[]{:S(2)}) collective-permute-start(bf16[128,1792]{1,0:T(8,128)(2,1)S(1)} %collective-permute-done), channel_id=1, source_target_pairs={{0,4},{1,5},{4,8},{5,9},{8,12},{9,13},{12,14},{13,15},{14,10},{15,... | collective-permute-start | bytes 1376264 | tf_op jit(solution)/shard_map/ppermute | solution.py:56
  43.4 12.6 %collective-permute-start.3 = (bf16[128,1792]{1,0:T(8,128)(2,1)S(1)}, bf16[128,1792]{1,0:T(8,128)(2,1)S(1)}, u32[]{:S(2)}, u32[]{:S(2)}) collective-permute-start(bf16[128,1792]{1,0:T(8,128)(2,1)S(1)} %collective-permute-done.1), channel_id=1, source_target_pairs={{4,0},{5,1},{8,4},{9,5},{12,8},{13,9},{14,12},{15,13},{10,14},{11,... | collective-permute-start | bytes 1376264 | tf_op jit(solution)/shard_map/ppermute | solution.py:57
  45.5 84.2 %collective-permute-start.8 = (bf16[128,1792]{1,0:T(8,128)(2,1)S(1)}, bf16[128,1792]{1,0:T(8,128)(2,1)S(1)}, u32[]{:S(2)}, u32[]{:S(2)}) collective-permute-start(bf16[128,1792]{1,0:T(8,128)(2,1)S(1)} %collective-permute-done), channel_id=1, source_target_pairs={{0,1},{1,0},{2,3},{3,2},{4,5},{5,4},{6,7},{7,6},{8,9},{9,8},{10,11... | collective-permute-start | bytes 1376264 | tf_op jit(solution)/shard_map/ppermute | solution.py:65
  55.9 73.9 %collective-permute-start.9 = (bf16[128,1792]{1,0:T(8,128)(2,1)S(1)}, bf16[128,1792]{1,0:T(8,128)(2,1)S(1)}, u32[]{:S(2)}, u32[]{:S(2)}) collective-permute-start(bf16[128,1792]{1,0:T(8,128)(2,1)S(1)} %collective-permute-done.1), channel_id=1, source_target_pairs={{0,1},{1,0},{2,3},{3,2},{4,5},{5,4},{6,7},{7,6},{8,9},{9,8},{10,11... | collective-permute-start | bytes 1376264 | tf_op jit(solution)/shard_map/ppermute | solution.py:65
  56.0 12.9 %collective-permute-start.17 = (bf16[128,1792]{1,0:T(8,128)(2,1)S(1)}, bf16[128,1792]{1,0:T(8,128)(2,1)S(1)}, u32[]{:S(2)}, u32[]{:S(2)}) collective-permute-start(bf16[128,1792]{1,0:T(8,128)(2,1)S(1)} %collective-permute-done.15), channel_id=1, source_target_pairs={{0,4},{1,5},{4,8},{5,9},{8,12},{9,13},{12,14},{13,15},{14,10},{15,... | collective-permute-start | bytes 1376264 | tf_op jit(solution)/shard_map/ppermute | solution.py:56
  68.9 12.1 %collective-permute-start.18 = (bf16[128,1792]{1,0:T(8,128)(2,1)S(1)}, bf16[128,1792]{1,0:T(8,128)(2,1)S(1)}, u32[]{:S(2)}, u32[]{:S(2)}) collective-permute-start(bf16[128,1792]{1,0:T(8,128)(2,1)S(1)} %collective-permute-done.16), channel_id=1, source_target_pairs={{4,0},{5,1},{8,4},{9,5},{12,8},{13,9},{14,12},{15,13},{10,14},{11,... | collective-permute-start | bytes 1376264 | tf_op jit(solution)/shard_map/ppermute | solution.py:57
  81.0 11.2 %collective-permute-start.4 = (bf16[128,1792]{1,0:T(8,128)(2,1)S(1)}, bf16[128,1792]{1,0:T(8,128)(2,1)S(1)}, u32[]{:S(2)}, u32[]{:S(2)}) collective-permute-start(bf16[128,1792]{1,0:T(8,128)(2,1)S(1)} %collective-permute-done.2), channel_id=1, source_target_pairs={{0,4},{1,5},{4,8},{5,9},{8,12},{9,13},{12,14},{13,15},{14,10},{15,... | collective-permute-start | bytes 1376264 | tf_op jit(solution)/shard_map/ppermute | solution.py:56
  92.3 10.3 %collective-permute-start.5 = (bf16[128,1792]{1,0:T(8,128)(2,1)S(1)}, bf16[128,1792]{1,0:T(8,128)(2,1)S(1)}, u32[]{:S(2)}, u32[]{:S(2)}) collective-permute-start(bf16[128,1792]{1,0:T(8,128)(2,1)S(1)} %collective-permute-done.3), channel_id=1, source_target_pairs={{4,0},{5,1},{8,4},{9,5},{12,8},{13,9},{14,12},{15,13},{10,14},{11,... | collective-permute-start | bytes 1376264 | tf_op jit(solution)/shard_map/ppermute | solution.py:57
  102.6 9.4 %collective-permute-start.19 = (bf16[128,1792]{1,0:T(8,128)(2,1)S(1)}, bf16[128,1792]{1,0:T(8,128)(2,1)S(1)}, u32[]{:S(2)}, u32[]{:S(2)}) collective-permute-start(bf16[128,1792]{1,0:T(8,128)(2,1)S(1)} %collective-permute-done.17), channel_id=1, source_target_pairs={{0,4},{1,5},{4,8},{5,9},{8,12},{9,13},{12,14},{13,15},{14,10},{15,... | collective-permute-start | bytes 1376264 | tf_op jit(solution)/shard_map/ppermute | solution.py:56
  112.0 8.5 %collective-permute-start.20 = (bf16[128,1792]{1,0:T(8,128)(2,1)S(1)}, bf16[128,1792]{1,0:T(8,128)(2,1)S(1)}, u32[]{:S(2)}, u32[]{:S(2)}) collective-permute-start(bf16[128,1792]{1,0:T(8,128)(2,1)S(1)} %collective-permute-done.18), channel_id=1, source_target_pairs={{4,0},{5,1},{8,4},{9,5},{12,8},{13,9},{14,12},{15,13},{10,14},{11,... | collective-permute-start | bytes 1376264 | tf_op jit(solution)/shard_map/ppermute | solution.py:57
  120.5 8.5 %collective-permute-start.6 = (bf16[128,1792]{1,0:T(8,128)(2,1)S(1)}, bf16[128,1792]{1,0:T(8,128)(2,1)S(1)}, u32[]{:S(2)}, u32[]{:S(2)}) collective-permute-start(bf16[128,1792]{1,0:T(8,128)(2,1)S(1)} %collective-permute-done.4), channel_id=1, source_target_pairs={{0,4},{1,5},{4,8},{5,9},{8,12},{9,13},{12,14},{13,15},{14,10},{15,... | collective-permute-start | bytes 1376264 | tf_op jit(solution)/shard_map/ppermute | solution.py:62
  129.0 20.6 %collective-permute-start.23 = (bf16[128,1792]{1,0:T(8,128)(2,1)S(1)}, bf16[128,1792]{1,0:T(8,128)(2,1)S(1)}, u32[]{:S(2)}, u32[]{:S(2)}) collective-permute-start(bf16[128,1792]{1,0:T(8,128)(2,1)S(1)} %collective-permute-done.15), channel_id=1, source_target_pairs={{0,1},{1,0},{2,3},{3,2},{4,5},{5,4},{6,7},{7,6},{8,9},{9,8},{10,11... | collective-permute-start | bytes 1376264 | tf_op jit(solution)/shard_map/ppermute | solution.py:65
  129.0 20.7 %collective-permute-start.24 = (bf16[128,1792]{1,0:T(8,128)(2,1)S(1)}, bf16[128,1792]{1,0:T(8,128)(2,1)S(1)}, u32[]{:S(2)}, u32[]{:S(2)}) collective-permute-start(bf16[128,1792]{1,0:T(8,128)(2,1)S(1)} %collective-permute-done.16), channel_id=1, source_target_pairs={{0,1},{1,0},{2,3},{3,2},{4,5},{5,4},{6,7},{7,6},{8,9},{9,8},{10,11... | collective-permute-start | bytes 1376264 | tf_op jit(solution)/shard_map/ppermute | solution.py:65
  129.6 2.5 %collective-permute-start.10 = (bf16[128,1792]{1,0:T(8,128)(2,1)S(1)}, bf16[128,1792]{1,0:T(8,128)(2,1)S(1)}, u32[]{:S(2)}, u32[]{:S(2)}) collective-permute-start(bf16[128,1792]{1,0:T(8,128)(2,1)S(1)} %collective-permute-done.2), channel_id=1, source_target_pairs={{0,1},{1,0},{2,3},{3,2},{4,5},{5,4},{6,7},{7,6},{8,9},{9,8},{10,11... | collective-permute-start | bytes 1376264 | tf_op jit(solution)/shard_map/ppermute | solution.py:65
  129.8 3.0 %collective-permute-start.11 = (bf16[128,1792]{1,0:T(8,128)(2,1)S(1)}, bf16[128,1792]{1,0:T(8,128)(2,1)S(1)}, u32[]{:S(2)}, u32[]{:S(2)}) collective-permute-start(bf16[128,1792]{1,0:T(8,128)(2,1)S(1)} %collective-permute-done.3), channel_id=1, source_target_pairs={{0,1},{1,0},{2,3},{3,2},{4,5},{5,4},{6,7},{7,6},{8,9},{9,8},{10,11... | collective-permute-start | bytes 1376264 | tf_op jit(solution)/shard_map/ppermute | solution.py:65
  132.1 18.2 %collective-permute-start.25 = (bf16[128,1792]{1,0:T(8,128)(2,1)S(1)}, bf16[128,1792]{1,0:T(8,128)(2,1)S(1)}, u32[]{:S(2)}, u32[]{:S(2)}) collective-permute-start(bf16[128,1792]{1,0:T(8,128)(2,1)S(1)} %collective-permute-done.17), channel_id=1, source_target_pairs={{0,1},{1,0},{2,3},{3,2},{4,5},{5,4},{6,7},{7,6},{8,9},{9,8},{10,11... | collective-permute-start | bytes 1376264 | tf_op jit(solution)/shard_map/ppermute | solution.py:65
  132.8 1.8 %collective-permute-start.12 = (bf16[128,1792]{1,0:T(8,128)(2,1)S(1)}, bf16[128,1792]{1,0:T(8,128)(2,1)S(1)}, u32[]{:S(2)}, u32[]{:S(2)}) collective-permute-start(bf16[128,1792]{1,0:T(8,128)(2,1)S(1)} %collective-permute-done.4), channel_id=1, source_target_pairs={{0,1},{1,0},{2,3},{3,2},{4,5},{5,4},{6,7},{7,6},{8,9},{9,8},{10,11... | collective-permute-start | bytes 1376264 | tf_op jit(solution)/shard_map/ppermute | solution.py:65
  134.6 1.8 %collective-permute-start.13 = (bf16[128,1792]{1,0:T(8,128)(2,1)S(1)}, bf16[128,1792]{1,0:T(8,128)(2,1)S(1)}, u32[]{:S(2)}, u32[]{:S(2)}) collective-permute-start(bf16[128,1792]{1,0:T(8,128)(2,1)S(1)} %collective-permute-done.5), channel_id=1, source_target_pairs={{0,1},{1,0},{2,3},{3,2},{4,5},{5,4},{6,7},{7,6},{8,9},{9,8},{10,11... | collective-permute-start | bytes 1376264 | tf_op jit(solution)/shard_map/ppermute | solution.py:65
  136.4 12.6 %collective-permute-start.21 = (bf16[128,1792]{1,0:T(8,128)(2,1)S(1)}, bf16[128,1792]{1,0:T(8,128)(2,1)S(1)}, u32[]{:S(2)}, u32[]{:S(2)}) collective-permute-start(bf16[128,1792]{1,0:T(8,128)(2,1)S(1)} %collective-permute-done.20), channel_id=1, source_target_pairs={{4,0},{5,1},{8,4},{9,5},{12,8},{13,9},{14,12},{15,13},{10,14},{11,... | collective-permute-start | bytes 1376264 | tf_op jit(solution)/shard_map/ppermute | solution.py:62
  149.0 1.8 %collective-permute-start.26 = (bf16[128,1792]{1,0:T(8,128)(2,1)S(1)}, bf16[128,1792]{1,0:T(8,128)(2,1)S(1)}, u32[]{:S(2)}, u32[]{:S(2)}) collective-permute-start(bf16[128,1792]{1,0:T(8,128)(2,1)S(1)} %collective-permute-done.18), channel_id=1, source_target_pairs={{0,1},{1,0},{2,3},{3,2},{4,5},{5,4},{6,7},{7,6},{8,9},{9,8},{10,11... | collective-permute-start | bytes 1376264 | tf_op jit(solution)/shard_map/ppermute | solution.py:65
  149.0 2.4 %collective-permute-start.27 = (bf16[128,1792]{1,0:T(8,128)(2,1)S(1)}, bf16[128,1792]{1,0:T(8,128)(2,1)S(1)}, u32[]{:S(2)}, u32[]{:S(2)}) collective-permute-start(bf16[128,1792]{1,0:T(8,128)(2,1)S(1)} %collective-permute-done.19), channel_id=1, source_target_pairs={{0,1},{1,0},{2,3},{3,2},{4,5},{5,4},{6,7},{7,6},{8,9},{9,8},{10,11... | collective-permute-start | bytes 1376264 | tf_op jit(solution)/shard_map/ppermute | solution.py:65
  149.6 2.5 %collective-permute-start.28 = (bf16[128,1792]{1,0:T(8,128)(2,1)S(1)}, bf16[128,1792]{1,0:T(8,128)(2,1)S(1)}, u32[]{:S(2)}, u32[]{:S(2)}) collective-permute-start(bf16[128,1792]{1,0:T(8,128)(2,1)S(1)} %collective-permute-done.20), channel_id=1, source_target_pairs={{0,1},{1,0},{2,3},{3,2},{4,5},{5,4},{6,7},{7,6},{8,9},{9,8},{10,11... | collective-permute-start | bytes 1376264 | tf_op jit(solution)/shard_map/ppermute | solution.py:65
  149.8 3.0 %collective-permute-start.14 = (bf16[128,1792]{1,0:T(8,128)(2,1)S(1)}, bf16[128,1792]{1,0:T(8,128)(2,1)S(1)}, u32[]{:S(2)}, u32[]{:S(2)}) collective-permute-start(bf16[128,1792]{1,0:T(8,128)(2,1)S(1)} %collective-permute-done.6), channel_id=1, source_target_pairs={{0,1},{1,0},{2,3},{3,2},{4,5},{5,4},{6,7},{7,6},{8,9},{9,8},{10,11... | collective-permute-start | bytes 1376264 | tf_op jit(solution)/shard_map/ppermute | solution.py:65
  150.4 3.5 %collective-permute-start.29 = (bf16[128,1792]{1,0:T(8,128)(2,1)S(1)}, bf16[128,1792]{1,0:T(8,128)(2,1)S(1)}, u32[]{:S(2)}, u32[]{:S(2)}) collective-permute-start(bf16[128,1792]{1,0:T(8,128)(2,1)S(1)} %collective-permute-done.21), channel_id=1, source_target_pairs={{0,1},{1,0},{2,3},{3,2},{4,5},{5,4},{6,7},{7,6},{8,9},{9,8},{10,11... | collective-permute-start | bytes 1376264 | tf_op jit(solution)/shard_map/ppermute | solution.py:65

commit v3 on v1

v3 whole, which is shorter than its diff:
```python
import functools
import math

import jax
import jax.numpy as jnp
from jax import lax
from jax.experimental import pallas as pl
from jax.experimental.pallas import tpu as pltpu
from jax.sharding import PartitionSpec as P

EXP = 8
CAP = 32
CORES = 2
TABLE = 128
VMEM = pl.BlockSpec(memory_space=pltpu.VMEM)
SMEM = pl.BlockSpec(memory_space=pltpu.SMEM)
F32 = jnp.float32
BF16 = jnp.bfloat16


def params(mib):
    return pltpu.CompilerParams(vmem_limit_bytes=mib * 2**20)


def message_kernel(tokens, ids, weights, out):
    rows, width = tokens.shape
    out[:, :width] = tokens[...]
    lane = lax.broadcasted_iota(jnp.int32, (rows, TABLE), 1)
    roots = jnp.zeros((rows, TABLE), F32)
    for e in range(EXP):
        root = jnp.sqrt(jnp.sum(jnp.where(ids[...] == e, weights[...], 0.0), axis=1, keepdims=True))
        roots = jnp.where(lane % EXP == e, root, roots)
    high = roots.astype(BF16).astype(F32)
    middle = (roots - high).astype(BF16).astype(F32)
    low = roots - high - middle
    table = jnp.where(lane < EXP, high, jnp.where(lane < 2 * EXP, middle, low))
    out[:, width:] = jnp.where(lane < 3 * EXP, table, 0.0).astype(BF16)


def make_message(tokens, ids, weights):
    rows, width = tokens.shape
    return pl.pallas_call(
        message_kernel,
        out_shape=jax.ShapeDtypeStruct((rows, width + TABLE), BF16),
        in_specs=[VMEM] * 3,
        out_specs=VMEM,
        compiler_params=params(16),
        name="make_message",
    )(tokens, ids, weights)


def absorb_kernel(counts, grid, first, *refs):
    scalars, refs = refs[0], refs[1:]
    total = sum(counts)
    flat, refs = refs[:total], refs[total:]
    if first:
        tile, packed, left, right = refs
    else:
        before, tile, packed, left, right = refs
    pieces, at = [], 0
    for count in counts:
        pieces.append(flat[at : at + count])
        at += count
    width = packed.shape[1]
    edge = tile.shape[0]
    tok_rows = sum(ref.shape[0] for ref in pieces[0])
    expert = scalars[0]
    for slot, which in ((1, left), (2, right)):
        for b in range(grid):

            @pl.when(scalars[slot] == b)
            def _(b=b, which=which):
                row = 0
                for ref in flat:
                    which[row : row + ref.shape[0], :] = ref[:, b * edge : (b + 1) * edge]
                    row += ref.shape[0]

    update = lax.dot_general(
        left[...], right[...], (((0,), (0,)), ((), ())), preferred_element_type=F32
    )
    tile[...] = update if first else before[...] + update
    lane = lax.broadcasted_iota(jnp.int32, (tok_rows, TABLE), 1)
    ours = jnp.logical_and(lane % EXP == expert, lane < 3 * EXP)
    row_at = lax.broadcasted_iota(jnp.int32, (tok_rows, tok_rows), 0)
    column_at = lax.broadcasted_iota(jnp.int32, (tok_rows, tok_rows), 1)
    upto = (column_at <= row_at).astype(F32).astype(BF16)
    slot_at = lax.broadcasted_iota(jnp.int32, (tok_rows, CAP), 1)
    for k, parts in enumerate(pieces):
        table = jnp.concatenate([ref[:, width:].astype(F32) for ref in parts], axis=0)
        root = jnp.sum(jnp.where(ours, table, 0.0), axis=1, keepdims=True)
        member = root > 0.0
        counted = jnp.dot(
            upto,
            jnp.broadcast_to(member.astype(F32), (tok_rows, TABLE)).astype(BF16),
            preferred_element_type=F32,
        )
        place = counted[:, :CAP].astype(jnp.int32) - 1
        select = jnp.logical_and(member, place == slot_at).astype(F32).astype(BF16)
        row, result = 0, None
        for ref in parts:
            rows = ref.shape[0]
            scaled = (ref[:, :width].astype(F32) * root[row : row + rows]).astype(BF16)
            term = lax.dot_general(
                select[row : row + rows], scaled, (((0,), (0,)), ((), ())),
                preferred_element_type=F32,
            )
            result = term if result is None else result + term
            row += rows
        packed[k * CAP : (k + 1) * CAP, :] = result.astype(BF16)


def absorb(scalars, pieces, tile, grid, edge, width):
    flat = [ref for parts in pieces for ref in parts]
    rows = sum(ref.shape[0] for ref in flat)
    first = tile is None
    return pl.pallas_call(
        functools.partial(absorb_kernel, [len(parts) for parts in pieces], grid, first),
        out_shape=(
            jax.ShapeDtypeStruct((edge, edge), F32),
            jax.ShapeDtypeStruct((len(pieces) * CAP, width), BF16),
        ),
        in_specs=[SMEM] + [VMEM] * (len(flat) + (0 if first else 1)),
        out_specs=(VMEM, VMEM),
        scratch_shapes=[pltpu.VMEM((rows, edge), BF16)] * 2,
        cost_estimate=pl.CostEstimate(
            flops=2 * rows * edge * edge + 2 * CAP * rows * width,
            bytes_accessed=2 * rows * width + 8 * edge * edge,
            transcendentals=0,
        ),
        input_output_aliases={} if first else {1 + len(flat): 0},
        compiler_params=params(32),
        name="absorb",
    )(scalars, *flat, *([] if first else [tile]))


def expert_kernel(scalars, *refs):
    *packs, out, across, rows = refs
    slab = out.shape[0]
    slabs = rows.shape[1] // slab

    @pl.when(pl.program_id(0) == 0)
    def _():
        at = 0
        for pack in packs:
            rows[at : at + pack.shape[0], :] = pack[...]
            at += pack.shape[0]
        for s in range(slabs):

            @pl.when(scalars[3] == s)
            def _(s=s):
                across[...] = rows[:, s * slab : (s + 1) * slab].T

    step = out.shape[1]
    start = pl.multiple_of(pl.program_id(0) * step, 128)
    out[...] = jnp.dot(
        across[...], rows[:, pl.ds(start, step)], preferred_element_type=F32
    ) * (1.0 / (16.0 * CAP))


def expert_product(scalars, packs, slab):
    width = packs[0].shape[1]
    total = sum(pack.shape[0] for pack in packs)
    step = 256
    return pl.pallas_call(
        expert_kernel,
        grid=(width // step,),
        out_shape=jax.ShapeDtypeStruct((slab, width), F32),
        in_specs=[SMEM] + [VMEM] * len(packs),
        out_specs=pl.BlockSpec((slab, step), lambda n: (0, n)),
        scratch_shapes=[pltpu.VMEM((slab, total), BF16), pltpu.VMEM((total, width), BF16)],
        cost_estimate=pl.CostEstimate(
            flops=2 * slab * total * width, bytes_accessed=4 * slab * width, transcendentals=0
        ),
        compiler_params=params(44),
        name="expert_product",
    )(scalars, *packs)


def ring_of(chips):
    return list(range(0, chips, 2)) + list(range(chips - 1, 0, -2))


def on_device(tokens, route_ids, route_weights):
    devices = lax.axis_size("tok")
    position = lax.axis_index("tok")
    tok_rows, width = tokens.shape
    grid = math.isqrt(devices)
    edge = width // grid
    group = devices // EXP
    slab_rows = width // group
    chips = devices // CORES
    ring = ring_of(chips)
    ahead = [
        (ring[i] * CORES + c, ring[(i + 1) % chips] * CORES + c)
        for i in range(chips)
        for c in range(CORES)
    ]
    back = [(b, a) for a, b in ahead]
    pair = [(d, d ^ 1) for d in range(devices)]
    scalars = jnp.stack(
        [position // group, position // grid, position % grid, position % group]
    ).astype(jnp.int32)

    def other_core(parts):
        return [lax.ppermute(rows, "tok", pair) for rows in parts]

    own = make_message(tokens, route_ids, route_weights)
    going, coming = own, own
    arrived = [[own]]
    tile, packs = None, []
    for step in range(1, chips // 2 + 1):
        if step < chips // 2:
            going = lax.ppermute(going, "tok", ahead)
            coming = lax.ppermute(coming, "tok", back)
            new = [[going], [coming]]
        else:
            half = tok_rows // 2
            new = [
                [
                    lax.ppermute(going[:half], "tok", ahead),
                    lax.ppermute(coming[half:], "tok", back),
                ]
            ]
        pieces = arrived + [other_core(parts) for parts in arrived]
        tile, packed = absorb(scalars, pieces, tile, grid, edge, width)
        packs.append(packed)
        arrived = new
    pieces = arrived + [other_core(parts) for parts in arrived]
    tile, packed = absorb(scalars, pieces, tile, grid, edge, width)
    packs.append(packed)
    expert_part = expert_product(scalars, packs, slab_rows)
    return (expert_part, (tile * (1.0 / (devices * tok_rows)))[None])


def solution(mesh):
    in_specs = (P(("grp", "tok"), None), P(("grp", "tok"), None), P(("grp", "tok"), None))
    out_specs = (P(("grp", "tok"), None), P(("grp", "tok"), None, None))
    return jax.shard_map(
        on_device, mesh=mesh, in_specs=in_specs, out_specs=out_specs, check_vma=False
    )
```

time: 160 us -> 130 us (0.81)
  Pallas kernels: 0 us -> 32.4 us
  waiting for transfers between devices: 94.8 us -> 68.5 us
  matrix products: 25.9 us -> 0 us
  blocking collectives: 23.7 us -> 0 us
  local copies, waits for them, and re-layouts: 0.03 us -> 15.5 us
  between operations: 14.2 us -> 0.79 us
  starting transfers between devices: 0.04 us -> 10.3 us
    all_gather x1 -> x0, waiting for transfers between devices: 94.1 us -> none  [on_device(): everyone = lax.all_gather(tokens, 'tok', tiled=True)]
    ppermute x0 -> x17, waiting for transfers between devices: none -> 68.5 us  [the longest x3 54.8 us: on_device(): coming = lax.ppermute(coming, 'tok', back)]
    pallas_call x0 -> x7, Pallas kernels: none -> 32.4 us  [the longest x5 17 us: absorb(): pl.pallas_call(functools.partial(absorb_kernel, [len(parts) for parts in...]
    dot_general x3 -> x0, matrix products: 25.9 us -> none  [the longest x1 12.7 us: on_device(): lax.dot_general(left_rows, all_rows, (((0,), (0,)), ((), ())), preferred_...]
    all_gather x1 -> x0, blocking collectives: 23.7 us -> none  [on_device(): lax.all_gather(weight_table(route_ids, route_weights), 'tok', tiled=True)]
    unnamed x8 -> x32, local copies, waits for them, and re-layouts: 0.02 us -> 15.4 us
    ppermute x0 -> x17, starting transfers between devices: none -> 10.3 us  [the longest x3 6.07 us: on_device(): coming = lax.ppermute(coming, 'tok', back)]
    broadcast_in_dim x0 -> x1, other arithmetic: none -> 1.89 us  [on_device(): return (expert_part, (tile * (1.0 / (devices * tok_rows)))[None])]
  transfers between devices with their start and end apart: 1 -> 17, of which waited for: 1 -> 6; matrix products, arithmetic and copies ran while one was open for 1% -> 0% of each run, Pallas kernels for 0% -> 11%
where the time goes in v3:
time: 130 us; the launch traced here: 129 us
  waiting for transfers between devices  68.5 us (53%)
  Pallas kernels  32.4 us (25%)
  local copies, waits for them, and re-layouts  15.5 us (12%)
  starting transfers between devices  10.3 us (8%)
  other arithmetic  1.97 us (2%)
    ppermute x3, waiting for transfers between devices, on_device(): coming = lax.ppermute(coming, 'tok', back)  54.8 us
    pallas_call x5, Pallas kernels, absorb(): pl.pallas_call(functools.partial(absorb_kernel, [len(parts) for parts in...  17 us
    unnamed x32, local copies, waits for them, and re-layouts  15.4 us
    pallas_call x1, Pallas kernels, expert_product(): pl.pallas_call(expert_kernel, grid=(width // step,), out_shape=jax.ShapeD...  15.2 us
    ppermute x1, waiting for transfers between devices, on_device(): lax.ppermute(coming[half:], 'tok', back)  10.3 us
    ppermute x3, starting transfers between devices, on_device(): coming = lax.ppermute(coming, 'tok', back)  6.07 us
  transfers between devices with their start and end apart: 17, of which 6 were waited for; matrix products, arithmetic and copies ran while one was open for 0% of the time, Pallas kernels for 11%

profile of v3, /device:TPU:0, one launch (start us, length us, event | category | flops | bytes accessed | tf_op | source)
XLA Modules:
  0.0 129.4 jit_solution(4701036847016604861)
XLA Ops:
  0.6 0.8 copy.9.ids
  1.4 0.8 copy.10.weights
  2.2 0.0 copy-start.14
  2.2 1.2 copy-done.14
  3.4 0.2 make_message.1.refs_1_
  3.6 3.0 %collective-permute-start.2 = (bf16[128,3712]{1,0:T(8,128)(2,1)S(1)}, bf16[128,3712]{1,0:T(8,128)(2,1)S(1)}, u32[]{:S(2)}, u32[]{:S(2)}) collective-permute-start(bf16[128,3712]{1,0:T(8,128)(2,1)S(1)} %make_message.1.refs_1_), channel_id=1, source_target_pairs={{4,0},{5,1},{8,4},{9,5},{12,8},{13,9},{14,12},{15,13},{10,14},{11,... | collective-permute-start | bytes 2850824 | tf_op jit(solution)/shard_map/ppermute | solution.py:214
  6.7 0.1 collective-permute-start.1
  6.8 21.0 %collective-permute-done.2.refs_2_ = bf16[128,3712]{1,0:T(8,128)(2,1)S(1)} collective-permute-done((bf16[128,3712]{1,0:T(8,128)(2,1)S(1)}, bf16[128,3712]{1,0:T(8,128)(2,1)S(1)}, u32[]{:S(2)}, u32[]{:S(2)}) %collective-permute-start.2) | collective-permute-done | bytes 950304 | tf_op jit(solution)/shard_map/ppermute | solution.py:214
  27.8 1.7 %collective-permute-start.6 = (bf16[128,3712]{1,0:T(8,128)(2,1)S(1)}, bf16[128,3712]{1,0:T(8,128)(2,1)S(1)}, u32[]{:S(2)}, u32[]{:S(2)}) collective-permute-start(bf16[128,3712]{1,0:T(8,128)(2,1)S(1)} %collective-permute-done.2.refs_2_), channel_id=1, source_target_pairs={{4,0},{5,1},{8,4},{9,5},{12,8},{13,9},{14,12},{15,13},{10,14},{11,... | collective-permute-start | bytes 2850824 | tf_op jit(solution)/shard_map/ppermute | solution.py:214
  29.5 0.0 collective-permute-done.1.refs_1_
  29.5 0.3 collective-permute-start.5
  29.8 0.0 collective-permute-start
  29.8 0.5 collective-permute-start.4
  30.3 0.0 copy-start.2
  30.3 1.0 copy-done.2
  31.3 18.7 %collective-permute-done.6.refs_2_ = bf16[128,3712]{1,0:T(8,128)(2,1)S(1)} collective-permute-done((bf16[128,3712]{1,0:T(8,128)(2,1)S(1)}, bf16[128,3712]{1,0:T(8,128)(2,1)S(1)}, u32[]{:S(2)}, u32[]{:S(2)}) %collective-permute-start.6) | collective-permute-done | bytes 950304 | tf_op jit(solution)/shard_map/ppermute | solution.py:214
  50.0 1.4 %collective-permute-start.10 = (bf16[128,3712]{1,0:T(8,128)(2,1)S(1)}, bf16[128,3712]{1,0:T(8,128)(2,1)S(1)}, u32[]{:S(2)}, u32[]{:S(2)}) collective-permute-start(bf16[128,3712]{1,0:T(8,128)(2,1)S(1)} %collective-permute-done.6.refs_2_), channel_id=1, source_target_pairs={{4,0},{5,1},{8,4},{9,5},{12,8},{13,9},{14,12},{15,13},{10,14},{11,... | collective-permute-start | bytes 2850824 | tf_op jit(solution)/shard_map/ppermute | solution.py:214
  51.4 0.0 collective-permute-done.5.refs_1_
  51.4 0.7 collective-permute-start.9
  52.0 0.0 collective-permute-start.3
  52.0 0.9 copy-done.6
  53.0 0.0 collective-permute-done.refs_2_
  53.0 0.9 copy-done
  53.9 0.5 collective-permute-start.8
  54.4 0.9 copy-done.4
  55.4 0.0 collective-permute-done.4.refs_4_
  55.4 1.0 copy-done.8
  56.3 0.0 collective-permute-start.7
  56.3 15.1 %collective-permute-done.10.refs_2_ = bf16[128,3712]{1,0:T(8,128)(2,1)S(1)} collective-permute-done((bf16[128,3712]{1,0:T(8,128)(2,1)S(1)}, bf16[128,3712]{1,0:T(8,128)(2,1)S(1)}, u32[]{:S(2)}, u32[]{:S(2)}) %collective-permute-start.10) | collective-permute-done | bytes 950304 | tf_op jit(solution)/shard_map/ppermute | solution.py:214
  71.4 0.0 collective-permute-start.12
  71.4 1.0 collective-permute-done.9.refs_1_
  72.4 0.0 collective-permute-start.11
  72.5 0.0 collective-permute-done.3.refs_3_
  72.5 0.0 copy-start.12
  72.5 1.0 copy-done.12
  73.5 1.6 %collective-permute-start.14 = (bf16[64,3712]{1,0:T(8,128)(2,1)S(1)}, bf16[64,3712]{1,0:T(8,128)(2,1)S(1)}, u32[]{:S(2)}, u32[]{:S(2)}) collective-permute-start(bf16[64,3712]{1,0:T(8,128)(2,1)S(1)} %slice.9), channel_id=1, source_target_pairs={{4,0},{5,1},{8,4},{9,5},{12,8},{13,9},{14,12},{15,13},{10,14},{11,... | collective-permute-start | bytes 1425416 | tf_op jit(solution)/shard_map/ppermute | solution.py:221
  75.1 0.0 collective-permute-done.8.refs_4_
  75.1 0.9 copy-done.10
  76.0 0.4 collective-permute-start.13
  76.5 10.3 %collective-permute-done.14.refs_2_ = bf16[64,3712]{1,0:T(8,128)(2,1)S(1)} collective-permute-done((bf16[64,3712]{1,0:T(8,128)(2,1)S(1)}, bf16[64,3712]{1,0:T(8,128)(2,1)S(1)}, u32[]{:S(2)}, u32[]{:S(2)}) %collective-permute-start.14) | collective-permute-done | bytes 475168 | tf_op jit(solution)/shard_map/ppermute | solution.py:221
  86.8 0.0 collective-permute-start.16
  86.8 2.3 %collective-permute-done.13.refs_1_ = bf16[64,3712]{1,0:T(8,128)(2,1)} collective-permute-done((bf16[64,3712]{1,0:T(8,128)(2,1)S(1)}, bf16[64,3712]{1,0:T(8,128)(2,1)}, u32[]{:S(2)}, u32[]{:S(2)}) %collective-permute-start.13) | collective-permute-done | bytes 475168 | tf_op jit(solution)/shard_map/ppermute | solution.py:220
  89.1 0.0 collective-permute-start.15
  89.1 0.1 pad_add_fusion.refs_0_.scalars
  89.2 1.2 copy-done.1
  90.4 2.0 %absorb.5 = (f32[896,896]{1,0:T(8,128)S(1)}, bf16[64,3584]{1,0:T(8,128)(2,1)S(1)}) custom-call(s32[4]{0:T(128)S(1)} %pad_add_fusion.refs_0_.scalars, bf16[128,3712]{1,0:T(8,128)(2,1)S(1)} %make_message.1.refs_1_, bf16[128,3712]{1,0:T(8,128)(2,1)S(1)} %copy-done.1), custom_call_target="tpu_custom_call" | custom-call | flops 469762048 | bytes 8257536 | tf_op jit(solution)/shard_map/absorb/pallas_call | solution.py:116
  92.4 0.0 copy-start.3
  92.4 1.2 copy-done.3
  93.6 1.2 copy-done.7
  94.8 1.2 copy-done.9
  96.0 1.2 copy-done.13
  97.1 3.4 %absorb.6 = (f32[896,896]{1,0:T(8,128)S(1)}, bf16[128,3584]{1,0:T(8,128)(2,1)S(1)}) custom-call(s32[4]{0:T(128)S(1)} %pad_add_fusion.refs_0_.scalars, bf16[128,3712]{1,0:T(8,128)(2,1)S(1)} %copy-done.7, bf16[128,3712]{1,0:T(8,128)(2,1)S(1)} %copy-done.3, bf16[128,3712]{1,0:T(8,128)(2,1)S(1)} %copy-done.13, ...), custom_call_target="tpu_custom_call", output_to_operand_aliasing={{0}: (5, {})} | custom-call | flops 939524096 | bytes 10092544 | tf_op jit(solution)/shard_map/absorb/pallas_call | solution.py:116
  100.6 0.0 collective-permute-done.7.refs_3_
  100.6 0.0 copy-done.5
  100.6 0.0 copy-done.11
  100.6 4.3 %absorb.7 = (f32[896,896]{1,0:T(8,128)S(1)}, bf16[128,3584]{1,0:T(8,128)(2,1)S(1)}) custom-call(s32[4]{0:T(128)S(1)} %pad_add_fusion.refs_0_.scalars, bf16[128,3712]{1,0:T(8,128)(2,1)} %collective-permute-done.5.refs_1_, bf16[128,3712]{1,0:T(8,128)(2,1)S(1)} %copy-done.5, ...), custom_call_target="tpu_custom_call", output_to_operand_aliasing={{0}: (5, {})} | custom-call | flops 939524096 | bytes 10092544 | tf_op jit(solution)/shard_map/absorb/pallas_call | solution.py:116
  104.9 0.0 collective-permute-done.12.refs_4_
  105.0 0.0 collective-permute-done.11.refs_3_
  105.0 4.2 %absorb.8 = (f32[896,896]{1,0:T(8,128)S(1)}, bf16[128,3584]{1,0:T(8,128)(2,1)S(1)}) custom-call(s32[4]{0:T(128)S(1)} %pad_add_fusion.refs_0_.scalars, bf16[128,3712]{1,0:T(8,128)(2,1)S(1)} %collective-permute-done.9.refs_1_, bf16[128,3712]{1,0:T(8,128)(2,1)S(1)} %collective-permute-done.10.refs_2_, ...), custom_call_target="tpu_custom_call", output_to_operand_aliasing={{0}: (5, {})} | custom-call | flops 939524096 | bytes 10092544 | tf_op jit(solution)/shard_map/absorb/pallas_call | solution.py:116
  109.2 0.0 collective-permute-done.16.refs_4_
  109.2 0.0 collective-permute-done.15.refs_3_
  109.2 3.1 %absorb.9 = (f32[896,896]{1,0:T(8,128)S(1)}, bf16[64,3584]{1,0:T(8,128)(2,1)S(1)}) custom-call(s32[4]{0:T(128)S(1)} %pad_add_fusion.refs_0_.scalars, bf16[64,3712]{1,0:T(8,128)(2,1)} %collective-permute-done.13.refs_1_, bf16[64,3712]{1,0:T(8,128)(2,1)S(1)} %collective-permute-done.14.refs_2_, ...), custom_call_target="tpu_custom_call", output_to_operand_aliasing={{0}: (5, {})} | custom-call | flops 469762048 | bytes 8257536 | tf_op jit(solution)/shard_map/absorb/pallas_call | solution.py:116
  112.3 1.9 %multiply_bitcast_fusion = f32[1,896,896]{2,1,0:T(8,128)} fusion(f32[896,896]{1,0:T(8,128)S(1)} %get-tuple-element.21), kind=kLoop, calls=%fused_computation | loop fusion | flops 802816 | bytes 6422528 | tf_op jit(solution)/shard_map/broadcast_in_dim | solution.py:232
  114.2 15.2 %expert_product.1 = f32[1792,3584]{1,0:T(8,128)} custom-call(s32[4]{0:T(128)S(1)} %pad_add_fusion.refs_0_.scalars, bf16[64,3584]{1,0:T(8,128)(2,1)S(1)} %get-tuple-element.12.refs_0_, bf16[128,3584]{1,0:T(8,128)(2,1)S(1)} %get-tuple-element.14.refs_1_, bf16[128,3584]{1,0:T(8,128)(2,1)S(1)} %get-tuple-element.16.refs_2_, ...), custom_call_target="tpu_custom_call" | custom-call | flops 6576668672 | bytes 25690112 | tf_op jit(solution)/shard_map/expert_product/pallas_call | solution.py:164
  (13 shorter events, 0.1 us)
Async XLA Ops:
  2.2 1.2 copy-start.14
  3.6 24.1 %collective-permute-start.2 = (bf16[128,3712]{1,0:T(8,128)(2,1)S(1)}, bf16[128,3712]{1,0:T(8,128)(2,1)S(1)}, u32[]{:S(2)}, u32[]{:S(2)}) collective-permute-start(bf16[128,3712]{1,0:T(8,128)(2,1)S(1)} %make_message.1.refs_1_), channel_id=1, source_target_pairs={{4,0},{5,1},{8,4},{9,5},{12,8},{13,9},{14,12},{15,13},{10,14},{11,... | collective-permute-start | bytes 2850824 | tf_op jit(solution)/shard_map/ppermute | solution.py:214
  6.7 22.8 %collective-permute-start.1 = (bf16[128,3712]{1,0:T(8,128)(2,1)S(1)}, bf16[128,3712]{1,0:T(8,128)(2,1)S(1)}, u32[]{:S(2)}, u32[]{:S(2)}) collective-permute-start(bf16[128,3712]{1,0:T(8,128)(2,1)S(1)} %make_message.1.refs_1_), channel_id=1, source_target_pairs={{0,4},{1,5},{4,8},{5,9},{8,12},{9,13},{12,14},{13,15},{14,10},{15,... | collective-permute-start | bytes 2850824 | tf_op jit(solution)/shard_map/ppermute | solution.py:213
  27.8 22.2 %collective-permute-start.6 = (bf16[128,3712]{1,0:T(8,128)(2,1)S(1)}, bf16[128,3712]{1,0:T(8,128)(2,1)S(1)}, u32[]{:S(2)}, u32[]{:S(2)}) collective-permute-start(bf16[128,3712]{1,0:T(8,128)(2,1)S(1)} %collective-permute-done.2.refs_2_), channel_id=1, source_target_pairs={{4,0},{5,1},{8,4},{9,5},{12,8},{13,9},{14,12},{15,13},{10,14},{11,... | collective-permute-start | bytes 2850824 | tf_op jit(solution)/shard_map/ppermute | solution.py:214
  29.5 21.9 %collective-permute-start.5 = (bf16[128,3712]{1,0:T(8,128)(2,1)S(1)}, bf16[128,3712]{1,0:T(8,128)(2,1)}, u32[]{:S(2)}, u32[]{:S(2)}) collective-permute-start(bf16[128,3712]{1,0:T(8,128)(2,1)S(1)} %collective-permute-done.1.refs_1_), channel_id=1, source_target_pairs={{0,4},{1,5},{4,8},{5,9},{8,12},{9,13},{12,14},{13,15},{14,10},{15,... | collective-permute-start | bytes 2850824 | tf_op jit(solution)/shard_map/ppermute | solution.py:213
  29.8 23.2 %collective-permute-start = (bf16[128,3712]{1,0:T(8,128)(2,1)S(1)}, bf16[128,3712]{1,0:T(8,128)(2,1)S(1)}, u32[]{:S(2)}, u32[]{:S(2)}) collective-permute-start(bf16[128,3712]{1,0:T(8,128)(2,1)S(1)} %make_message.1.refs_1_), channel_id=1, source_target_pairs={{0,1},{1,0},{2,3},{3,2},{4,5},{5,4},{6,7},{7,6},{8,9},{9,8},{10,11... | collective-permute-start | bytes 2850824 | tf_op jit(solution)/shard_map/ppermute | solution.py:205
  29.8 25.6 %collective-permute-start.4 = (bf16[128,3712]{1,0:T(8,128)(2,1)S(1)}, bf16[128,3712]{1,0:T(8,128)(2,1)S(1)}, u32[]{:S(2)}, u32[]{:S(2)}) collective-permute-start(bf16[128,3712]{1,0:T(8,128)(2,1)S(1)} %collective-permute-done.2.refs_2_), channel_id=1, source_target_pairs={{0,1},{1,0},{2,3},{3,2},{4,5},{5,4},{6,7},{7,6},{8,9},{9,8},{10,11... | collective-permute-start | bytes 2850824 | tf_op jit(solution)/shard_map/ppermute | solution.py:205
  30.3 1.0 copy-start.2
  50.0 21.4 %collective-permute-start.10 = (bf16[128,3712]{1,0:T(8,128)(2,1)S(1)}, bf16[128,3712]{1,0:T(8,128)(2,1)S(1)}, u32[]{:S(2)}, u32[]{:S(2)}) collective-permute-start(bf16[128,3712]{1,0:T(8,128)(2,1)S(1)} %collective-permute-done.6.refs_2_), channel_id=1, source_target_pairs={{4,0},{5,1},{8,4},{9,5},{12,8},{13,9},{14,12},{15,13},{10,14},{11,... | collective-permute-start | bytes 2850824 | tf_op jit(solution)/shard_map/ppermute | solution.py:214
  51.4 21.0 %collective-permute-start.9 = (bf16[128,3712]{1,0:T(8,128)(2,1)}, bf16[128,3712]{1,0:T(8,128)(2,1)S(1)}, u32[]{:S(2)}, u32[]{:S(2)}) collective-permute-start(bf16[128,3712]{1,0:T(8,128)(2,1)} %collective-permute-done.5.refs_1_), channel_id=1, source_target_pairs={{0,4},{1,5},{4,8},{5,9},{8,12},{9,13},{12,14},{13,15},{14,10},{15,... | collective-permute-start | bytes 2850824 | tf_op jit(solution)/shard_map/ppermute | solution.py:213
  52.0 20.5 %collective-permute-start.3 = (bf16[128,3712]{1,0:T(8,128)(2,1)S(1)}, bf16[128,3712]{1,0:T(8,128)(2,1)S(1)}, u32[]{:S(2)}, u32[]{:S(2)}) collective-permute-start(bf16[128,3712]{1,0:T(8,128)(2,1)S(1)} %collective-permute-done.1.refs_1_), channel_id=1, source_target_pairs={{0,1},{1,0},{2,3},{3,2},{4,5},{5,4},{6,7},{7,6},{8,9},{9,8},{10,11... | collective-permute-start | bytes 2850824 | tf_op jit(solution)/shard_map/ppermute | solution.py:205
  52.0 0.9 copy-start.6
  53.0 0.9 copy-start
  53.9 21.2 %collective-permute-start.8 = (bf16[128,3712]{1,0:T(8,128)(2,1)S(1)}, bf16[128,3712]{1,0:T(8,128)(2,1)S(1)}, u32[]{:S(2)}, u32[]{:S(2)}) collective-permute-start(bf16[128,3712]{1,0:T(8,128)(2,1)S(1)} %collective-permute-done.6.refs_2_), channel_id=1, source_target_pairs={{0,1},{1,0},{2,3},{3,2},{4,5},{5,4},{6,7},{7,6},{8,9},{9,8},{10,11... | collective-permute-start | bytes 2850824 | tf_op jit(solution)/shard_map/ppermute | solution.py:205
  54.4 0.9 copy-start.4
  55.4 1.0 copy-start.8
  56.3 44.3 %collective-permute-start.7 = (bf16[128,3712]{1,0:T(8,128)(2,1)}, bf16[128,3712]{1,0:T(8,128)(2,1)}, u32[]{:S(2)}, u32[]{:S(2)}) collective-permute-start(bf16[128,3712]{1,0:T(8,128)(2,1)} %collective-permute-done.5.refs_1_), channel_id=1, source_target_pairs={{0,1},{1,0},{2,3},{3,2},{4,5},{5,4},{6,7},{7,6},{8,9},{9,8},{10,11... | collective-permute-start | bytes 2850824 | tf_op jit(solution)/shard_map/ppermute | solution.py:205
  71.4 33.5 %collective-permute-start.12 = (bf16[128,3712]{1,0:T(8,128)(2,1)S(1)}, bf16[128,3712]{1,0:T(8,128)(2,1)}, u32[]{:S(2)}, u32[]{:S(2)}) collective-permute-start(bf16[128,3712]{1,0:T(8,128)(2,1)S(1)} %collective-permute-done.10.refs_2_), channel_id=1, source_target_pairs={{0,1},{1,0},{2,3},{3,2},{4,5},{5,4},{6,7},{7,6},{8,9},{9,8},{10,11... | collective-permute-start | bytes 2850824 | tf_op jit(solution)/shard_map/ppermute | solution.py:205
  72.4 32.5 %collective-permute-start.11 = (bf16[128,3712]{1,0:T(8,128)(2,1)S(1)}, bf16[128,3712]{1,0:T(8,128)(2,1)}, u32[]{:S(2)}, u32[]{:S(2)}) collective-permute-start(bf16[128,3712]{1,0:T(8,128)(2,1)S(1)} %collective-permute-done.9.refs_1_), channel_id=1, source_target_pairs={{0,1},{1,0},{2,3},{3,2},{4,5},{5,4},{6,7},{7,6},{8,9},{9,8},{10,11... | collective-permute-start | bytes 2850824 | tf_op jit(solution)/shard_map/ppermute | solution.py:205
  72.5 1.0 copy-start.12
  73.5 13.3 %collective-permute-start.14 = (bf16[64,3712]{1,0:T(8,128)(2,1)S(1)}, bf16[64,3712]{1,0:T(8,128)(2,1)S(1)}, u32[]{:S(2)}, u32[]{:S(2)}) collective-permute-start(bf16[64,3712]{1,0:T(8,128)(2,1)S(1)} %slice.9), channel_id=1, source_target_pairs={{4,0},{5,1},{8,4},{9,5},{12,8},{13,9},{14,12},{15,13},{10,14},{11,... | collective-permute-start | bytes 1425416 | tf_op jit(solution)/shard_map/ppermute | solution.py:221
  75.1 0.9 copy-start.10
  76.0 13.1 %collective-permute-start.13 = (bf16[64,3712]{1,0:T(8,128)(2,1)S(1)}, bf16[64,3712]{1,0:T(8,128)(2,1)}, u32[]{:S(2)}, u32[]{:S(2)}) collective-permute-start(bf16[64,3712]{1,0:T(8,128)(2,1)S(1)} %slice.8), channel_id=1, source_target_pairs={{0,4},{1,5},{4,8},{5,9},{8,12},{9,13},{12,14},{13,15},{14,10},{15,... | collective-permute-start | bytes 1425416 | tf_op jit(solution)/shard_map/ppermute | solution.py:220
  86.8 22.4 %collective-permute-start.16 = (bf16[64,3712]{1,0:T(8,128)(2,1)S(1)}, bf16[64,3712]{1,0:T(8,128)(2,1)}, u32[]{:S(2)}, u32[]{:S(2)}) collective-permute-start(bf16[64,3712]{1,0:T(8,128)(2,1)S(1)} %collective-permute-done.14.refs_2_), channel_id=1, source_target_pairs={{0,1},{1,0},{2,3},{3,2},{4,5},{5,4},{6,7},{7,6},{8,9},{9,8},{10,11... | collective-permute-start | bytes 1425416 | tf_op jit(solution)/shard_map/ppermute | solution.py:205
  89.1 20.1 %collective-permute-start.15 = (bf16[64,3712]{1,0:T(8,128)(2,1)}, bf16[64,3712]{1,0:T(8,128)(2,1)}, u32[]{:S(2)}, u32[]{:S(2)}) collective-permute-start(bf16[64,3712]{1,0:T(8,128)(2,1)} %collective-permute-done.13.refs_1_), channel_id=1, source_target_pairs={{0,1},{1,0},{2,3},{3,2},{4,5},{5,4},{6,7},{7,6},{8,9},{9,8},{10,11... | collective-permute-start | bytes 1425416 | tf_op jit(solution)/shard_map/ppermute | solution.py:205
  89.2 1.2 copy-start.1
  92.4 1.2 copy-start.3
  93.6 1.2 copy-start.7
  94.8 1.2 copy-start.9
  96.0 1.2 copy-start.13
  97.1 3.5 %copy-start.5 = (bf16[128,3712]{1,0:T(8,128)(2,1)S(1)}, bf16[128,3712]{1,0:T(8,128)(2,1)}, u32[]{:S(2)}) copy-start(bf16[128,3712]{1,0:T(8,128)(2,1)} %copy-done.4) | copy-start | bytes 2850820
  97.1 3.5 %copy-start.11 = (bf16[128,3712]{1,0:T(8,128)(2,1)S(1)}, bf16[128,3712]{1,0:T(8,128)(2,1)}, u32[]{:S(2)}) copy-start(bf16[128,3712]{1,0:T(8,128)(2,1)} %copy-done.10) | copy-start | bytes 2850820

commit v4 on v3

v4 whole, which is shorter than its diff:
```python
import functools
import math

import jax
import jax.numpy as jnp
from jax import lax
from jax.experimental import pallas as pl
from jax.experimental.pallas import tpu as pltpu
from jax.sharding import PartitionSpec as P

EXP = 8
CAP = 32
CORES = 2
TABLE = 128
STEP = 256
BUFFERS = 3
VMEM = pl.BlockSpec(memory_space=pltpu.VMEM)
SMEM = pl.BlockSpec(memory_space=pltpu.SMEM)
ANY = pl.BlockSpec(memory_space=pl.ANY)
F32 = jnp.float32
BF16 = jnp.bfloat16
ROWS_WITH_ROWS = (((0,), (0,)), ((), ()))


def params(mib):
    return pltpu.CompilerParams(vmem_limit_bytes=mib * 2**20)


def message_kernel(tokens, ids, weights, out, arrived):
    rows, width = tokens.shape
    copy = pltpu.make_async_copy(tokens, out.at[:, :width], arrived)
    copy.start()
    row_at = lax.broadcasted_iota(jnp.int32, (TABLE, rows), 0)
    roots = jnp.zeros((TABLE, rows), F32)
    for e in range(EXP):
        root = jnp.sqrt(jnp.sum(jnp.where(ids[...] == e, weights[...], 0.0), axis=0, keepdims=True))
        roots = jnp.where(row_at % EXP == e, root, roots)
    high = roots.astype(BF16).astype(F32)
    middle = (roots - high).astype(BF16).astype(F32)
    low = roots - high - middle
    table = jnp.where(row_at < EXP, high, jnp.where(row_at < 2 * EXP, middle, low))
    out[:, width:] = jnp.where(row_at < 3 * EXP, table, 0.0).T.astype(BF16)
    copy.wait()


def make_message(tokens, ids, weights):
    rows, width = tokens.shape
    return pl.pallas_call(
        message_kernel,
        out_shape=jax.ShapeDtypeStruct((rows, width + TABLE), BF16),
        in_specs=[ANY, VMEM, VMEM],
        out_specs=VMEM,
        scratch_shapes=[pltpu.SemaphoreType.DMA],
        compiler_params=params(16),
        name="make_message",
    )(tokens, ids.T, weights.T)


def absorb_kernel(counts, grid, received, final, *refs):
    scalars, refs = refs[0], refs[1:]
    total = sum(counts)
    flat, refs = refs[:total], refs[total:]
    before, refs = refs[:received], refs[received:]
    tiles, packed, scratch = refs[: 1 if final else 2], refs[1 if final else 2], refs[-3:]
    if final:
        scratch = refs[-2:]
    pieces, at = [], 0
    for count in counts:
        pieces.append(flat[at : at + count])
        at += count
    width = packed.shape[1]
    edge = tiles[0].shape[-1]
    tok_rows = sum(ref.shape[0] for ref in pieces[0])
    expert = scalars[0]
    for slot, which in enumerate(scratch, start=1):
        for b in range(grid):

            @pl.when(scalars[slot] == b)
            def _(b=b, which=which):
                row = 0
                for ref in flat:
                    which[row : row + ref.shape[0], :] = ref[:, b * edge : (b + 1) * edge]
                    row += ref.shape[0]

    for k, tile in enumerate(tiles):
        update = lax.dot_general(
            scratch[0][...], scratch[1 + k][...], ROWS_WITH_ROWS, preferred_element_type=F32
        )
        if final:
            for ref in before:
                update = update + ref[...]
            tile[0, :, :] = update * final
        else:
            tile[...] = before[k][...] + update if before else update
    lane = lax.broadcasted_iota(jnp.int32, (tok_rows, TABLE), 1)
    ours = jnp.logical_and(lane % EXP == expert, lane < 3 * EXP)
    row_at = lax.broadcasted_iota(jnp.int32, (tok_rows, tok_rows), 0)
    column_at = lax.broadcasted_iota(jnp.int32, (tok_rows, tok_rows), 1)
    upto = (column_at <= row_at).astype(F32).astype(BF16)
    slot_at = lax.broadcasted_iota(jnp.int32, (tok_rows, CAP), 1)
    for k, parts in enumerate(pieces):
        table = jnp.concatenate([ref[:, width:].astype(F32) for ref in parts], axis=0)
        root = jnp.sum(jnp.where(ours, table, 0.0), axis=1, keepdims=True)
        member = root > 0.0
        counted = jnp.dot(
            upto,
            jnp.broadcast_to(member.astype(F32), (tok_rows, TABLE)).astype(BF16),
            preferred_element_type=F32,
        )
        place = counted[:, :CAP].astype(jnp.int32) - 1
        select = jnp.logical_and(member, place == slot_at).astype(F32).astype(BF16)
        row, result = 0, None
        for ref in parts:
            rows = ref.shape[0]
            scaled = (ref[:, :width].astype(F32) * root[row : row + rows]).astype(BF16)
            term = lax.dot_general(
                select[row : row + rows], scaled, ROWS_WITH_ROWS, preferred_element_type=F32
            )
            result = term if result is None else result + term
            row += rows
        packed[k * CAP : (k + 1) * CAP, :] = result.astype(BF16)


def absorb(scalars, pieces, before, grid, edge, width, final=None):
    flat = [ref for parts in pieces for ref in parts]
    rows = sum(ref.shape[0] for ref in flat)
    tiles = 1 if final else 2
    tile_shape = (1, edge, edge) if final else (edge, edge)
    return pl.pallas_call(
        functools.partial(
            absorb_kernel, [len(parts) for parts in pieces], grid, len(before), final
        ),
        out_shape=[jax.ShapeDtypeStruct(tile_shape, F32)] * tiles
        + [jax.ShapeDtypeStruct((len(pieces) * CAP, width), BF16)],
        in_specs=[SMEM] + [VMEM] * (len(flat) + len(before)),
        out_specs=[VMEM] * (tiles + 1),
        scratch_shapes=[pltpu.VMEM((rows, edge), BF16)] * (tiles + 1),
        cost_estimate=pl.CostEstimate(
            flops=2 * tiles * rows * edge * edge + 2 * CAP * rows * width,
            bytes_accessed=2 * rows * width + 8 * edge * edge,
            transcendentals=0,
        ),
        input_output_aliases={} if final or not before else {1 + len(flat): 0, 2 + len(flat): 1},
        compiler_params=params(32),
        name="absorb",
    )(scalars, *flat, *before)


def place_rows(scalars, pack, at, rows, across, slab):
    rows[at : at + pack.shape[0], :] = pack[...]
    for s in range(rows.shape[1] // slab):

        @pl.when(scalars[4] == s)
        def _(s=s):
            across[:, at : at + pack.shape[0]] = pack[:, s * slab : (s + 1) * slab].T


def prepare_kernel(scalars, *refs):
    *packs, rows, across = refs
    at = 0
    for pack in packs:
        place_rows(scalars, pack, at, rows, across, across.shape[0])
        at += pack.shape[0]


def expert_kernel(scalars, rows_in, across_in, pack, out, rows, across, block, sent):
    slab, width = out.shape
    total = rows.shape[0]
    first = total - pack.shape[0]
    place_rows(scalars, pack, first, rows, across, slab)

    def copy(n, slot):
        start = pl.multiple_of(n * STEP, STEP)
        return pltpu.make_async_copy(
            block.at[slot], out.at[:, pl.ds(start, STEP)], sent.at[slot]
        )

    def body(n, _):
        slot = lax.rem(n, BUFFERS)

        @pl.when(n >= BUFFERS)
        def _():
            copy(n - BUFFERS, slot).wait()

        start = pl.multiple_of(n * STEP, STEP)
        block[slot] = jnp.dot(
            across[...], rows[:, pl.ds(start, STEP)], preferred_element_type=F32
        ) * (1.0 / (16.0 * CAP))
        copy(n, slot).start()
        return 0

    count = width // STEP
    lax.fori_loop(0, count, body, 0)
    for n in range(max(count - BUFFERS, 0), count):
        copy(n, n % BUFFERS).wait()


def expert_product(scalars, packs, last, slab):
    width = last.shape[1]
    ready = sum(pack.shape[0] for pack in packs)
    total = ready + last.shape[0]
    shapes = [jax.ShapeDtypeStruct((total, width), BF16), jax.ShapeDtypeStruct((slab, total), BF16)]
    rows, across = pl.pallas_call(
        prepare_kernel,
        out_shape=shapes,
        in_specs=[SMEM] + [VMEM] * len(packs),
        out_specs=[VMEM] * 2,
        compiler_params=params(32),
        name="prepare_rows",
    )(scalars, *packs)
    return pl.pallas_call(
        expert_kernel,
        out_shape=[jax.ShapeDtypeStruct((slab, width), F32)] + shapes,
        in_specs=[SMEM] + [VMEM] * 3,
        out_specs=[ANY, VMEM, VMEM],
        scratch_shapes=[
            pltpu.VMEM((BUFFERS, slab, STEP), F32),
            pltpu.SemaphoreType.DMA((BUFFERS,)),
        ],
        input_output_aliases={1: 1, 2: 2},
        cost_estimate=pl.CostEstimate(
            flops=2 * slab * total * width, bytes_accessed=4 * slab * width, transcendentals=0
        ),
        compiler_params=params(40),
        name="expert_product",
    )(scalars, rows, across, last)[0]


def ring_of(chips):
    return list(range(0, chips, 2)) + list(range(chips - 1, 0, -2))


def on_device(tokens, route_ids, route_weights):
    devices = lax.axis_size("tok")
    position = lax.axis_index("tok")
    tok_rows, width = tokens.shape
    grid = math.isqrt(devices)
    edge = width // grid
    group = devices // EXP
    slab_rows = width // group
    chips = devices // CORES
    ring = ring_of(chips)
    ahead = [
        (ring[i] * CORES + c, ring[(i + 1) % chips] * CORES + c)
        for i in range(chips)
        for c in range(CORES)
    ]
    back = [(b, a) for a, b in ahead]
    pair = [(d, d ^ 1) for d in range(devices)]
    column = position % grid
    scalars = jnp.stack(
        [
            position // group,
            position // grid,
            column,
            column + 1 - 2 * (column % 2),
            position % group,
        ]
    ).astype(jnp.int32)

    own = make_message(tokens, route_ids, route_weights)
    going, coming = own, own
    arrived = [[own]]
    tiles, packs, exchanged = [], [], []
    for step in range(1, chips // 2):
        going = lax.ppermute(going, "tok", ahead)
        coming = lax.ppermute(coming, "tok", back)
        *tiles, packed = absorb(scalars, arrived, tiles, grid, edge, width)
        going, coming, packed, *tiles = lax.optimization_barrier((going, coming, packed, *tiles))
        packs.append(packed)
        exchanged.append(lax.ppermute(packed, "tok", pair))
        arrived = [[going], [coming]]
    half = tok_rows // 2
    last = [
        lax.ppermute(going[:half], "tok", ahead),
        lax.ppermute(coming[half:], "tok", back),
    ]
    *tiles, packed = absorb(scalars, arrived, tiles, grid, edge, width)
    other_tile = lax.ppermute(tiles[1], "tok", pair)
    packs.append(packed)
    exchanged.append(lax.ppermute(packed, "tok", pair))
    pieces = [last, [lax.ppermute(rows, "tok", pair) for rows in last]]
    tile, packed = absorb(
        scalars, pieces, [tiles[0], other_tile], grid, edge, width, 1.0 / (devices * tok_rows)
    )
    return (expert_product(scalars, packs + exchanged, packed, slab_rows), tile)


def solution(mesh):
    in_specs = (P(("grp", "tok"), None), P(("grp", "tok"), None), P(("grp", "tok"), None))
    out_specs = (P(("grp", "tok"), None), P(("grp", "tok"), None, None))
    return jax.shard_map(
        on_device, mesh=mesh, in_specs=in_specs, out_specs=out_specs, check_vma=False
    )
```

time: 130 us -> 113 us (0.87)
  local copies, waits for them, and re-layouts: 15.5 us -> 2.7 us
  Pallas kernels: 32.4 us -> 29.2 us
  other arithmetic: 1.97 us -> 0 us
    ppermute x3, waiting for transfers between devices: 54.8 us -> 20.4 us  [on_device(): coming = lax.ppermute(coming, 'tok', back)]
    ppermute x3, waiting for transfers between devices: 0.98 us -> 34.1 us  [on_device(): going = lax.ppermute(going, 'tok', ahead)]
    unnamed x32 -> x6, local copies, waits for them, and re-layouts: 15.4 us -> 2.54 us
    ppermute x1, waiting for transfers between devices: 10.3 us -> 1.37 us  [on_device(): lax.ppermute(coming[half:], 'tok', back)]
    ppermute x1, waiting for transfers between devices: 2.35 us -> 10.6 us  [on_device(): lax.ppermute(going[:half], 'tok', ahead)]
    pallas_call x5, Pallas kernels: 17 us -> 14 us  [absorb(): pl.pallas_call(functools.partial(absorb_kernel, [len(parts) for parts in...]
    ppermute x9 -> x7, waiting for transfers between devices: 0.03 us -> 2.58 us  [the longest x4 2.57 us: on_device(): exchanged.append(lax.ppermute(packed, 'tok', pair))]
    broadcast_in_dim x1 -> x0, other arithmetic: 1.89 us -> none  [on_device(): return (expert_part, (tile * (1.0 / (devices * tok_rows)))[None])]
  transfers between devices with their start and end apart: 17 -> 15, of which waited for: 6 -> 10; matrix products, arithmetic and copies ran while one was open for 0% -> 0% of each run, Pallas kernels for 11% -> 10%
where the time goes in v4:
time: 113 us; the launch traced here: 112 us
  waiting for transfers between devices  69 us (61%)
  Pallas kernels  29.2 us (26%)
  starting transfers between devices  10.5 us (9%)
  local copies, waits for them, and re-layouts  2.7 us (2%)
    ppermute x3, waiting for transfers between devices, on_device(): going = lax.ppermute(going, 'tok', ahead)  34.1 us
    ppermute x3, waiting for transfers between devices, on_device(): coming = lax.ppermute(coming, 'tok', back)  20.4 us
    pallas_call x5, Pallas kernels, absorb(): pl.pallas_call(functools.partial(absorb_kernel, [len(parts) for parts in...  14 us
    pallas_call x1, Pallas kernels, expert_product(): pl.pallas_call(expert_kernel, out_shape=[jax.ShapeDtypeStruct((slab, widt...  11.3 us
    ppermute x1, waiting for transfers between devices, on_device(): lax.ppermute(going[:half], 'tok', ahead)  10.6 us
    ppermute x3, starting transfers between devices, on_device(): coming = lax.ppermute(coming, 'tok', back)  5.15 us
    pallas_call x1, Pallas kernels, expert_product(): pl.pallas_call(prepare_kernel, out_shape=shapes, in_specs=[SMEM] + [VMEM]...  3.6 us
    ppermute x4, waiting for transfers between devices, on_device(): exchanged.append(lax.ppermute(packed, 'tok', pair))  2.57 us
  transfers between devices with their start and end apart: 15, of which 10 were waited for; matrix products, arithmetic and copies ran while one was open for 0% of the time, Pallas kernels for 10%

profile of v4, /device:TPU:0, one launch (start us, length us, event | category | flops | bytes accessed | tf_op | source)
XLA Modules:
  0.0 112.3 jit_solution(12259474740544542881)
XLA Ops:
  0.6 0.0 copy-start
  0.6 1.2 %copy-done = bf16[128,3584]{1,0:T(8,128)(2,1)S(1)} copy-done((bf16[128,3584]{1,0:T(8,128)(2,1)S(1)}, bf16[128,3584]{1,0:T(8,128)(2,1)}, u32[]{:S(2)}) %copy-start) | copy-done | bytes 917528
  1.8 0.0 copy-start.1
  1.8 0.7 copy-done.1
  2.5 0.0 copy-start.2
  2.5 0.7 copy-done.2
  3.2 0.2 make_message.1.refs_1_
  3.4 3.0 %collective-permute-start.1 = (bf16[128,3712]{1,0:T(8,128)(2,1)S(1)}, bf16[128,3712]{1,0:T(8,128)(2,1)S(1)}, u32[]{:S(2)}, u32[]{:S(2)}) collective-permute-start(bf16[128,3712]{1,0:T(8,128)(2,1)S(1)} %make_message.1.refs_1_), channel_id=1, source_target_pairs={{4,0},{5,1},{8,4},{9,5},{12,8},{13,9},{14,12},{15,13},{10,14},{11,... | collective-permute-start | bytes 2850824 | tf_op jit(solution)/shard_map/ppermute | solution.py:267
  6.4 0.1 collective-permute-start
  6.5 0.1 stack.23.refs_0_.scalars
  6.6 2.0 %absorb.5 = (f32[896,896]{1,0:T(8,128)S(1)}, f32[896,896]{1,0:T(8,128)S(1)}, bf16[32,3584]{1,0:T(8,128)(2,1)S(1)}) custom-call(s32[5]{0:T(128)S(1)} %stack.23.refs_0_.scalars, bf16[128,3712]{1,0:T(8,128)(2,1)S(1)} %make_message.1.refs_1_), custom_call_target="tpu_custom_call" | custom-call | flops 440401920 | bytes 7340032 | tf_op jit(solution)/shard_map/absorb/pallas_call | solution.py:129
  8.6 18.9 %collective-permute-done.1.refs_2_ = bf16[128,3712]{1,0:T(8,128)(2,1)S(1)} collective-permute-done((bf16[128,3712]{1,0:T(8,128)(2,1)S(1)}, bf16[128,3712]{1,0:T(8,128)(2,1)S(1)}, u32[]{:S(2)}, u32[]{:S(2)}) %collective-permute-start.1) | collective-permute-done | bytes 950304 | tf_op jit(solution)/shard_map/ppermute | solution.py:267
  27.5 1.4 %collective-permute-done.refs_1_ = bf16[128,3712]{1,0:T(8,128)(2,1)S(1)} collective-permute-done((bf16[128,3712]{1,0:T(8,128)(2,1)S(1)}, bf16[128,3712]{1,0:T(8,128)(2,1)S(1)}, u32[]{:S(2)}, u32[]{:S(2)}) %collective-permute-start) | collective-permute-done | bytes 950304 | tf_op jit(solution)/shard_map/ppermute | solution.py:266
  28.9 0.4 collective-permute-start.2
  29.3 1.6 %collective-permute-start.3 = (bf16[128,3712]{1,0:T(8,128)(2,1)S(1)}, bf16[128,3712]{1,0:T(8,128)(2,1)S(1)}, u32[]{:S(2)}, u32[]{:S(2)}) collective-permute-start(bf16[128,3712]{1,0:T(8,128)(2,1)S(1)} %collective-permute-done.1.refs_2_), channel_id=1, source_target_pairs={{4,0},{5,1},{8,4},{9,5},{12,8},{13,9},{14,12},{15,13},{10,14},{11,... | collective-permute-start | bytes 2850824 | tf_op jit(solution)/shard_map/ppermute | solution.py:267
  31.0 2.8 %absorb.6 = (f32[896,896]{1,0:T(8,128)S(1)}, f32[896,896]{1,0:T(8,128)S(1)}, bf16[64,3584]{1,0:T(8,128)(2,1)S(1)}) custom-call(s32[5]{0:T(128)S(1)} %stack.23.refs_0_.scalars, bf16[128,3712]{1,0:T(8,128)(2,1)S(1)} %collective-permute-done.refs_1_, ...), custom_call_target="tpu_custom_call", output_to_operand_aliasing={{0}: (3, {}), {1}: (4, {})} | custom-call | flops 880803840 | bytes 8257536 | tf_op jit(solution)/shard_map/absorb/pallas_call | solution.py:129
  33.7 16.8 %collective-permute-done.2.refs_1_ = bf16[128,3712]{1,0:T(8,128)(2,1)S(1)} collective-permute-done((bf16[128,3712]{1,0:T(8,128)(2,1)S(1)}, bf16[128,3712]{1,0:T(8,128)(2,1)S(1)}, u32[]{:S(2)}, u32[]{:S(2)}) %collective-permute-start.2) | collective-permute-done | bytes 950304 | tf_op jit(solution)/shard_map/ppermute | solution.py:266
  50.5 0.4 collective-permute-done.3.refs_2_
  51.0 1.5 %collective-permute-start.4 = (bf16[128,3712]{1,0:T(8,128)(2,1)S(1)}, bf16[128,3712]{1,0:T(8,128)(2,1)S(1)}, u32[]{:S(2)}, u32[]{:S(2)}) collective-permute-start(bf16[128,3712]{1,0:T(8,128)(2,1)S(1)} %collective-permute-done.2.refs_1_), channel_id=1, source_target_pairs={{0,4},{1,5},{4,8},{5,9},{8,12},{9,13},{12,14},{13,15},{14,10},{15,... | collective-permute-start | bytes 2850824 | tf_op jit(solution)/shard_map/ppermute | solution.py:266
  52.5 0.5 collective-permute-start.5
  53.0 2.8 %absorb.7 = (f32[896,896]{1,0:T(8,128)S(1)}, f32[896,896]{1,0:T(8,128)S(1)}, bf16[64,3584]{1,0:T(8,128)(2,1)S(1)}) custom-call(s32[5]{0:T(128)S(1)} %stack.23.refs_0_.scalars, bf16[128,3712]{1,0:T(8,128)(2,1)S(1)} %collective-permute-done.2.refs_1_, ...), custom_call_target="tpu_custom_call", output_to_operand_aliasing={{0}: (3, {}), {1}: (4, {})} | custom-call | flops 880803840 | bytes 8257536 | tf_op jit(solution)/shard_map/absorb/pallas_call | solution.py:129
  55.8 15.9 %collective-permute-done.4.refs_1_ = bf16[128,3712]{1,0:T(8,128)(2,1)S(1)} collective-permute-done((bf16[128,3712]{1,0:T(8,128)(2,1)S(1)}, bf16[128,3712]{1,0:T(8,128)(2,1)S(1)}, u32[]{:S(2)}, u32[]{:S(2)}) %collective-permute-start.4) | collective-permute-done | bytes 950304 | tf_op jit(solution)/shard_map/ppermute | solution.py:266
  71.7 1.1 collective-permute-done.5.refs_2_
  72.8 2.8 %absorb.8 = (f32[896,896]{1,0:T(8,128)S(1)}, f32[896,896]{1,0:T(8,128)S(1)}, bf16[64,3584]{1,0:T(8,128)(2,1)S(1)}) custom-call(s32[5]{0:T(128)S(1)} %stack.23.refs_0_.scalars, bf16[128,3712]{1,0:T(8,128)(2,1)S(1)} %collective-permute-done.4.refs_1_, ...), custom_call_target="tpu_custom_call", output_to_operand_aliasing={{0}: (3, {}), {1}: (4, {})} | custom-call | flops 880803840 | bytes 8257536 | tf_op jit(solution)/shard_map/absorb/pallas_call | solution.py:129
  75.6 0.1 collective-permute-start.14
  75.7 1.6 %collective-permute-start.10 = (bf16[64,3712]{1,0:T(8,128)(2,1)S(1)}, bf16[64,3712]{1,0:T(8,128)(2,1)S(1)}, u32[]{:S(2)}, u32[]{:S(2)}) collective-permute-start(bf16[64,3712]{1,0:T(8,128)(2,1)S(1)} %slice.6), channel_id=1, source_target_pairs={{0,4},{1,5},{4,8},{5,9},{8,12},{9,13},{12,14},{13,15},{14,10},{15,... | collective-permute-start | bytes 1425416 | tf_op jit(solution)/shard_map/ppermute | solution.py:275
  77.4 0.5 collective-permute-start.11
  77.9 0.0 collective-permute-start.7
  77.9 0.5 collective-permute-start.6
  78.4 10.6 %collective-permute-done.10.refs_1_ = bf16[64,3712]{1,0:T(8,128)(2,1)S(1)} collective-permute-done((bf16[64,3712]{1,0:T(8,128)(2,1)S(1)}, bf16[64,3712]{1,0:T(8,128)(2,1)S(1)}, u32[]{:S(2)}, u32[]{:S(2)}) %collective-permute-start.10) | collective-permute-done | bytes 475168 | tf_op jit(solution)/shard_map/ppermute | solution.py:275
  89.0 0.0 collective-permute-start.12
  89.0 1.4 %collective-permute-done.11.refs_2_ = bf16[64,3712]{1,0:T(8,128)(2,1)S(1)} collective-permute-done((bf16[64,3712]{1,0:T(8,128)(2,1)S(1)}, bf16[64,3712]{1,0:T(8,128)(2,1)S(1)}, u32[]{:S(2)}, u32[]{:S(2)}) %collective-permute-start.11) | collective-permute-done | bytes 475168 | tf_op jit(solution)/shard_map/ppermute | solution.py:276
  90.4 0.0 collective-permute-start.13
  90.4 0.0 collective-permute-done.6.refs_4_
  90.4 0.5 collective-permute-start.9
  90.9 0.0 collective-permute-done.7.refs_5_
  90.9 0.1 collective-permute-start.8
  91.0 1.9 %collective-permute-done.9.refs_7_ = bf16[64,3584]{1,0:T(8,128)(2,1)S(1)} collective-permute-done((bf16[64,3584]{1,0:T(8,128)(2,1)S(1)}, bf16[64,3584]{1,0:T(8,128)(2,1)S(1)}, u32[]{:S(2)}, u32[]{:S(2)}) %collective-permute-start.9) | collective-permute-done | bytes 458784 | tf_op jit(solution)/shard_map/ppermute | solution.py:281
  92.9 0.7 collective-permute-done.8.refs_6_
  93.6 3.6 %prepare_rows.1 = (bf16[512,3584]{1,0:T(8,128)(2,1)S(1)}, bf16[1792,512]{1,0:T(8,128)(2,1)S(1)}) custom-call(s32[5]{0:T(128)S(1)} %stack.23.refs_0_.scalars, bf16[32,3584]{1,0:T(8,128)(2,1)S(1)} %get-tuple-element.37.refs_0_, bf16[64,3584]{1,0:T(8,128)(2,1)S(1)} %get-tuple-element.45.refs_1_, bf16[64,3584]{1,0:T(8,128)(2,1)S(1)} %get-tuple-element.53.refs_2_, ...), custom_call_target="tpu_custom_call" | custom-call | tf_op jit(solution)/shard_map/prepare_rows/pallas_call | solution.py:203
  97.2 0.0 collective-permute-done.12.refs_3_
  97.2 0.0 collective-permute-done.13.refs_4_
  97.2 0.0 collective-permute-done.14.refs_6_
  97.2 3.6 %absorb.9 = (f32[1,896,896]{2,1,0:T(8,128)}, bf16[64,3584]{1,0:T(8,128)(2,1)S(1)}) custom-call(s32[5]{0:T(128)S(1)} %stack.23.refs_0_.scalars, bf16[64,3712]{1,0:T(8,128)(2,1)S(1)} %collective-permute-done.10.refs_1_, bf16[64,3712]{1,0:T(8,128)(2,1)S(1)} %collective-permute-done.11.refs_2_, bf16[64,3712]{1,0:T(8,128)(2,1)S(1)} %collective-permute-done.12.refs_3_, ...), custom_call_target="tpu_custom_call" | custom-call | flops 469762048 | bytes 8257536 | tf_op jit(solution)/shard_map/absorb/pallas_call | solution.py:129
  100.8 11.3 %expert_product.1 = (f32[1792,3584]{1,0:T(8,128)}, bf16[512,3584]{1,0:T(8,128)(2,1)S(1)}, bf16[1792,512]{1,0:T(8,128)(2,1)S(1)}) custom-call(s32[5]{0:T(128)S(1)} %stack.23.refs_0_.scalars, bf16[512,3584]{1,0:T(8,128)(2,1)S(1)} %get-tuple-element.59.rows_in, ...), custom_call_target="tpu_custom_call", output_to_operand_aliasing={{1}: (1, {}), {2}: (2, {})} | custom-call | flops 6576668672 | bytes 25690112 | tf_op jit(solution)/shard_map/expert_product/pallas_call | solution.py:211
  (2 shorter events, 0.1 us)
Async XLA Ops:
  0.6 1.2 %copy-start = (bf16[128,3584]{1,0:T(8,128)(2,1)S(1)}, bf16[128,3584]{1,0:T(8,128)(2,1)}, u32[]{:S(2)}) copy-start(bf16[128,3584]{1,0:T(8,128)(2,1)} %tokens.1) | copy-start | bytes 2752516
  1.8 0.7 copy-start.1
  2.5 0.7 copy-start.2
  3.4 24.1 %collective-permute-start.1 = (bf16[128,3712]{1,0:T(8,128)(2,1)S(1)}, bf16[128,3712]{1,0:T(8,128)(2,1)S(1)}, u32[]{:S(2)}, u32[]{:S(2)}) collective-permute-start(bf16[128,3712]{1,0:T(8,128)(2,1)S(1)} %make_message.1.refs_1_), channel_id=1, source_target_pairs={{4,0},{5,1},{8,4},{9,5},{12,8},{13,9},{14,12},{15,13},{10,14},{11,... | collective-permute-start | bytes 2850824 | tf_op jit(solution)/shard_map/ppermute | solution.py:267
  6.4 22.5 %collective-permute-start = (bf16[128,3712]{1,0:T(8,128)(2,1)S(1)}, bf16[128,3712]{1,0:T(8,128)(2,1)S(1)}, u32[]{:S(2)}, u32[]{:S(2)}) collective-permute-start(bf16[128,3712]{1,0:T(8,128)(2,1)S(1)} %make_message.1.refs_1_), channel_id=1, source_target_pairs={{0,4},{1,5},{4,8},{5,9},{8,12},{9,13},{12,14},{13,15},{14,10},{15,... | collective-permute-start | bytes 2850824 | tf_op jit(solution)/shard_map/ppermute | solution.py:266
  28.9 21.6 %collective-permute-start.2 = (bf16[128,3712]{1,0:T(8,128)(2,1)S(1)}, bf16[128,3712]{1,0:T(8,128)(2,1)S(1)}, u32[]{:S(2)}, u32[]{:S(2)}) collective-permute-start(bf16[128,3712]{1,0:T(8,128)(2,1)S(1)} %collective-permute-done.refs_1_), channel_id=1, source_target_pairs={{0,4},{1,5},{4,8},{5,9},{8,12},{9,13},{12,14},{13,15},{14,10},{15,... | collective-permute-start | bytes 2850824 | tf_op jit(solution)/shard_map/ppermute | solution.py:266
  29.3 21.6 %collective-permute-start.3 = (bf16[128,3712]{1,0:T(8,128)(2,1)S(1)}, bf16[128,3712]{1,0:T(8,128)(2,1)S(1)}, u32[]{:S(2)}, u32[]{:S(2)}) collective-permute-start(bf16[128,3712]{1,0:T(8,128)(2,1)S(1)} %collective-permute-done.1.refs_2_), channel_id=1, source_target_pairs={{4,0},{5,1},{8,4},{9,5},{12,8},{13,9},{14,12},{15,13},{10,14},{11,... | collective-permute-start | bytes 2850824 | tf_op jit(solution)/shard_map/ppermute | solution.py:267
  51.0 20.7 %collective-permute-start.4 = (bf16[128,3712]{1,0:T(8,128)(2,1)S(1)}, bf16[128,3712]{1,0:T(8,128)(2,1)S(1)}, u32[]{:S(2)}, u32[]{:S(2)}) collective-permute-start(bf16[128,3712]{1,0:T(8,128)(2,1)S(1)} %collective-permute-done.2.refs_1_), channel_id=1, source_target_pairs={{0,4},{1,5},{4,8},{5,9},{8,12},{9,13},{12,14},{13,15},{14,10},{15,... | collective-permute-start | bytes 2850824 | tf_op jit(solution)/shard_map/ppermute | solution.py:266
  52.5 20.3 %collective-permute-start.5 = (bf16[128,3712]{1,0:T(8,128)(2,1)S(1)}, bf16[128,3712]{1,0:T(8,128)(2,1)S(1)}, u32[]{:S(2)}, u32[]{:S(2)}) collective-permute-start(bf16[128,3712]{1,0:T(8,128)(2,1)S(1)} %collective-permute-done.3.refs_2_), channel_id=1, source_target_pairs={{4,0},{5,1},{8,4},{9,5},{12,8},{13,9},{14,12},{15,13},{10,14},{11,... | collective-permute-start | bytes 2850824 | tf_op jit(solution)/shard_map/ppermute | solution.py:267
  75.6 21.6 %collective-permute-start.14 = (f32[896,896]{1,0:T(8,128)S(1)}, f32[896,896]{1,0:T(8,128)S(1)}, u32[]{:S(2)}, u32[]{:S(2)}) collective-permute-start(f32[896,896]{1,0:T(8,128)S(1)} %get-tuple-element.62), channel_id=1, source_target_pairs={{0,1},{1,0},{2,3},{3,2},{4,5},{5,4},{6,7},{7,6},{8,9},{9,8},{10,11... | collective-permute-start | bytes 9633800 | tf_op jit(solution)/shard_map/ppermute | solution.py:279
  75.7 13.3 %collective-permute-start.10 = (bf16[64,3712]{1,0:T(8,128)(2,1)S(1)}, bf16[64,3712]{1,0:T(8,128)(2,1)S(1)}, u32[]{:S(2)}, u32[]{:S(2)}) collective-permute-start(bf16[64,3712]{1,0:T(8,128)(2,1)S(1)} %slice.6), channel_id=1, source_target_pairs={{0,4},{1,5},{4,8},{5,9},{8,12},{9,13},{12,14},{13,15},{14,10},{15,... | collective-permute-start | bytes 1425416 | tf_op jit(solution)/shard_map/ppermute | solution.py:275
  77.4 13.0 %collective-permute-start.11 = (bf16[64,3712]{1,0:T(8,128)(2,1)S(1)}, bf16[64,3712]{1,0:T(8,128)(2,1)S(1)}, u32[]{:S(2)}, u32[]{:S(2)}) collective-permute-start(bf16[64,3712]{1,0:T(8,128)(2,1)S(1)} %slice.7), channel_id=1, source_target_pairs={{4,0},{5,1},{8,4},{9,5},{12,8},{13,9},{14,12},{15,13},{10,14},{11,... | collective-permute-start | bytes 1425416 | tf_op jit(solution)/shard_map/ppermute | solution.py:276
  77.9 13.0 %collective-permute-start.7 = (bf16[64,3584]{1,0:T(8,128)(2,1)S(1)}, bf16[64,3584]{1,0:T(8,128)(2,1)S(1)}, u32[]{:S(2)}, u32[]{:S(2)}) collective-permute-start(bf16[64,3584]{1,0:T(8,128)(2,1)S(1)} %get-tuple-element.45.refs_1_), channel_id=1, source_target_pairs={{0,1},{1,0},{2,3},{3,2},{4,5},{5,4},{6,7},{7,6},{8,9},{9,8},{10,11... | collective-permute-start | bytes 1376264 | tf_op jit(solution)/shard_map/ppermute | solution.py:271
  77.9 12.5 %collective-permute-start.6 = (bf16[32,3584]{1,0:T(8,128)(2,1)S(1)}, bf16[32,3584]{1,0:T(8,128)(2,1)S(1)}, u32[]{:S(2)}, u32[]{:S(2)}) collective-permute-start(bf16[32,3584]{1,0:T(8,128)(2,1)S(1)} %get-tuple-element.37.refs_0_), channel_id=1, source_target_pairs={{0,1},{1,0},{2,3},{3,2},{4,5},{5,4},{6,7},{7,6},{8,9},{9,8},{10,11... | collective-permute-start | bytes 688136 | tf_op jit(solution)/shard_map/ppermute | solution.py:271
  89.0 8.1 %collective-permute-start.12 = (bf16[64,3712]{1,0:T(8,128)(2,1)S(1)}, bf16[64,3712]{1,0:T(8,128)(2,1)S(1)}, u32[]{:S(2)}, u32[]{:S(2)}) collective-permute-start(bf16[64,3712]{1,0:T(8,128)(2,1)S(1)} %collective-permute-done.10.refs_1_), channel_id=1, source_target_pairs={{0,1},{1,0},{2,3},{3,2},{4,5},{5,4},{6,7},{7,6},{8,9},{9,8},{10,11... | collective-permute-start | bytes 1425416 | tf_op jit(solution)/shard_map/ppermute | solution.py:282
  90.4 6.8 %collective-permute-start.13 = (bf16[64,3712]{1,0:T(8,128)(2,1)S(1)}, bf16[64,3712]{1,0:T(8,128)(2,1)S(1)}, u32[]{:S(2)}, u32[]{:S(2)}) collective-permute-start(bf16[64,3712]{1,0:T(8,128)(2,1)S(1)} %collective-permute-done.11.refs_2_), channel_id=1, source_target_pairs={{0,1},{1,0},{2,3},{3,2},{4,5},{5,4},{6,7},{7,6},{8,9},{9,8},{10,11... | collective-permute-start | bytes 1425416 | tf_op jit(solution)/shard_map/ppermute | solution.py:282
  90.4 2.5 %collective-permute-start.9 = (bf16[64,3584]{1,0:T(8,128)(2,1)S(1)}, bf16[64,3584]{1,0:T(8,128)(2,1)S(1)}, u32[]{:S(2)}, u32[]{:S(2)}) collective-permute-start(bf16[64,3584]{1,0:T(8,128)(2,1)S(1)} %get-tuple-element.58.refs_3_), channel_id=1, source_target_pairs={{0,1},{1,0},{2,3},{3,2},{4,5},{5,4},{6,7},{7,6},{8,9},{9,8},{10,11... | collective-permute-start | bytes 1376264 | tf_op jit(solution)/shard_map/ppermute | solution.py:281
  90.9 2.6 %collective-permute-start.8 = (bf16[64,3584]{1,0:T(8,128)(2,1)S(1)}, bf16[64,3584]{1,0:T(8,128)(2,1)S(1)}, u32[]{:S(2)}, u32[]{:S(2)}) collective-permute-start(bf16[64,3584]{1,0:T(8,128)(2,1)S(1)} %get-tuple-element.53.refs_2_), channel_id=1, source_target_pairs={{0,1},{1,0},{2,3},{3,2},{4,5},{5,4},{6,7},{7,6},{8,9},{9,8},{10,11... | collective-permute-start | bytes 1376264 | tf_op jit(solution)/shard_map/ppermute | solution.py:271

commit v5 on v1

v5 whole, which is shorter than its diff:
```python
import functools
import math

import jax
import jax.numpy as jnp
from jax import lax
from jax.experimental import pallas as pl
from jax.experimental.pallas import tpu as pltpu
from jax.sharding import PartitionSpec as P

EXP = 8
CAP = 32
CORES = 2
TABLE = 128
VMEM = pl.BlockSpec(memory_space=pltpu.VMEM)
SMEM = pl.BlockSpec(memory_space=pltpu.SMEM)
ANY = pl.BlockSpec(memory_space=pl.ANY)
F32 = jnp.float32
BF16 = jnp.bfloat16
ROWS_WITH_ROWS = (((0,), (0,)), ((), ()))
INVERSE = 1.0 / (16.0 * CAP)
SMALL = pl.CostEstimate(flops=1, bytes_accessed=1, transcendentals=0)


def params(mib):
    return pltpu.CompilerParams(vmem_limit_bytes=mib * 2**20)


def cuts_of(edge):
    first = edge * 4 // 7
    return [(0, first), (first, edge - first)] if edge % 896 == 0 else [(0, edge)]


def message_kernel(cuts, edge, *refs):
    tokens, ids_from, weights_from, *outs = refs
    *outs, ids, weights, small, arrived = outs
    tables = [
        pltpu.make_async_copy(ids_from, ids, small.at[0]),
        pltpu.make_async_copy(weights_from, weights, small.at[1]),
    ]
    for copy in tables:
        copy.start()
    rows, width = tokens.shape
    copies = []
    if len(cuts) == 1:
        copies = [pltpu.make_async_copy(tokens, outs[0].at[:, :width], arrived.at[0])]
    else:
        for (start, length), out in zip(cuts, outs):
            for b in range(width // edge):
                copies.append(
                    pltpu.make_async_copy(
                        tokens.at[:, b * edge + start : b * edge + start + length],
                        out.at[:, b * length : (b + 1) * length],
                        arrived.at[len(copies)],
                    )
                )
    for copy in copies:
        copy.start()
    for copy in tables:
        copy.wait()
    row_at = lax.broadcasted_iota(jnp.int32, (TABLE, rows), 0)
    roots = jnp.zeros((TABLE, rows), F32)
    for e in range(EXP):
        root = jnp.sqrt(jnp.sum(jnp.where(ids[...] == e, weights[...], 0.0), axis=0, keepdims=True))
        roots = jnp.where(row_at % EXP == e, root, roots)
    high = roots.astype(BF16).astype(F32)
    middle = (roots - high).astype(BF16).astype(F32)
    low = roots - high - middle
    table = jnp.where(row_at < EXP, high, jnp.where(row_at < 2 * EXP, middle, low))
    at = width // edge * cuts[0][1]
    outs[0][:, at : at + TABLE] = jnp.where(row_at < 3 * EXP, table, 0.0).T.astype(BF16)
    for copy in copies:
        copy.wait()


def make_message(tokens, ids, weights, cuts, edge):
    rows, width = tokens.shape
    grid = width // edge
    extra = [TABLE] + [0] * (len(cuts) - 1)
    return pl.pallas_call(
        functools.partial(message_kernel, cuts, edge),
        out_shape=[
            jax.ShapeDtypeStruct((rows, grid * length + more), BF16)
            for (_, length), more in zip(cuts, extra)
        ],
        in_specs=[ANY] * 3,
        out_specs=[VMEM] * len(cuts),
        scratch_shapes=[
            pltpu.VMEM(ids.shape[::-1], jnp.int32),
            pltpu.VMEM(ids.shape[::-1], F32),
            pltpu.SemaphoreType.DMA((2,)),
            pltpu.SemaphoreType.DMA((len(cuts) * grid,)),
        ],
        compiler_params=params(16),
        cost_estimate=SMALL,
        name="make_message",
    )(tokens, ids.T, weights.T)


def choose(expert, first, width):
    rows = first.shape[0]
    lane = lax.broadcasted_iota(jnp.int32, (rows, TABLE), 1)
    ours = jnp.logical_and(lane % EXP == expert, lane < 3 * EXP)
    table = first[:, width : width + TABLE].astype(F32)
    root = jnp.sum(jnp.where(ours, table, 0.0), axis=1, keepdims=True)
    member = root > 0.0
    row_at = lax.broadcasted_iota(jnp.int32, (rows, rows), 0)
    column_at = lax.broadcasted_iota(jnp.int32, (rows, rows), 1)
    upto = (column_at <= row_at).astype(F32).astype(BF16)
    counted = jnp.dot(
        upto,
        jnp.broadcast_to(member.astype(F32), (rows, TABLE)).astype(BF16),
        preferred_element_type=F32,
    )
    place = counted[:, :CAP].astype(jnp.int32) - 1
    slot_at = lax.broadcasted_iota(jnp.int32, (rows, CAP), 1)
    return root, jnp.logical_and(member, place == slot_at).astype(F32).astype(BF16)


def pack(root, select, piece, width):
    scaled = (piece[:, :width].astype(F32) * root).astype(BF16)
    return lax.dot_general(
        select, scaled, ROWS_WITH_ROWS, preferred_element_type=F32
    ).astype(BF16)


def fetch_tile(index, pieces, cuts, grid, scratch):
    for b in range(grid):

        @pl.when(index == b)
        def _(b=b):
            row = 0
            for piece in pieces:
                rows = piece[0].shape[0]
                for (start, length), part in zip(cuts, piece):
                    scratch[row : row + rows, start : start + length] = part[
                        :, b * length : (b + 1) * length
                    ]
                row += rows


def pack_kernel(*refs):
    scalars, *firsts, out = refs
    width = out.shape[1]
    for k, first in enumerate(firsts):
        root, select = choose(scalars[0], first, width)
        out[k * CAP : (k + 1) * CAP, :] = pack(root, select, first, width)


def pack_first(scalars, firsts):
    rows, width = firsts[0].shape
    width -= TABLE
    return pl.pallas_call(
        pack_kernel,
        out_shape=jax.ShapeDtypeStruct((len(firsts) * CAP, width), BF16),
        in_specs=[SMEM] + [VMEM] * len(firsts),
        out_specs=VMEM,
        cost_estimate=SMALL,
        compiler_params=params(12),
        name="pack_first",
    )(scalars, *firsts)


def absorb_kernel(cuts, grid, count, started, chosen, *refs):
    scalars, refs = refs[0], refs[1:]
    parts = len(cuts)
    pieces = [refs[k * parts : (k + 1) * parts] for k in range(count)]
    refs = refs[count * parts :]
    before, refs = refs[: 2 * started], refs[2 * started :]
    tiles, packed, scratch = refs[:2], refs[2:-3], refs[-3:]
    for slot, which in enumerate(scratch, start=1):
        fetch_tile(scalars[slot], pieces, cuts, grid, which)
    for k, tile in enumerate(tiles):
        update = lax.dot_general(
            scratch[0][...], scratch[1 + k][...], ROWS_WITH_ROWS, preferred_element_type=F32
        )
        tile[...] = before[k][...] + update if started else update
    if chosen:
        for k, piece in enumerate(pieces):
            root, select = choose(scalars[0], piece[0], grid * cuts[0][1])
            at = 0
            for p in chosen:
                size = grid * cuts[p][1]
                packed[0][k * CAP : (k + 1) * CAP, at : at + size] = pack(
                    root, select, piece[p], size
                )
                at += size


def absorb(scalars, pieces, before, cuts, grid, chosen):
    edge = sum(length for _, length in cuts)
    flat = [part for piece in pieces for part in piece]
    rows = sum(piece[0].shape[0] for piece in pieces)
    width = sum(grid * cuts[p][1] for p in chosen)
    shapes = [jax.ShapeDtypeStruct((edge, edge), F32)] * 2
    if chosen:
        shapes.append(jax.ShapeDtypeStruct((len(pieces) * CAP, width), BF16))
    out = pl.pallas_call(
        functools.partial(absorb_kernel, cuts, grid, len(pieces), bool(before), chosen),
        out_shape=shapes,
        in_specs=[SMEM] + [VMEM] * (len(flat) + len(before)),
        out_specs=[VMEM] * len(shapes),
        scratch_shapes=[pltpu.VMEM((rows, edge), BF16)] * 3,
        cost_estimate=SMALL,
        input_output_aliases={1 + len(flat): 0, 2 + len(flat): 1} if before else {},
        compiler_params=params(14),
        name="absorb",
    )(scalars, *flat, *before)
    return out[:2], out[2:]


def place_rows(slab_at, slabs, packed, begin, at, rows, across):
    count = packed.shape[0]
    width, share = rows.shape[1], across.shape[0]
    rows[at : at + count, :] = packed[:, begin : begin + width]
    for s in range(slabs):

        @pl.when(slab_at == s)
        def _(s=s):
            first = begin + s * share
            across[:, at : at + count] = packed[:, first : first + share].T


def prepare_kernel(slabs, places, *refs):
    scalars, *refs = refs
    rows, across = refs[-2:]
    for (at, begin), packed in zip(places, refs):
        place_rows(scalars[4], slabs, packed, begin, at, rows, across)


def prepare(scalars, packs, places, operands, shape, slabs):
    total, width = shape
    return pl.pallas_call(
        functools.partial(prepare_kernel, slabs, places),
        out_shape=[
            jax.ShapeDtypeStruct((total, width), BF16),
            jax.ShapeDtypeStruct((width // slabs, total), BF16),
        ],
        in_specs=[SMEM] + [VMEM] * (len(packs) + len(operands)),
        out_specs=[VMEM] * 2,
        input_output_aliases={1 + len(packs) + k: k for k in range(len(operands))},
        cost_estimate=SMALL,
        compiler_params=params(12),
        name="prepare_rows",
    )(scalars, *packs, *operands)


def pack_last(scalars, slabs, firsts, parts, rows, across):
    at = rows.shape[0] - CAP * len(parts)
    for first, part in zip(firsts, parts):
        root, select = choose(scalars[0], first, first.shape[1] - TABLE)
        packed = pack(root, select, part, rows.shape[1])
        rows[at : at + CAP, :] = packed
        share = across.shape[0]
        for s in range(slabs):

            @pl.when(scalars[4] == s)
            def _(s=s, at=at, packed=packed):
                across[:, at : at + CAP] = packed[:, s * share : (s + 1) * share].T

        at += CAP


def finish_first_kernel(cuts, grid, slabs, *refs):
    scalars, mine, other, _, _, out, rows, across, staging, sent = refs
    edge = sum(length for _, length in cuts)
    length = cuts[0][1]
    pack_last(scalars, slabs, [mine, other], [mine, other], rows, across)
    left = across[...]
    jobs = []
    if len(cuts) == 1:
        step = staging.shape[2]
        for n in range(staging.shape[0]):
            span = slice(n * step, (n + 1) * step)
            jobs.append(
                (left, rows.at[:, span], staging.at[n], [(slice(None), slice(None), span)])
            )
    else:
        for b in range(grid):
            places = [
                (
                    slice(i * length, (i + 1) * length),
                    slice(i * edge, i * edge + length),
                    slice(b * edge, b * edge + length),
                )
                for i in range(grid // slabs)
            ]
            jobs.append(
                (left, rows.at[:, b * length : (b + 1) * length], staging.at[b], places)
            )
    copies = []
    for left, right, stage, places in jobs:
        stage[...] = jnp.dot(left, right[...], preferred_element_type=F32) * INVERSE
        for source, rows_to, columns_to in places:
            copy = pltpu.make_async_copy(
                stage.at[source], out.at[rows_to, columns_to], sent.at[len(copies)]
            )
            copy.start()
            copies.append(copy)
    for copy in copies:
        copy.wait()


def finish_first(scalars, mine, other, operands, cuts, grid, slabs):
    edge = sum(length for _, length in cuts)
    slab, width = edge * grid // slabs, edge * grid
    rows, across = operands
    if len(cuts) == 1:
        step = 512
        staging = (width // step, slab, step)
        writes = width // step
    else:
        staging = (grid, across.shape[0], cuts[0][1])
        writes = grid * (grid // slabs)
    return pl.pallas_call(
        functools.partial(finish_first_kernel, cuts, grid, slabs),
        out_shape=[
            jax.ShapeDtypeStruct((slab, width), F32),
            jax.ShapeDtypeStruct(rows.shape, BF16),
            jax.ShapeDtypeStruct(across.shape, BF16),
        ],
        in_specs=[SMEM] + [VMEM] * 4,
        out_specs=[ANY, VMEM, VMEM],
        scratch_shapes=[pltpu.VMEM(staging, F32), pltpu.SemaphoreType.DMA((writes,))],
        input_output_aliases={3: 1, 4: 2},
        cost_estimate=SMALL,
        compiler_params=params(20),
        name="finish_first",
    )(scalars, mine, other, rows, across)


def finish_second_kernel(cuts, grid, slabs, final, *refs):
    parts = len(cuts)
    scalars, refs = refs[0], refs[1:]
    mine, refs = refs[:parts], refs[parts:]
    other, refs = refs[:parts], refs[parts:]
    before, refs = refs[:2], refs[2:]
    edge = sum(length for _, length in cuts)
    copies = []
    if parts == 2:
        rows_a, across_a, _, _, _, tile, out, rows_b, across_b = refs[:9]
        left, right, stage_ab, stage_ba, stage_bb, sent = refs[9:]
        pack_last(scalars, slabs, [mine[0], other[0]], [mine[1], other[1]], rows_b, across_b)
        (_, first), (start, length) = cuts
        tiles = grid // slabs

        def write(stage, source, rows_to, columns_to):
            copy = pltpu.make_async_copy(
                stage.at[source], out.at[rows_to, columns_to], sent.at[len(copies)]
            )
            copy.start()
            copies.append(copy)

        for pair in range(grid // 2):
            span = slice(2 * pair * length, 2 * (pair + 1) * length)
            for stage, across, begin, size in (
                (stage_ab.at[pair], across_a, 0, first),
                (stage_bb.at[pair], across_b, start, length),
            ):
                stage[...] = (
                    jnp.dot(across[...], rows_b[:, span], preferred_element_type=F32) * INVERSE
                )
                for j in range(2):
                    column = (2 * pair + j) * edge + start
                    for i in range(tiles):
                        write(
                            stage,
                            (slice(i * size, (i + 1) * size), slice(j * length, (j + 1) * length)),
                            slice(i * edge + begin, i * edge + begin + size),
                            slice(column, column + length),
                        )
        for b in range(grid):
            stage = stage_ba.at[b]
            stage[...] = (
                jnp.dot(
                    across_b[...], rows_a[:, b * first : (b + 1) * first],
                    preferred_element_type=F32,
                )
                * INVERSE
            )
            for i in range(tiles):
                write(
                    stage,
                    slice(i * length, (i + 1) * length),
                    slice(i * edge + start, i * edge + edge),
                    slice(b * edge, b * edge + first),
                )
    else:
        tile, left, right = refs
    pieces = [mine, other]
    fetch_tile(scalars[1], pieces, cuts, grid, left)
    fetch_tile(scalars[2], pieces, cuts, grid, right)
    update = lax.dot_general(left[...], right[...], ROWS_WITH_ROWS, preferred_element_type=F32)
    tile[0, :, :] = (before[0][...] + before[1][...] + update) * final
    for copy in copies:
        copy.wait()


def finish_second(scalars, mine, other, before, hessian, operands, cuts, grid, slabs, final):
    edge = sum(length for _, length in cuts)
    count = 2 * mine[0].shape[0]
    tile = jax.ShapeDtypeStruct((1, edge, edge), F32)
    scratch = [pltpu.VMEM((count, edge), BF16)] * 2
    inputs = [scalars, *mine, *other, *before]
    kernel = functools.partial(finish_second_kernel, cuts, grid, slabs, final)
    if len(cuts) == 1:
        return hessian, pl.pallas_call(
            kernel,
            out_shape=tile,
            in_specs=[SMEM] + [VMEM] * (len(inputs) - 1),
            out_specs=VMEM,
            scratch_shapes=scratch,
            compiler_params=params(20),
            name="finish_tile",
        )(*inputs)
    rows_a, across_a, rows_b, across_b = operands
    length = cuts[1][1]
    at = len(inputs)
    scratch += [
        pltpu.VMEM((grid // 2, across_a.shape[0], 2 * length), F32),
        pltpu.VMEM((grid, across_b.shape[0], cuts[0][1]), F32),
        pltpu.VMEM((grid // 2, across_b.shape[0], 2 * length), F32),
        pltpu.SemaphoreType.DMA((3 * grid * (grid // slabs),)),
    ]
    tile, hessian, _, _ = pl.pallas_call(
        kernel,
        out_shape=[
            tile,
            jax.ShapeDtypeStruct(hessian.shape, F32),
            jax.ShapeDtypeStruct(rows_b.shape, BF16),
            jax.ShapeDtypeStruct(across_b.shape, BF16),
        ],
        in_specs=[SMEM] + [VMEM] * (len(inputs) + 3) + [ANY],
        out_specs=[VMEM, ANY, VMEM, VMEM],
        scratch_shapes=scratch,
        input_output_aliases={at + 4: 1, at + 2: 2, at + 3: 3},
        compiler_params=params(32),
        cost_estimate=SMALL,
        name="finish_second",
    )(*inputs, rows_a, across_a, rows_b, across_b, hessian)
    return hessian, tile


def ring_of(chips):
    return list(range(0, chips, 2)) + list(range(chips - 1, 0, -2))


def on_device(tokens, route_ids, route_weights):
    devices = lax.axis_size("tok")
    position = lax.axis_index("tok")
    tok_rows, width = tokens.shape
    grid = math.isqrt(devices)
    edge = width // grid
    group = devices // EXP
    chips = devices // CORES
    cuts = cuts_of(edge)
    ring = ring_of(chips)
    ahead = [(ring[i], ring[(i + 1) % chips]) for i in range(chips)]
    streams = [
        [(a * CORES + s, b * CORES + s) for a, b in ahead]
        + [(b * CORES + 1 - s, a * CORES + 1 - s) for a, b in ahead]
        for s in range(CORES)
    ]
    pair = [(d, d ^ 1) for d in range(devices)]
    column = position % grid
    scalars = jnp.stack(
        [
            position // group,
            position // grid,
            column,
            column + 1 - 2 * (column % 2),
            position % group,
        ]
    ).astype(jnp.int32)

    def swap(array):
        return lax.ppermute(array, "tok", pair)

    def advance(held, count):
        return [lax.ppermute(held[k], "tok", streams[k]) for k in range(count)]

    def offset(index):
        return 4 * CAP * (index - 1) if index else total - 4 * CAP

    def prepared(packs, begins, operands, part):
        arrays, places = [], []
        for index in sorted(packs):
            for k, array in enumerate(packs[index]):
                arrays.append(array)
                places.append((offset(index) + k * array.shape[0], begins[index]))
        shape = (total, grid * cuts[part][1])
        return prepare(scalars, arrays, places, operands, shape, group)

    rounds = chips // 2
    total = 4 * CAP * rounds
    parts = len(cuts)
    own = make_message(tokens, route_ids, route_weights, cuts, edge)
    firsts = {0: [own[0]]}
    seconds = {0: [own[-1]]}
    packs, late, tiles, waiting = {}, {}, [], None

    def absorbed(index, chosen):
        pieces = [list(piece) for piece in zip(firsts[index], seconds[index])]
        pieces = [piece[:parts] for piece in pieces]
        return absorb(scalars, pieces, tiles, cuts, grid, chosen)

    every = list(range(parts))
    lag = parts - 1
    for step in range(1, rounds + 1 + lag):
        new_first, new_second, made, operands = [], [], {}, []
        if step <= rounds:
            sources = firsts[step - 1] * (CORES if step == 1 else 1)
            new_first = advance(sources, CORES if step < rounds else 1)
        if lag and step > 1:
            sources = seconds[step - 2] * (CORES if step == 2 else 1)
            new_second = advance(sources, CORES if step - 1 < rounds else 1)
        if waiting is not None:
            packs[waiting].append(swap(packs[waiting][0]))
            waiting = None
        if step == rounds:
            late_first = pack_first(scalars, firsts[step - 1])
            late[0] = [late_first, swap(late_first)]
            packs, tiles = lax.optimization_barrier((packs, tiles))
        ready = 0 if step == 1 else step - 1 - lag if step > 1 + lag else None
        if ready is not None and ready < rounds - 1:
            tiles, packed = absorbed(ready, every)
            packs[ready] = list(packed)
            waiting = ready
            if step == rounds:
                packs[ready] = [*packed, swap(packed[0])]
                waiting = None
        elif ready == rounds - 1:
            tiles, packed = absorbed(ready, every[1:])
            if lag:
                late[1] = [*packed, swap(packed[0])]
        if step == rounds:
            begins = [0] * rounds
            joined = {**packs, rounds - 1: late[0]}
            operands = [prepared(joined, begins, [], 0)]
            if lag:
                begins = [grid * cuts[0][1]] * rounds
                operands.append(prepared(packs, begins, [], 1))
        elif step > rounds:
            operands = [held[0], prepared({rounds - 1: late[1]}, [0] * rounds, held[1], 1)]
            made["other"] = swap(firsts[rounds][0])
        state = (new_first, new_second, packs, late, tiles, operands, made)
        state = lax.optimization_barrier(state)
        new_first, new_second, packs, late, tiles, held, made = state
        if step <= rounds:
            firsts[step] = new_first
        if not lag:
            seconds[step] = new_first
        elif step > 1:
            seconds[step - 1] = new_second
    mine = [firsts[rounds][0], seconds[rounds][0]][:parts]
    other = [made["other"] if lag else swap(mine[0])] + [swap(part) for part in mine[1:]]
    other_tile = swap(tiles[1])
    hessian, *first_operands = finish_first(
        scalars, mine[0], other[0], held[0], cuts, grid, group
    )
    hessian, tile = finish_second(
        scalars, mine, other, [tiles[0], other_tile], hessian,
        first_operands + [array for pair_of in held[1:] for array in pair_of],
        cuts, grid, group, 1.0 / (devices * tok_rows),
    )
    return (hessian, tile)


def solution(mesh):
    in_specs = (P(("grp", "tok"), None), P(("grp", "tok"), None), P(("grp", "tok"), None))
    out_specs = (P(("grp", "tok"), None), P(("grp", "tok"), None, None))
    return jax.shard_map(
        on_device, mesh=mesh, in_specs=in_specs, out_specs=out_specs, check_vma=False
    )
```

time: 160 us -> 111 us (0.69)
  waiting for transfers between devices: 94.8 us -> 56.9 us
  Pallas kernels: 0 us -> 33.7 us
  matrix products: 25.9 us -> 0 us
  blocking collectives: 23.7 us -> 0 us
  starting transfers between devices: 0.04 us -> 16.5 us
  between operations: 14.2 us -> 0.96 us
  local copies, waits for them, and re-layouts: 0.03 us -> 2.63 us
    all_gather x1 -> x0, waiting for transfers between devices: 94.1 us -> none  [on_device(): everyone = lax.all_gather(tokens, 'tok', tiled=True)]
    ppermute x0 -> x22, waiting for transfers between devices: none -> 56.9 us  [the longest x14 54.5 us: advance(): return [lax.ppermute(held[k], 'tok', streams[k]) for k in range(count)]]
    pallas_call x0 -> x11, Pallas kernels: none -> 33.7 us  [the longest x1 10.9 us: finish_second(): pl.pallas_call(kernel, out_shape=[tile, jax.ShapeDtypeStruct(hessian.shap...]
    dot_general x3 -> x0, matrix products: 25.9 us -> none  [the longest x1 12.7 us: on_device(): lax.dot_general(left_rows, all_rows, (((0,), (0,)), ((), ())), preferred_...]
    all_gather x1 -> x0, blocking collectives: 23.7 us -> none  [on_device(): lax.all_gather(weight_table(route_ids, route_weights), 'tok', tiled=True)]
    ppermute x0 -> x22, starting transfers between devices: none -> 16.5 us  [the longest x14 14.7 us: advance(): return [lax.ppermute(held[k], 'tok', streams[k]) for k in range(count)]]
    unnamed x8 -> x6, local copies, waits for them, and re-layouts: 0.02 us -> 2.54 us
  transfers between devices with their start and end apart: 1 -> 22, of which waited for: 1 -> 7; matrix products, arithmetic and copies ran while one was open for 1% -> 0% of each run, Pallas kernels for 0% -> 20%
where the time goes in v5:
time: 111 us
  waiting for transfers between devices  56.9 us (51%)
  Pallas kernels  33.7 us (30%)
  starting transfers between devices  16.5 us (15%)
  local copies, waits for them, and re-layouts  2.63 us (2%)
    ppermute x14, waiting for transfers between devices, advance(): return [lax.ppermute(held[k], 'tok', streams[k]) for k in range(count)]  54.5 us
    ppermute x14, starting transfers between devices, advance(): return [lax.ppermute(held[k], 'tok', streams[k]) for k in range(count)]  14.7 us
    pallas_call x1, Pallas kernels, finish_second(): pl.pallas_call(kernel, out_shape=[tile, jax.ShapeDtypeStruct(hessian.shap...  10.9 us
    pallas_call x4, Pallas kernels, absorb(): pl.pallas_call(functools.partial(absorb_kernel, cuts, grid, len(pieces),...  10.3 us
    pallas_call x1, Pallas kernels, finish_first(): pl.pallas_call(functools.partial(finish_first_kernel, cuts, grid, slabs),...  6.14 us
    pallas_call x3, Pallas kernels, prepare(): pl.pallas_call(functools.partial(prepare_kernel, slabs, places), out_shap...  4.72 us
    unnamed x6, local copies, waits for them, and re-layouts  2.54 us
    ppermute x8, waiting for transfers between devices, swap(): return lax.ppermute(array, 'tok', pair)  2.41 us
  transfers between devices with their start and end apart: 22, of which 7 were waited for; matrix products, arithmetic and copies ran while one was open for 0% of the time, Pallas kernels for 20%

profile of v5, /device:TPU:0, one launch (start us, length us, event | category | flops | bytes accessed | tf_op | source)
XLA Modules:
  0.0 110.7 jit_solution(15752843661114893768)
XLA Ops:
  0.6 0.0 copy-start
  0.6 1.2 %copy-done = bf16[128,3584]{1,0:T(8,128)(2,1)S(1)} copy-done((bf16[128,3584]{1,0:T(8,128)(2,1)S(1)}, bf16[128,3584]{1,0:T(8,128)(2,1)}, u32[]{:S(2)}) %copy-start) | copy-done | bytes 917528
  1.8 0.0 copy-start.1
  1.8 0.7 copy-done.1
  2.5 0.0 copy-start.2
  2.5 0.7 copy-done.2
  3.2 0.3 make_message.1
  3.5 3.0 %collective-permute-start.1 = (bf16[128,2176]{1,0:T(8,128)(2,1)S(1)}, bf16[128,2176]{1,0:T(8,128)(2,1)S(1)}, u32[]{:S(2)}, u32[]{:S(2)}) collective-permute-start(bf16[128,2176]{1,0:T(8,128)(2,1)S(1)} %get-tuple-element.72.refs_1_), channel_id=1, source_target_pairs={{1,5},{5,9},{9,13},{13,15},{15,11},{11,7},{7,3},{3,1},{4,0},{8,4},... | collective-permute-start | bytes 1671176 | tf_op jit(solution)/shard_map/ppermute | solution.py:480
  6.5 0.1 collective-permute-start
  6.7 0.1 stack.23.refs_0_
  6.7 2.0 %absorb.4 = (f32[896,896]{1,0:T(8,128)S(1)}, f32[896,896]{1,0:T(8,128)S(1)}, bf16[32,3584]{1,0:T(8,128)(2,1)S(1)}) custom-call(s32[5]{0:T(128)S(1)} %stack.23.refs_0_, bf16[128,2176]{1,0:T(8,128)(2,1)S(1)} %get-tuple-element.72.refs_1_, bf16[128,1536]{1,0:T(8,128)(2,1)S(1)} %get-tuple-element.73.refs_2_), custom_call_target="tpu_custom_call" | custom-call | flops 1 | bytes 1 | tf_op jit(solution)/shard_map/absorb/pallas_call | solution.py:198
  8.7 10.8 %collective-permute-done.1.refs_3_ = bf16[128,2176]{1,0:T(8,128)(2,1)S(1)} collective-permute-done((bf16[128,2176]{1,0:T(8,128)(2,1)S(1)}, bf16[128,2176]{1,0:T(8,128)(2,1)S(1)}, u32[]{:S(2)}, u32[]{:S(2)}) %collective-permute-start.1) | collective-permute-done | bytes 557088 | tf_op jit(solution)/shard_map/ppermute | solution.py:480
  19.5 0.0 collective-permute-done.refs_1_
  19.5 2.4 %collective-permute-start.2 = (bf16[128,2176]{1,0:T(8,128)(2,1)S(1)}, bf16[128,2176]{1,0:T(8,128)(2,1)S(1)}, u32[]{:S(2)}, u32[]{:S(2)}) collective-permute-start(bf16[128,2176]{1,0:T(8,128)(2,1)S(1)} %collective-permute-done.refs_1_), channel_id=1, source_target_pairs={{0,4},{4,8},{8,12},{12,14},{14,10},{10,6},{6,2},{2,0},{5,1},{9,5},... | collective-permute-start | bytes 1671176 | tf_op jit(solution)/shard_map/ppermute | solution.py:480
  21.9 0.0 collective-permute-start.3
  21.9 1.1 collective-permute-start.5
  23.0 1.0 collective-permute-start.4
  24.0 0.0 collective-permute-start.6
  24.0 19.3 %collective-permute-done.5.refs_4_ = bf16[128,1536]{1,0:T(8,128)(2,1)S(1)} collective-permute-done((bf16[128,1536]{1,0:T(8,128)(2,1)S(1)}, bf16[128,1536]{1,0:T(8,128)(2,1)S(1)}, u32[]{:S(2)}, u32[]{:S(2)}) %collective-permute-start.5) | collective-permute-done | bytes 393248 | tf_op jit(solution)/shard_map/ppermute | solution.py:480
  43.3 0.0 collective-permute-done.4.refs_2_
  43.3 0.0 collective-permute-done.6.refs_2_
  43.3 0.0 collective-permute-done.2.refs_1_
  43.3 0.0 collective-permute-done.3.refs_3_
  43.3 1.8 %collective-permute-start.7 = (bf16[128,2176]{1,0:T(8,128)(2,1)S(1)}, bf16[128,2176]{1,0:T(8,128)(2,1)S(1)}, u32[]{:S(2)}, u32[]{:S(2)}) collective-permute-start(bf16[128,2176]{1,0:T(8,128)(2,1)S(1)} %collective-permute-done.2.refs_1_), channel_id=1, source_target_pairs={{0,4},{4,8},{8,12},{12,14},{14,10},{10,6},{6,2},{2,0},{5,1},{9,5},... | collective-permute-start | bytes 1671176 | tf_op jit(solution)/shard_map/ppermute | solution.py:480
  45.1 0.3 collective-permute-start.8
  45.4 1.7 %collective-permute-start.9 = (bf16[128,1536]{1,0:T(8,128)(2,1)S(1)}, bf16[128,1536]{1,0:T(8,128)(2,1)S(1)}, u32[]{:S(2)}, u32[]{:S(2)}) collective-permute-start(bf16[128,1536]{1,0:T(8,128)(2,1)S(1)} %collective-permute-done.4.refs_2_), channel_id=1, source_target_pairs={{0,4},{4,8},{8,12},{12,14},{14,10},{10,6},{6,2},{2,0},{5,1},{9,5},... | collective-permute-start | bytes 1179656 | tf_op jit(solution)/shard_map/ppermute | solution.py:480
  47.1 0.3 collective-permute-start.10
  47.4 2.8 %absorb.5 = (f32[896,896]{1,0:T(8,128)S(1)}, f32[896,896]{1,0:T(8,128)S(1)}, bf16[64,3584]{1,0:T(8,128)(2,1)S(1)}) custom-call(s32[5]{0:T(128)S(1)} %stack.23.refs_0_, bf16[128,2176]{1,0:T(8,128)(2,1)S(1)} %collective-permute-done.refs_1_, bf16[128,1536]{1,0:T(8,128)(2,1)S(1)} %collective-permute-done.4.refs_2_, ...), custom_call_target="tpu_custom_call", output_to_operand_aliasing={{0}: (5, {}), {1}: (6, {})} | custom-call | flops 1 | bytes 1 | tf_op jit(solution)/shard_map/absorb/pallas_call | solution.py:198
  50.2 16.8 %collective-permute-done.9.refs_2_ = bf16[128,1536]{1,0:T(8,128)(2,1)S(1)} collective-permute-done((bf16[128,1536]{1,0:T(8,128)(2,1)S(1)}, bf16[128,1536]{1,0:T(8,128)(2,1)S(1)}, u32[]{:S(2)}, u32[]{:S(2)}) %collective-permute-start.9) | collective-permute-done | bytes 393248 | tf_op jit(solution)/shard_map/ppermute | solution.py:480
  67.0 0.0 collective-permute-done.10.refs_4_
  67.0 0.0 collective-permute-done.7.refs_1_
  67.0 0.0 collective-permute-done.8.refs_2_.refs_3_
  67.0 0.1 collective-permute-start.14
  67.1 0.5 collective-permute-start.11
  67.6 1.3 %collective-permute-done.14.refs_4_ = bf16[64,3584]{1,0:T(8,128)(2,1)S(1)} collective-permute-done((bf16[64,3584]{1,0:T(8,128)(2,1)S(1)}, bf16[64,3584]{1,0:T(8,128)(2,1)S(1)}, u32[]{:S(2)}, u32[]{:S(2)}) %collective-permute-start.14) | collective-permute-done | bytes 458784 | tf_op jit(solution)/shard_map/ppermute | solution.py:477
  68.9 2.8 %absorb.6 = (f32[896,896]{1,0:T(8,128)S(1)}, f32[896,896]{1,0:T(8,128)S(1)}, bf16[64,3584]{1,0:T(8,128)(2,1)S(1)}) custom-call(s32[5]{0:T(128)S(1)} %stack.23.refs_0_, bf16[128,2176]{1,0:T(8,128)(2,1)S(1)} %collective-permute-done.2.refs_1_, bf16[128,1536]{1,0:T(8,128)(2,1)S(1)} %collective-permute-done.9.refs_2_, ...), custom_call_target="tpu_custom_call", output_to_operand_aliasing={{0}: (5, {}), {1}: (6, {})} | custom-call | flops 1 | bytes 1 | tf_op jit(solution)/shard_map/absorb/pallas_call | solution.py:198
  71.7 0.2 collective-permute-start.15
  71.9 0.5 collective-permute-start.12
  72.4 1.5 %collective-permute-start.13 = (bf16[128,1536]{1,0:T(8,128)(2,1)S(1)}, bf16[128,1536]{1,0:T(8,128)(2,1)S(1)}, u32[]{:S(2)}, u32[]{:S(2)}) collective-permute-start(bf16[128,1536]{1,0:T(8,128)(2,1)S(1)} %collective-permute-done.10.refs_4_), channel_id=1, source_target_pairs={{1,5},{5,9},{9,13},{13,15},{15,11},{11,7},{7,3},{3,1},{4,0},{8,4},... | collective-permute-start | bytes 1179656 | tf_op jit(solution)/shard_map/ppermute | solution.py:480
  74.0 1.3 %pack_first.1.refs_7_ = bf16[64,2048]{1,0:T(8,128)(2,1)S(1)} custom-call(s32[5]{0:T(128)S(1)} %stack.23.refs_0_, bf16[128,2176]{1,0:T(8,128)(2,1)S(1)} %collective-permute-done.7.refs_1_, bf16[128,2176]{1,0:T(8,128)(2,1)S(1)} %collective-permute-done.8.refs_2_.refs_3_), custom_call_target="tpu_custom_call" | custom-call | flops 1 | bytes 1 | tf_op jit(solution)/shard_map/pack_first/pallas_call | solution.py:153
  75.2 0.1 collective-permute-start.16
  75.3 0.0 collective-permute-done.15.refs_6_
  75.3 1.6 %prepare_rows.4 = (bf16[512,1536]{1,0:T(8,128)(2,1)S(1)}, bf16[768,512]{1,0:T(8,128)(2,1)S(1)}) custom-call(s32[5]{0:T(128)S(1)} %stack.23.refs_0_, bf16[32,3584]{1,0:T(8,128)(2,1)S(1)} %get-tuple-element.101.refs_1_, bf16[32,3584]{1,0:T(8,128)(2,1)S(1)} %collective-permute-done.6.refs_2_, bf16[64,3584]{1,0:T(8,128)(2,1)S(1)} %get-tuple-element.103.refs_3_, ...), custom_call_target="tpu_custom_call" | custom-call | flops 1 | bytes 1 | tf_op jit(solution)/shard_map/prepare_rows/pallas_call | solution.py:233
  76.9 0.0 collective-permute-done.16.refs_8_
  76.9 2.2 %prepare_rows.3 = (bf16[512,2048]{1,0:T(8,128)(2,1)S(1)}, bf16[1024,512]{1,0:T(8,128)(2,1)S(1)}) custom-call(s32[5]{0:T(128)S(1)} %stack.23.refs_0_, bf16[32,3584]{1,0:T(8,128)(2,1)S(1)} %get-tuple-element.101.refs_1_, bf16[32,3584]{1,0:T(8,128)(2,1)S(1)} %collective-permute-done.6.refs_2_, bf16[64,3584]{1,0:T(8,128)(2,1)S(1)} %get-tuple-element.103.refs_3_, ...), custom_call_target="tpu_custom_call" | custom-call | flops 1 | bytes 1 | tf_op jit(solution)/shard_map/prepare_rows/pallas_call | solution.py:233
  79.2 5.9 %collective-permute-done.12.refs_2_ = bf16[128,1536]{1,0:T(8,128)(2,1)S(1)} collective-permute-done((bf16[128,1536]{1,0:T(8,128)(2,1)S(1)}, bf16[128,1536]{1,0:T(8,128)(2,1)S(1)}, u32[]{:S(2)}, u32[]{:S(2)}) %collective-permute-start.12) | collective-permute-done | bytes 393248 | tf_op jit(solution)/shard_map/ppermute | solution.py:480
  85.1 0.0 collective-permute-done.13.refs_4_
  85.1 0.0 collective-permute-done.11.refs_1_
  85.1 0.0 collective-permute-start.19
  85.1 0.5 collective-permute-start.17
  85.6 2.8 %absorb.7 = (f32[896,896]{1,0:T(8,128)S(1)}, f32[896,896]{1,0:T(8,128)S(1)}, bf16[64,1536]{1,0:T(8,128)(2,1)S(1)}) custom-call(s32[5]{0:T(128)S(1)} %stack.23.refs_0_, bf16[128,2176]{1,0:T(8,128)(2,1)S(1)} %collective-permute-done.7.refs_1_, bf16[128,1536]{1,0:T(8,128)(2,1)S(1)} %collective-permute-done.12.refs_2_, ...), custom_call_target="tpu_custom_call", output_to_operand_aliasing={{0}: (5, {}), {1}: (6, {})} | custom-call | flops 1 | bytes 1 | tf_op jit(solution)/shard_map/absorb/pallas_call | solution.py:198
  88.4 1.0 collective-permute-start.18
  89.3 1.1 collective-permute-done.18.refs_2_
  90.4 0.9 prepare_rows.5
  91.3 1.6 %collective-permute-done.17.refs_2_ = bf16[128,1536]{1,0:T(8,128)(2,1)S(1)} collective-permute-done((bf16[128,1536]{1,0:T(8,128)(2,1)S(1)}, bf16[128,1536]{1,0:T(8,128)(2,1)S(1)}, u32[]{:S(2)}, u32[]{:S(2)}) %collective-permute-start.17) | collective-permute-done | bytes 393248 | tf_op jit(solution)/shard_map/ppermute | solution.py:480
  93.0 0.0 collective-permute-done.19.refs_2_.refs_3_
  93.0 0.0 collective-permute-start.21
  93.0 0.5 collective-permute-start.20
  93.5 6.1 %finish_first.1 = (f32[1792,3584]{1,0:T(8,128)}, bf16[512,2048]{1,0:T(8,128)(2,1)S(1)}, bf16[1024,512]{1,0:T(8,128)(2,1)S(1)}) custom-call(s32[5]{0:T(128)S(1)} %stack.23.refs_0_, bf16[128,2176]{1,0:T(8,128)(2,1)S(1)} %collective-permute-done.11.refs_1_, ...), custom_call_target="tpu_custom_call", output_to_operand_aliasing={{1}: (3, {}), {2}: (4, {})} | custom-call | flops 1 | bytes 1 | tf_op jit(solution)/shard_map/finish_first/pallas_call | solution.py:315
  99.6 0.0 collective-permute-done.20.refs_4_
  99.6 0.0 collective-permute-done.21.refs_6_
  99.6 10.9 %finish_second.1 = (f32[1,896,896]{2,1,0:T(8,128)}, f32[1792,3584]{1,0:T(8,128)}, bf16[512,1536]{1,0:T(8,128)(2,1)S(1)}, bf16[768,512]{1,0:T(8,128)(2,1)S(1)}) custom-call(s32[5]{0:T(128)S(1)} %stack.23.refs_0_, bf16[128,2176]{1,0:T(8,128)(2,1)S(1)} %collective-permute-done.11.refs_1_, ...), custom_call_target="tpu_custom_call", output_to_operand_aliasing={{1}: (11, {}), {2}: (9, {}), {3}: (10, {})} | custom-call | flops 1 | bytes 1 | tf_op jit(solution)/shard_map/finish_second/pallas_call | solution.py:425
Async XLA Ops:
  0.6 1.2 %copy-start = (bf16[128,3584]{1,0:T(8,128)(2,1)S(1)}, bf16[128,3584]{1,0:T(8,128)(2,1)}, u32[]{:S(2)}) copy-start(bf16[128,3584]{1,0:T(8,128)(2,1)} %refs_0_.1) | copy-start | bytes 2752516
  1.8 0.7 copy-start.1
  2.5 0.7 copy-start.2
  3.5 16.0 %collective-permute-start.1 = (bf16[128,2176]{1,0:T(8,128)(2,1)S(1)}, bf16[128,2176]{1,0:T(8,128)(2,1)S(1)}, u32[]{:S(2)}, u32[]{:S(2)}) collective-permute-start(bf16[128,2176]{1,0:T(8,128)(2,1)S(1)} %get-tuple-element.72.refs_1_), channel_id=1, source_target_pairs={{1,5},{5,9},{9,13},{13,15},{15,11},{11,7},{7,3},{3,1},{4,0},{8,4},... | collective-permute-start | bytes 1671176 | tf_op jit(solution)/shard_map/ppermute | solution.py:480
  6.5 13.0 %collective-permute-start = (bf16[128,2176]{1,0:T(8,128)(2,1)S(1)}, bf16[128,2176]{1,0:T(8,128)(2,1)S(1)}, u32[]{:S(2)}, u32[]{:S(2)}) collective-permute-start(bf16[128,2176]{1,0:T(8,128)(2,1)S(1)} %get-tuple-element.72.refs_1_), channel_id=1, source_target_pairs={{0,4},{4,8},{8,12},{12,14},{14,10},{10,6},{6,2},{2,0},{5,1},{9,5},... | collective-permute-start | bytes 1671176 | tf_op jit(solution)/shard_map/ppermute | solution.py:480
  19.5 23.7 %collective-permute-start.2 = (bf16[128,2176]{1,0:T(8,128)(2,1)S(1)}, bf16[128,2176]{1,0:T(8,128)(2,1)S(1)}, u32[]{:S(2)}, u32[]{:S(2)}) collective-permute-start(bf16[128,2176]{1,0:T(8,128)(2,1)S(1)} %collective-permute-done.refs_1_), channel_id=1, source_target_pairs={{0,4},{4,8},{8,12},{12,14},{14,10},{10,6},{6,2},{2,0},{5,1},{9,5},... | collective-permute-start | bytes 1671176 | tf_op jit(solution)/shard_map/ppermute | solution.py:480
  21.9 21.3 %collective-permute-start.3 = (bf16[128,2176]{1,0:T(8,128)(2,1)S(1)}, bf16[128,2176]{1,0:T(8,128)(2,1)S(1)}, u32[]{:S(2)}, u32[]{:S(2)}) collective-permute-start(bf16[128,2176]{1,0:T(8,128)(2,1)S(1)} %collective-permute-done.1.refs_3_), channel_id=1, source_target_pairs={{1,5},{5,9},{9,13},{13,15},{15,11},{11,7},{7,3},{3,1},{4,0},{8,4},... | collective-permute-start | bytes 1671176 | tf_op jit(solution)/shard_map/ppermute | solution.py:480
  21.9 21.3 %collective-permute-start.5 = (bf16[128,1536]{1,0:T(8,128)(2,1)S(1)}, bf16[128,1536]{1,0:T(8,128)(2,1)S(1)}, u32[]{:S(2)}, u32[]{:S(2)}) collective-permute-start(bf16[128,1536]{1,0:T(8,128)(2,1)S(1)} %get-tuple-element.73.refs_2_), channel_id=1, source_target_pairs={{1,5},{5,9},{9,13},{13,15},{15,11},{11,7},{7,3},{3,1},{4,0},{8,4},... | collective-permute-start | bytes 1179656 | tf_op jit(solution)/shard_map/ppermute | solution.py:480
  23.0 20.2 %collective-permute-start.4 = (bf16[128,1536]{1,0:T(8,128)(2,1)S(1)}, bf16[128,1536]{1,0:T(8,128)(2,1)S(1)}, u32[]{:S(2)}, u32[]{:S(2)}) collective-permute-start(bf16[128,1536]{1,0:T(8,128)(2,1)S(1)} %get-tuple-element.73.refs_2_), channel_id=1, source_target_pairs={{0,4},{4,8},{8,12},{12,14},{14,10},{10,6},{6,2},{2,0},{5,1},{9,5},... | collective-permute-start | bytes 1179656 | tf_op jit(solution)/shard_map/ppermute | solution.py:480
  24.0 19.3 %collective-permute-start.6 = (bf16[32,3584]{1,0:T(8,128)(2,1)S(1)}, bf16[32,3584]{1,0:T(8,128)(2,1)S(1)}, u32[]{:S(2)}, u32[]{:S(2)}) collective-permute-start(bf16[32,3584]{1,0:T(8,128)(2,1)S(1)} %get-tuple-element.101.refs_1_), channel_id=1, source_target_pairs={{0,1},{1,0},{2,3},{3,2},{4,5},{5,4},{6,7},{7,6},{8,9},{9,8},{10,11... | collective-permute-start | bytes 688136 | tf_op jit(solution)/shard_map/ppermute | solution.py:477
  43.3 23.7 %collective-permute-start.7 = (bf16[128,2176]{1,0:T(8,128)(2,1)S(1)}, bf16[128,2176]{1,0:T(8,128)(2,1)S(1)}, u32[]{:S(2)}, u32[]{:S(2)}) collective-permute-start(bf16[128,2176]{1,0:T(8,128)(2,1)S(1)} %collective-permute-done.2.refs_1_), channel_id=1, source_target_pairs={{0,4},{4,8},{8,12},{12,14},{14,10},{10,6},{6,2},{2,0},{5,1},{9,5},... | collective-permute-start | bytes 1671176 | tf_op jit(solution)/shard_map/ppermute | solution.py:480
  45.1 21.9 %collective-permute-start.8 = (bf16[128,2176]{1,0:T(8,128)(2,1)S(1)}, bf16[128,2176]{1,0:T(8,128)(2,1)S(1)}, u32[]{:S(2)}, u32[]{:S(2)}) collective-permute-start(bf16[128,2176]{1,0:T(8,128)(2,1)S(1)} %collective-permute-done.3.refs_3_), channel_id=1, source_target_pairs={{1,5},{5,9},{9,13},{13,15},{15,11},{11,7},{7,3},{3,1},{4,0},{8,4},... | collective-permute-start | bytes 1671176 | tf_op jit(solution)/shard_map/ppermute | solution.py:480
  45.4 21.6 %collective-permute-start.9 = (bf16[128,1536]{1,0:T(8,128)(2,1)S(1)}, bf16[128,1536]{1,0:T(8,128)(2,1)S(1)}, u32[]{:S(2)}, u32[]{:S(2)}) collective-permute-start(bf16[128,1536]{1,0:T(8,128)(2,1)S(1)} %collective-permute-done.4.refs_2_), channel_id=1, source_target_pairs={{0,4},{4,8},{8,12},{12,14},{14,10},{10,6},{6,2},{2,0},{5,1},{9,5},... | collective-permute-start | bytes 1179656 | tf_op jit(solution)/shard_map/ppermute | solution.py:480
  47.1 19.9 %collective-permute-start.10 = (bf16[128,1536]{1,0:T(8,128)(2,1)S(1)}, bf16[128,1536]{1,0:T(8,128)(2,1)S(1)}, u32[]{:S(2)}, u32[]{:S(2)}) collective-permute-start(bf16[128,1536]{1,0:T(8,128)(2,1)S(1)} %collective-permute-done.5.refs_4_), channel_id=1, source_target_pairs={{1,5},{5,9},{9,13},{13,15},{15,11},{11,7},{7,3},{3,1},{4,0},{8,4},... | collective-permute-start | bytes 1179656 | tf_op jit(solution)/shard_map/ppermute | solution.py:480
  67.0 1.9 %collective-permute-start.14 = (bf16[64,3584]{1,0:T(8,128)(2,1)S(1)}, bf16[64,3584]{1,0:T(8,128)(2,1)S(1)}, u32[]{:S(2)}, u32[]{:S(2)}) collective-permute-start(bf16[64,3584]{1,0:T(8,128)(2,1)S(1)} %get-tuple-element.103.refs_3_), channel_id=1, source_target_pairs={{0,1},{1,0},{2,3},{3,2},{4,5},{5,4},{6,7},{7,6},{8,9},{9,8},{10,11... | collective-permute-start | bytes 1376264 | tf_op jit(solution)/shard_map/ppermute | solution.py:477
  67.1 18.0 %collective-permute-start.11 = (bf16[128,2176]{1,0:T(8,128)(2,1)S(1)}, bf16[128,2176]{1,0:T(8,128)(2,1)S(1)}, u32[]{:S(2)}, u32[]{:S(2)}) collective-permute-start(bf16[128,2176]{1,0:T(8,128)(2,1)S(1)} %collective-permute-done.7.refs_1_), channel_id=1, source_target_pairs={{0,4},{4,8},{8,12},{12,14},{14,10},{10,6},{6,2},{2,0},{5,1},{9,5},... | collective-permute-start | bytes 1671176 | tf_op jit(solution)/shard_map/ppermute | solution.py:480
  71.7 3.6 %collective-permute-start.15 = (bf16[64,3584]{1,0:T(8,128)(2,1)S(1)}, bf16[64,3584]{1,0:T(8,128)(2,1)S(1)}, u32[]{:S(2)}, u32[]{:S(2)}) collective-permute-start(bf16[64,3584]{1,0:T(8,128)(2,1)S(1)} %get-tuple-element.107.refs_5_), channel_id=1, source_target_pairs={{0,1},{1,0},{2,3},{3,2},{4,5},{5,4},{6,7},{7,6},{8,9},{9,8},{10,11... | collective-permute-start | bytes 1376264 | tf_op jit(solution)/shard_map/ppermute | solution.py:477
  71.9 13.2 %collective-permute-start.12 = (bf16[128,1536]{1,0:T(8,128)(2,1)S(1)}, bf16[128,1536]{1,0:T(8,128)(2,1)S(1)}, u32[]{:S(2)}, u32[]{:S(2)}) collective-permute-start(bf16[128,1536]{1,0:T(8,128)(2,1)S(1)} %collective-permute-done.9.refs_2_), channel_id=1, source_target_pairs={{0,4},{4,8},{8,12},{12,14},{14,10},{10,6},{6,2},{2,0},{5,1},{9,5},... | collective-permute-start | bytes 1179656 | tf_op jit(solution)/shard_map/ppermute | solution.py:480
  72.4 12.7 %collective-permute-start.13 = (bf16[128,1536]{1,0:T(8,128)(2,1)S(1)}, bf16[128,1536]{1,0:T(8,128)(2,1)S(1)}, u32[]{:S(2)}, u32[]{:S(2)}) collective-permute-start(bf16[128,1536]{1,0:T(8,128)(2,1)S(1)} %collective-permute-done.10.refs_4_), channel_id=1, source_target_pairs={{1,5},{5,9},{9,13},{13,15},{15,11},{11,7},{7,3},{3,1},{4,0},{8,4},... | collective-permute-start | bytes 1179656 | tf_op jit(solution)/shard_map/ppermute | solution.py:480
  75.2 1.7 %collective-permute-start.16 = (bf16[64,2048]{1,0:T(8,128)(2,1)S(1)}, bf16[64,2048]{1,0:T(8,128)(2,1)S(1)}, u32[]{:S(2)}, u32[]{:S(2)}) collective-permute-start(bf16[64,2048]{1,0:T(8,128)(2,1)S(1)} %pack_first.1.refs_7_), channel_id=1, source_target_pairs={{0,1},{1,0},{2,3},{3,2},{4,5},{5,4},{6,7},{7,6},{8,9},{9,8},{10,11... | collective-permute-start | bytes 786440 | tf_op jit(solution)/shard_map/ppermute | solution.py:477
  85.1 7.8 %collective-permute-start.19 = (bf16[128,2176]{1,0:T(8,128)(2,1)S(1)}, bf16[128,2176]{1,0:T(8,128)(2,1)S(1)}, u32[]{:S(2)}, u32[]{:S(2)}) collective-permute-start(bf16[128,2176]{1,0:T(8,128)(2,1)S(1)} %collective-permute-done.11.refs_1_), channel_id=1, source_target_pairs={{0,1},{1,0},{2,3},{3,2},{4,5},{5,4},{6,7},{7,6},{8,9},{9,8},{10,11... | collective-permute-start | bytes 1671176 | tf_op jit(solution)/shard_map/ppermute | solution.py:477
  85.1 7.8 %collective-permute-start.17 = (bf16[128,1536]{1,0:T(8,128)(2,1)S(1)}, bf16[128,1536]{1,0:T(8,128)(2,1)S(1)}, u32[]{:S(2)}, u32[]{:S(2)}) collective-permute-start(bf16[128,1536]{1,0:T(8,128)(2,1)S(1)} %collective-permute-done.12.refs_2_), channel_id=1, source_target_pairs={{0,4},{4,8},{8,12},{12,14},{14,10},{10,6},{6,2},{2,0},{5,1},{9,5},... | collective-permute-start | bytes 1179656 | tf_op jit(solution)/shard_map/ppermute | solution.py:480
  88.4 2.0 %collective-permute-start.18 = (bf16[64,1536]{1,0:T(8,128)(2,1)S(1)}, bf16[64,1536]{1,0:T(8,128)(2,1)S(1)}, u32[]{:S(2)}, u32[]{:S(2)}) collective-permute-start(bf16[64,1536]{1,0:T(8,128)(2,1)S(1)} %get-tuple-element.120.refs_1_), channel_id=1, source_target_pairs={{0,1},{1,0},{2,3},{3,2},{4,5},{5,4},{6,7},{7,6},{8,9},{9,8},{10,11... | collective-permute-start | bytes 589832 | tf_op jit(solution)/shard_map/ppermute | solution.py:477
  93.0 6.7 %collective-permute-start.21 = (f32[896,896]{1,0:T(8,128)S(1)}, f32[896,896]{1,0:T(8,128)S(1)}, u32[]{:S(2)}, u32[]{:S(2)}) collective-permute-start(f32[896,896]{1,0:T(8,128)S(1)} %get-tuple-element.132), channel_id=1, source_target_pairs={{0,1},{1,0},{2,3},{3,2},{4,5},{5,4},{6,7},{7,6},{8,9},{9,8},{10,11... | collective-permute-start | bytes 9633800 | tf_op jit(solution)/shard_map/ppermute | solution.py:477
  93.0 6.7 %collective-permute-start.20 = (bf16[128,1536]{1,0:T(8,128)(2,1)S(1)}, bf16[128,1536]{1,0:T(8,128)(2,1)S(1)}, u32[]{:S(2)}, u32[]{:S(2)}) collective-permute-start(bf16[128,1536]{1,0:T(8,128)(2,1)S(1)} %collective-permute-done.17.refs_2_), channel_id=1, source_target_pairs={{0,1},{1,0},{2,3},{3,2},{4,5},{5,4},{6,7},{7,6},{8,9},{9,8},{10,11... | collective-permute-start | bytes 1179656 | tf_op jit(solution)/shard_map/ppermute | solution.py:477

commit v6 on v1

v6 whole, which is shorter than its diff:
```python
import functools
import math

import jax
import jax.numpy as jnp
from jax import lax
from jax.experimental import pallas as pl
from jax.experimental.pallas import tpu as pltpu
from jax.sharding import PartitionSpec as P

EXP = 8
CAP = 32
CORES = 2
STEP = 256
HALVES = 2
VMEM = pl.BlockSpec(memory_space=pltpu.VMEM)
SMEM = pl.BlockSpec(memory_space=pltpu.SMEM)
ANY = pl.BlockSpec(memory_space=pl.ANY)
F32 = jnp.float32
BF16 = jnp.bfloat16
ROWS_WITH_ROWS = (((0,), (0,)), ((), ()))
INVERSE = 1.0 / (16.0 * CAP)
SMALL = pl.CostEstimate(flops=1, bytes_accessed=1, transcendentals=0)


def params(mib):
    return pltpu.CompilerParams(vmem_limit_bytes=mib * 2**20)


def table_kernel(ids, weights, roots):
    row_at = lax.broadcasted_iota(jnp.int32, roots.shape, 0)
    table = jnp.zeros(roots.shape, F32)
    for e in range(EXP):
        weight = jnp.sum(jnp.where(ids[...] == e, weights[...], 0.0), axis=0, keepdims=True)
        table = jnp.where(row_at == e, weight, table)
    roots[...] = jnp.sqrt(table)


def make_table(ids, weights):
    return pl.pallas_call(
        table_kernel,
        out_shape=jax.ShapeDtypeStruct((EXP, ids.shape[0]), F32),
        in_specs=[VMEM] * 2,
        out_specs=VMEM,
        cost_estimate=SMALL,
        compiler_params=params(8),
        name="make_table",
    )(ids.T, weights.T)


def choose(expert, roots):
    rows = roots.shape[1]
    row_at = lax.broadcasted_iota(jnp.int32, roots.shape, 0)
    root = jnp.sum(jnp.where(row_at == expert, roots[...], 0.0), axis=0, keepdims=True)
    root = jnp.broadcast_to(root, (CAP, rows))
    member = root > 0.0
    from_at = lax.broadcasted_iota(jnp.int32, (rows, rows), 0)
    to_at = lax.broadcasted_iota(jnp.int32, (rows, rows), 1)
    upto = (from_at <= to_at).astype(F32).astype(BF16)
    counted = jnp.dot(member.astype(F32).astype(BF16), upto, preferred_element_type=F32)
    place = counted.astype(jnp.int32) - 1
    slot_at = lax.broadcasted_iota(jnp.int32, (CAP, rows), 0)
    select = jnp.logical_and(member, place == slot_at)
    scale = jnp.sum(jnp.where(select, root, 0.0), axis=1, keepdims=True)
    return select.astype(F32).astype(BF16), scale


def pack(expert, roots, piece):
    select, scale = choose(expert, roots)
    picked = jnp.dot(select, piece[...], preferred_element_type=F32)
    return (picked * scale).astype(BF16)


def fetch_tile(index, pieces, scratch):
    edge = scratch.shape[1]
    for b in range(pieces[0].shape[1] // edge):

        @pl.when(index == b)
        def _(b=b):
            row = 0
            for piece in pieces:
                rows = piece.shape[0]
                scratch[row : row + rows, :] = piece[:, b * edge : (b + 1) * edge]
                row += rows


def absorb_kernel(count, started, *refs):
    scalars, refs = refs[0], refs[1:]
    pieces, tables, refs = refs[:count], refs[count : 2 * count], refs[2 * count :]
    sums = 1 + HALVES
    before, refs = refs[: sums * started], refs[sums * started :]
    tiles, packed, scratch = refs[:sums], refs[sums], refs[sums + 1 :]
    for slot, which in enumerate(scratch, start=1):
        fetch_tile(scalars[slot], pieces, which)
    for k, own in enumerate((tiles[:1], tiles[1:])):
        update = lax.dot_general(
            scratch[0][...], scratch[1 + k][...], ROWS_WITH_ROWS, preferred_element_type=F32
        )
        rows = update.shape[0] // len(own)
        for h, tile in enumerate(own):
            part = update[h * rows : (h + 1) * rows]
            tile[...] = before[k + h][...] + part if started else part
    for k in range(count):
        packed[k * CAP : (k + 1) * CAP, :] = pack(scalars[0], tables[k], pieces[k])


def absorb(scalars, pieces, tables, before, edge):
    rows, width = pieces[0].shape
    count = len(pieces)
    *tiles, packed = pl.pallas_call(
        functools.partial(absorb_kernel, count, bool(before)),
        out_shape=[jax.ShapeDtypeStruct((edge, edge), F32)]
        + [jax.ShapeDtypeStruct((edge // HALVES, edge), F32)] * HALVES
        + [jax.ShapeDtypeStruct((count * CAP, width), BF16)],
        in_specs=[SMEM] + [VMEM] * (2 * count + len(before)),
        out_specs=[VMEM] * (2 + HALVES),
        scratch_shapes=[pltpu.VMEM((count * rows, edge), BF16)] * 3,
        cost_estimate=SMALL,
        input_output_aliases={1 + 2 * count + k: k for k in range(len(before))},
        compiler_params=params(14),
        name="absorb",
    )(scalars, *pieces, *tables, *before)
    return tiles, packed


def place_rows(slab_at, packed, at, rows, across):
    count, width = packed.shape
    slab = across.shape[0]
    rows[at : at + count, :] = packed
    for s in range(width // slab):

        @pl.when(slab_at == s)
        def _():
            across[:, at : at + count] = packed[:, s * slab : (s + 1) * slab].T


def prepare_kernel(places, *refs):
    scalars, *refs = refs
    rows, across = refs[-2:]
    for at, packed in zip(places, refs):
        place_rows(scalars[4], packed[...], at, rows, across)


def prepare(scalars, packs, places, operands, total, slab):
    width = packs[0].shape[1]
    return pl.pallas_call(
        functools.partial(prepare_kernel, places),
        out_shape=[
            jax.ShapeDtypeStruct((total, width), BF16),
            jax.ShapeDtypeStruct((slab, total), BF16),
        ],
        in_specs=[SMEM] + [VMEM] * (len(packs) + len(operands)),
        out_specs=[VMEM] * 2,
        input_output_aliases={1 + len(packs) + k: k for k in range(len(operands))},
        cost_estimate=SMALL,
        compiler_params=params(12),
        name="prepare_rows",
    )(scalars, *packs, *operands)


def finish_kernel(final, *refs):
    scalars, *refs = refs
    pieces, tables, refs = refs[:2], refs[2:4], refs[4:]
    before, refs = refs[: 1 + HALVES], refs[3 + HALVES :]
    hessian, tile, rows, across, staging, sum_of_tile, left, right, sent = refs
    at = rows.shape[0] - CAP * len(pieces)
    packed = jnp.concatenate(
        [pack(scalars[0], table, piece) for piece, table in zip(pieces, tables)], axis=0
    )
    place_rows(scalars[4], packed, at, rows, across)
    copies = []
    for n in range(staging.shape[0]):
        span = slice(n * STEP, (n + 1) * STEP)
        staging[n, :, :] = (
            jnp.dot(across[...], rows[:, span], preferred_element_type=F32) * INVERSE
        )
        copies.append(pltpu.make_async_copy(staging.at[n], hessian.at[:, span], sent.at[n]))
        copies[-1].start()
    fetch_tile(scalars[1], pieces, left)
    fetch_tile(scalars[2], pieces, right)
    update = lax.dot_general(left[...], right[...], ROWS_WITH_ROWS, preferred_element_type=F32)
    received = jnp.concatenate([part[...] for part in before[1:]], axis=0)
    sum_of_tile[...] = (before[0][...] + received + update) * final
    copies.append(pltpu.make_async_copy(sum_of_tile, tile.at[0], sent.at[len(copies)]))
    copies[-1].start()
    for copy in copies:
        copy.wait()


def finish(scalars, pieces, tables, before, operands, final):
    edge = before[0].shape[0]
    rows, across = operands
    slab, width = across.shape[0], rows.shape[1]
    count = sum(piece.shape[0] for piece in pieces)
    blocks = width // STEP
    return pl.pallas_call(
        functools.partial(finish_kernel, final),
        out_shape=[
            jax.ShapeDtypeStruct((slab, width), F32),
            jax.ShapeDtypeStruct((1, edge, edge), F32),
            jax.ShapeDtypeStruct(rows.shape, BF16),
            jax.ShapeDtypeStruct(across.shape, BF16),
        ],
        in_specs=[SMEM] + [VMEM] * (7 + HALVES),
        out_specs=[ANY, ANY, VMEM, VMEM],
        scratch_shapes=[
            pltpu.VMEM((blocks, slab, STEP), F32),
            pltpu.VMEM((edge, edge), F32),
            pltpu.VMEM((count, edge), BF16),
            pltpu.VMEM((count, edge), BF16),
            pltpu.SemaphoreType.DMA((blocks + 1,)),
        ],
        input_output_aliases={6 + HALVES: 2, 7 + HALVES: 3},
        cost_estimate=SMALL,
        compiler_params=params(38),
        name="finish",
    )(scalars, *pieces, *tables, *before, rows, across)[:2]


def ring_of(chips):
    return list(range(0, chips, 2)) + list(range(chips - 1, 0, -2))


def on_device(tokens, route_ids, route_weights):
    devices = lax.axis_size("tok")
    position = lax.axis_index("tok")
    tok_rows, width = tokens.shape
    grid = math.isqrt(devices)
    edge = width // grid
    group = devices // EXP
    slab = width // group
    chips = devices // CORES
    ring = ring_of(chips)
    ahead = [(ring[i], ring[(i + 1) % chips]) for i in range(chips)]
    streams = [
        [(a * CORES + s, b * CORES + s) for a, b in ahead]
        + [(b * CORES + 1 - s, a * CORES + 1 - s) for a, b in ahead]
        for s in range(CORES)
    ]
    pair = [(d, d ^ 1) for d in range(devices)]
    column = position % grid
    scalars = jnp.stack(
        [
            position // group,
            position // grid,
            column,
            column + 1 - 2 * (column % 2),
            position % group,
        ]
    ).astype(jnp.int32)

    def swap(array):
        return lax.ppermute(array, "tok", pair)

    def advance(held, count):
        return [lax.ppermute(held[k], "tok", streams[k]) for k in range(count)]

    rounds = chips // 2
    total = 4 * CAP * rounds

    def place(index):
        at = 4 * CAP * (index - 1) if index else total - 4 * CAP
        return [at, at + (2 if index else 1) * CAP]

    roots = make_table(route_ids, route_weights)
    pieces, tables = [tokens], [roots]
    packs, tiles = {}, []
    for step in range(1, rounds + 1):
        count = CORES if step < rounds else 1
        repeat = CORES if step == 1 else 1
        new_pieces = advance(pieces * repeat, count)
        new_tables = advance(tables * repeat, count)
        if step > 1:
            packs[step - 2] = [packs[step - 2][0], swap(packs[step - 2][0])]
        tiles, packed = absorb(scalars, pieces, tables, tiles, edge)
        packs[step - 1] = [packed]
        if step < rounds:
            state = (new_pieces, new_tables, packs, tiles)
            new_pieces, new_tables, packs, tiles = lax.optimization_barrier(state)
        pieces, tables = new_pieces, new_tables
    packs[rounds - 1].append(swap(packs[rounds - 1][0]))
    other_sums = [swap(part) for part in tiles[1:]]
    tables = [tables[0], swap(tables[0])]
    operands = []
    for chosen in (range(rounds - 1), [rounds - 1]):
        operands = prepare(
            scalars,
            [array for index in chosen for array in packs[index]],
            [at for index in chosen for at in place(index)],
            operands, total, slab,
        )
    pieces, tables, operands = lax.optimization_barrier((pieces, tables, operands))
    return tuple(
        finish(
            scalars, [pieces[0], swap(pieces[0])], tables, [tiles[0], *other_sums], operands,
            1.0 / (devices * tok_rows),
        )
    )


def solution(mesh):
    in_specs = (P(("grp", "tok"), None), P(("grp", "tok"), None), P(("grp", "tok"), None))
    out_specs = (P(("grp", "tok"), None), P(("grp", "tok"), None, None))
    return jax.shard_map(
        on_device, mesh=mesh, in_specs=in_specs, out_specs=out_specs, check_vma=False
    )
```

time: 160 us -> 104 us (0.65)
  waiting for transfers between devices: 94.8 us -> 55.9 us
  Pallas kernels: 0 us -> 26.1 us
  matrix products: 25.9 us -> 0 us
  blocking collectives: 23.7 us -> 0 us
  starting transfers between devices: 0.04 us -> 18.5 us
  between operations: 14.2 us -> 0.89 us
  local copies, waits for them, and re-layouts: 0.03 us -> 2.64 us
    all_gather x1 -> x0, waiting for transfers between devices: 94.1 us -> none  [on_device(): everyone = lax.all_gather(tokens, 'tok', tiled=True)]
    ppermute x0 -> x22, waiting for transfers between devices: none -> 55.9 us  [the longest x14 53.4 us: advance(): return [lax.ppermute(held[k], 'tok', streams[k]) for k in range(count)]]
    pallas_call x0 -> x8, Pallas kernels: none -> 26.1 us  [the longest x1 12.4 us: finish(): pl.pallas_call(functools.partial(finish_kernel, final), out_shape=[jax.Sh...]
    dot_general x3 -> x0, matrix products: 25.9 us -> none  [the longest x1 12.7 us: on_device(): lax.dot_general(left_rows, all_rows, (((0,), (0,)), ((), ())), preferred_...]
    all_gather x1 -> x0, blocking collectives: 23.7 us -> none  [on_device(): lax.all_gather(weight_table(route_ids, route_weights), 'tok', tiled=True)]
    ppermute x0 -> x22, starting transfers between devices: none -> 18.5 us  [the longest x14 16.5 us: advance(): return [lax.ppermute(held[k], 'tok', streams[k]) for k in range(count)]]
    unnamed x8 -> x6, local copies, waits for them, and re-layouts: 0.02 us -> 2.55 us
  transfers between devices with their start and end apart: 1 -> 22, of which waited for: 1 -> 7; matrix products, arithmetic and copies ran while one was open for 1% -> 0% of each run, Pallas kernels for 0% -> 13%
where the time goes in v6:
time: 104 us
  waiting for transfers between devices  55.9 us (54%)
  Pallas kernels  26.1 us (25%)
  starting transfers between devices  18.5 us (18%)
  local copies, waits for them, and re-layouts  2.64 us (3%)
    ppermute x14, waiting for transfers between devices, advance(): return [lax.ppermute(held[k], 'tok', streams[k]) for k in range(count)]  53.4 us
    ppermute x14, starting transfers between devices, advance(): return [lax.ppermute(held[k], 'tok', streams[k]) for k in range(count)]  16.5 us
    pallas_call x1, Pallas kernels, finish(): pl.pallas_call(functools.partial(finish_kernel, final), out_shape=[jax.Sh...  12.4 us
    pallas_call x4, Pallas kernels, absorb(): pl.pallas_call(functools.partial(absorb_kernel, count, bool(before)), out...  9.69 us
    pallas_call x2, Pallas kernels, prepare(): pl.pallas_call(functools.partial(prepare_kernel, places), out_shape=[jax....  3.97 us
    unnamed x6, local copies, waits for them, and re-layouts  2.55 us
    ppermute x8, waiting for transfers between devices, swap(): return lax.ppermute(array, 'tok', pair)  2.46 us
  transfers between devices with their start and end apart: 22, of which 7 were waited for; matrix products, arithmetic and copies ran while one was open for 0% of the time, Pallas kernels for 13%

profile of v6, /device:TPU:0, one launch (start us, length us, event | category | flops | bytes accessed | tf_op | source)
XLA Modules:
  0.0 103.9 jit_solution(13253202513224950369)
XLA Ops:
  0.6 3.1 %collective-permute-start = (bf16[128,3584]{1,0:T(8,128)(2,1)}, bf16[128,3584]{1,0:T(8,128)(2,1)S(1)}, u32[]{:S(2)}, u32[]{:S(2)}) collective-permute-start(bf16[128,3584]{1,0:T(8,128)(2,1)} %refs_1_.1), channel_id=1, source_target_pairs={{0,4},{4,8},{8,12},{12,14},{14,10},{10,6},{6,2},{2,0},{5,1},{9,5},... | collective-permute-start | bytes 2752520 | tf_op jit(solution)/shard_map/ppermute | solution.py:256
  3.7 0.0 collective-permute-start.1
  3.7 0.0 copy-start.1
  3.7 0.7 copy-done.1
  4.4 0.0 copy-start.2
  4.4 0.7 copy-done.2
  5.1 2.0 %collective-permute-start.3 = (f32[8,128]{1,0:T(8,128)S(1)}, f32[8,128]{1,0:T(8,128)S(1)}, u32[]{:S(2)}, u32[]{:S(2)}) collective-permute-start(f32[8,128]{1,0:T(8,128)S(1)} %make_table.1.refs_2_), channel_id=1, source_target_pairs={{1,5},{5,9},{9,13},{13,15},{15,11},{11,7},{7,3},{3,1},{4,0},{8,4},... | collective-permute-start | bytes 12296 | tf_op jit(solution)/shard_map/ppermute | solution.py:256
  7.1 0.1 collective-permute-start.2
  7.2 0.1 stack.23.refs_0_
  7.3 0.0 copy-start
  7.3 1.2 %copy-done = bf16[128,3584]{1,0:T(8,128)(2,1)S(1)} copy-done((bf16[128,3584]{1,0:T(8,128)(2,1)S(1)}, bf16[128,3584]{1,0:T(8,128)(2,1)}, u32[]{:S(2)}) %copy-start) | copy-done | bytes 917528
  8.5 1.9 %absorb.4 = (f32[896,896]{1,0:T(8,128)S(1)}, f32[448,896]{1,0:T(8,128)S(1)}, f32[448,896]{1,0:T(8,128)S(1)}, bf16[32,3584]{1,0:T(8,128)(2,1)S(1)}) custom-call(s32[5]{0:T(128)S(1)} %stack.23.refs_0_, bf16[128,3584]{1,0:T(8,128)(2,1)S(1)} %copy-done, f32[8,128]{1,0:T(8,128)S(1)} %make_table.1.refs_2_), custom_call_target="tpu_custom_call" | custom-call | flops 1 | bytes 1 | tf_op jit(solution)/shard_map/absorb/pallas_call | solution.py:110
  10.4 13.9 %collective-permute-done.3.refs_4_ = f32[8,128]{1,0:T(8,128)S(1)} collective-permute-done((f32[8,128]{1,0:T(8,128)S(1)}, f32[8,128]{1,0:T(8,128)S(1)}, u32[]{:S(2)}, u32[]{:S(2)}) %collective-permute-start.3) | collective-permute-done | bytes 4128 | tf_op jit(solution)/shard_map/ppermute | solution.py:256
  24.4 0.3 collective-permute-done.2.refs_3_
  24.6 0.0 collective-permute-done.refs_1_
  24.6 0.0 collective-permute-done.1.refs_2_
  24.6 1.6 %collective-permute-start.4 = (bf16[128,3584]{1,0:T(8,128)(2,1)S(1)}, bf16[128,3584]{1,0:T(8,128)(2,1)S(1)}, u32[]{:S(2)}, u32[]{:S(2)}) collective-permute-start(bf16[128,3584]{1,0:T(8,128)(2,1)S(1)} %collective-permute-done.refs_1_), channel_id=1, source_target_pairs={{0,4},{4,8},{8,12},{12,14},{14,10},{10,6},{6,2},{2,0},{5,1},{9,5},... | collective-permute-start | bytes 2752520 | tf_op jit(solution)/shard_map/ppermute | solution.py:256
  26.2 0.9 collective-permute-start.5
  27.1 0.0 collective-permute-start.8
  27.1 1.1 %collective-permute-start.6 = (f32[8,128]{1,0:T(8,128)S(1)}, f32[8,128]{1,0:T(8,128)S(1)}, u32[]{:S(2)}, u32[]{:S(2)}) collective-permute-start(f32[8,128]{1,0:T(8,128)S(1)} %collective-permute-done.2.refs_3_), channel_id=1, source_target_pairs={{0,4},{4,8},{8,12},{12,14},{14,10},{10,6},{6,2},{2,0},{5,1},{9,5},... | collective-permute-start | bytes 12296 | tf_op jit(solution)/shard_map/ppermute | solution.py:256
  28.2 0.9 collective-permute-start.7
  29.1 2.6 %absorb.5 = (f32[896,896]{1,0:T(8,128)S(1)}, f32[448,896]{1,0:T(8,128)S(1)}, f32[448,896]{1,0:T(8,128)S(1)}, bf16[64,3584]{1,0:T(8,128)(2,1)S(1)}) custom-call(s32[5]{0:T(128)S(1)} %stack.23.refs_0_, bf16[128,3584]{1,0:T(8,128)(2,1)S(1)} %collective-permute-done.refs_1_, ...), custom_call_target="tpu_custom_call", output_to_operand_aliasing={{0}: (5, {}), {1}: (6, {}), {2}: (7, {})} | custom-call | flops 1 | bytes 1 | tf_op jit(solution)/shard_map/absorb/pallas_call | solution.py:110
  31.7 15.7 %collective-permute-done.6.refs_3_ = f32[8,128]{1,0:T(8,128)S(1)} collective-permute-done((f32[8,128]{1,0:T(8,128)S(1)}, f32[8,128]{1,0:T(8,128)S(1)}, u32[]{:S(2)}, u32[]{:S(2)}) %collective-permute-start.6) | collective-permute-done | bytes 4128 | tf_op jit(solution)/shard_map/ppermute | solution.py:256
  47.4 0.0 collective-permute-done.7.refs_4_
  47.4 0.0 collective-permute-done.8.refs_2_
  47.4 0.0 collective-permute-done.4.refs_1_
  47.4 0.0 collective-permute-done.5.refs_2_
  47.4 2.1 %collective-permute-start.9 = (bf16[128,3584]{1,0:T(8,128)(2,1)S(1)}, bf16[128,3584]{1,0:T(8,128)(2,1)S(1)}, u32[]{:S(2)}, u32[]{:S(2)}) collective-permute-start(bf16[128,3584]{1,0:T(8,128)(2,1)S(1)} %collective-permute-done.4.refs_1_), channel_id=1, source_target_pairs={{0,4},{4,8},{8,12},{12,14},{14,10},{10,6},{6,2},{2,0},{5,1},{9,5},... | collective-permute-start | bytes 2752520 | tf_op jit(solution)/shard_map/ppermute | solution.py:256
  49.5 0.5 collective-permute-start.10
  50.0 0.0 collective-permute-start.13
  50.0 1.5 %collective-permute-start.11 = (f32[8,128]{1,0:T(8,128)S(1)}, f32[8,128]{1,0:T(8,128)S(1)}, u32[]{:S(2)}, u32[]{:S(2)}) collective-permute-start(f32[8,128]{1,0:T(8,128)S(1)} %collective-permute-done.6.refs_3_), channel_id=1, source_target_pairs={{0,4},{4,8},{8,12},{12,14},{14,10},{10,6},{6,2},{2,0},{5,1},{9,5},... | collective-permute-start | bytes 12296 | tf_op jit(solution)/shard_map/ppermute | solution.py:256
  51.6 0.5 collective-permute-start.12
  52.1 2.6 %absorb.6 = (f32[896,896]{1,0:T(8,128)S(1)}, f32[448,896]{1,0:T(8,128)S(1)}, f32[448,896]{1,0:T(8,128)S(1)}, bf16[64,3584]{1,0:T(8,128)(2,1)S(1)}) custom-call(s32[5]{0:T(128)S(1)} %stack.23.refs_0_, bf16[128,3584]{1,0:T(8,128)(2,1)S(1)} %collective-permute-done.4.refs_1_, ...), custom_call_target="tpu_custom_call", output_to_operand_aliasing={{0}: (5, {}), {1}: (6, {}), {2}: (7, {})} | custom-call | flops 1 | bytes 1 | tf_op jit(solution)/shard_map/absorb/pallas_call | solution.py:110
  54.7 15.6 %collective-permute-done.11.refs_3_ = f32[8,128]{1,0:T(8,128)S(1)} collective-permute-done((f32[8,128]{1,0:T(8,128)S(1)}, f32[8,128]{1,0:T(8,128)S(1)}, u32[]{:S(2)}, u32[]{:S(2)}) %collective-permute-start.11) | collective-permute-done | bytes 4128 | tf_op jit(solution)/shard_map/ppermute | solution.py:256
  70.3 0.3 collective-permute-done.12.refs_4_
  70.5 0.0 collective-permute-done.13.refs_4_
  70.5 0.0 collective-permute-done.9.refs_1_
  70.5 0.0 collective-permute-done.10.refs_2_
  70.5 2.1 %collective-permute-start.14 = (bf16[128,3584]{1,0:T(8,128)(2,1)S(1)}, bf16[128,3584]{1,0:T(8,128)(2,1)S(1)}, u32[]{:S(2)}, u32[]{:S(2)}) collective-permute-start(bf16[128,3584]{1,0:T(8,128)(2,1)S(1)} %collective-permute-done.9.refs_1_), channel_id=1, source_target_pairs={{0,4},{4,8},{8,12},{12,14},{14,10},{10,6},{6,2},{2,0},{5,1},{9,5},... | collective-permute-start | bytes 2752520 | tf_op jit(solution)/shard_map/ppermute | solution.py:256
  72.6 2.6 %absorb.7 = (f32[896,896]{1,0:T(8,128)S(1)}, f32[448,896]{1,0:T(8,128)S(1)}, f32[448,896]{1,0:T(8,128)S(1)}, bf16[64,3584]{1,0:T(8,128)(2,1)S(1)}) custom-call(s32[5]{0:T(128)S(1)} %stack.23.refs_0_, bf16[128,3584]{1,0:T(8,128)(2,1)S(1)} %collective-permute-done.9.refs_1_, ...), custom_call_target="tpu_custom_call", output_to_operand_aliasing={{0}: (5, {}), {1}: (6, {}), {2}: (7, {})} | custom-call | flops 1 | bytes 1 | tf_op jit(solution)/shard_map/absorb/pallas_call | solution.py:110
  75.2 0.3 collective-permute-start.20
  75.6 0.2 collective-permute-start.21
  75.8 0.0 collective-permute-start.15
  75.8 0.8 collective-permute-start.18
  76.6 7.6 %collective-permute-done.15.refs_3_ = f32[8,128]{1,0:T(8,128)S(1)} collective-permute-done((f32[8,128]{1,0:T(8,128)S(1)}, f32[8,128]{1,0:T(8,128)S(1)}, u32[]{:S(2)}, u32[]{:S(2)}) %collective-permute-start.15) | collective-permute-done | bytes 4128 | tf_op jit(solution)/shard_map/ppermute | solution.py:256
  84.3 0.0 collective-permute-start.17
  84.3 0.0 collective-permute-done.18.refs_6_
  84.3 0.5 collective-permute-start.16
  84.8 2.6 %prepare_rows.2 = (bf16[512,3584]{1,0:T(8,128)(2,1)S(1)}, bf16[1792,512]{1,0:T(8,128)(2,1)S(1)}) custom-call(s32[5]{0:T(128)S(1)} %stack.23.refs_0_, bf16[32,3584]{1,0:T(8,128)(2,1)S(1)} %get-tuple-element.97.refs_1_, bf16[32,3584]{1,0:T(8,128)(2,1)S(1)} %collective-permute-done.8.refs_2_, bf16[64,3584]{1,0:T(8,128)(2,1)S(1)} %get-tuple-element.99.refs_3_, ...), custom_call_target="tpu_custom_call" | custom-call | flops 1 | bytes 1 | tf_op jit(solution)/shard_map/prepare_rows/pallas_call | solution.py:146
  87.4 0.0 collective-permute-done.17.refs_2_
  87.4 1.4 %prepare_rows.3 = (bf16[512,3584]{1,0:T(8,128)(2,1)S(1)}, bf16[1792,512]{1,0:T(8,128)(2,1)S(1)}) custom-call(s32[5]{0:T(128)S(1)} %stack.23.refs_0_, bf16[64,3584]{1,0:T(8,128)(2,1)S(1)} %get-tuple-element.96.refs_1_, bf16[64,3584]{1,0:T(8,128)(2,1)S(1)} %collective-permute-done.17.refs_2_, ...), custom_call_target="tpu_custom_call", output_to_operand_aliasing={{0}: (3, {}), {1}: (4, {})} | custom-call | flops 1 | bytes 1 | tf_op jit(solution)/shard_map/prepare_rows/pallas_call | solution.py:146
  88.8 0.0 collective-permute-done.16.refs_4_
  88.8 0.0 collective-permute-done.14.refs_1_
  88.8 0.1 collective-permute-start.19
  88.9 0.0 collective-permute-done.20.refs_6_
  88.9 0.0 collective-permute-done.21.refs_7_
  88.9 2.4 %collective-permute-done.19.refs_2_ = bf16[128,3584]{1,0:T(8,128)(2,1)S(1)} collective-permute-done((bf16[128,3584]{1,0:T(8,128)(2,1)S(1)}, bf16[128,3584]{1,0:T(8,128)(2,1)S(1)}, u32[]{:S(2)}, u32[]{:S(2)}) %collective-permute-start.19) | collective-permute-done | bytes 917536 | tf_op jit(solution)/shard_map/ppermute | solution.py:253
  91.4 12.4 %finish.1 = (f32[1792,3584]{1,0:T(8,128)}, f32[1,896,896]{2,1,0:T(8,128)}, bf16[512,3584]{1,0:T(8,128)(2,1)S(1)}, bf16[1792,512]{1,0:T(8,128)(2,1)S(1)}) custom-call(s32[5]{0:T(128)S(1)} %stack.23.refs_0_, bf16[128,3584]{1,0:T(8,128)(2,1)S(1)} %collective-permute-done.14.refs_1_, ...), custom_call_target="tpu_custom_call", output_to_operand_aliasing={{2}: (8, {}), {3}: (9, {})} | custom-call | flops 1 | bytes 1 | tf_op jit(solution)/shard_map/finish/pallas_call | solution.py:196
  (1 shorter events, 0.0 us)
Async XLA Ops:
  0.6 24.0 %collective-permute-start = (bf16[128,3584]{1,0:T(8,128)(2,1)}, bf16[128,3584]{1,0:T(8,128)(2,1)S(1)}, u32[]{:S(2)}, u32[]{:S(2)}) collective-permute-start(bf16[128,3584]{1,0:T(8,128)(2,1)} %refs_1_.1), channel_id=1, source_target_pairs={{0,4},{4,8},{8,12},{12,14},{14,10},{10,6},{6,2},{2,0},{5,1},{9,5},... | collective-permute-start | bytes 2752520 | tf_op jit(solution)/shard_map/ppermute | solution.py:256
  3.7 20.9 %collective-permute-start.1 = (bf16[128,3584]{1,0:T(8,128)(2,1)}, bf16[128,3584]{1,0:T(8,128)(2,1)S(1)}, u32[]{:S(2)}, u32[]{:S(2)}) collective-permute-start(bf16[128,3584]{1,0:T(8,128)(2,1)} %refs_1_.1), channel_id=1, source_target_pairs={{1,5},{5,9},{9,13},{13,15},{15,11},{11,7},{7,3},{3,1},{4,0},{8,4},... | collective-permute-start | bytes 2752520 | tf_op jit(solution)/shard_map/ppermute | solution.py:256
  3.7 0.7 copy-start.1
  4.4 0.7 copy-start.2
  5.1 19.2 %collective-permute-start.3 = (f32[8,128]{1,0:T(8,128)S(1)}, f32[8,128]{1,0:T(8,128)S(1)}, u32[]{:S(2)}, u32[]{:S(2)}) collective-permute-start(f32[8,128]{1,0:T(8,128)S(1)} %make_table.1.refs_2_), channel_id=1, source_target_pairs={{1,5},{5,9},{9,13},{13,15},{15,11},{11,7},{7,3},{3,1},{4,0},{8,4},... | collective-permute-start | bytes 12296 | tf_op jit(solution)/shard_map/ppermute | solution.py:256
  7.1 17.5 %collective-permute-start.2 = (f32[8,128]{1,0:T(8,128)S(1)}, f32[8,128]{1,0:T(8,128)S(1)}, u32[]{:S(2)}, u32[]{:S(2)}) collective-permute-start(f32[8,128]{1,0:T(8,128)S(1)} %make_table.1.refs_2_), channel_id=1, source_target_pairs={{0,4},{4,8},{8,12},{12,14},{14,10},{10,6},{6,2},{2,0},{5,1},{9,5},... | collective-permute-start | bytes 12296 | tf_op jit(solution)/shard_map/ppermute | solution.py:256
  7.3 1.2 %copy-start = (bf16[128,3584]{1,0:T(8,128)(2,1)S(1)}, bf16[128,3584]{1,0:T(8,128)(2,1)}, u32[]{:S(2)}) copy-start(bf16[128,3584]{1,0:T(8,128)(2,1)} %refs_1_.1) | copy-start | bytes 2752516
  24.6 22.8 %collective-permute-start.4 = (bf16[128,3584]{1,0:T(8,128)(2,1)S(1)}, bf16[128,3584]{1,0:T(8,128)(2,1)S(1)}, u32[]{:S(2)}, u32[]{:S(2)}) collective-permute-start(bf16[128,3584]{1,0:T(8,128)(2,1)S(1)} %collective-permute-done.refs_1_), channel_id=1, source_target_pairs={{0,4},{4,8},{8,12},{12,14},{14,10},{10,6},{6,2},{2,0},{5,1},{9,5},... | collective-permute-start | bytes 2752520 | tf_op jit(solution)/shard_map/ppermute | solution.py:256
  26.2 21.2 %collective-permute-start.5 = (bf16[128,3584]{1,0:T(8,128)(2,1)S(1)}, bf16[128,3584]{1,0:T(8,128)(2,1)S(1)}, u32[]{:S(2)}, u32[]{:S(2)}) collective-permute-start(bf16[128,3584]{1,0:T(8,128)(2,1)S(1)} %collective-permute-done.1.refs_2_), channel_id=1, source_target_pairs={{1,5},{5,9},{9,13},{13,15},{15,11},{11,7},{7,3},{3,1},{4,0},{8,4},... | collective-permute-start | bytes 2752520 | tf_op jit(solution)/shard_map/ppermute | solution.py:256
  27.1 20.3 %collective-permute-start.8 = (bf16[32,3584]{1,0:T(8,128)(2,1)S(1)}, bf16[32,3584]{1,0:T(8,128)(2,1)S(1)}, u32[]{:S(2)}, u32[]{:S(2)}) collective-permute-start(bf16[32,3584]{1,0:T(8,128)(2,1)S(1)} %get-tuple-element.97.refs_1_), channel_id=1, source_target_pairs={{0,1},{1,0},{2,3},{3,2},{4,5},{5,4},{6,7},{7,6},{8,9},{9,8},{10,11... | collective-permute-start | bytes 688136 | tf_op jit(solution)/shard_map/ppermute | solution.py:253
  27.1 20.3 %collective-permute-start.6 = (f32[8,128]{1,0:T(8,128)S(1)}, f32[8,128]{1,0:T(8,128)S(1)}, u32[]{:S(2)}, u32[]{:S(2)}) collective-permute-start(f32[8,128]{1,0:T(8,128)S(1)} %collective-permute-done.2.refs_3_), channel_id=1, source_target_pairs={{0,4},{4,8},{8,12},{12,14},{14,10},{10,6},{6,2},{2,0},{5,1},{9,5},... | collective-permute-start | bytes 12296 | tf_op jit(solution)/shard_map/ppermute | solution.py:256
  28.2 19.2 %collective-permute-start.7 = (f32[8,128]{1,0:T(8,128)S(1)}, f32[8,128]{1,0:T(8,128)S(1)}, u32[]{:S(2)}, u32[]{:S(2)}) collective-permute-start(f32[8,128]{1,0:T(8,128)S(1)} %collective-permute-done.3.refs_4_), channel_id=1, source_target_pairs={{1,5},{5,9},{9,13},{13,15},{15,11},{11,7},{7,3},{3,1},{4,0},{8,4},... | collective-permute-start | bytes 12296 | tf_op jit(solution)/shard_map/ppermute | solution.py:256
  47.4 23.1 %collective-permute-start.9 = (bf16[128,3584]{1,0:T(8,128)(2,1)S(1)}, bf16[128,3584]{1,0:T(8,128)(2,1)S(1)}, u32[]{:S(2)}, u32[]{:S(2)}) collective-permute-start(bf16[128,3584]{1,0:T(8,128)(2,1)S(1)} %collective-permute-done.4.refs_1_), channel_id=1, source_target_pairs={{0,4},{4,8},{8,12},{12,14},{14,10},{10,6},{6,2},{2,0},{5,1},{9,5},... | collective-permute-start | bytes 2752520 | tf_op jit(solution)/shard_map/ppermute | solution.py:256
  49.5 21.0 %collective-permute-start.10 = (bf16[128,3584]{1,0:T(8,128)(2,1)S(1)}, bf16[128,3584]{1,0:T(8,128)(2,1)S(1)}, u32[]{:S(2)}, u32[]{:S(2)}) collective-permute-start(bf16[128,3584]{1,0:T(8,128)(2,1)S(1)} %collective-permute-done.5.refs_2_), channel_id=1, source_target_pairs={{1,5},{5,9},{9,13},{13,15},{15,11},{11,7},{7,3},{3,1},{4,0},{8,4},... | collective-permute-start | bytes 2752520 | tf_op jit(solution)/shard_map/ppermute | solution.py:256
  50.0 20.5 %collective-permute-start.13 = (bf16[64,3584]{1,0:T(8,128)(2,1)S(1)}, bf16[64,3584]{1,0:T(8,128)(2,1)S(1)}, u32[]{:S(2)}, u32[]{:S(2)}) collective-permute-start(bf16[64,3584]{1,0:T(8,128)(2,1)S(1)} %get-tuple-element.99.refs_3_), channel_id=1, source_target_pairs={{0,1},{1,0},{2,3},{3,2},{4,5},{5,4},{6,7},{7,6},{8,9},{9,8},{10,11... | collective-permute-start | bytes 1376264 | tf_op jit(solution)/shard_map/ppermute | solution.py:253
  50.0 20.2 %collective-permute-start.11 = (f32[8,128]{1,0:T(8,128)S(1)}, f32[8,128]{1,0:T(8,128)S(1)}, u32[]{:S(2)}, u32[]{:S(2)}) collective-permute-start(f32[8,128]{1,0:T(8,128)S(1)} %collective-permute-done.6.refs_3_), channel_id=1, source_target_pairs={{0,4},{4,8},{8,12},{12,14},{14,10},{10,6},{6,2},{2,0},{5,1},{9,5},... | collective-permute-start | bytes 12296 | tf_op jit(solution)/shard_map/ppermute | solution.py:256
  51.6 19.0 %collective-permute-start.12 = (f32[8,128]{1,0:T(8,128)S(1)}, f32[8,128]{1,0:T(8,128)S(1)}, u32[]{:S(2)}, u32[]{:S(2)}) collective-permute-start(f32[8,128]{1,0:T(8,128)S(1)} %collective-permute-done.7.refs_4_), channel_id=1, source_target_pairs={{1,5},{5,9},{9,13},{13,15},{15,11},{11,7},{7,3},{3,1},{4,0},{8,4},... | collective-permute-start | bytes 12296 | tf_op jit(solution)/shard_map/ppermute | solution.py:256
  70.5 18.3 %collective-permute-start.14 = (bf16[128,3584]{1,0:T(8,128)(2,1)S(1)}, bf16[128,3584]{1,0:T(8,128)(2,1)S(1)}, u32[]{:S(2)}, u32[]{:S(2)}) collective-permute-start(bf16[128,3584]{1,0:T(8,128)(2,1)S(1)} %collective-permute-done.9.refs_1_), channel_id=1, source_target_pairs={{0,4},{4,8},{8,12},{12,14},{14,10},{10,6},{6,2},{2,0},{5,1},{9,5},... | collective-permute-start | bytes 2752520 | tf_op jit(solution)/shard_map/ppermute | solution.py:256
  75.2 13.7 %collective-permute-start.20 = (f32[448,896]{1,0:T(8,128)S(1)}, f32[448,896]{1,0:T(8,128)S(1)}, u32[]{:S(2)}, u32[]{:S(2)}) collective-permute-start(f32[448,896]{1,0:T(8,128)S(1)} %get-tuple-element.110), channel_id=1, source_target_pairs={{0,1},{1,0},{2,3},{3,2},{4,5},{5,4},{6,7},{7,6},{8,9},{9,8},{10,11... | collective-permute-start | bytes 4816904 | tf_op jit(solution)/shard_map/ppermute | solution.py:253
  75.6 13.3 %collective-permute-start.21 = (f32[448,896]{1,0:T(8,128)S(1)}, f32[448,896]{1,0:T(8,128)S(1)}, u32[]{:S(2)}, u32[]{:S(2)}) collective-permute-start(f32[448,896]{1,0:T(8,128)S(1)} %get-tuple-element.111), channel_id=1, source_target_pairs={{0,1},{1,0},{2,3},{3,2},{4,5},{5,4},{6,7},{7,6},{8,9},{9,8},{10,11... | collective-permute-start | bytes 4816904 | tf_op jit(solution)/shard_map/ppermute | solution.py:253
  75.8 8.5 %collective-permute-start.15 = (f32[8,128]{1,0:T(8,128)S(1)}, f32[8,128]{1,0:T(8,128)S(1)}, u32[]{:S(2)}, u32[]{:S(2)}) collective-permute-start(f32[8,128]{1,0:T(8,128)S(1)} %collective-permute-done.11.refs_3_), channel_id=1, source_target_pairs={{0,4},{4,8},{8,12},{12,14},{14,10},{10,6},{6,2},{2,0},{5,1},{9,5},... | collective-permute-start | bytes 12296 | tf_op jit(solution)/shard_map/ppermute | solution.py:256
  75.8 8.5 %collective-permute-start.18 = (bf16[64,3584]{1,0:T(8,128)(2,1)S(1)}, bf16[64,3584]{1,0:T(8,128)(2,1)S(1)}, u32[]{:S(2)}, u32[]{:S(2)}) collective-permute-start(bf16[64,3584]{1,0:T(8,128)(2,1)S(1)} %get-tuple-element.101.refs_5_), channel_id=1, source_target_pairs={{0,1},{1,0},{2,3},{3,2},{4,5},{5,4},{6,7},{7,6},{8,9},{9,8},{10,11... | collective-permute-start | bytes 1376264 | tf_op jit(solution)/shard_map/ppermute | solution.py:253
  84.3 3.1 %collective-permute-start.17 = (bf16[64,3584]{1,0:T(8,128)(2,1)S(1)}, bf16[64,3584]{1,0:T(8,128)(2,1)S(1)}, u32[]{:S(2)}, u32[]{:S(2)}) collective-permute-start(bf16[64,3584]{1,0:T(8,128)(2,1)S(1)} %get-tuple-element.96.refs_1_), channel_id=1, source_target_pairs={{0,1},{1,0},{2,3},{3,2},{4,5},{5,4},{6,7},{7,6},{8,9},{9,8},{10,11... | collective-permute-start | bytes 1376264 | tf_op jit(solution)/shard_map/ppermute | solution.py:253
  84.3 4.5 %collective-permute-start.16 = (f32[8,128]{1,0:T(8,128)S(1)}, f32[8,128]{1,0:T(8,128)S(1)}, u32[]{:S(2)}, u32[]{:S(2)}) collective-permute-start(f32[8,128]{1,0:T(8,128)S(1)} %collective-permute-done.15.refs_3_), channel_id=1, source_target_pairs={{0,1},{1,0},{2,3},{3,2},{4,5},{5,4},{6,7},{7,6},{8,9},{9,8},{10,11... | collective-permute-start | bytes 12296 | tf_op jit(solution)/shard_map/ppermute | solution.py:253
  88.8 2.5 %collective-permute-start.19 = (bf16[128,3584]{1,0:T(8,128)(2,1)S(1)}, bf16[128,3584]{1,0:T(8,128)(2,1)S(1)}, u32[]{:S(2)}, u32[]{:S(2)}) collective-permute-start(bf16[128,3584]{1,0:T(8,128)(2,1)S(1)} %collective-permute-done.14.refs_1_), channel_id=1, source_target_pairs={{0,1},{1,0},{2,3},{3,2},{4,5},{5,4},{6,7},{7,6},{8,9},{9,8},{10,11... | collective-permute-start | bytes 2752520 | tf_op jit(solution)/shard_map/ppermute | solution.py:253

commit v7 on v6

--- a/solution.py
+++ b/solution.py
@@ -11,6 +11,7 @@
 EXP = 8
 CAP = 32
 CORES = 2
+TABLE = 128
 STEP = 256
 HALVES = 2
 VMEM = pl.BlockSpec(memory_space=pltpu.VMEM)
@@ -27,31 +28,62 @@
     return pltpu.CompilerParams(vmem_limit_bytes=mib * 2**20)
 
 
-def table_kernel(ids, weights, roots):
-    row_at = lax.broadcasted_iota(jnp.int32, roots.shape, 0)
-    table = jnp.zeros(roots.shape, F32)
+def message_kernel(tokens, ids_from, weights_from, out, ids, weights, table, arrived):
+    rows, width = tokens.shape
+    copies = [
+        pltpu.make_async_copy(source, target, arrived.at[k])
+        for k, (source, target) in enumerate(
+            [
+                (ids_from, ids),
+                (weights_from, weights),
+                (tokens, out.at[:, :width]),
+                (table, out.at[:, width:]),
+            ]
+        )
+    ]
+    for copy in copies[:3]:
+        copy.start()
+    for copy in copies[:2]:
+        copy.wait()
+    row_at = lax.broadcasted_iota(jnp.int32, (TABLE, rows), 0)
+    roots = jnp.zeros((TABLE, rows), F32)
     for e in range(EXP):
         weight = jnp.sum(jnp.where(ids[...] == e, weights[...], 0.0), axis=0, keepdims=True)
-        table = jnp.where(row_at == e, weight, table)
-    roots[...] = jnp.sqrt(table)
-
-
-def make_table(ids, weights):
+        roots = jnp.where(row_at % EXP == e, jnp.sqrt(weight), roots)
+    high = roots.astype(BF16).astype(F32)
+    middle = (roots - high).astype(BF16).astype(F32)
+    low = roots - high - middle
+    terms = jnp.where(row_at < EXP, high, jnp.where(row_at < 2 * EXP, middle, low))
+    table[...] = jnp.where(row_at < 3 * EXP, terms, 0.0).T.astype(BF16)
+    copies[3].start()
+    for copy in copies[2:]:
+        copy.wait()
+
+
+def make_message(tokens, ids, weights):
+    rows, width = tokens.shape
     return pl.pallas_call(
-        table_kernel,
-        out_shape=jax.ShapeDtypeStruct((EXP, ids.shape[0]), F32),
-        in_specs=[VMEM] * 2,
-        out_specs=VMEM,
+        message_kernel,
+        out_shape=jax.ShapeDtypeStruct((rows, width + TABLE), BF16),
+        in_specs=[ANY] * 3,
+        out_specs=ANY,
+        scratch_shapes=[
+            pltpu.VMEM(ids.shape[::-1], jnp.int32),
+            pltpu.VMEM(ids.shape[::-1], F32),
+            pltpu.VMEM((rows, TABLE), BF16),
+            pltpu.SemaphoreType.DMA((4,)),
+        ],
         cost_estimate=SMALL,
-        compiler_params=params(8),
-        name="make_table",
-    )(ids.T, weights.T)
-
-
-def choose(expert, roots):
-    rows = roots.shape[1]
-    row_at = lax.broadcasted_iota(jnp.int32, roots.shape, 0)
-    root = jnp.sum(jnp.where(row_at == expert, roots[...], 0.0), axis=0, keepdims=True)
+        compiler_params=params(57),
+        name="make_message",
+    )(tokens, ids.T, weights.T)
+
+
+def choose(expert, table):
+    rows = table.shape[0]
+    row_at = lax.broadcasted_iota(jnp.int32, (TABLE, rows), 0)
+    ours = jnp.logical_and(row_at % EXP == expert, row_at < 3 * EXP)
+    root = jnp.sum(jnp.where(ours, table.astype(F32).T, 0.0), axis=0, keepdims=True)
     root = jnp.broadcast_to(root, (CAP, rows))
     member = root > 0.0
     from_at = lax.broadcasted_iota(jnp.int32, (rows, rows), 0)
@@ -65,15 +97,16 @@
     return select.astype(F32).astype(BF16), scale
 
 
-def pack(expert, roots, piece):
-    select, scale = choose(expert, roots)
-    picked = jnp.dot(select, piece[...], preferred_element_type=F32)
+def pack(expert, piece):
+    width = piece.shape[1] - TABLE
+    select, scale = choose(expert, piece[:, width:])
+    picked = jnp.dot(select, piece[:, :width], preferred_element_type=F32)
     return (picked * scale).astype(BF16)
 
 
 def fetch_tile(index, pieces, scratch):
     edge = scratch.shape[1]
-    for b in range(pieces[0].shape[1] // edge):
+    for b in range((pieces[0].shape[1] - TABLE) // edge):
 
         @pl.when(index == b)
         def _(b=b):
@@ -86,7 +119,7 @@
 
 def absorb_kernel(count, started, *refs):
     scalars, refs = refs[0], refs[1:]
-    pieces, tables, refs = refs[:count], refs[count : 2 * count], refs[2 * count :]
+    pieces, refs = refs[:count], refs[count:]
     sums = 1 + HALVES
     before, refs = refs[: sums * started], refs[sums * started :]
     tiles, packed, scratch = refs[:sums], refs[sums], refs[sums + 1 :]
@@ -101,25 +134,26 @@
             part = update[h * rows : (h + 1) * rows]
             tile[...] = before[k + h][...] + part if started else part
     for k in range(count):
-        packed[k * CAP : (k + 1) * CAP, :] = pack(scalars[0], tables[k], pieces[k])
-
-
-def absorb(scalars, pieces, tables, before, edge):
+        packed[k * CAP : (k + 1) * CAP, :] = pack(scalars[0], pieces[k])
+
+
+def absorb(scalars, pieces, before, edge):
     rows, width = pieces[0].shape
+    width -= TABLE
     count = len(pieces)
     *tiles, packed = pl.pallas_call(
         functools.partial(absorb_kernel, count, bool(before)),
         out_shape=[jax.ShapeDtypeStruct((edge, edge), F32)]
         + [jax.ShapeDtypeStruct((edge // HALVES, edge), F32)] * HALVES
         + [jax.ShapeDtypeStruct((count * CAP, width), BF16)],
-        in_specs=[SMEM] + [VMEM] * (2 * count + len(before)),
+        in_specs=[SMEM] + [VMEM] * (count + len(before)),
         out_specs=[VMEM] * (2 + HALVES),
         scratch_shapes=[pltpu.VMEM((count * rows, edge), BF16)] * 3,
         cost_estimate=SMALL,
-        input_output_aliases={1 + 2 * count + k: k for k in range(len(before))},
+        input_output_aliases={1 + count + k: k for k in range(len(before))},
         compiler_params=params(14),
         name="absorb",
-    )(scalars, *pieces, *tables, *before)
+    )(scalars, *pieces, *before)
     return tiles, packed
 
 
@@ -160,12 +194,12 @@
 
 def finish_kernel(final, *refs):
     scalars, *refs = refs
-    pieces, tables, refs = refs[:2], refs[2:4], refs[4:]
+    pieces, refs = refs[:2], refs[2:]
     before, refs = refs[: 1 + HALVES], refs[3 + HALVES :]
     hessian, tile, rows, across, staging, sum_of_tile, left, right, sent = refs
     at = rows.shape[0] - CAP * len(pieces)
     packed = jnp.concatenate(
-        [pack(scalars[0], table, piece) for piece, table in zip(pieces, tables)], axis=0
+        [pack(scalars[0], piece) for piece in pieces], axis=0
     )
     place_rows(scalars[4], packed, at, rows, across)
     copies = []
@@ -187,7 +221,7 @@
         copy.wait()
 
 
-def finish(scalars, pieces, tables, before, operands, final):
+def finish(scalars, pieces, before, operands, final):
     edge = before[0].shape[0]
     rows, across = operands
     slab, width = across.shape[0], rows.shape[1]
@@ -201,7 +235,7 @@
             jax.ShapeDtypeStruct(rows.shape, BF16),
             jax.ShapeDtypeStruct(across.shape, BF16),
         ],
-        in_specs=[SMEM] + [VMEM] * (7 + HALVES),
+        in_specs=[SMEM] + [VMEM] * (5 + HALVES),
         out_specs=[ANY, ANY, VMEM, VMEM],
         scratch_shapes=[
             pltpu.VMEM((blocks, slab, STEP), F32),
@@ -210,11 +244,11 @@
             pltpu.VMEM((count, edge), BF16),
             pltpu.SemaphoreType.DMA((blocks + 1,)),
         ],
-        input_output_aliases={6 + HALVES: 2, 7 + HALVES: 3},
+        input_output_aliases={4 + HALVES: 2, 5 + HALVES: 3},
         cost_estimate=SMALL,
         compiler_params=params(38),
         name="finish",
-    )(scalars, *pieces, *tables, *before, rows, across)[:2]
+    )(scalars, *pieces, *before, rows, across)[:2]
 
 
 def ring_of(chips):
@@ -262,25 +296,22 @@
         at = 4 * CAP * (index - 1) if index else total - 4 * CAP
         return [at, at + (2 if index else 1) * CAP]
 
-    roots = make_table(route_ids, route_weights)
-    pieces, tables = [tokens], [roots]
+    pieces = [make_message(tokens, route_ids, route_weights)]
     packs, tiles = {}, []
     for step in range(1, rounds + 1):
         count = CORES if step < rounds else 1
         repeat = CORES if step == 1 else 1
         new_pieces = advance(pieces * repeat, count)
-        new_tables = advance(tables * repeat, count)
         if step > 1:
             packs[step - 2] = [packs[step - 2][0], swap(packs[step - 2][0])]
-        tiles, packed = absorb(scalars, pieces, tables, tiles, edge)
+        tiles, packed = absorb(scalars, pieces, tiles, edge)
         packs[step - 1] = [packed]
         if step < rounds:
-            state = (new_pieces, new_tables, packs, tiles)
-            new_pieces, new_tables, packs, tiles = lax.optimization_barrier(state)
-        pieces, tables = new_pieces, new_tables
+            state = (new_pieces, packs, tiles)
+            new_pieces, packs, tiles = lax.optimization_barrier(state)
+        pieces = new_pieces
     packs[rounds - 1].append(swap(packs[rounds - 1][0]))
     other_sums = [swap(part) for part in tiles[1:]]
-    tables = [tables[0], swap(tables[0])]
     operands = []
     for chosen in (range(rounds - 1), [rounds - 1]):
         operands = prepare(
@@ -289,10 +320,10 @@
             [at for index in chosen for at in place(index)],
             operands, total, slab,
         )
-    pieces, tables, operands = lax.optimization_barrier((pieces, tables, operands))
+    pieces, operands = lax.optimization_barrier((pieces, operands))
     return tuple(
         finish(
-            scalars, [pieces[0], swap(pieces[0])], tables, [tiles[0], *other_sums], operands,
+            scalars, [pieces[0], swap(pieces[0])], [tiles[0], *other_sums], operands,
             1.0 / (devices * tok_rows),
         )
     )

time: 104 us -> 131 us (1.26)
  Pallas kernels: 26.1 us -> 55.1 us
  starting transfers between devices: 18.5 us -> 9.72 us
  waiting for transfers between devices: 55.9 us -> 63.7 us
  local copies, waits for them, and re-layouts: 2.64 us -> 1.27 us
    pallas_call x1, Pallas kernels: 0.02 us -> 28.9 us  [make_message(): pl.pallas_call(message_kernel, out_shape=jax.ShapeDtypeStruct((rows, widt...]
    ppermute x14 -> x7, starting transfers between devices: 16.5 us -> 8.1 us  [advance(): return [lax.ppermute(held[k], 'tok', streams[k]) for k in range(count)]]
    ppermute x8 -> x7, waiting for transfers between devices: 2.46 us -> 7.6 us  [swap(): return lax.ppermute(array, 'tok', pair)]
    ppermute x14 -> x7, waiting for transfers between devices: 53.4 us -> 56.1 us  [advance(): return [lax.ppermute(held[k], 'tok', streams[k]) for k in range(count)]]
    unnamed x6 -> x2, local copies, waits for them, and re-layouts: 2.55 us -> 1.19 us
  transfers between devices with their start and end apart: 22 -> 14, of which waited for: 7 -> 6; matrix products, arithmetic and copies ran while one was open for 0% -> 0% of each run, Pallas kernels for 13% -> 10%
where the time goes in v7:
time: 131 us
  waiting for transfers between devices  63.7 us (49%)
  Pallas kernels  55.1 us (42%)
  starting transfers between devices  9.72 us (7%)
    ppermute x7, waiting for transfers between devices, advance(): return [lax.ppermute(held[k], 'tok', streams[k]) for k in range(count)]  56.1 us
    pallas_call x1, Pallas kernels, make_message(): pl.pallas_call(message_kernel, out_shape=jax.ShapeDtypeStruct((rows, widt...  28.9 us
    pallas_call x1, Pallas kernels, finish(): pl.pallas_call(functools.partial(finish_kernel, final), out_shape=[jax.Sh...  12.5 us
    pallas_call x4, Pallas kernels, absorb(): pl.pallas_call(functools.partial(absorb_kernel, count, bool(before)), out...  9.68 us
    ppermute x7, starting transfers between devices, advance(): return [lax.ppermute(held[k], 'tok', streams[k]) for k in range(count)]  8.1 us
    ppermute x7, waiting for transfers between devices, swap(): return lax.ppermute(array, 'tok', pair)  7.6 us
    pallas_call x2, Pallas kernels, prepare(): pl.pallas_call(functools.partial(prepare_kernel, places), out_shape=[jax....  3.97 us
  transfers between devices with their start and end apart: 14, of which 6 were waited for; matrix products, arithmetic and copies ran while one was open for 0% of the time, Pallas kernels for 10%

profile of v7, /device:TPU:0, one launch (start us, length us, event | category | flops | bytes accessed | tf_op | source)
XLA Modules:
  0.0 130.6 jit_solution(5860670522739309214)
XLA Ops:
  0.6 28.9 %make_message.1.refs_1_ = bf16[128,3712]{1,0:T(8,128)(2,1)} custom-call(bf16[128,3584]{1,0:T(8,128)(2,1)} %tokens.1, s32[8,128]{1,0:T(8,128)} %bitcast.7, f32[8,128]{1,0:T(8,128)} %bitcast.8), custom_call_target="tpu_custom_call" | custom-call | flops 1 | bytes 1 | tf_op jit(solution)/shard_map/make_message/pallas_call | solution.py:65
  29.6 3.0 %collective-permute-start.1 = (bf16[128,3712]{1,0:T(8,128)(2,1)}, bf16[128,3712]{1,0:T(8,128)(2,1)S(1)}, u32[]{:S(2)}, u32[]{:S(2)}) collective-permute-start(bf16[128,3712]{1,0:T(8,128)(2,1)} %make_message.1.refs_1_), channel_id=1, source_target_pairs={{1,5},{5,9},{9,13},{13,15},{15,11},{11,7},{7,3},{3,1},{4,0},{8,4},... | collective-permute-start | bytes 2850824 | tf_op jit(solution)/shard_map/ppermute | solution.py:290
  32.6 0.1 collective-permute-start
  32.7 0.1 stack.23.refs_0_
  32.8 0.0 copy-start
  32.8 1.2 copy-done
  34.0 1.9 %absorb.4 = (f32[896,896]{1,0:T(8,128)S(1)}, f32[448,896]{1,0:T(8,128)S(1)}, f32[448,896]{1,0:T(8,128)S(1)}, bf16[32,3584]{1,0:T(8,128)(2,1)S(1)}) custom-call(s32[5]{0:T(128)S(1)} %stack.23.refs_0_, bf16[128,3712]{1,0:T(8,128)(2,1)S(1)} %copy-done), custom_call_target="tpu_custom_call" | custom-call | flops 1 | bytes 1 | tf_op jit(solution)/shard_map/absorb/pallas_call | solution.py:144
  35.9 18.3 %collective-permute-done.1.refs_2_ = bf16[128,3712]{1,0:T(8,128)(2,1)S(1)} collective-permute-done((bf16[128,3712]{1,0:T(8,128)(2,1)}, bf16[128,3712]{1,0:T(8,128)(2,1)S(1)}, u32[]{:S(2)}, u32[]{:S(2)}) %collective-permute-start.1) | collective-permute-done | bytes 950304 | tf_op jit(solution)/shard_map/ppermute | solution.py:290
  54.2 0.0 collective-permute-done.refs_1_
  54.2 2.4 %collective-permute-start.2 = (bf16[128,3712]{1,0:T(8,128)(2,1)S(1)}, bf16[128,3712]{1,0:T(8,128)(2,1)S(1)}, u32[]{:S(2)}, u32[]{:S(2)}) collective-permute-start(bf16[128,3712]{1,0:T(8,128)(2,1)S(1)} %collective-permute-done.refs_1_), channel_id=1, source_target_pairs={{0,4},{4,8},{8,12},{12,14},{14,10},{10,6},{6,2},{2,0},{5,1},{9,5},... | collective-permute-start | bytes 2850824 | tf_op jit(solution)/shard_map/ppermute | solution.py:290
  56.6 0.0 collective-permute-start.3
  56.6 0.0 collective-permute-start.4
  56.6 2.6 %absorb.5 = (f32[896,896]{1,0:T(8,128)S(1)}, f32[448,896]{1,0:T(8,128)S(1)}, f32[448,896]{1,0:T(8,128)S(1)}, bf16[64,3584]{1,0:T(8,128)(2,1)S(1)}) custom-call(s32[5]{0:T(128)S(1)} %stack.23.refs_0_, bf16[128,3712]{1,0:T(8,128)(2,1)S(1)} %collective-permute-done.refs_1_, ...), custom_call_target="tpu_custom_call", output_to_operand_aliasing={{0}: (3, {}), {1}: (4, {}), {2}: (5, {})} | custom-call | flops 1 | bytes 1 | tf_op jit(solution)/shard_map/absorb/pallas_call | solution.py:144
  59.2 0.0 collective-permute-done.4.refs_2_
  59.2 18.3 %collective-permute-done.2.refs_1_ = bf16[128,3712]{1,0:T(8,128)(2,1)S(1)} collective-permute-done((bf16[128,3712]{1,0:T(8,128)(2,1)S(1)}, bf16[128,3712]{1,0:T(8,128)(2,1)S(1)}, u32[]{:S(2)}, u32[]{:S(2)}) %collective-permute-start.2) | collective-permute-done | bytes 950304 | tf_op jit(solution)/shard_map/ppermute | solution.py:290
  77.5 0.4 collective-permute-done.3.refs_2_
  78.0 1.8 %collective-permute-start.5 = (bf16[128,3712]{1,0:T(8,128)(2,1)S(1)}, bf16[128,3712]{1,0:T(8,128)(2,1)S(1)}, u32[]{:S(2)}, u32[]{:S(2)}) collective-permute-start(bf16[128,3712]{1,0:T(8,128)(2,1)S(1)} %collective-permute-done.2.refs_1_), channel_id=1, source_target_pairs={{0,4},{4,8},{8,12},{12,14},{14,10},{10,6},{6,2},{2,0},{5,1},{9,5},... | collective-permute-start | bytes 2850824 | tf_op jit(solution)/shard_map/ppermute | solution.py:290
  79.7 0.3 collective-permute-start.6
  80.0 0.0 collective-permute-start.7
  80.0 2.6 %absorb.6 = (f32[896,896]{1,0:T(8,128)S(1)}, f32[448,896]{1,0:T(8,128)S(1)}, f32[448,896]{1,0:T(8,128)S(1)}, bf16[64,3584]{1,0:T(8,128)(2,1)S(1)}) custom-call(s32[5]{0:T(128)S(1)} %stack.23.refs_0_, bf16[128,3712]{1,0:T(8,128)(2,1)S(1)} %collective-permute-done.2.refs_1_, ...), custom_call_target="tpu_custom_call", output_to_operand_aliasing={{0}: (3, {}), {1}: (4, {}), {2}: (5, {})} | custom-call | flops 1 | bytes 1 | tf_op jit(solution)/shard_map/absorb/pallas_call | solution.py:144
  82.6 0.0 collective-permute-done.7.refs_4_
  82.6 19.0 %collective-permute-done.5.refs_1_ = bf16[128,3712]{1,0:T(8,128)(2,1)S(1)} collective-permute-done((bf16[128,3712]{1,0:T(8,128)(2,1)S(1)}, bf16[128,3712]{1,0:T(8,128)(2,1)S(1)}, u32[]{:S(2)}, u32[]{:S(2)}) %collective-permute-start.5) | collective-permute-done | bytes 950304 | tf_op jit(solution)/shard_map/ppermute | solution.py:290
  101.6 0.0 collective-permute-done.6.refs_2_
  101.6 0.5 collective-permute-start.8
  102.1 2.6 %absorb.7 = (f32[896,896]{1,0:T(8,128)S(1)}, f32[448,896]{1,0:T(8,128)S(1)}, f32[448,896]{1,0:T(8,128)S(1)}, bf16[64,3584]{1,0:T(8,128)(2,1)S(1)}) custom-call(s32[5]{0:T(128)S(1)} %stack.23.refs_0_, bf16[128,3712]{1,0:T(8,128)(2,1)S(1)} %collective-permute-done.5.refs_1_, ...), custom_call_target="tpu_custom_call", output_to_operand_aliasing={{0}: (3, {}), {1}: (4, {}), {2}: (5, {})} | custom-call | flops 1 | bytes 1 | tf_op jit(solution)/shard_map/absorb/pallas_call | solution.py:144
  104.7 0.6 collective-permute-start.12
  105.3 0.1 collective-permute-start.13
  105.4 0.4 collective-permute-start.10
  105.8 0.1 collective-permute-start.9
  105.9 5.4 %collective-permute-done.10.refs_6_ = bf16[64,3584]{1,0:T(8,128)(2,1)S(1)} collective-permute-done((bf16[64,3584]{1,0:T(8,128)(2,1)S(1)}, bf16[64,3584]{1,0:T(8,128)(2,1)S(1)}, u32[]{:S(2)}, u32[]{:S(2)}) %collective-permute-start.10) | collective-permute-done | bytes 458784 | tf_op jit(solution)/shard_map/ppermute | solution.py:287
  111.3 2.6 %prepare_rows.2 = (bf16[512,3584]{1,0:T(8,128)(2,1)S(1)}, bf16[1792,512]{1,0:T(8,128)(2,1)S(1)}) custom-call(s32[5]{0:T(128)S(1)} %stack.23.refs_0_, bf16[32,3584]{1,0:T(8,128)(2,1)S(1)} %get-tuple-element.83.refs_1_, bf16[32,3584]{1,0:T(8,128)(2,1)S(1)} %collective-permute-done.4.refs_2_, bf16[64,3584]{1,0:T(8,128)(2,1)S(1)} %get-tuple-element.85.refs_3_, ...), custom_call_target="tpu_custom_call" | custom-call | flops 1 | bytes 1 | tf_op jit(solution)/shard_map/prepare_rows/pallas_call | solution.py:180
  113.9 0.0 collective-permute-done.9.refs_2_
  113.9 1.4 %prepare_rows.3 = (bf16[512,3584]{1,0:T(8,128)(2,1)S(1)}, bf16[1792,512]{1,0:T(8,128)(2,1)S(1)}) custom-call(s32[5]{0:T(128)S(1)} %stack.23.refs_0_, bf16[64,3584]{1,0:T(8,128)(2,1)S(1)} %get-tuple-element.82.refs_1_, bf16[64,3584]{1,0:T(8,128)(2,1)S(1)} %collective-permute-done.9.refs_2_, ...), custom_call_target="tpu_custom_call", output_to_operand_aliasing={{0}: (3, {}), {1}: (4, {})} | custom-call | flops 1 | bytes 1 | tf_op jit(solution)/shard_map/prepare_rows/pallas_call | solution.py:180
  115.3 0.0 collective-permute-done.8.refs_1_
  115.4 0.4 collective-permute-start.11
  115.8 0.0 collective-permute-done.12.refs_4_
  115.8 0.0 collective-permute-done.13.refs_5_
  115.8 2.1 %collective-permute-done.11.refs_2_ = bf16[128,3712]{1,0:T(8,128)(2,1)S(1)} collective-permute-done((bf16[128,3712]{1,0:T(8,128)(2,1)S(1)}, bf16[128,3712]{1,0:T(8,128)(2,1)S(1)}, u32[]{:S(2)}, u32[]{:S(2)}) %collective-permute-start.11) | collective-permute-done | bytes 950304 | tf_op jit(solution)/shard_map/ppermute | solution.py:287
  117.9 12.5 %finish.1 = (f32[1792,3584]{1,0:T(8,128)}, f32[1,896,896]{2,1,0:T(8,128)}, bf16[512,3584]{1,0:T(8,128)(2,1)S(1)}, bf16[1792,512]{1,0:T(8,128)(2,1)S(1)}) custom-call(s32[5]{0:T(128)S(1)} %stack.23.refs_0_, bf16[128,3712]{1,0:T(8,128)(2,1)S(1)} %collective-permute-done.8.refs_1_, ...), custom_call_target="tpu_custom_call", output_to_operand_aliasing={{2}: (6, {}), {3}: (7, {})} | custom-call | flops 1 | bytes 1 | tf_op jit(solution)/shard_map/finish/pallas_call | solution.py:230
Async XLA Ops:
  29.6 24.6 %collective-permute-start.1 = (bf16[128,3712]{1,0:T(8,128)(2,1)}, bf16[128,3712]{1,0:T(8,128)(2,1)S(1)}, u32[]{:S(2)}, u32[]{:S(2)}) collective-permute-start(bf16[128,3712]{1,0:T(8,128)(2,1)} %make_message.1.refs_1_), channel_id=1, source_target_pairs={{1,5},{5,9},{9,13},{13,15},{15,11},{11,7},{7,3},{3,1},{4,0},{8,4},... | collective-permute-start | bytes 2850824 | tf_op jit(solution)/shard_map/ppermute | solution.py:290
  32.6 21.6 %collective-permute-start = (bf16[128,3712]{1,0:T(8,128)(2,1)}, bf16[128,3712]{1,0:T(8,128)(2,1)S(1)}, u32[]{:S(2)}, u32[]{:S(2)}) collective-permute-start(bf16[128,3712]{1,0:T(8,128)(2,1)} %make_message.1.refs_1_), channel_id=1, source_target_pairs={{0,4},{4,8},{8,12},{12,14},{14,10},{10,6},{6,2},{2,0},{5,1},{9,5},... | collective-permute-start | bytes 2850824 | tf_op jit(solution)/shard_map/ppermute | solution.py:290
  32.8 1.2 copy-start
  54.2 23.3 %collective-permute-start.2 = (bf16[128,3712]{1,0:T(8,128)(2,1)S(1)}, bf16[128,3712]{1,0:T(8,128)(2,1)S(1)}, u32[]{:S(2)}, u32[]{:S(2)}) collective-permute-start(bf16[128,3712]{1,0:T(8,128)(2,1)S(1)} %collective-permute-done.refs_1_), channel_id=1, source_target_pairs={{0,4},{4,8},{8,12},{12,14},{14,10},{10,6},{6,2},{2,0},{5,1},{9,5},... | collective-permute-start | bytes 2850824 | tf_op jit(solution)/shard_map/ppermute | solution.py:290
  56.6 21.3 %collective-permute-start.3 = (bf16[128,3712]{1,0:T(8,128)(2,1)S(1)}, bf16[128,3712]{1,0:T(8,128)(2,1)S(1)}, u32[]{:S(2)}, u32[]{:S(2)}) collective-permute-start(bf16[128,3712]{1,0:T(8,128)(2,1)S(1)} %collective-permute-done.1.refs_2_), channel_id=1, source_target_pairs={{1,5},{5,9},{9,13},{13,15},{15,11},{11,7},{7,3},{3,1},{4,0},{8,4},... | collective-permute-start | bytes 2850824 | tf_op jit(solution)/shard_map/ppermute | solution.py:290
  56.6 2.6 %collective-permute-start.4 = (bf16[32,3584]{1,0:T(8,128)(2,1)S(1)}, bf16[32,3584]{1,0:T(8,128)(2,1)S(1)}, u32[]{:S(2)}, u32[]{:S(2)}) collective-permute-start(bf16[32,3584]{1,0:T(8,128)(2,1)S(1)} %get-tuple-element.83.refs_1_), channel_id=1, source_target_pairs={{0,1},{1,0},{2,3},{3,2},{4,5},{5,4},{6,7},{7,6},{8,9},{9,8},{10,11... | collective-permute-start | bytes 688136 | tf_op jit(solution)/shard_map/ppermute | solution.py:287
  78.0 23.6 %collective-permute-start.5 = (bf16[128,3712]{1,0:T(8,128)(2,1)S(1)}, bf16[128,3712]{1,0:T(8,128)(2,1)S(1)}, u32[]{:S(2)}, u32[]{:S(2)}) collective-permute-start(bf16[128,3712]{1,0:T(8,128)(2,1)S(1)} %collective-permute-done.2.refs_1_), channel_id=1, source_target_pairs={{0,4},{4,8},{8,12},{12,14},{14,10},{10,6},{6,2},{2,0},{5,1},{9,5},... | collective-permute-start | bytes 2850824 | tf_op jit(solution)/shard_map/ppermute | solution.py:290
  79.7 21.9 %collective-permute-start.6 = (bf16[128,3712]{1,0:T(8,128)(2,1)S(1)}, bf16[128,3712]{1,0:T(8,128)(2,1)S(1)}, u32[]{:S(2)}, u32[]{:S(2)}) collective-permute-start(bf16[128,3712]{1,0:T(8,128)(2,1)S(1)} %collective-permute-done.3.refs_2_), channel_id=1, source_target_pairs={{1,5},{5,9},{9,13},{13,15},{15,11},{11,7},{7,3},{3,1},{4,0},{8,4},... | collective-permute-start | bytes 2850824 | tf_op jit(solution)/shard_map/ppermute | solution.py:290
  80.0 2.6 %collective-permute-start.7 = (bf16[64,3584]{1,0:T(8,128)(2,1)S(1)}, bf16[64,3584]{1,0:T(8,128)(2,1)S(1)}, u32[]{:S(2)}, u32[]{:S(2)}) collective-permute-start(bf16[64,3584]{1,0:T(8,128)(2,1)S(1)} %get-tuple-element.85.refs_3_), channel_id=1, source_target_pairs={{0,1},{1,0},{2,3},{3,2},{4,5},{5,4},{6,7},{7,6},{8,9},{9,8},{10,11... | collective-permute-start | bytes 1376264 | tf_op jit(solution)/shard_map/ppermute | solution.py:287
  101.6 13.7 %collective-permute-start.8 = (bf16[128,3712]{1,0:T(8,128)(2,1)S(1)}, bf16[128,3712]{1,0:T(8,128)(2,1)S(1)}, u32[]{:S(2)}, u32[]{:S(2)}) collective-permute-start(bf16[128,3712]{1,0:T(8,128)(2,1)S(1)} %collective-permute-done.5.refs_1_), channel_id=1, source_target_pairs={{0,4},{4,8},{8,12},{12,14},{14,10},{10,6},{6,2},{2,0},{5,1},{9,5},... | collective-permute-start | bytes 2850824 | tf_op jit(solution)/shard_map/ppermute | solution.py:290
  104.7 11.1 %collective-permute-start.12 = (f32[448,896]{1,0:T(8,128)S(1)}, f32[448,896]{1,0:T(8,128)S(1)}, u32[]{:S(2)}, u32[]{:S(2)}) collective-permute-start(f32[448,896]{1,0:T(8,128)S(1)} %get-tuple-element.94), channel_id=1, source_target_pairs={{0,1},{1,0},{2,3},{3,2},{4,5},{5,4},{6,7},{7,6},{8,9},{9,8},{10,11... | collective-permute-start | bytes 4816904 | tf_op jit(solution)/shard_map/ppermute | solution.py:287
  105.3 10.5 %collective-permute-start.13 = (f32[448,896]{1,0:T(8,128)S(1)}, f32[448,896]{1,0:T(8,128)S(1)}, u32[]{:S(2)}, u32[]{:S(2)}) collective-permute-start(f32[448,896]{1,0:T(8,128)S(1)} %get-tuple-element.95), channel_id=1, source_target_pairs={{0,1},{1,0},{2,3},{3,2},{4,5},{5,4},{6,7},{7,6},{8,9},{9,8},{10,11... | collective-permute-start | bytes 4816904 | tf_op jit(solution)/shard_map/ppermute | solution.py:287
  105.4 6.0 %collective-permute-start.10 = (bf16[64,3584]{1,0:T(8,128)(2,1)S(1)}, bf16[64,3584]{1,0:T(8,128)(2,1)S(1)}, u32[]{:S(2)}, u32[]{:S(2)}) collective-permute-start(bf16[64,3584]{1,0:T(8,128)(2,1)S(1)} %get-tuple-element.87.refs_5_), channel_id=1, source_target_pairs={{0,1},{1,0},{2,3},{3,2},{4,5},{5,4},{6,7},{7,6},{8,9},{9,8},{10,11... | collective-permute-start | bytes 1376264 | tf_op jit(solution)/shard_map/ppermute | solution.py:287
  105.8 8.1 %collective-permute-start.9 = (bf16[64,3584]{1,0:T(8,128)(2,1)S(1)}, bf16[64,3584]{1,0:T(8,128)(2,1)S(1)}, u32[]{:S(2)}, u32[]{:S(2)}) collective-permute-start(bf16[64,3584]{1,0:T(8,128)(2,1)S(1)} %get-tuple-element.82.refs_1_), channel_id=1, source_target_pairs={{0,1},{1,0},{2,3},{3,2},{4,5},{5,4},{6,7},{7,6},{8,9},{9,8},{10,11... | collective-permute-start | bytes 1376264 | tf_op jit(solution)/shard_map/ppermute | solution.py:287
  115.4 2.6 %collective-permute-start.11 = (bf16[128,3712]{1,0:T(8,128)(2,1)S(1)}, bf16[128,3712]{1,0:T(8,128)(2,1)S(1)}, u32[]{:S(2)}, u32[]{:S(2)}) collective-permute-start(bf16[128,3712]{1,0:T(8,128)(2,1)S(1)} %collective-permute-done.8.refs_1_), channel_id=1, source_target_pairs={{0,1},{1,0},{2,3},{3,2},{4,5},{5,4},{6,7},{7,6},{8,9},{9,8},{10,11... | collective-permute-start | bytes 2850824 | tf_op jit(solution)/shard_map/ppermute | solution.py:287

commit v8 on v7

v8 whole, which is shorter than its diff:
```python
import functools
import math

import jax
import jax.numpy as jnp
from jax import lax
from jax.experimental import pallas as pl
from jax.experimental.pallas import tpu as pltpu
from jax.sharding import PartitionSpec as P

EXP = 8
CAP = 32
CORES = 2
TABLE = 128
STEP = 256
VMEM = pl.BlockSpec(memory_space=pltpu.VMEM)
SMEM = pl.BlockSpec(memory_space=pltpu.SMEM)
ANY = pl.BlockSpec(memory_space=pl.ANY)
F32 = jnp.float32
BF16 = jnp.bfloat16
ROWS_WITH_ROWS = (((0,), (0,)), ((), ()))
INVERSE = 1.0 / (16.0 * CAP)
SMALL = pl.CostEstimate(flops=1, bytes_accessed=1, transcendentals=0)


def params(mib):
    return pltpu.CompilerParams(vmem_limit_bytes=mib * 2**20)


def message_kernel(tokens, ids, weights, out, arrived):
    rows, width = tokens.shape
    copy = pltpu.make_async_copy(tokens, out.at[:, :width], arrived)
    copy.start()
    row_at = lax.broadcasted_iota(jnp.int32, (TABLE, rows), 0)
    roots = jnp.zeros((TABLE, rows), F32)
    for e in range(EXP):
        weight = jnp.sum(jnp.where(ids[...] == e, weights[...], 0.0), axis=0, keepdims=True)
        roots = jnp.where(row_at % EXP == e, jnp.sqrt(weight), roots)
    high = roots.astype(BF16).astype(F32)
    middle = (roots - high).astype(BF16).astype(F32)
    low = roots - high - middle
    terms = jnp.where(row_at < EXP, high, jnp.where(row_at < 2 * EXP, middle, low))
    out[:, width:] = jnp.where(row_at < 3 * EXP, terms, 0.0).T.astype(BF16)
    copy.wait()


def make_message(tokens, ids, weights):
    rows, width = tokens.shape
    return pl.pallas_call(
        message_kernel,
        out_shape=jax.ShapeDtypeStruct((rows, width + TABLE), BF16),
        in_specs=[ANY, VMEM, VMEM],
        out_specs=VMEM,
        scratch_shapes=[pltpu.SemaphoreType.DMA],
        cost_estimate=SMALL,
        compiler_params=params(8),
        name="make_message",
    )(tokens, ids.T, weights.T)


def choose(expert, table):
    rows = table.shape[0]
    row_at = lax.broadcasted_iota(jnp.int32, (TABLE, rows), 0)
    ours = jnp.logical_and(row_at % EXP == expert, row_at < 3 * EXP)
    root = jnp.sum(jnp.where(ours, table.astype(F32).T, 0.0), axis=0, keepdims=True)
    root = jnp.broadcast_to(root, (CAP, rows))
    member = root > 0.0
    from_at = lax.broadcasted_iota(jnp.int32, (rows, rows), 0)
    to_at = lax.broadcasted_iota(jnp.int32, (rows, rows), 1)
    upto = (from_at <= to_at).astype(F32).astype(BF16)
    counted = jnp.dot(member.astype(F32).astype(BF16), upto, preferred_element_type=F32)
    place = counted.astype(jnp.int32) - 1
    slot_at = lax.broadcasted_iota(jnp.int32, (CAP, rows), 0)
    select = jnp.logical_and(member, place == slot_at)
    scale = jnp.sum(jnp.where(select, root, 0.0), axis=1, keepdims=True)
    return select.astype(F32).astype(BF16), scale


def pack(expert, piece):
    width = piece.shape[1] - TABLE
    select, scale = choose(expert, piece[:, width:])
    picked = jnp.dot(select, piece[:, :width], preferred_element_type=F32)
    return (picked * scale).astype(BF16)


def fetch_tile(index, pieces, scratch):
    edge = scratch.shape[1]
    for b in range((pieces[0].shape[1] - TABLE) // edge):

        @pl.when(index == b)
        def _(b=b):
            row = 0
            for piece in pieces:
                rows = piece.shape[0]
                scratch[row : row + rows, :] = piece[:, b * edge : (b + 1) * edge]
                row += rows


def place_rows(slab_at, packed, at, rows, across):
    count, width = packed.shape
    slab = across.shape[0]
    rows[at : at + count, :] = packed
    for s in range(width // slab):

        @pl.when(slab_at == s)
        def _():
            across[:, at : at + count] = packed[:, s * slab : (s + 1) * slab].T


def take_in(scalars, pieces, left, right):
    fetch_tile(scalars[1], pieces, left)
    fetch_tile(scalars[2], pieces, right)
    packed = jnp.concatenate([pack(scalars[0], piece) for piece in pieces], axis=0)
    update = lax.dot_general(left[...], right[...], ROWS_WITH_ROWS, preferred_element_type=F32)
    return packed, update


def absorb_kernel(count, started, at, *refs):
    scalars, refs = refs[0], refs[1:]
    pieces, before, (tile, rows, across, left, right) = refs[:count], refs[count:-5], refs[-5:]
    packed, update = take_in(scalars, pieces, left, right)
    place_rows(scalars[3], packed, at, rows, across)
    tile[...] = before[0][...] + update if started else update


def absorb(scalars, pieces, at, before, shapes):
    rows, edge, count = pieces[0].shape[0], shapes[0].shape[0], len(pieces)
    return pl.pallas_call(
        functools.partial(absorb_kernel, count, bool(before), at),
        out_shape=shapes,
        in_specs=[SMEM] + [VMEM] * (count + len(before)),
        out_specs=[VMEM] * 3,
        scratch_shapes=[pltpu.VMEM((count * rows, edge), BF16)] * 2,
        cost_estimate=SMALL,
        input_output_aliases={1 + count + k: k for k in range(len(before))},
        compiler_params=params(14),
        name="absorb",
    )(scalars, *pieces, *before)


def finish_kernel(final, *refs):
    scalars, mine, other, before, _, _, hessian, tile, rows, across, *scratch = refs
    staging, sums, left, right, sent = scratch
    pieces = [mine, other]
    packed, update = take_in(scalars, pieces, left, right)
    place_rows(scalars[3], packed, rows.shape[0] - packed.shape[0], rows, across)
    copies = []
    for n in range(staging.shape[0]):
        span = slice(n * STEP, (n + 1) * STEP)
        staging[n, :, :] = (
            jnp.dot(across[...], rows[:, span], preferred_element_type=F32) * INVERSE
        )
        copies.append(pltpu.make_async_copy(staging.at[n], hessian.at[:, span], sent.at[n]))
        copies[-1].start()
    sums[...] = (before[...] + update) * final
    copies.append(pltpu.make_async_copy(sums, tile.at[0], sent.at[len(copies)]))
    copies[-1].start()
    for copy in copies:
        copy.wait()


def finish(scalars, pieces, before, final):
    tile, rows, across = before
    edge, slab, width = tile.shape[0], across.shape[0], rows.shape[1]
    count = sum(piece.shape[0] for piece in pieces)
    blocks = width // STEP
    return pl.pallas_call(
        functools.partial(finish_kernel, final),
        out_shape=[
            jax.ShapeDtypeStruct((slab, width), F32),
            jax.ShapeDtypeStruct((1, edge, edge), F32),
            jax.ShapeDtypeStruct(rows.shape, BF16),
            jax.ShapeDtypeStruct(across.shape, BF16),
        ],
        in_specs=[SMEM] + [VMEM] * 5,
        out_specs=[ANY, ANY, VMEM, VMEM],
        scratch_shapes=[
            pltpu.VMEM((blocks, slab, STEP), F32),
            pltpu.VMEM((edge, edge), F32),
            pltpu.VMEM((count, edge), BF16),
            pltpu.VMEM((count, edge), BF16),
            pltpu.SemaphoreType.DMA((blocks + 1,)),
        ],
        input_output_aliases={4: 2, 5: 3},
        cost_estimate=SMALL,
        compiler_params=params(40),
        name="finish",
    )(scalars, *pieces, *before)[:2]


def ring_of(chips):
    return list(range(0, chips, 2)) + list(range(chips - 1, 0, -2))


def on_device(tokens, route_ids, route_weights):
    devices = lax.axis_size("tok")
    position = lax.axis_index("tok")
    tok_rows, width = tokens.shape
    grid = math.isqrt(devices)
    edge = width // grid
    group = devices // EXP
    slab = width // group
    chips = devices // CORES
    ring = ring_of(chips)
    ahead = [
        (ring[i] * CORES + c, ring[(i + 1) % chips] * CORES + c)
        for i in range(chips)
        for c in range(CORES)
    ]
    streams = [ahead, [(b, a) for a, b in ahead]]
    pair = [(d, d ^ 1) for d in range(devices)]
    scalars = jnp.stack(
        [position // group, position // grid, position % grid, position % group]
    ).astype(jnp.int32)
    core = position % CORES
    last_hop = [hop for k in range(CORES) for hop in streams[k][k::CORES]]

    def swap(array):
        return lax.ppermute(array, "tok", pair)

    def advance(held):
        return [lax.ppermute(array, "tok", stream) for array, stream in zip(held, streams)]

    rounds = chips // 2
    total = 4 * CAP * rounds
    shapes = [
        jax.ShapeDtypeStruct((edge, edge), F32),
        jax.ShapeDtypeStruct((total, width), BF16),
        jax.ShapeDtypeStruct((slab, total), BF16),
    ]
    pieces = [make_message(tokens, route_ids, route_weights)]
    sums, waiting = [], []
    for step in range(1, rounds + 1):
        held = pieces * CORES if step == 1 else pieces
        if step < rounds:
            moved = advance(held)
        else:
            moved = [lax.ppermute(jnp.where(core == 0, *held), "tok", last_hop)]
        at = 4 * CAP * (step - 2) if step > 1 else total - 4 * CAP
        waiting.append((at, pieces + [swap(piece) for piece in pieces]))
        while len(waiting) > (1 if step < rounds else 0):
            at, both = waiting.pop(0)
            sums = absorb(scalars, both, at, sums, shapes)
        moved, sums, arrays = lax.optimization_barrier(
            (moved, sums, [both for _, both in waiting])
        )
        waiting = [(at, both) for (at, _), both in zip(waiting, arrays)]
        pieces = moved
    pieces = pieces + [swap(piece) for piece in pieces]
    return tuple(finish(scalars, pieces, sums, 1.0 / (devices * tok_rows)))


def solution(mesh):
    in_specs = (P(("grp", "tok"), None), P(("grp", "tok"), None), P(("grp", "tok"), None))
    out_specs = (P(("grp", "tok"), None), P(("grp", "tok"), None, None))
    return jax.shard_map(
        on_device, mesh=mesh, in_specs=in_specs, out_specs=out_specs, check_vma=False
    )
```

time: 131 us -> 116 us (0.89)
  Pallas kernels: 55.1 us -> 30.3 us
  local copies, waits for them, and re-layouts: 1.27 us -> 20 us
  waiting for transfers between devices: 63.7 us -> 52.5 us
  other arithmetic: 0 us -> 1.37 us
    pallas_call x1, Pallas kernels: 28.9 us -> 0.2 us  [make_message(): pl.pallas_call(message_kernel, out_shape=jax.ShapeDtypeStruct((rows, widt...]
    unnamed x2 -> x30, local copies, waits for them, and re-layouts: 1.19 us -> 20 us
    ppermute x7, waiting for transfers between devices: 56.1 us -> 49.9 us  [the longest x6 49.9 us: advance(): lax.ppermute(array, 'tok', stream)]
    ppermute x7 -> x8, waiting for transfers between devices: 7.6 us -> 2.54 us  [swap(): return lax.ppermute(array, 'tok', pair)]
    pallas_call x6 -> x4, Pallas kernels: 13.7 us -> 17 us  [absorb(): pl.pallas_call(functools.partial(absorb_kernel, count, bool(before), at),...]
  transfers between devices with their start and end apart: 14 -> 15, of which waited for: 6 -> 7; matrix products, arithmetic and copies ran while one was open for 0% -> 1% of each run, Pallas kernels for 10% -> 15%
where the time goes in v8:
time: 116 us; the launch traced here: 115 us
  waiting for transfers between devices  52.5 us (45%)
  Pallas kernels  30.3 us (26%)
  local copies, waits for them, and re-layouts  20 us (17%)
  starting transfers between devices  9.89 us (9%)
  other arithmetic  1.37 us (1%)
    ppermute x6, waiting for transfers between devices, advance(): lax.ppermute(array, 'tok', stream)  49.9 us
    unnamed x30, local copies, waits for them, and re-layouts  20 us
    pallas_call x4, Pallas kernels, absorb(): pl.pallas_call(functools.partial(absorb_kernel, count, bool(before), at),...  17 us
    pallas_call x1, Pallas kernels, finish(): pl.pallas_call(functools.partial(finish_kernel, final), out_shape=[jax.Sh...  13.1 us
    ppermute x6, starting transfers between devices, advance(): lax.ppermute(array, 'tok', stream)  6.77 us
    ppermute x8, waiting for transfers between devices, swap(): return lax.ppermute(array, 'tok', pair)  2.54 us
  transfers between devices with their start and end apart: 15, of which 7 were waited for; matrix products, arithmetic and copies ran while one was open for 1% of the time, Pallas kernels for 15%

profile of v8, /device:TPU:0, one launch (start us, length us, event | category | flops | bytes accessed | tf_op | source)
XLA Modules:
  0.0 115.0 jit_solution(9923802681542549909)
XLA Ops:
  0.6 0.0 copy-start.12
  0.6 1.2 %copy-done.12 = bf16[128,3584]{1,0:T(8,128)(2,1)S(1)} copy-done((bf16[128,3584]{1,0:T(8,128)(2,1)S(1)}, bf16[128,3584]{1,0:T(8,128)(2,1)}, u32[]{:S(2)}) %copy-start.12) | copy-done | bytes 917528
  1.8 0.0 copy-start.13
  1.8 0.7 copy-done.13
  2.5 0.0 copy-start.14
  2.5 0.7 copy-done.14
  3.2 0.2 make_message.1.refs_1_
  3.4 0.5 collective-permute-start.2
  3.9 2.6 %collective-permute-start.1 = (bf16[128,3712]{1,0:T(8,128)(2,1)S(1)}, bf16[128,3712]{1,0:T(8,128)(2,1)}, u32[]{:S(2)}, u32[]{:S(2)}) collective-permute-start(bf16[128,3712]{1,0:T(8,128)(2,1)S(1)} %make_message.1.refs_1_), channel_id=1, source_target_pairs={{4,0},{5,1},{8,4},{9,5},{12,8},{13,9},{14,12},{15,13},{10,14},{11,... | collective-permute-start | bytes 2850824 | tf_op jit(solution)/shard_map/ppermute | solution.py:222
  6.5 0.1 collective-permute-start
  6.6 0.0 copy-start.8
  6.6 0.9 copy-done.8
  7.6 0.0 collective-permute-done.2.refs_2_
  7.6 0.0 copy-start.10
  7.6 0.9 copy-done.10
  8.5 19.8 %collective-permute-done.1.refs_2_ = bf16[128,3712]{1,0:T(8,128)(2,1)} collective-permute-done((bf16[128,3712]{1,0:T(8,128)(2,1)S(1)}, bf16[128,3712]{1,0:T(8,128)(2,1)}, u32[]{:S(2)}, u32[]{:S(2)}) %collective-permute-start.1) | collective-permute-done | bytes 950304 | tf_op jit(solution)/shard_map/ppermute | solution.py:222
  28.3 1.4 %collective-permute-done.refs_1_ = bf16[128,3712]{1,0:T(8,128)(2,1)} collective-permute-done((bf16[128,3712]{1,0:T(8,128)(2,1)S(1)}, bf16[128,3712]{1,0:T(8,128)(2,1)}, u32[]{:S(2)}, u32[]{:S(2)}) %collective-permute-start) | collective-permute-done | bytes 950304 | tf_op jit(solution)/shard_map/ppermute | solution.py:222
  29.7 0.0 collective-permute-start.5
  29.7 0.3 collective-permute-start.3
  30.1 0.2 collective-permute-start.6
  30.3 1.7 %collective-permute-start.4 = (bf16[128,3712]{1,0:T(8,128)(2,1)}, bf16[128,3712]{1,0:T(8,128)(2,1)}, u32[]{:S(2)}, u32[]{:S(2)}) collective-permute-start(bf16[128,3712]{1,0:T(8,128)(2,1)} %collective-permute-done.1.refs_2_), channel_id=1, source_target_pairs={{4,0},{5,1},{8,4},{9,5},{12,8},{13,9},{14,12},{15,13},{10,14},{11,... | collective-permute-start | bytes 2850824 | tf_op jit(solution)/shard_map/ppermute | solution.py:222
  32.0 0.1 pad_add_fusion.refs_0_
  32.1 0.0 copy-start.9
  32.1 1.2 %copy-done.9 = bf16[128,3712]{1,0:T(8,128)(2,1)S(1)} copy-done((bf16[128,3712]{1,0:T(8,128)(2,1)S(1)}, bf16[128,3712]{1,0:T(8,128)(2,1)}, u32[]{:S(2)}) %copy-start.9) | copy-done | bytes 950296
  33.2 0.0 copy-start.11
  33.3 1.2 %copy-done.11 = bf16[128,3712]{1,0:T(8,128)(2,1)S(1)} copy-done((bf16[128,3712]{1,0:T(8,128)(2,1)S(1)}, bf16[128,3712]{1,0:T(8,128)(2,1)}, u32[]{:S(2)}) %copy-start.11) | copy-done | bytes 950296
  34.4 2.3 %absorb.4 = (f32[896,896]{1,0:T(8,128)S(1)}, bf16[512,3584]{1,0:T(8,128)(2,1)S(1)}, bf16[1792,512]{1,0:T(8,128)(2,1)S(1)}) custom-call(s32[4]{0:T(128)S(1)} %pad_add_fusion.refs_0_, bf16[128,3712]{1,0:T(8,128)(2,1)S(1)} %copy-done.9, bf16[128,3712]{1,0:T(8,128)(2,1)S(1)} %copy-done.11), custom_call_target="tpu_custom_call" | custom-call | flops 1 | bytes 1 | tf_op jit(solution)/shard_map/absorb/pallas_call | solution.py:128
  36.7 0.0 copy-start
  36.7 1.8 %copy-done = bf16[512,3584]{1,0:T(8,128)(2,1)} copy-done((bf16[512,3584]{1,0:T(8,128)(2,1)}, bf16[512,3584]{1,0:T(8,128)(2,1)S(1)}, u32[]{:S(2)}) %copy-start) | copy-done | bytes 3670040
  38.6 0.0 copy-start.4
  38.6 1.2 %copy-done.4 = bf16[1792,512]{1,0:T(8,128)(2,1)} copy-done((bf16[1792,512]{1,0:T(8,128)(2,1)}, bf16[1792,512]{1,0:T(8,128)(2,1)S(1)}, u32[]{:S(2)}) %copy-start.4) | copy-done | bytes 1835032
  39.8 0.0 collective-permute-done.5.refs_3_
  39.8 13.7 %collective-permute-done.3.refs_1_ = bf16[128,3712]{1,0:T(8,128)(2,1)} collective-permute-done((bf16[128,3712]{1,0:T(8,128)(2,1)}, bf16[128,3712]{1,0:T(8,128)(2,1)}, u32[]{:S(2)}, u32[]{:S(2)}) %collective-permute-start.3) | collective-permute-done | bytes 950304 | tf_op jit(solution)/shard_map/ppermute | solution.py:222
  53.5 0.0 collective-permute-done.6.refs_4_
  53.5 0.3 collective-permute-done.4.refs_2_
  53.9 0.0 collective-permute-start.9
  53.9 1.7 %collective-permute-start.7 = (bf16[128,3712]{1,0:T(8,128)(2,1)}, bf16[128,3712]{1,0:T(8,128)(2,1)}, u32[]{:S(2)}, u32[]{:S(2)}) collective-permute-start(bf16[128,3712]{1,0:T(8,128)(2,1)} %collective-permute-done.3.refs_1_), channel_id=1, source_target_pairs={{0,4},{1,5},{4,8},{5,9},{8,12},{9,13},{12,14},{13,15},{14,10},{15,... | collective-permute-start | bytes 2850824 | tf_op jit(solution)/shard_map/ppermute | solution.py:222
  55.6 0.2 collective-permute-start.10
  55.8 0.3 collective-permute-start.8
  56.1 0.0 copy-start.1
  56.1 2.0 %copy-done.1 = bf16[512,3584]{1,0:T(8,128)(2,1)S(1)} copy-done((bf16[512,3584]{1,0:T(8,128)(2,1)S(1)}, bf16[512,3584]{1,0:T(8,128)(2,1)}, u32[]{:S(2)}) %copy-start.1) | copy-done | bytes 3670040
  58.1 1.5 %copy-done.5 = bf16[1792,512]{1,0:T(8,128)(2,1)S(1)} copy-done((bf16[1792,512]{1,0:T(8,128)(2,1)S(1)}, bf16[1792,512]{1,0:T(8,128)(2,1)}, u32[]{:S(2)}) %copy-start.5) | copy-done | bytes 1835032
  59.6 5.0 %absorb.5 = (f32[896,896]{1,0:T(8,128)S(1)}, bf16[512,3584]{1,0:T(8,128)(2,1)S(1)}, bf16[1792,512]{1,0:T(8,128)(2,1)S(1)}) custom-call(s32[4]{0:T(128)S(1)} %pad_add_fusion.refs_0_, bf16[128,3712]{1,0:T(8,128)(2,1)} %collective-permute-done.refs_1_, ...), custom_call_target="tpu_custom_call", output_to_operand_aliasing={{0}: (5, {}), {1}: (6, {}), {2}: (7, {})} | custom-call | flops 1 | bytes 1 | tf_op jit(solution)/shard_map/absorb/pallas_call | solution.py:128
  64.7 0.0 collective-permute-done.9.refs_3_
  64.7 12.9 %collective-permute-done.7.refs_1_ = bf16[128,3712]{1,0:T(8,128)(2,1)} collective-permute-done((bf16[128,3712]{1,0:T(8,128)(2,1)}, bf16[128,3712]{1,0:T(8,128)(2,1)}, u32[]{:S(2)}, u32[]{:S(2)}) %collective-permute-start.7) | collective-permute-done | bytes 950304 | tf_op jit(solution)/shard_map/ppermute | solution.py:222
  77.6 0.0 collective-permute-done.10.refs_4_
  77.6 1.7 %collective-permute-done.8.refs_2_ = bf16[128,3712]{1,0:T(8,128)(2,1)} collective-permute-done((bf16[128,3712]{1,0:T(8,128)(2,1)}, bf16[128,3712]{1,0:T(8,128)(2,1)}, u32[]{:S(2)}, u32[]{:S(2)}) %collective-permute-start.8) | collective-permute-done | bytes 950304 | tf_op jit(solution)/shard_map/ppermute | solution.py:222
  79.4 0.0 collective-permute-start.12
  79.4 0.5 collective-permute-start.13
  79.9 1.3 %broadcast_select_fusion = bf16[128,3712]{1,0:T(8,128)(2,1)S(1)} fusion(bf16[128,3712]{1,0:T(8,128)(2,1)} %collective-permute-done.7.refs_1_, bf16[128,3712]{1,0:T(8,128)(2,1)} %collective-permute-done.8.refs_2_, pred[]{:T(512)S(6)} %eq.7), kind=kLoop, calls=%fused_computation | loop fusion | flops 475136 | bytes 2850817 | tf_op jit(solution)/shard_map/jit(_where)/select_n | solution.py:238
  81.2 1.6 %collective-permute-start.11 = (bf16[128,3712]{1,0:T(8,128)(2,1)S(1)}, bf16[128,3712]{1,0:T(8,128)(2,1)S(1)}, u32[]{:S(2)}, u32[]{:S(2)}) collective-permute-start(bf16[128,3712]{1,0:T(8,128)(2,1)S(1)} %broadcast_select_fusion), channel_id=1, source_target_pairs={{0,4},{4,8},{8,12},{12,14},{14,10},{10,6},{6,2},{2,0},{5,1},{9,5},... | collective-permute-start | bytes 2850824 | tf_op jit(solution)/shard_map/ppermute | solution.py:238
  82.8 5.0 %absorb.6 = (f32[896,896]{1,0:T(8,128)S(1)}, bf16[512,3584]{1,0:T(8,128)(2,1)S(1)}, bf16[1792,512]{1,0:T(8,128)(2,1)S(1)}) custom-call(s32[4]{0:T(128)S(1)} %pad_add_fusion.refs_0_, bf16[128,3712]{1,0:T(8,128)(2,1)} %collective-permute-done.3.refs_1_, ...), custom_call_target="tpu_custom_call", output_to_operand_aliasing={{0}: (5, {}), {1}: (6, {}), {2}: (7, {})} | custom-call | flops 1 | bytes 1 | tf_op jit(solution)/shard_map/absorb/pallas_call | solution.py:128
  87.9 0.0 collective-permute-done.12.refs_3_
  87.9 0.0 collective-permute-done.13.refs_4_
  87.9 4.7 %absorb.7 = (f32[896,896]{1,0:T(8,128)S(1)}, bf16[512,3584]{1,0:T(8,128)(2,1)S(1)}, bf16[1792,512]{1,0:T(8,128)(2,1)S(1)}) custom-call(s32[4]{0:T(128)S(1)} %pad_add_fusion.refs_0_, bf16[128,3712]{1,0:T(8,128)(2,1)} %collective-permute-done.7.refs_1_, ...), custom_call_target="tpu_custom_call", output_to_operand_aliasing={{0}: (5, {}), {1}: (6, {}), {2}: (7, {})} | custom-call | flops 1 | bytes 1 | tf_op jit(solution)/shard_map/absorb/pallas_call | solution.py:128
  92.6 0.0 copy-start.2
  92.6 1.8 %copy-done.2 = bf16[512,3584]{1,0:T(8,128)(2,1)} copy-done((bf16[512,3584]{1,0:T(8,128)(2,1)}, bf16[512,3584]{1,0:T(8,128)(2,1)S(1)}, u32[]{:S(2)}) %copy-start.2) | copy-done | bytes 3670040
  94.4 1.2 %copy-done.6 = bf16[1792,512]{1,0:T(8,128)(2,1)} copy-done((bf16[1792,512]{1,0:T(8,128)(2,1)}, bf16[1792,512]{1,0:T(8,128)(2,1)S(1)}, u32[]{:S(2)}) %copy-start.6) | copy-done | bytes 1835032
  95.6 0.0 collective-permute-done.11.refs_1_
  95.6 0.0 collective-permute-start.14
  95.6 2.5 %collective-permute-done.14.refs_2_ = bf16[128,3712]{1,0:T(8,128)(2,1)S(1)} collective-permute-done((bf16[128,3712]{1,0:T(8,128)(2,1)S(1)}, bf16[128,3712]{1,0:T(8,128)(2,1)S(1)}, u32[]{:S(2)}, u32[]{:S(2)}) %collective-permute-start.14) | collective-permute-done | bytes 950304 | tf_op jit(solution)/shard_map/ppermute | solution.py:219
  98.2 2.0 %copy-done.3 = bf16[512,3584]{1,0:T(8,128)(2,1)S(1)} copy-done((bf16[512,3584]{1,0:T(8,128)(2,1)S(1)}, bf16[512,3584]{1,0:T(8,128)(2,1)}, u32[]{:S(2)}) %copy-start.3) | copy-done | bytes 3670040
  100.2 1.5 %copy-done.7 = bf16[1792,512]{1,0:T(8,128)(2,1)S(1)} copy-done((bf16[1792,512]{1,0:T(8,128)(2,1)S(1)}, bf16[1792,512]{1,0:T(8,128)(2,1)}, u32[]{:S(2)}) %copy-start.7) | copy-done | bytes 1835032
  101.7 13.1 %finish.1 = (f32[1792,3584]{1,0:T(8,128)}, f32[1,896,896]{2,1,0:T(8,128)}, bf16[512,3584]{1,0:T(8,128)(2,1)S(1)}, bf16[1792,512]{1,0:T(8,128)(2,1)S(1)}) custom-call(s32[4]{0:T(128)S(1)} %pad_add_fusion.refs_0_, bf16[128,3712]{1,0:T(8,128)(2,1)S(1)} %collective-permute-done.11.refs_1_, ...), custom_call_target="tpu_custom_call", output_to_operand_aliasing={{2}: (4, {}), {3}: (5, {})} | custom-call | flops 1 | bytes 1 | tf_op jit(solution)/shard_map/finish/pallas_call | solution.py:167
  (4 shorter events, 0.0 us)
Async XLA Ops:
  0.6 1.2 %copy-start.12 = (bf16[128,3584]{1,0:T(8,128)(2,1)S(1)}, bf16[128,3584]{1,0:T(8,128)(2,1)}, u32[]{:S(2)}) copy-start(bf16[128,3584]{1,0:T(8,128)(2,1)} %tokens.1) | copy-start | bytes 2752516
  1.8 0.7 copy-start.13
  2.5 0.7 copy-start.14
  3.4 4.2 %collective-permute-start.2 = (bf16[128,3712]{1,0:T(8,128)(2,1)S(1)}, bf16[128,3712]{1,0:T(8,128)(2,1)S(1)}, u32[]{:S(2)}, u32[]{:S(2)}) collective-permute-start(bf16[128,3712]{1,0:T(8,128)(2,1)S(1)} %make_message.1.refs_1_), channel_id=1, source_target_pairs={{0,1},{1,0},{2,3},{3,2},{4,5},{5,4},{6,7},{7,6},{8,9},{9,8},{10,11... | collective-permute-start | bytes 2850824 | tf_op jit(solution)/shard_map/ppermute | solution.py:219
  3.9 24.4 %collective-permute-start.1 = (bf16[128,3712]{1,0:T(8,128)(2,1)S(1)}, bf16[128,3712]{1,0:T(8,128)(2,1)}, u32[]{:S(2)}, u32[]{:S(2)}) collective-permute-start(bf16[128,3712]{1,0:T(8,128)(2,1)S(1)} %make_message.1.refs_1_), channel_id=1, source_target_pairs={{4,0},{5,1},{8,4},{9,5},{12,8},{13,9},{14,12},{15,13},{10,14},{11,... | collective-permute-start | bytes 2850824 | tf_op jit(solution)/shard_map/ppermute | solution.py:222
  6.5 23.2 %collective-permute-start = (bf16[128,3712]{1,0:T(8,128)(2,1)S(1)}, bf16[128,3712]{1,0:T(8,128)(2,1)}, u32[]{:S(2)}, u32[]{:S(2)}) collective-permute-start(bf16[128,3712]{1,0:T(8,128)(2,1)S(1)} %make_message.1.refs_1_), channel_id=1, source_target_pairs={{0,4},{1,5},{4,8},{5,9},{8,12},{9,13},{12,14},{13,15},{14,10},{15,... | collective-permute-start | bytes 2850824 | tf_op jit(solution)/shard_map/ppermute | solution.py:222
  6.6 0.9 copy-start.8
  7.6 0.9 copy-start.10
  29.7 10.1 %collective-permute-start.5 = (bf16[128,3712]{1,0:T(8,128)(2,1)}, bf16[128,3712]{1,0:T(8,128)(2,1)}, u32[]{:S(2)}, u32[]{:S(2)}) collective-permute-start(bf16[128,3712]{1,0:T(8,128)(2,1)} %collective-permute-done.refs_1_), channel_id=1, source_target_pairs={{0,1},{1,0},{2,3},{3,2},{4,5},{5,4},{6,7},{7,6},{8,9},{9,8},{10,11... | collective-permute-start | bytes 2850824 | tf_op jit(solution)/shard_map/ppermute | solution.py:219
  29.7 23.8 %collective-permute-start.3 = (bf16[128,3712]{1,0:T(8,128)(2,1)}, bf16[128,3712]{1,0:T(8,128)(2,1)}, u32[]{:S(2)}, u32[]{:S(2)}) collective-permute-start(bf16[128,3712]{1,0:T(8,128)(2,1)} %collective-permute-done.refs_1_), channel_id=1, source_target_pairs={{0,4},{1,5},{4,8},{5,9},{8,12},{9,13},{12,14},{13,15},{14,10},{15,... | collective-permute-start | bytes 2850824 | tf_op jit(solution)/shard_map/ppermute | solution.py:222
  30.1 23.4 %collective-permute-start.6 = (bf16[128,3712]{1,0:T(8,128)(2,1)}, bf16[128,3712]{1,0:T(8,128)(2,1)}, u32[]{:S(2)}, u32[]{:S(2)}) collective-permute-start(bf16[128,3712]{1,0:T(8,128)(2,1)} %collective-permute-done.1.refs_2_), channel_id=1, source_target_pairs={{0,1},{1,0},{2,3},{3,2},{4,5},{5,4},{6,7},{7,6},{8,9},{9,8},{10,11... | collective-permute-start | bytes 2850824 | tf_op jit(solution)/shard_map/ppermute | solution.py:219
  30.3 23.6 %collective-permute-start.4 = (bf16[128,3712]{1,0:T(8,128)(2,1)}, bf16[128,3712]{1,0:T(8,128)(2,1)}, u32[]{:S(2)}, u32[]{:S(2)}) collective-permute-start(bf16[128,3712]{1,0:T(8,128)(2,1)} %collective-permute-done.1.refs_2_), channel_id=1, source_target_pairs={{4,0},{5,1},{8,4},{9,5},{12,8},{13,9},{14,12},{15,13},{10,14},{11,... | collective-permute-start | bytes 2850824 | tf_op jit(solution)/shard_map/ppermute | solution.py:222
  32.1 1.2 %copy-start.9 = (bf16[128,3712]{1,0:T(8,128)(2,1)S(1)}, bf16[128,3712]{1,0:T(8,128)(2,1)}, u32[]{:S(2)}) copy-start(bf16[128,3712]{1,0:T(8,128)(2,1)} %copy-done.8) | copy-start | bytes 2850820
  33.2 1.2 %copy-start.11 = (bf16[128,3712]{1,0:T(8,128)(2,1)S(1)}, bf16[128,3712]{1,0:T(8,128)(2,1)}, u32[]{:S(2)}) copy-start(bf16[128,3712]{1,0:T(8,128)(2,1)} %copy-done.10) | copy-start | bytes 2850820
  36.7 1.8 %copy-start = (bf16[512,3584]{1,0:T(8,128)(2,1)}, bf16[512,3584]{1,0:T(8,128)(2,1)S(1)}, u32[]{:S(2)}) copy-start(bf16[512,3584]{1,0:T(8,128)(2,1)S(1)} %get-tuple-element.56.refs_6_) | copy-start | bytes 11010052
  38.6 1.2 %copy-start.4 = (bf16[1792,512]{1,0:T(8,128)(2,1)}, bf16[1792,512]{1,0:T(8,128)(2,1)S(1)}, u32[]{:S(2)}) copy-start(bf16[1792,512]{1,0:T(8,128)(2,1)S(1)} %get-tuple-element.57.refs_7_) | copy-start | bytes 5505028
  53.9 10.9 %collective-permute-start.9 = (bf16[128,3712]{1,0:T(8,128)(2,1)}, bf16[128,3712]{1,0:T(8,128)(2,1)}, u32[]{:S(2)}, u32[]{:S(2)}) collective-permute-start(bf16[128,3712]{1,0:T(8,128)(2,1)} %collective-permute-done.3.refs_1_), channel_id=1, source_target_pairs={{0,1},{1,0},{2,3},{3,2},{4,5},{5,4},{6,7},{7,6},{8,9},{9,8},{10,11... | collective-permute-start | bytes 2850824 | tf_op jit(solution)/shard_map/ppermute | solution.py:219
  53.9 23.8 %collective-permute-start.7 = (bf16[128,3712]{1,0:T(8,128)(2,1)}, bf16[128,3712]{1,0:T(8,128)(2,1)}, u32[]{:S(2)}, u32[]{:S(2)}) collective-permute-start(bf16[128,3712]{1,0:T(8,128)(2,1)} %collective-permute-done.3.refs_1_), channel_id=1, source_target_pairs={{0,4},{1,5},{4,8},{5,9},{8,12},{9,13},{12,14},{13,15},{14,10},{15,... | collective-permute-start | bytes 2850824 | tf_op jit(solution)/shard_map/ppermute | solution.py:222
  55.6 22.0 %collective-permute-start.10 = (bf16[128,3712]{1,0:T(8,128)(2,1)}, bf16[128,3712]{1,0:T(8,128)(2,1)}, u32[]{:S(2)}, u32[]{:S(2)}) collective-permute-start(bf16[128,3712]{1,0:T(8,128)(2,1)} %collective-permute-done.4.refs_2_), channel_id=1, source_target_pairs={{0,1},{1,0},{2,3},{3,2},{4,5},{5,4},{6,7},{7,6},{8,9},{9,8},{10,11... | collective-permute-start | bytes 2850824 | tf_op jit(solution)/shard_map/ppermute | solution.py:219
  55.8 23.6 %collective-permute-start.8 = (bf16[128,3712]{1,0:T(8,128)(2,1)}, bf16[128,3712]{1,0:T(8,128)(2,1)}, u32[]{:S(2)}, u32[]{:S(2)}) collective-permute-start(bf16[128,3712]{1,0:T(8,128)(2,1)} %collective-permute-done.4.refs_2_), channel_id=1, source_target_pairs={{4,0},{5,1},{8,4},{9,5},{12,8},{13,9},{14,12},{15,13},{10,14},{11,... | collective-permute-start | bytes 2850824 | tf_op jit(solution)/shard_map/ppermute | solution.py:222
  56.1 2.0 %copy-start.1 = (bf16[512,3584]{1,0:T(8,128)(2,1)S(1)}, bf16[512,3584]{1,0:T(8,128)(2,1)}, u32[]{:S(2)}) copy-start(bf16[512,3584]{1,0:T(8,128)(2,1)} %copy-done) | copy-start | bytes 11010052
  58.1 1.5 %copy-start.5 = (bf16[1792,512]{1,0:T(8,128)(2,1)S(1)}, bf16[1792,512]{1,0:T(8,128)(2,1)}, u32[]{:S(2)}) copy-start(bf16[1792,512]{1,0:T(8,128)(2,1)} %copy-done.4) | copy-start | bytes 5505028
  79.4 8.5 %collective-permute-start.12 = (bf16[128,3712]{1,0:T(8,128)(2,1)}, bf16[128,3712]{1,0:T(8,128)(2,1)S(1)}, u32[]{:S(2)}, u32[]{:S(2)}) collective-permute-start(bf16[128,3712]{1,0:T(8,128)(2,1)} %collective-permute-done.7.refs_1_), channel_id=1, source_target_pairs={{0,1},{1,0},{2,3},{3,2},{4,5},{5,4},{6,7},{7,6},{8,9},{9,8},{10,11... | collective-permute-start | bytes 2850824 | tf_op jit(solution)/shard_map/ppermute | solution.py:219
  79.4 8.5 %collective-permute-start.13 = (bf16[128,3712]{1,0:T(8,128)(2,1)}, bf16[128,3712]{1,0:T(8,128)(2,1)S(1)}, u32[]{:S(2)}, u32[]{:S(2)}) collective-permute-start(bf16[128,3712]{1,0:T(8,128)(2,1)} %collective-permute-done.8.refs_2_), channel_id=1, source_target_pairs={{0,1},{1,0},{2,3},{3,2},{4,5},{5,4},{6,7},{7,6},{8,9},{9,8},{10,11... | collective-permute-start | bytes 2850824 | tf_op jit(solution)/shard_map/ppermute | solution.py:219
  81.2 14.4 %collective-permute-start.11 = (bf16[128,3712]{1,0:T(8,128)(2,1)S(1)}, bf16[128,3712]{1,0:T(8,128)(2,1)S(1)}, u32[]{:S(2)}, u32[]{:S(2)}) collective-permute-start(bf16[128,3712]{1,0:T(8,128)(2,1)S(1)} %broadcast_select_fusion), channel_id=1, source_target_pairs={{0,4},{4,8},{8,12},{12,14},{14,10},{10,6},{6,2},{2,0},{5,1},{9,5},... | collective-permute-start | bytes 2850824 | tf_op jit(solution)/shard_map/ppermute | solution.py:238
  92.6 1.8 %copy-start.2 = (bf16[512,3584]{1,0:T(8,128)(2,1)}, bf16[512,3584]{1,0:T(8,128)(2,1)S(1)}, u32[]{:S(2)}) copy-start(bf16[512,3584]{1,0:T(8,128)(2,1)S(1)} %get-tuple-element.78.refs_4_) | copy-start | bytes 11010052
  94.4 1.2 %copy-start.6 = (bf16[1792,512]{1,0:T(8,128)(2,1)}, bf16[1792,512]{1,0:T(8,128)(2,1)S(1)}, u32[]{:S(2)}) copy-start(bf16[1792,512]{1,0:T(8,128)(2,1)S(1)} %get-tuple-element.79.refs_5_) | copy-start | bytes 5505028
  95.6 2.5 %collective-permute-start.14 = (bf16[128,3712]{1,0:T(8,128)(2,1)S(1)}, bf16[128,3712]{1,0:T(8,128)(2,1)S(1)}, u32[]{:S(2)}, u32[]{:S(2)}) collective-permute-start(bf16[128,3712]{1,0:T(8,128)(2,1)S(1)} %collective-permute-done.11.refs_1_), channel_id=1, source_target_pairs={{0,1},{1,0},{2,3},{3,2},{4,5},{5,4},{6,7},{7,6},{8,9},{9,8},{10,11... | collective-permute-start | bytes 2850824 | tf_op jit(solution)/shard_map/ppermute | solution.py:219
  98.2 2.0 %copy-start.3 = (bf16[512,3584]{1,0:T(8,128)(2,1)S(1)}, bf16[512,3584]{1,0:T(8,128)(2,1)}, u32[]{:S(2)}) copy-start(bf16[512,3584]{1,0:T(8,128)(2,1)} %copy-done.2) | copy-start | bytes 11010052
  100.2 1.5 %copy-start.7 = (bf16[1792,512]{1,0:T(8,128)(2,1)S(1)}, bf16[1792,512]{1,0:T(8,128)(2,1)}, u32[]{:S(2)}) copy-start(bf16[1792,512]{1,0:T(8,128)(2,1)} %copy-done.6) | copy-start | bytes 5505028

commit v9 on v8

--- a/solution.py
+++ b/solution.py
@@ -96,6 +96,44 @@
                 row += rows
 
 
+def product(left, right):
+    return lax.dot_general(left[...], right[...], ROWS_WITH_ROWS, preferred_element_type=F32)
+
+
+def absorb_kernel(count, started, *refs):
+    scalars, refs = refs[0], refs[1:]
+    pieces, before, refs = refs[:count], refs[count : count + 3 * started], refs[count + 3 * started :]
+    tile, left, theirs, *packs, mine = refs
+    for slot, which in enumerate((left, mine, theirs), start=1):
+        fetch_tile(scalars[slot], pieces, which)
+    update = product(left, mine)
+    if started:
+        update = before[0][...] + update + product(before[1], before[2])
+    tile[...] = update
+    for piece, packed in zip(pieces, packs):
+        packed[...] = pack(scalars[0], piece)
+
+
+def absorb(scalars, pieces, before, edge):
+    rows, width = pieces[0].shape
+    width -= TABLE
+    count = len(pieces)
+    columns = jax.ShapeDtypeStruct((count * rows, edge), BF16)
+    out = pl.pallas_call(
+        functools.partial(absorb_kernel, count, bool(before)),
+        out_shape=[jax.ShapeDtypeStruct((edge, edge), F32), columns, columns]
+        + [jax.ShapeDtypeStruct((CAP, width), BF16)] * count,
+        in_specs=[SMEM] + [VMEM] * (count + len(before)),
+        out_specs=[VMEM] * (3 + count),
+        scratch_shapes=[pltpu.VMEM((count * rows, edge), BF16)],
+        cost_estimate=SMALL,
+        input_output_aliases={1 + count: 0} if before else {},
+        compiler_params=params(14),
+        name="absorb",
+    )(scalars, *pieces, *before)
+    return out[0], out[1:3], out[3:]
+
+
 def place_rows(slab_at, packed, at, rows, across):
     count, width = packed.shape
     slab = across.shape[0]
@@ -107,43 +145,39 @@
             across[:, at : at + count] = packed[:, s * slab : (s + 1) * slab].T
 
 
-def take_in(scalars, pieces, left, right):
-    fetch_tile(scalars[1], pieces, left)
-    fetch_tile(scalars[2], pieces, right)
+def prepare_kernel(places, *refs):
+    scalars, *refs = refs
+    rows, across = refs[-2:]
+    for at, packed in zip(places, refs):
+        place_rows(scalars[4], packed[...], at, rows, across)
+
+
+def prepare(scalars, packs, places, operands, total, slab):
+    width = packs[0].shape[1]
+    return pl.pallas_call(
+        functools.partial(prepare_kernel, places),
+        out_shape=[
+            jax.ShapeDtypeStruct((total, width), BF16),
+            jax.ShapeDtypeStruct((slab, total), BF16),
+        ],
+        in_specs=[SMEM] + [VMEM] * (len(packs) + len(operands)),
+        out_specs=[VMEM] * 2,
+        input_output_aliases={1 + len(packs) + k: k for k in range(len(operands))},
+        cost_estimate=SMALL,
+        compiler_params=params(12),
+        name="prepare_rows",
+    )(scalars, *packs, *operands)
+
+
+def finish_kernel(final, *refs):
+    scalars, halves, refs = refs[0], refs[1:5], refs[5:]
+    before, (hessian, tile, rows, across, *scratch) = refs[:3], refs[5:]
+    staging, sums, left, right, sent = scratch
+    pieces = [
+        jnp.concatenate([halves[k][...], halves[k + 1][...]], axis=0) for k in range(0, 4, 2)
+    ]
     packed = jnp.concatenate([pack(scalars[0], piece) for piece in pieces], axis=0)
-    update = lax.dot_general(left[...], right[...], ROWS_WITH_ROWS, preferred_element_type=F32)
-    return packed, update
-
-
-def absorb_kernel(count, started, at, *refs):
-    scalars, refs = refs[0], refs[1:]
-    pieces, before, (tile, rows, across, left, right) = refs[:count], refs[count:-5], refs[-5:]
-    packed, update = take_in(scalars, pieces, left, right)
-    place_rows(scalars[3], packed, at, rows, across)
-    tile[...] = before[0][...] + update if started else update
-
-
-def absorb(scalars, pieces, at, before, shapes):
-    rows, edge, count = pieces[0].shape[0], shapes[0].shape[0], len(pieces)
-    return pl.pallas_call(
-        functools.partial(absorb_kernel, count, bool(before), at),
-        out_shape=shapes,
-        in_specs=[SMEM] + [VMEM] * (count + len(before)),
-        out_specs=[VMEM] * 3,
-        scratch_shapes=[pltpu.VMEM((count * rows, edge), BF16)] * 2,
-        cost_estimate=SMALL,
-        input_output_aliases={1 + count + k: k for k in range(len(before))},
-        compiler_params=params(14),
-        name="absorb",
-    )(scalars, *pieces, *before)
-
-
-def finish_kernel(final, *refs):
-    scalars, mine, other, before, _, _, hessian, tile, rows, across, *scratch = refs
-    staging, sums, left, right, sent = scratch
-    pieces = [mine, other]
-    packed, update = take_in(scalars, pieces, left, right)
-    place_rows(scalars[3], packed, rows.shape[0] - packed.shape[0], rows, across)
+    place_rows(scalars[4], packed, rows.shape[0] - packed.shape[0], rows, across)
     copies = []
     for n in range(staging.shape[0]):
         span = slice(n * STEP, (n + 1) * STEP)
@@ -152,17 +186,22 @@
         )
         copies.append(pltpu.make_async_copy(staging.at[n], hessian.at[:, span], sent.at[n]))
         copies[-1].start()
-    sums[...] = (before[...] + update) * final
+    fetch_tile(scalars[1], halves, left)
+    fetch_tile(scalars[2], halves, right)
+    sums[...] = (
+        before[0][...] + product(before[1], before[2]) + product(left, right)
+    ) * final
     copies.append(pltpu.make_async_copy(sums, tile.at[0], sent.at[len(copies)]))
     copies[-1].start()
     for copy in copies:
         copy.wait()
 
 
-def finish(scalars, pieces, before, final):
-    tile, rows, across = before
-    edge, slab, width = tile.shape[0], across.shape[0], rows.shape[1]
-    count = sum(piece.shape[0] for piece in pieces)
+def finish(scalars, halves, before, operands, final):
+    edge = before[0].shape[0]
+    rows, across = operands
+    slab, width = across.shape[0], rows.shape[1]
+    count = sum(half.shape[0] for half in halves)
     blocks = width // STEP
     return pl.pallas_call(
         functools.partial(finish_kernel, final),
@@ -172,7 +211,7 @@
             jax.ShapeDtypeStruct(rows.shape, BF16),
             jax.ShapeDtypeStruct(across.shape, BF16),
         ],
-        in_specs=[SMEM] + [VMEM] * 5,
+        in_specs=[SMEM] + [VMEM] * 9,
         out_specs=[ANY, ANY, VMEM, VMEM],
         scratch_shapes=[
             pltpu.VMEM((blocks, slab, STEP), F32),
@@ -181,11 +220,11 @@
             pltpu.VMEM((count, edge), BF16),
             pltpu.SemaphoreType.DMA((blocks + 1,)),
         ],
-        input_output_aliases={4: 2, 5: 3},
+        input_output_aliases={8: 2, 9: 3},
         cost_estimate=SMALL,
-        compiler_params=params(40),
+        compiler_params=params(38),
         name="finish",
-    )(scalars, *pieces, *before)[:2]
+    )(scalars, *halves, *before, rows, across)[:2]
 
 
 def ring_of(chips):
@@ -209,11 +248,16 @@
     ]
     streams = [ahead, [(b, a) for a, b in ahead]]
     pair = [(d, d ^ 1) for d in range(devices)]
+    column = position % grid
     scalars = jnp.stack(
-        [position // group, position // grid, position % grid, position % group]
+        [
+            position // group,
+            position // grid,
+            column,
+            column + 1 - 2 * (column % 2),
+            position % group,
+        ]
     ).astype(jnp.int32)
-    core = position % CORES
-    last_hop = [hop for k in range(CORES) for hop in streams[k][k::CORES]]
 
     def swap(array):
         return lax.ppermute(array, "tok", pair)
@@ -223,31 +267,36 @@
 
     rounds = chips // 2
     total = 4 * CAP * rounds
-    shapes = [
-        jax.ShapeDtypeStruct((edge, edge), F32),
-        jax.ShapeDtypeStruct((total, width), BF16),
-        jax.ShapeDtypeStruct((slab, total), BF16),
-    ]
+
+    def place(index):
+        at = 4 * CAP * (index - 1) if index else total - 4 * CAP
+        return [at + k * CAP for k in range(4 if index else 2)]
+
     pieces = [make_message(tokens, route_ids, route_weights)]
-    sums, waiting = [], []
+    packs, sums = {}, []
+    half = tok_rows // 2
     for step in range(1, rounds + 1):
         held = pieces * CORES if step == 1 else pieces
+        if step == rounds:
+            held = [held[0][:half], held[1][half:]]
+        moved = advance(held)
+        tile, columns, packed = absorb(scalars, pieces, sums, edge)
+        packs[step - 1] = list(packed) + [swap(array) for array in packed]
+        sums = [tile] + [swap(array) for array in columns]
         if step < rounds:
-            moved = advance(held)
-        else:
-            moved = [lax.ppermute(jnp.where(core == 0, *held), "tok", last_hop)]
-        at = 4 * CAP * (step - 2) if step > 1 else total - 4 * CAP
-        waiting.append((at, pieces + [swap(piece) for piece in pieces]))
-        while len(waiting) > (1 if step < rounds else 0):
-            at, both = waiting.pop(0)
-            sums = absorb(scalars, both, at, sums, shapes)
-        moved, sums, arrays = lax.optimization_barrier(
-            (moved, sums, [both for _, both in waiting])
+            moved, packs, sums = lax.optimization_barrier((moved, packs, sums))
+        pieces = moved
+    operands = []
+    for chosen in (range(rounds - 1), [rounds - 1]):
+        operands = prepare(
+            scalars,
+            [array for index in chosen for array in packs[index]],
+            [at for index in chosen for at in place(index)],
+            operands, total, slab,
         )
-        waiting = [(at, both) for (at, _), both in zip(waiting, arrays)]
-        pieces = moved
-    pieces = pieces + [swap(piece) for piece in pieces]
-    return tuple(finish(scalars, pieces, sums, 1.0 / (devices * tok_rows)))
+    pieces, operands, sums = lax.optimization_barrier((pieces, operands, sums))
+    others = [swap(piece) for piece in pieces]
+    return tuple(finish(scalars, pieces + others, sums, operands, 1.0 / (devices * tok_rows)))
 
 
 def solution(mesh):

time: 116 us -> 101 us (0.87)
  local copies, waits for them, and re-layouts: 20 us -> 2.7 us
  waiting for transfers between devices: 52.5 us -> 56.2 us
  starting transfers between devices: 9.89 us -> 12.8 us
  Pallas kernels: 30.3 us -> 28.4 us
  other arithmetic: 1.37 us -> 0 us
    unnamed x30 -> x6, local copies, waits for them, and re-layouts: 20 us -> 2.54 us
    ppermute x8 -> x17, waiting for transfers between devices: 2.54 us -> 9.32 us  [swap(): return lax.ppermute(array, 'tok', pair)]
    ppermute x6 -> x8, waiting for transfers between devices: 49.9 us -> 46.9 us  [advance(): lax.ppermute(array, 'tok', stream)]
    ppermute x6 -> x8, starting transfers between devices: 6.77 us -> 9.27 us  [advance(): lax.ppermute(array, 'tok', stream)]
    ppermute x8 -> x17, starting transfers between devices: 1.49 us -> 3.57 us  [swap(): return lax.ppermute(array, 'tok', pair)]
    ppermute x1 -> x0, starting transfers between devices: 1.63 us -> none  [on_device(): moved = [lax.ppermute(jnp.where(core == 0, *held), 'tok', last_hop)]]
    pallas_call x4 -> x6, Pallas kernels: 17 us -> 15.7 us  [the longest x4 9.19 us: absorb(): pl.pallas_call(functools.partial(absorb_kernel, count, bool(before)), out...]
    select_n x1 -> x0, other arithmetic: 1.3 us -> none  [on_device(): moved = [lax.ppermute(jnp.where(core == 0, *held), 'tok', last_hop)]]
  transfers between devices with their start and end apart: 15 -> 25, of which waited for: 7 -> 16; matrix products, arithmetic and copies ran while one was open for 1% -> 0% of each run, Pallas kernels for 15% -> 15%
where the time goes in v9:
time: 101 us
  waiting for transfers between devices  56.2 us (56%)
  Pallas kernels  28.4 us (28%)
  starting transfers between devices  12.8 us (13%)
  local copies, waits for them, and re-layouts  2.7 us (3%)
    ppermute x8, waiting for transfers between devices, advance(): lax.ppermute(array, 'tok', stream)  46.9 us
    pallas_call x1, Pallas kernels, finish(): pl.pallas_call(functools.partial(finish_kernel, final), out_shape=[jax.Sh...  12.6 us
    ppermute x17, waiting for transfers between devices, swap(): return lax.ppermute(array, 'tok', pair)  9.32 us
    ppermute x8, starting transfers between devices, advance(): lax.ppermute(array, 'tok', stream)  9.27 us
    pallas_call x4, Pallas kernels, absorb(): pl.pallas_call(functools.partial(absorb_kernel, count, bool(before)), out...  9.19 us
    pallas_call x2, Pallas kernels, prepare(): pl.pallas_call(functools.partial(prepare_kernel, places), out_shape=[jax....  6.47 us
    ppermute x17, starting transfers between devices, swap(): return lax.ppermute(array, 'tok', pair)  3.57 us
    unnamed x6, local copies, waits for them, and re-layouts  2.54 us
  transfers between devices with their start and end apart: 25, of which 16 were waited for; matrix products, arithmetic and copies ran while one was open for 0% of the time, Pallas kernels for 15%

profile of v9, /device:TPU:0, one launch (start us, length us, event | category | flops | bytes accessed | tf_op | source)
XLA Modules:
  0.0 101.1 jit_solution(2212040403529109025)
XLA Ops:
  0.6 0.0 copy-start
  0.6 1.2 %copy-done = bf16[128,3584]{1,0:T(8,128)(2,1)S(1)} copy-done((bf16[128,3584]{1,0:T(8,128)(2,1)S(1)}, bf16[128,3584]{1,0:T(8,128)(2,1)}, u32[]{:S(2)}) %copy-start) | copy-done | bytes 917528
  1.8 0.7 copy-done.1
  2.5 0.0 copy-start.2
  2.5 0.7 copy-done.2
  3.2 0.2 make_message.1.refs_1_
  3.4 3.0 %collective-permute-start.1 = (bf16[128,3712]{1,0:T(8,128)(2,1)S(1)}, bf16[128,3712]{1,0:T(8,128)(2,1)S(1)}, u32[]{:S(2)}, u32[]{:S(2)}) collective-permute-start(bf16[128,3712]{1,0:T(8,128)(2,1)S(1)} %make_message.1.refs_1_), channel_id=1, source_target_pairs={{4,0},{5,1},{8,4},{9,5},{12,8},{13,9},{14,12},{15,13},{10,14},{11,... | collective-permute-start | bytes 2850824 | tf_op jit(solution)/shard_map/ppermute | solution.py:266
  6.4 0.1 collective-permute-start
  6.5 0.1 stack.23.refs_0_
  6.6 1.5 %absorb.4 = (f32[896,896]{1,0:T(8,128)S(1)}, bf16[128,896]{1,0:T(8,128)(2,1)S(1)}, bf16[128,896]{1,0:T(8,128)(2,1)S(1)}, bf16[32,3584]{1,0:T(8,128)(2,1)S(1)}) custom-call(s32[5]{0:T(128)S(1)} %stack.23.refs_0_, bf16[128,3712]{1,0:T(8,128)(2,1)S(1)} %make_message.1.refs_1_), custom_call_target="tpu_custom_call" | custom-call | flops 1 | bytes 1 | tf_op jit(solution)/shard_map/absorb/pallas_call | solution.py:122
  8.1 0.1 collective-permute-start.3
  8.2 0.5 collective-permute-start.4
  8.7 0.1 collective-permute-start.2
  8.7 0.9 collective-permute-done.3.refs_4_
  9.6 0.3 collective-permute-done.4.refs_5_
  10.0 0.3 collective-permute-done.2.refs_2_
  10.3 17.2 %collective-permute-done.1.refs_2_ = bf16[128,3712]{1,0:T(8,128)(2,1)S(1)} collective-permute-done((bf16[128,3712]{1,0:T(8,128)(2,1)S(1)}, bf16[128,3712]{1,0:T(8,128)(2,1)S(1)}, u32[]{:S(2)}, u32[]{:S(2)}) %collective-permute-start.1) | collective-permute-done | bytes 950304 | tf_op jit(solution)/shard_map/ppermute | solution.py:266
  27.5 1.4 %collective-permute-done.refs_1_ = bf16[128,3712]{1,0:T(8,128)(2,1)S(1)} collective-permute-done((bf16[128,3712]{1,0:T(8,128)(2,1)S(1)}, bf16[128,3712]{1,0:T(8,128)(2,1)S(1)}, u32[]{:S(2)}, u32[]{:S(2)}) %collective-permute-start) | collective-permute-done | bytes 950304 | tf_op jit(solution)/shard_map/ppermute | solution.py:266
  28.9 0.4 collective-permute-start.5
  29.3 1.6 %collective-permute-start.6 = (bf16[128,3712]{1,0:T(8,128)(2,1)S(1)}, bf16[128,3712]{1,0:T(8,128)(2,1)S(1)}, u32[]{:S(2)}, u32[]{:S(2)}) collective-permute-start(bf16[128,3712]{1,0:T(8,128)(2,1)S(1)} %collective-permute-done.1.refs_2_), channel_id=1, source_target_pairs={{4,0},{5,1},{8,4},{9,5},{12,8},{13,9},{14,12},{15,13},{10,14},{11,... | collective-permute-start | bytes 2850824 | tf_op jit(solution)/shard_map/ppermute | solution.py:266
  31.0 2.5 %absorb.5 = (f32[896,896]{1,0:T(8,128)S(1)}, bf16[256,896]{1,0:T(8,128)(2,1)S(1)}, bf16[256,896]{1,0:T(8,128)(2,1)S(1)}, bf16[32,3584]{1,0:T(8,128)(2,1)S(1)}, bf16[32,3584]{1,0:T(8,128)(2,1)S(1)}) custom-call(s32[5]{0:T(128)S(1)} %stack.23.refs_0_, bf16[128,3712]{1,0:T(8,128)(2,1)S(1)} %collective-permute-done.refs_1_, ...), custom_call_target="tpu_custom_call", output_to_operand_aliasing={{0}: (3, {})} | custom-call | flops 1 | bytes 1 | tf_op jit(solution)/shard_map/absorb/pallas_call | solution.py:122
  33.5 0.1 collective-permute-start.7
  33.6 0.5 collective-permute-start.9
  34.1 0.1 collective-permute-start.10
  34.2 0.9 collective-permute-done.7.refs_5_
  35.1 0.1 collective-permute-start.8
  35.2 1.5 %collective-permute-done.8.refs_6_ = bf16[32,3584]{1,0:T(8,128)(2,1)S(1)} collective-permute-done((bf16[32,3584]{1,0:T(8,128)(2,1)S(1)}, bf16[32,3584]{1,0:T(8,128)(2,1)S(1)}, u32[]{:S(2)}, u32[]{:S(2)}) %collective-permute-start.8) | collective-permute-done | bytes 229408 | tf_op jit(solution)/shard_map/ppermute | solution.py:263
  36.7 0.0 collective-permute-done.9.refs_4_
  36.7 0.0 collective-permute-done.10.refs_5_
  36.7 13.8 %collective-permute-done.5.refs_1_ = bf16[128,3712]{1,0:T(8,128)(2,1)S(1)} collective-permute-done((bf16[128,3712]{1,0:T(8,128)(2,1)S(1)}, bf16[128,3712]{1,0:T(8,128)(2,1)S(1)}, u32[]{:S(2)}, u32[]{:S(2)}) %collective-permute-start.5) | collective-permute-done | bytes 950304 | tf_op jit(solution)/shard_map/ppermute | solution.py:266
  50.5 0.4 collective-permute-done.6.refs_2_
  51.0 1.5 %collective-permute-start.11 = (bf16[128,3712]{1,0:T(8,128)(2,1)S(1)}, bf16[128,3712]{1,0:T(8,128)(2,1)S(1)}, u32[]{:S(2)}, u32[]{:S(2)}) collective-permute-start(bf16[128,3712]{1,0:T(8,128)(2,1)S(1)} %collective-permute-done.5.refs_1_), channel_id=1, source_target_pairs={{0,4},{1,5},{4,8},{5,9},{8,12},{9,13},{12,14},{13,15},{14,10},{15,... | collective-permute-start | bytes 2850824 | tf_op jit(solution)/shard_map/ppermute | solution.py:266
  52.5 0.5 collective-permute-start.12
  53.0 2.6 %absorb.6 = (f32[896,896]{1,0:T(8,128)S(1)}, bf16[256,896]{1,0:T(8,128)(2,1)S(1)}, bf16[256,896]{1,0:T(8,128)(2,1)S(1)}, bf16[32,3584]{1,0:T(8,128)(2,1)S(1)}, bf16[32,3584]{1,0:T(8,128)(2,1)S(1)}) custom-call(s32[5]{0:T(128)S(1)} %stack.23.refs_0_, bf16[128,3712]{1,0:T(8,128)(2,1)S(1)} %collective-permute-done.5.refs_1_, ...), custom_call_target="tpu_custom_call", output_to_operand_aliasing={{0}: (3, {})} | custom-call | flops 1 | bytes 1 | tf_op jit(solution)/shard_map/absorb/pallas_call | solution.py:122
  55.6 0.1 collective-permute-start.13
  55.7 0.5 collective-permute-start.15
  56.2 0.1 collective-permute-start.16
  56.2 0.9 collective-permute-done.13.refs_9_
  57.1 0.1 collective-permute-start.14
  57.3 1.5 %collective-permute-done.14.refs_10_ = bf16[32,3584]{1,0:T(8,128)(2,1)S(1)} collective-permute-done((bf16[32,3584]{1,0:T(8,128)(2,1)S(1)}, bf16[32,3584]{1,0:T(8,128)(2,1)S(1)}, u32[]{:S(2)}, u32[]{:S(2)}) %collective-permute-start.14) | collective-permute-done | bytes 229408 | tf_op jit(solution)/shard_map/ppermute | solution.py:263
  58.8 0.0 collective-permute-done.15.refs_4_
  58.8 0.0 collective-permute-done.16.refs_5_
  58.8 12.9 %collective-permute-done.11.refs_1_ = bf16[128,3712]{1,0:T(8,128)(2,1)S(1)} collective-permute-done((bf16[128,3712]{1,0:T(8,128)(2,1)S(1)}, bf16[128,3712]{1,0:T(8,128)(2,1)S(1)}, u32[]{:S(2)}, u32[]{:S(2)}) %collective-permute-start.11) | collective-permute-done | bytes 950304 | tf_op jit(solution)/shard_map/ppermute | solution.py:266
  71.7 1.1 %collective-permute-done.12.refs_2_ = bf16[128,3712]{1,0:T(8,128)(2,1)S(1)} collective-permute-done((bf16[128,3712]{1,0:T(8,128)(2,1)S(1)}, bf16[128,3712]{1,0:T(8,128)(2,1)S(1)}, u32[]{:S(2)}, u32[]{:S(2)}) %collective-permute-start.12) | collective-permute-done | bytes 950304 | tf_op jit(solution)/shard_map/ppermute | solution.py:266
  72.8 1.6 %collective-permute-start.17 = (bf16[64,3712]{1,0:T(8,128)(2,1)S(1)}, bf16[64,3712]{1,0:T(8,128)(2,1)S(1)}, u32[]{:S(2)}, u32[]{:S(2)}) collective-permute-start(bf16[64,3712]{1,0:T(8,128)(2,1)S(1)} %slice.6), channel_id=1, source_target_pairs={{0,4},{1,5},{4,8},{5,9},{8,12},{9,13},{12,14},{13,15},{14,10},{15,... | collective-permute-start | bytes 1425416 | tf_op jit(solution)/shard_map/ppermute | solution.py:266
  74.5 0.5 collective-permute-start.18
  74.9 2.6 %absorb.7 = (f32[896,896]{1,0:T(8,128)S(1)}, bf16[256,896]{1,0:T(8,128)(2,1)S(1)}, bf16[256,896]{1,0:T(8,128)(2,1)S(1)}, bf16[32,3584]{1,0:T(8,128)(2,1)S(1)}, bf16[32,3584]{1,0:T(8,128)(2,1)S(1)}) custom-call(s32[5]{0:T(128)S(1)} %stack.23.refs_0_, bf16[128,3712]{1,0:T(8,128)(2,1)S(1)} %collective-permute-done.11.refs_1_, ...), custom_call_target="tpu_custom_call", output_to_operand_aliasing={{0}: (3, {})} | custom-call | flops 1 | bytes 1 | tf_op jit(solution)/shard_map/absorb/pallas_call | solution.py:122
  77.5 0.1 collective-permute-start.19
  77.6 0.5 collective-permute-start.21
  78.1 0.1 collective-permute-start.22
  78.2 0.9 collective-permute-done.19.refs_3_
  79.1 0.1 collective-permute-start.20
  79.2 4.4 %prepare_rows.2 = (bf16[512,3584]{1,0:T(8,128)(2,1)S(1)}, bf16[1792,512]{1,0:T(8,128)(2,1)S(1)}) custom-call(s32[5]{0:T(128)S(1)} %stack.23.refs_0_, bf16[32,3584]{1,0:T(8,128)(2,1)S(1)} %get-tuple-element.106.refs_1_, bf16[32,3584]{1,0:T(8,128)(2,1)S(1)} %collective-permute-done.2.refs_2_, bf16[32,3584]{1,0:T(8,128)(2,1)S(1)} %get-tuple-element.108.refs_3_, ...), custom_call_target="tpu_custom_call" | custom-call | flops 1 | bytes 1 | tf_op jit(solution)/shard_map/prepare_rows/pallas_call | solution.py:157
  83.6 0.0 collective-permute-done.20.refs_4_
  83.6 2.1 %prepare_rows.3 = (bf16[512,3584]{1,0:T(8,128)(2,1)S(1)}, bf16[1792,512]{1,0:T(8,128)(2,1)S(1)}) custom-call(s32[5]{0:T(128)S(1)} %stack.23.refs_0_, bf16[32,3584]{1,0:T(8,128)(2,1)S(1)} %get-tuple-element.104.refs_1_, bf16[32,3584]{1,0:T(8,128)(2,1)S(1)} %get-tuple-element.105.refs_2_, ...), custom_call_target="tpu_custom_call", output_to_operand_aliasing={{0}: (5, {}), {1}: (6, {})} | custom-call | flops 1 | bytes 1 | tf_op jit(solution)/shard_map/prepare_rows/pallas_call | solution.py:157
  85.7 0.0 collective-permute-done.21.refs_6_
  85.7 0.0 collective-permute-done.22.refs_7_
  85.7 0.0 collective-permute-done.17.refs_1_
  85.7 0.0 collective-permute-done.18.refs_2_
  85.7 0.5 collective-permute-start.23
  86.2 0.1 collective-permute-start.24
  86.3 1.4 %collective-permute-done.23.refs_3_ = bf16[64,3712]{1,0:T(8,128)(2,1)S(1)} collective-permute-done((bf16[64,3712]{1,0:T(8,128)(2,1)S(1)}, bf16[64,3712]{1,0:T(8,128)(2,1)S(1)}, u32[]{:S(2)}, u32[]{:S(2)}) %collective-permute-start.23) | collective-permute-done | bytes 475168 | tf_op jit(solution)/shard_map/ppermute | solution.py:263
  87.7 0.7 collective-permute-done.24.refs_4_
  88.4 12.6 %finish.1 = (f32[1792,3584]{1,0:T(8,128)}, f32[1,896,896]{2,1,0:T(8,128)}, bf16[512,3584]{1,0:T(8,128)(2,1)S(1)}, bf16[1792,512]{1,0:T(8,128)(2,1)S(1)}) custom-call(s32[5]{0:T(128)S(1)} %stack.23.refs_0_, bf16[64,3712]{1,0:T(8,128)(2,1)S(1)} %collective-permute-done.17.refs_1_, ...), custom_call_target="tpu_custom_call", output_to_operand_aliasing={{2}: (8, {}), {3}: (9, {})} | custom-call | flops 1 | bytes 1 | tf_op jit(solution)/shard_map/finish/pallas_call | solution.py:206
  (3 shorter events, 0.1 us)
Async XLA Ops:
  0.6 1.2 %copy-start = (bf16[128,3584]{1,0:T(8,128)(2,1)S(1)}, bf16[128,3584]{1,0:T(8,128)(2,1)}, u32[]{:S(2)}) copy-start(bf16[128,3584]{1,0:T(8,128)(2,1)} %tokens.1) | copy-start | bytes 2752516
  1.8 0.7 copy-start.1
  2.5 0.7 copy-start.2
  3.4 24.1 %collective-permute-start.1 = (bf16[128,3712]{1,0:T(8,128)(2,1)S(1)}, bf16[128,3712]{1,0:T(8,128)(2,1)S(1)}, u32[]{:S(2)}, u32[]{:S(2)}) collective-permute-start(bf16[128,3712]{1,0:T(8,128)(2,1)S(1)} %make_message.1.refs_1_), channel_id=1, source_target_pairs={{4,0},{5,1},{8,4},{9,5},{12,8},{13,9},{14,12},{15,13},{10,14},{11,... | collective-permute-start | bytes 2850824 | tf_op jit(solution)/shard_map/ppermute | solution.py:266
  6.4 22.5 %collective-permute-start = (bf16[128,3712]{1,0:T(8,128)(2,1)S(1)}, bf16[128,3712]{1,0:T(8,128)(2,1)S(1)}, u32[]{:S(2)}, u32[]{:S(2)}) collective-permute-start(bf16[128,3712]{1,0:T(8,128)(2,1)S(1)} %make_message.1.refs_1_), channel_id=1, source_target_pairs={{0,4},{1,5},{4,8},{5,9},{8,12},{9,13},{12,14},{13,15},{14,10},{15,... | collective-permute-start | bytes 2850824 | tf_op jit(solution)/shard_map/ppermute | solution.py:266
  8.1 1.6 %collective-permute-start.3 = (bf16[128,896]{1,0:T(8,128)(2,1)S(1)}, bf16[128,896]{1,0:T(8,128)(2,1)S(1)}, u32[]{:S(2)}, u32[]{:S(2)}) collective-permute-start(bf16[128,896]{1,0:T(8,128)(2,1)S(1)} %get-tuple-element.69), channel_id=1, source_target_pairs={{0,1},{1,0},{2,3},{3,2},{4,5},{5,4},{6,7},{7,6},{8,9},{9,8},{10,11... | collective-permute-start | bytes 688136 | tf_op jit(solution)/shard_map/ppermute | solution.py:263
  8.2 1.8 %collective-permute-start.4 = (bf16[128,896]{1,0:T(8,128)(2,1)S(1)}, bf16[128,896]{1,0:T(8,128)(2,1)S(1)}, u32[]{:S(2)}, u32[]{:S(2)}) collective-permute-start(bf16[128,896]{1,0:T(8,128)(2,1)S(1)} %get-tuple-element.70), channel_id=1, source_target_pairs={{0,1},{1,0},{2,3},{3,2},{4,5},{5,4},{6,7},{7,6},{8,9},{9,8},{10,11... | collective-permute-start | bytes 688136 | tf_op jit(solution)/shard_map/ppermute | solution.py:263
  8.7 1.6 %collective-permute-start.2 = (bf16[32,3584]{1,0:T(8,128)(2,1)S(1)}, bf16[32,3584]{1,0:T(8,128)(2,1)S(1)}, u32[]{:S(2)}, u32[]{:S(2)}) collective-permute-start(bf16[32,3584]{1,0:T(8,128)(2,1)S(1)} %get-tuple-element.106.refs_1_), channel_id=1, source_target_pairs={{0,1},{1,0},{2,3},{3,2},{4,5},{5,4},{6,7},{7,6},{8,9},{9,8},{10,11... | collective-permute-start | bytes 688136 | tf_op jit(solution)/shard_map/ppermute | solution.py:263
  28.9 21.6 %collective-permute-start.5 = (bf16[128,3712]{1,0:T(8,128)(2,1)S(1)}, bf16[128,3712]{1,0:T(8,128)(2,1)S(1)}, u32[]{:S(2)}, u32[]{:S(2)}) collective-permute-start(bf16[128,3712]{1,0:T(8,128)(2,1)S(1)} %collective-permute-done.refs_1_), channel_id=1, source_target_pairs={{0,4},{1,5},{4,8},{5,9},{8,12},{9,13},{12,14},{13,15},{14,10},{15,... | collective-permute-start | bytes 2850824 | tf_op jit(solution)/shard_map/ppermute | solution.py:266
  29.3 21.6 %collective-permute-start.6 = (bf16[128,3712]{1,0:T(8,128)(2,1)S(1)}, bf16[128,3712]{1,0:T(8,128)(2,1)S(1)}, u32[]{:S(2)}, u32[]{:S(2)}) collective-permute-start(bf16[128,3712]{1,0:T(8,128)(2,1)S(1)} %collective-permute-done.1.refs_2_), channel_id=1, source_target_pairs={{4,0},{5,1},{8,4},{9,5},{12,8},{13,9},{14,12},{15,13},{10,14},{11,... | collective-permute-start | bytes 2850824 | tf_op jit(solution)/shard_map/ppermute | solution.py:266
  33.5 1.6 %collective-permute-start.7 = (bf16[32,3584]{1,0:T(8,128)(2,1)S(1)}, bf16[32,3584]{1,0:T(8,128)(2,1)S(1)}, u32[]{:S(2)}, u32[]{:S(2)}) collective-permute-start(bf16[32,3584]{1,0:T(8,128)(2,1)S(1)} %get-tuple-element.108.refs_3_), channel_id=1, source_target_pairs={{0,1},{1,0},{2,3},{3,2},{4,5},{5,4},{6,7},{7,6},{8,9},{9,8},{10,11... | collective-permute-start | bytes 688136 | tf_op jit(solution)/shard_map/ppermute | solution.py:263
  33.6 3.1 %collective-permute-start.9 = (bf16[256,896]{1,0:T(8,128)(2,1)S(1)}, bf16[256,896]{1,0:T(8,128)(2,1)S(1)}, u32[]{:S(2)}, u32[]{:S(2)}) collective-permute-start(bf16[256,896]{1,0:T(8,128)(2,1)S(1)} %get-tuple-element.81), channel_id=1, source_target_pairs={{0,1},{1,0},{2,3},{3,2},{4,5},{5,4},{6,7},{7,6},{8,9},{9,8},{10,11... | collective-permute-start | bytes 1376264 | tf_op jit(solution)/shard_map/ppermute | solution.py:263
  34.1 2.6 %collective-permute-start.10 = (bf16[256,896]{1,0:T(8,128)(2,1)S(1)}, bf16[256,896]{1,0:T(8,128)(2,1)S(1)}, u32[]{:S(2)}, u32[]{:S(2)}) collective-permute-start(bf16[256,896]{1,0:T(8,128)(2,1)S(1)} %get-tuple-element.82), channel_id=1, source_target_pairs={{0,1},{1,0},{2,3},{3,2},{4,5},{5,4},{6,7},{7,6},{8,9},{9,8},{10,11... | collective-permute-start | bytes 1376264 | tf_op jit(solution)/shard_map/ppermute | solution.py:263
  35.1 1.6 %collective-permute-start.8 = (bf16[32,3584]{1,0:T(8,128)(2,1)S(1)}, bf16[32,3584]{1,0:T(8,128)(2,1)S(1)}, u32[]{:S(2)}, u32[]{:S(2)}) collective-permute-start(bf16[32,3584]{1,0:T(8,128)(2,1)S(1)} %get-tuple-element.109.refs_4_), channel_id=1, source_target_pairs={{0,1},{1,0},{2,3},{3,2},{4,5},{5,4},{6,7},{7,6},{8,9},{9,8},{10,11... | collective-permute-start | bytes 688136 | tf_op jit(solution)/shard_map/ppermute | solution.py:263
  51.0 20.7 %collective-permute-start.11 = (bf16[128,3712]{1,0:T(8,128)(2,1)S(1)}, bf16[128,3712]{1,0:T(8,128)(2,1)S(1)}, u32[]{:S(2)}, u32[]{:S(2)}) collective-permute-start(bf16[128,3712]{1,0:T(8,128)(2,1)S(1)} %collective-permute-done.5.refs_1_), channel_id=1, source_target_pairs={{0,4},{1,5},{4,8},{5,9},{8,12},{9,13},{12,14},{13,15},{14,10},{15,... | collective-permute-start | bytes 2850824 | tf_op jit(solution)/shard_map/ppermute | solution.py:266
  52.5 20.3 %collective-permute-start.12 = (bf16[128,3712]{1,0:T(8,128)(2,1)S(1)}, bf16[128,3712]{1,0:T(8,128)(2,1)S(1)}, u32[]{:S(2)}, u32[]{:S(2)}) collective-permute-start(bf16[128,3712]{1,0:T(8,128)(2,1)S(1)} %collective-permute-done.6.refs_2_), channel_id=1, source_target_pairs={{4,0},{5,1},{8,4},{9,5},{12,8},{13,9},{14,12},{15,13},{10,14},{11,... | collective-permute-start | bytes 2850824 | tf_op jit(solution)/shard_map/ppermute | solution.py:266
  55.6 1.6 %collective-permute-start.13 = (bf16[32,3584]{1,0:T(8,128)(2,1)S(1)}, bf16[32,3584]{1,0:T(8,128)(2,1)S(1)}, u32[]{:S(2)}, u32[]{:S(2)}) collective-permute-start(bf16[32,3584]{1,0:T(8,128)(2,1)S(1)} %get-tuple-element.112.refs_7_), channel_id=1, source_target_pairs={{0,1},{1,0},{2,3},{3,2},{4,5},{5,4},{6,7},{7,6},{8,9},{9,8},{10,11... | collective-permute-start | bytes 688136 | tf_op jit(solution)/shard_map/ppermute | solution.py:263
  55.7 3.1 %collective-permute-start.15 = (bf16[256,896]{1,0:T(8,128)(2,1)S(1)}, bf16[256,896]{1,0:T(8,128)(2,1)S(1)}, u32[]{:S(2)}, u32[]{:S(2)}) collective-permute-start(bf16[256,896]{1,0:T(8,128)(2,1)S(1)} %get-tuple-element.97), channel_id=1, source_target_pairs={{0,1},{1,0},{2,3},{3,2},{4,5},{5,4},{6,7},{7,6},{8,9},{9,8},{10,11... | collective-permute-start | bytes 1376264 | tf_op jit(solution)/shard_map/ppermute | solution.py:263
  56.2 2.6 %collective-permute-start.16 = (bf16[256,896]{1,0:T(8,128)(2,1)S(1)}, bf16[256,896]{1,0:T(8,128)(2,1)S(1)}, u32[]{:S(2)}, u32[]{:S(2)}) collective-permute-start(bf16[256,896]{1,0:T(8,128)(2,1)S(1)} %get-tuple-element.98), channel_id=1, source_target_pairs={{0,1},{1,0},{2,3},{3,2},{4,5},{5,4},{6,7},{7,6},{8,9},{9,8},{10,11... | collective-permute-start | bytes 1376264 | tf_op jit(solution)/shard_map/ppermute | solution.py:263
  57.1 1.6 %collective-permute-start.14 = (bf16[32,3584]{1,0:T(8,128)(2,1)S(1)}, bf16[32,3584]{1,0:T(8,128)(2,1)S(1)}, u32[]{:S(2)}, u32[]{:S(2)}) collective-permute-start(bf16[32,3584]{1,0:T(8,128)(2,1)S(1)} %get-tuple-element.113.refs_8_), channel_id=1, source_target_pairs={{0,1},{1,0},{2,3},{3,2},{4,5},{5,4},{6,7},{7,6},{8,9},{9,8},{10,11... | collective-permute-start | bytes 688136 | tf_op jit(solution)/shard_map/ppermute | solution.py:263
  72.8 12.9 %collective-permute-start.17 = (bf16[64,3712]{1,0:T(8,128)(2,1)S(1)}, bf16[64,3712]{1,0:T(8,128)(2,1)S(1)}, u32[]{:S(2)}, u32[]{:S(2)}) collective-permute-start(bf16[64,3712]{1,0:T(8,128)(2,1)S(1)} %slice.6), channel_id=1, source_target_pairs={{0,4},{1,5},{4,8},{5,9},{8,12},{9,13},{12,14},{13,15},{14,10},{15,... | collective-permute-start | bytes 1425416 | tf_op jit(solution)/shard_map/ppermute | solution.py:266
  74.5 11.3 %collective-permute-start.18 = (bf16[64,3712]{1,0:T(8,128)(2,1)S(1)}, bf16[64,3712]{1,0:T(8,128)(2,1)S(1)}, u32[]{:S(2)}, u32[]{:S(2)}) collective-permute-start(bf16[64,3712]{1,0:T(8,128)(2,1)S(1)} %slice.7), channel_id=1, source_target_pairs={{4,0},{5,1},{8,4},{9,5},{12,8},{13,9},{14,12},{15,13},{10,14},{11,... | collective-permute-start | bytes 1425416 | tf_op jit(solution)/shard_map/ppermute | solution.py:266
  77.5 1.6 %collective-permute-start.19 = (bf16[32,3584]{1,0:T(8,128)(2,1)S(1)}, bf16[32,3584]{1,0:T(8,128)(2,1)S(1)}, u32[]{:S(2)}, u32[]{:S(2)}) collective-permute-start(bf16[32,3584]{1,0:T(8,128)(2,1)S(1)} %get-tuple-element.104.refs_1_), channel_id=1, source_target_pairs={{0,1},{1,0},{2,3},{3,2},{4,5},{5,4},{6,7},{7,6},{8,9},{9,8},{10,11... | collective-permute-start | bytes 688136 | tf_op jit(solution)/shard_map/ppermute | solution.py:263
  77.6 8.1 %collective-permute-start.21 = (bf16[256,896]{1,0:T(8,128)(2,1)S(1)}, bf16[256,896]{1,0:T(8,128)(2,1)S(1)}, u32[]{:S(2)}, u32[]{:S(2)}) collective-permute-start(bf16[256,896]{1,0:T(8,128)(2,1)S(1)} %get-tuple-element.121), channel_id=1, source_target_pairs={{0,1},{1,0},{2,3},{3,2},{4,5},{5,4},{6,7},{7,6},{8,9},{9,8},{10,11... | collective-permute-start | bytes 1376264 | tf_op jit(solution)/shard_map/ppermute | solution.py:263
  78.1 7.6 %collective-permute-start.22 = (bf16[256,896]{1,0:T(8,128)(2,1)S(1)}, bf16[256,896]{1,0:T(8,128)(2,1)S(1)}, u32[]{:S(2)}, u32[]{:S(2)}) collective-permute-start(bf16[256,896]{1,0:T(8,128)(2,1)S(1)} %get-tuple-element.122), channel_id=1, source_target_pairs={{0,1},{1,0},{2,3},{3,2},{4,5},{5,4},{6,7},{7,6},{8,9},{9,8},{10,11... | collective-permute-start | bytes 1376264 | tf_op jit(solution)/shard_map/ppermute | solution.py:263
  79.1 4.6 %collective-permute-start.20 = (bf16[32,3584]{1,0:T(8,128)(2,1)S(1)}, bf16[32,3584]{1,0:T(8,128)(2,1)S(1)}, u32[]{:S(2)}, u32[]{:S(2)}) collective-permute-start(bf16[32,3584]{1,0:T(8,128)(2,1)S(1)} %get-tuple-element.105.refs_2_), channel_id=1, source_target_pairs={{0,1},{1,0},{2,3},{3,2},{4,5},{5,4},{6,7},{7,6},{8,9},{9,8},{10,11... | collective-permute-start | bytes 688136 | tf_op jit(solution)/shard_map/ppermute | solution.py:263
  85.7 1.9 %collective-permute-start.23 = (bf16[64,3712]{1,0:T(8,128)(2,1)S(1)}, bf16[64,3712]{1,0:T(8,128)(2,1)S(1)}, u32[]{:S(2)}, u32[]{:S(2)}) collective-permute-start(bf16[64,3712]{1,0:T(8,128)(2,1)S(1)} %collective-permute-done.17.refs_1_), channel_id=1, source_target_pairs={{0,1},{1,0},{2,3},{3,2},{4,5},{5,4},{6,7},{7,6},{8,9},{9,8},{10,11... | collective-permute-start | bytes 1425416 | tf_op jit(solution)/shard_map/ppermute | solution.py:263
  86.2 2.1 %collective-permute-start.24 = (bf16[64,3712]{1,0:T(8,128)(2,1)S(1)}, bf16[64,3712]{1,0:T(8,128)(2,1)S(1)}, u32[]{:S(2)}, u32[]{:S(2)}) collective-permute-start(bf16[64,3712]{1,0:T(8,128)(2,1)S(1)} %collective-permute-done.18.refs_2_), channel_id=1, source_target_pairs={{0,1},{1,0},{2,3},{3,2},{4,5},{5,4},{6,7},{7,6},{8,9},{9,8},{10,11... | collective-permute-start | bytes 1425416 | tf_op jit(solution)/shard_map/ppermute | solution.py:263

commit v10 on v9

--- a/solution.py
+++ b/solution.py
@@ -12,7 +12,7 @@
 CAP = 32
 CORES = 2
 TABLE = 128
-STEP = 256
+STEP = 512
 VMEM = pl.BlockSpec(memory_space=pltpu.VMEM)
 SMEM = pl.BlockSpec(memory_space=pltpu.SMEM)
 ANY = pl.BlockSpec(memory_space=pl.ANY)
@@ -145,17 +145,16 @@
             across[:, at : at + count] = packed[:, s * slab : (s + 1) * slab].T
 
 
-def prepare_kernel(places, *refs):
-    scalars, *refs = refs
-    rows, across = refs[-2:]
-    for at, packed in zip(places, refs):
-        place_rows(scalars[4], packed[...], at, rows, across)
-
-
-def prepare(scalars, packs, places, operands, total, slab):
+def prepare_kernel(count, at, *refs):
+    scalars, packs, (rows, across) = refs[0], refs[1 : 1 + count], refs[-2:]
+    packed = jnp.concatenate([array[...] for array in packs], axis=0)
+    place_rows(scalars[4], packed, at, rows, across)
+
+
+def prepare(scalars, packs, at, operands, total, slab):
     width = packs[0].shape[1]
     return pl.pallas_call(
-        functools.partial(prepare_kernel, places),
+        functools.partial(prepare_kernel, len(packs), at),
         out_shape=[
             jax.ShapeDtypeStruct((total, width), BF16),
             jax.ShapeDtypeStruct((slab, total), BF16),
@@ -268,12 +267,8 @@
     rounds = chips // 2
     total = 4 * CAP * rounds
 
-    def place(index):
-        at = 4 * CAP * (index - 1) if index else total - 4 * CAP
-        return [at + k * CAP for k in range(4 if index else 2)]
-
     pieces = [make_message(tokens, route_ids, route_weights)]
-    packs, sums = {}, []
+    operands, sums = [], []
     half = tok_rows // 2
     for step in range(1, rounds + 1):
         held = pieces * CORES if step == 1 else pieces
@@ -281,19 +276,13 @@
             held = [held[0][:half], held[1][half:]]
         moved = advance(held)
         tile, columns, packed = absorb(scalars, pieces, sums, edge)
-        packs[step - 1] = list(packed) + [swap(array) for array in packed]
         sums = [tile] + [swap(array) for array in columns]
+        at = 4 * CAP * (step - 2) if step > 1 else total - 4 * CAP
+        packs = list(packed) + [swap(array) for array in packed]
+        operands = prepare(scalars, packs, at, operands, total, slab)
         if step < rounds:
-            moved, packs, sums = lax.optimization_barrier((moved, packs, sums))
+            moved, operands, sums = lax.optimization_barrier((moved, operands, sums))
         pieces = moved
-    operands = []
-    for chosen in (range(rounds - 1), [rounds - 1]):
-        operands = prepare(
-            scalars,
-            [array for index in chosen for array in packs[index]],
-            [at for index in chosen for at in place(index)],
-            operands, total, slab,
-        )
     pieces, operands, sums = lax.optimization_barrier((pieces, operands, sums))
     others = [swap(piece) for piece in pieces]
     return tuple(finish(scalars, pieces + others, sums, operands, 1.0 / (devices * tok_rows)))

time: 101 us -> 98.9 us (0.979)
  Pallas kernels: 28.4 us -> 25.3 us
    pallas_call x2 -> x4, Pallas kernels: 6.47 us -> 3.21 us  [prepare(): pl.pallas_call(functools.partial(prepare_kernel, len(packs), at), out_sha...]
  transfers between devices with their start and end apart: 25 -> 25, of which waited for: 16 -> 17; matrix products, arithmetic and copies ran while one was open for 0% -> 0% of each run, Pallas kernels for 15% -> 13%
where the time goes in v10:
time: 98.9 us; the launch traced here: 98.7 us
  waiting for transfers between devices  57 us (58%)
  Pallas kernels  25.3 us (26%)
  starting transfers between devices  12.8 us (13%)
  local copies, waits for them, and re-layouts  2.7 us (3%)
    ppermute x8, waiting for transfers between devices, advance(): lax.ppermute(array, 'tok', stream)  46.8 us
    pallas_call x1, Pallas kernels, finish(): pl.pallas_call(functools.partial(finish_kernel, final), out_shape=[jax.Sh...  12.7 us
    ppermute x17, waiting for transfers between devices, swap(): return lax.ppermute(array, 'tok', pair)  10.1 us
    ppermute x8, starting transfers between devices, advance(): lax.ppermute(array, 'tok', stream)  9.27 us
    pallas_call x4, Pallas kernels, absorb(): pl.pallas_call(functools.partial(absorb_kernel, count, bool(before)), out...  9.2 us
    ppermute x17, starting transfers between devices, swap(): return lax.ppermute(array, 'tok', pair)  3.5 us
    pallas_call x4, Pallas kernels, prepare(): pl.pallas_call(functools.partial(prepare_kernel, len(packs), at), out_sha...  3.21 us
    unnamed x6, local copies, waits for them, and re-layouts  2.54 us
  transfers between devices with their start and end apart: 25, of which 17 were waited for; matrix products, arithmetic and copies ran while one was open for 0% of the time, Pallas kernels for 13%

profile of v10, /device:TPU:0, one launch (start us, length us, event | category | flops | bytes accessed | tf_op | source)
XLA Modules:
  0.0 98.7 jit_solution(11317727856950391841)
XLA Ops:
  0.6 1.2 %copy-done = bf16[128,3584]{1,0:T(8,128)(2,1)S(1)} copy-done((bf16[128,3584]{1,0:T(8,128)(2,1)S(1)}, bf16[128,3584]{1,0:T(8,128)(2,1)}, u32[]{:S(2)}) %copy-start) | copy-done | bytes 917528
  1.8 0.7 copy-done.1
  2.5 0.7 copy-done.2
  3.2 0.2 make_message.1.refs_1_
  3.4 3.0 %collective-permute-start.1 = (bf16[128,3712]{1,0:T(8,128)(2,1)S(1)}, bf16[128,3712]{1,0:T(8,128)(2,1)S(1)}, u32[]{:S(2)}, u32[]{:S(2)}) collective-permute-start(bf16[128,3712]{1,0:T(8,128)(2,1)S(1)} %make_message.1.refs_1_), channel_id=1, source_target_pairs={{4,0},{5,1},{8,4},{9,5},{12,8},{13,9},{14,12},{15,13},{10,14},{11,... | collective-permute-start | bytes 2850824 | tf_op jit(solution)/shard_map/ppermute | solution.py:265
  6.4 0.1 collective-permute-start
  6.5 0.1 stack.23.refs_0_
  6.6 1.5 %absorb.4 = (f32[896,896]{1,0:T(8,128)S(1)}, bf16[128,896]{1,0:T(8,128)(2,1)S(1)}, bf16[128,896]{1,0:T(8,128)(2,1)S(1)}, bf16[32,3584]{1,0:T(8,128)(2,1)S(1)}) custom-call(s32[5]{0:T(128)S(1)} %stack.23.refs_0_, bf16[128,3712]{1,0:T(8,128)(2,1)S(1)} %make_message.1.refs_1_), custom_call_target="tpu_custom_call" | custom-call | flops 1 | bytes 1 | tf_op jit(solution)/shard_map/absorb/pallas_call | solution.py:122
  8.1 0.1 collective-permute-start.2
  8.2 0.5 collective-permute-start.3
  8.7 0.1 collective-permute-start.4
  8.7 0.9 collective-permute-done.2.refs_2_
  9.6 0.8 prepare_rows.4
  10.4 0.0 collective-permute-done.3.refs_4_
  10.4 0.0 collective-permute-done.4.refs_5_
  10.4 17.1 %collective-permute-done.1.refs_2_ = bf16[128,3712]{1,0:T(8,128)(2,1)S(1)} collective-permute-done((bf16[128,3712]{1,0:T(8,128)(2,1)S(1)}, bf16[128,3712]{1,0:T(8,128)(2,1)S(1)}, u32[]{:S(2)}, u32[]{:S(2)}) %collective-permute-start.1) | collective-permute-done | bytes 950304 | tf_op jit(solution)/shard_map/ppermute | solution.py:265
  27.5 1.4 %collective-permute-done.refs_1_ = bf16[128,3712]{1,0:T(8,128)(2,1)S(1)} collective-permute-done((bf16[128,3712]{1,0:T(8,128)(2,1)S(1)}, bf16[128,3712]{1,0:T(8,128)(2,1)S(1)}, u32[]{:S(2)}, u32[]{:S(2)}) %collective-permute-start) | collective-permute-done | bytes 950304 | tf_op jit(solution)/shard_map/ppermute | solution.py:265
  28.9 0.4 collective-permute-start.5
  29.3 1.6 %collective-permute-start.6 = (bf16[128,3712]{1,0:T(8,128)(2,1)S(1)}, bf16[128,3712]{1,0:T(8,128)(2,1)S(1)}, u32[]{:S(2)}, u32[]{:S(2)}) collective-permute-start(bf16[128,3712]{1,0:T(8,128)(2,1)S(1)} %collective-permute-done.1.refs_2_), channel_id=1, source_target_pairs={{4,0},{5,1},{8,4},{9,5},{12,8},{13,9},{14,12},{15,13},{10,14},{11,... | collective-permute-start | bytes 2850824 | tf_op jit(solution)/shard_map/ppermute | solution.py:265
  31.0 2.6 %absorb.5 = (f32[896,896]{1,0:T(8,128)S(1)}, bf16[256,896]{1,0:T(8,128)(2,1)S(1)}, bf16[256,896]{1,0:T(8,128)(2,1)S(1)}, bf16[32,3584]{1,0:T(8,128)(2,1)S(1)}, bf16[32,3584]{1,0:T(8,128)(2,1)S(1)}) custom-call(s32[5]{0:T(128)S(1)} %stack.23.refs_0_, bf16[128,3712]{1,0:T(8,128)(2,1)S(1)} %collective-permute-done.refs_1_, ...), custom_call_target="tpu_custom_call", output_to_operand_aliasing={{0}: (3, {})} | custom-call | flops 1 | bytes 1 | tf_op jit(solution)/shard_map/absorb/pallas_call | solution.py:122
  33.5 0.1 collective-permute-start.7
  33.6 0.5 collective-permute-start.9
  34.1 0.1 collective-permute-start.10
  34.2 0.9 collective-permute-done.7.refs_3_
  35.1 0.1 collective-permute-start.8
  35.2 1.5 %collective-permute-done.8.refs_4_ = bf16[32,3584]{1,0:T(8,128)(2,1)S(1)} collective-permute-done((bf16[32,3584]{1,0:T(8,128)(2,1)S(1)}, bf16[32,3584]{1,0:T(8,128)(2,1)S(1)}, u32[]{:S(2)}, u32[]{:S(2)}) %collective-permute-start.8) | collective-permute-done | bytes 229408 | tf_op jit(solution)/shard_map/ppermute | solution.py:262
  36.7 0.8 prepare_rows.5
  37.5 0.0 collective-permute-done.9.refs_4_
  37.5 0.0 collective-permute-done.10.refs_5_
  37.5 13.0 %collective-permute-done.5.refs_1_ = bf16[128,3712]{1,0:T(8,128)(2,1)S(1)} collective-permute-done((bf16[128,3712]{1,0:T(8,128)(2,1)S(1)}, bf16[128,3712]{1,0:T(8,128)(2,1)S(1)}, u32[]{:S(2)}, u32[]{:S(2)}) %collective-permute-start.5) | collective-permute-done | bytes 950304 | tf_op jit(solution)/shard_map/ppermute | solution.py:265
  50.5 0.4 collective-permute-done.6.refs_2_
  51.0 1.5 %collective-permute-start.11 = (bf16[128,3712]{1,0:T(8,128)(2,1)S(1)}, bf16[128,3712]{1,0:T(8,128)(2,1)S(1)}, u32[]{:S(2)}, u32[]{:S(2)}) collective-permute-start(bf16[128,3712]{1,0:T(8,128)(2,1)S(1)} %collective-permute-done.5.refs_1_), channel_id=1, source_target_pairs={{0,4},{1,5},{4,8},{5,9},{8,12},{9,13},{12,14},{13,15},{14,10},{15,... | collective-permute-start | bytes 2850824 | tf_op jit(solution)/shard_map/ppermute | solution.py:265
  52.5 0.5 collective-permute-start.12
  53.0 2.6 %absorb.6 = (f32[896,896]{1,0:T(8,128)S(1)}, bf16[256,896]{1,0:T(8,128)(2,1)S(1)}, bf16[256,896]{1,0:T(8,128)(2,1)S(1)}, bf16[32,3584]{1,0:T(8,128)(2,1)S(1)}, bf16[32,3584]{1,0:T(8,128)(2,1)S(1)}) custom-call(s32[5]{0:T(128)S(1)} %stack.23.refs_0_, bf16[128,3712]{1,0:T(8,128)(2,1)S(1)} %collective-permute-done.5.refs_1_, ...), custom_call_target="tpu_custom_call", output_to_operand_aliasing={{0}: (3, {})} | custom-call | flops 1 | bytes 1 | tf_op jit(solution)/shard_map/absorb/pallas_call | solution.py:122
  55.6 0.1 collective-permute-start.13
  55.7 0.5 collective-permute-start.15
  56.2 0.1 collective-permute-start.16
  56.2 0.9 collective-permute-done.13.refs_3_
  57.1 0.1 collective-permute-start.14
  57.3 1.5 %collective-permute-done.14.refs_4_ = bf16[32,3584]{1,0:T(8,128)(2,1)S(1)} collective-permute-done((bf16[32,3584]{1,0:T(8,128)(2,1)S(1)}, bf16[32,3584]{1,0:T(8,128)(2,1)S(1)}, u32[]{:S(2)}, u32[]{:S(2)}) %collective-permute-start.14) | collective-permute-done | bytes 229408 | tf_op jit(solution)/shard_map/ppermute | solution.py:262
  58.8 0.8 prepare_rows.6
  59.6 0.0 collective-permute-done.15.refs_4_
  59.6 0.0 collective-permute-done.16.refs_5_
  59.6 12.1 %collective-permute-done.11.refs_1_ = bf16[128,3712]{1,0:T(8,128)(2,1)S(1)} collective-permute-done((bf16[128,3712]{1,0:T(8,128)(2,1)S(1)}, bf16[128,3712]{1,0:T(8,128)(2,1)S(1)}, u32[]{:S(2)}, u32[]{:S(2)}) %collective-permute-start.11) | collective-permute-done | bytes 950304 | tf_op jit(solution)/shard_map/ppermute | solution.py:265
  71.7 1.1 %collective-permute-done.12.refs_2_ = bf16[128,3712]{1,0:T(8,128)(2,1)S(1)} collective-permute-done((bf16[128,3712]{1,0:T(8,128)(2,1)S(1)}, bf16[128,3712]{1,0:T(8,128)(2,1)S(1)}, u32[]{:S(2)}, u32[]{:S(2)}) %collective-permute-start.12) | collective-permute-done | bytes 950304 | tf_op jit(solution)/shard_map/ppermute | solution.py:265
  72.8 1.6 %collective-permute-start.17 = (bf16[64,3712]{1,0:T(8,128)(2,1)S(1)}, bf16[64,3712]{1,0:T(8,128)(2,1)S(1)}, u32[]{:S(2)}, u32[]{:S(2)}) collective-permute-start(bf16[64,3712]{1,0:T(8,128)(2,1)S(1)} %slice.6), channel_id=1, source_target_pairs={{0,4},{1,5},{4,8},{5,9},{8,12},{9,13},{12,14},{13,15},{14,10},{15,... | collective-permute-start | bytes 1425416 | tf_op jit(solution)/shard_map/ppermute | solution.py:265
  74.5 0.5 collective-permute-start.18
  74.9 2.6 %absorb.7 = (f32[896,896]{1,0:T(8,128)S(1)}, bf16[256,896]{1,0:T(8,128)(2,1)S(1)}, bf16[256,896]{1,0:T(8,128)(2,1)S(1)}, bf16[32,3584]{1,0:T(8,128)(2,1)S(1)}, bf16[32,3584]{1,0:T(8,128)(2,1)S(1)}) custom-call(s32[5]{0:T(128)S(1)} %stack.23.refs_0_, bf16[128,3712]{1,0:T(8,128)(2,1)S(1)} %collective-permute-done.11.refs_1_, ...), custom_call_target="tpu_custom_call", output_to_operand_aliasing={{0}: (3, {})} | custom-call | flops 1 | bytes 1 | tf_op jit(solution)/shard_map/absorb/pallas_call | solution.py:122
  77.5 0.1 collective-permute-start.19
  77.6 0.5 collective-permute-start.21
  78.1 0.1 collective-permute-start.22
  78.2 0.9 collective-permute-done.19.refs_3_
  79.1 0.1 collective-permute-start.20
  79.2 1.5 %collective-permute-done.20.refs_4_ = bf16[32,3584]{1,0:T(8,128)(2,1)S(1)} collective-permute-done((bf16[32,3584]{1,0:T(8,128)(2,1)S(1)}, bf16[32,3584]{1,0:T(8,128)(2,1)S(1)}, u32[]{:S(2)}, u32[]{:S(2)}) %collective-permute-start.20) | collective-permute-done | bytes 229408 | tf_op jit(solution)/shard_map/ppermute | solution.py:262
  80.7 0.8 prepare_rows.7
  81.5 0.0 collective-permute-done.21.refs_6_
  81.5 0.0 collective-permute-done.22.refs_7_
  81.6 0.5 collective-permute-done.17.refs_1_
  82.1 1.3 %collective-permute-done.18.refs_2_ = bf16[64,3712]{1,0:T(8,128)(2,1)S(1)} collective-permute-done((bf16[64,3712]{1,0:T(8,128)(2,1)S(1)}, bf16[64,3712]{1,0:T(8,128)(2,1)S(1)}, u32[]{:S(2)}, u32[]{:S(2)}) %collective-permute-start.18) | collective-permute-done | bytes 475168 | tf_op jit(solution)/shard_map/ppermute | solution.py:265
  83.4 0.0 collective-permute-start.23
  83.4 0.5 collective-permute-start.24
  83.9 1.3 %collective-permute-done.23.refs_3_ = bf16[64,3712]{1,0:T(8,128)(2,1)S(1)} collective-permute-done((bf16[64,3712]{1,0:T(8,128)(2,1)S(1)}, bf16[64,3712]{1,0:T(8,128)(2,1)S(1)}, u32[]{:S(2)}, u32[]{:S(2)}) %collective-permute-start.23) | collective-permute-done | bytes 475168 | tf_op jit(solution)/shard_map/ppermute | solution.py:262
  85.2 0.7 collective-permute-done.24.refs_4_
  85.9 12.7 %finish.1 = (f32[1792,3584]{1,0:T(8,128)}, f32[1,896,896]{2,1,0:T(8,128)}, bf16[512,3584]{1,0:T(8,128)(2,1)S(1)}, bf16[1792,512]{1,0:T(8,128)(2,1)S(1)}) custom-call(s32[5]{0:T(128)S(1)} %stack.23.refs_0_, bf16[64,3712]{1,0:T(8,128)(2,1)S(1)} %collective-permute-done.17.refs_1_, ...), custom_call_target="tpu_custom_call", output_to_operand_aliasing={{2}: (8, {}), {3}: (9, {})} | custom-call | flops 1 | bytes 1 | tf_op jit(solution)/shard_map/finish/pallas_call | solution.py:205
  (5 shorter events, 0.1 us)
Async XLA Ops:
  0.6 1.2 %copy-start = (bf16[128,3584]{1,0:T(8,128)(2,1)S(1)}, bf16[128,3584]{1,0:T(8,128)(2,1)}, u32[]{:S(2)}) copy-start(bf16[128,3584]{1,0:T(8,128)(2,1)} %tokens.1) | copy-start | bytes 2752516
  1.8 0.7 copy-start.1
  2.5 0.7 copy-start.2
  3.4 24.1 %collective-permute-start.1 = (bf16[128,3712]{1,0:T(8,128)(2,1)S(1)}, bf16[128,3712]{1,0:T(8,128)(2,1)S(1)}, u32[]{:S(2)}, u32[]{:S(2)}) collective-permute-start(bf16[128,3712]{1,0:T(8,128)(2,1)S(1)} %make_message.1.refs_1_), channel_id=1, source_target_pairs={{4,0},{5,1},{8,4},{9,5},{12,8},{13,9},{14,12},{15,13},{10,14},{11,... | collective-permute-start | bytes 2850824 | tf_op jit(solution)/shard_map/ppermute | solution.py:265
  6.4 22.5 %collective-permute-start = (bf16[128,3712]{1,0:T(8,128)(2,1)S(1)}, bf16[128,3712]{1,0:T(8,128)(2,1)S(1)}, u32[]{:S(2)}, u32[]{:S(2)}) collective-permute-start(bf16[128,3712]{1,0:T(8,128)(2,1)S(1)} %make_message.1.refs_1_), channel_id=1, source_target_pairs={{0,4},{1,5},{4,8},{5,9},{8,12},{9,13},{12,14},{13,15},{14,10},{15,... | collective-permute-start | bytes 2850824 | tf_op jit(solution)/shard_map/ppermute | solution.py:265
  8.1 1.6 %collective-permute-start.2 = (bf16[32,3584]{1,0:T(8,128)(2,1)S(1)}, bf16[32,3584]{1,0:T(8,128)(2,1)S(1)}, u32[]{:S(2)}, u32[]{:S(2)}) collective-permute-start(bf16[32,3584]{1,0:T(8,128)(2,1)S(1)} %get-tuple-element.59.refs_1_), channel_id=1, source_target_pairs={{0,1},{1,0},{2,3},{3,2},{4,5},{5,4},{6,7},{7,6},{8,9},{9,8},{10,11... | collective-permute-start | bytes 688136 | tf_op jit(solution)/shard_map/ppermute | solution.py:262
  8.2 2.2 %collective-permute-start.3 = (bf16[128,896]{1,0:T(8,128)(2,1)S(1)}, bf16[128,896]{1,0:T(8,128)(2,1)S(1)}, u32[]{:S(2)}, u32[]{:S(2)}) collective-permute-start(bf16[128,896]{1,0:T(8,128)(2,1)S(1)} %get-tuple-element.63), channel_id=1, source_target_pairs={{0,1},{1,0},{2,3},{3,2},{4,5},{5,4},{6,7},{7,6},{8,9},{9,8},{10,11... | collective-permute-start | bytes 688136 | tf_op jit(solution)/shard_map/ppermute | solution.py:262
  8.7 1.8 %collective-permute-start.4 = (bf16[128,896]{1,0:T(8,128)(2,1)S(1)}, bf16[128,896]{1,0:T(8,128)(2,1)S(1)}, u32[]{:S(2)}, u32[]{:S(2)}) collective-permute-start(bf16[128,896]{1,0:T(8,128)(2,1)S(1)} %get-tuple-element.64), channel_id=1, source_target_pairs={{0,1},{1,0},{2,3},{3,2},{4,5},{5,4},{6,7},{7,6},{8,9},{9,8},{10,11... | collective-permute-start | bytes 688136 | tf_op jit(solution)/shard_map/ppermute | solution.py:262
  28.9 21.6 %collective-permute-start.5 = (bf16[128,3712]{1,0:T(8,128)(2,1)S(1)}, bf16[128,3712]{1,0:T(8,128)(2,1)S(1)}, u32[]{:S(2)}, u32[]{:S(2)}) collective-permute-start(bf16[128,3712]{1,0:T(8,128)(2,1)S(1)} %collective-permute-done.refs_1_), channel_id=1, source_target_pairs={{0,4},{1,5},{4,8},{5,9},{8,12},{9,13},{12,14},{13,15},{14,10},{15,... | collective-permute-start | bytes 2850824 | tf_op jit(solution)/shard_map/ppermute | solution.py:265
  29.3 21.6 %collective-permute-start.6 = (bf16[128,3712]{1,0:T(8,128)(2,1)S(1)}, bf16[128,3712]{1,0:T(8,128)(2,1)S(1)}, u32[]{:S(2)}, u32[]{:S(2)}) collective-permute-start(bf16[128,3712]{1,0:T(8,128)(2,1)S(1)} %collective-permute-done.1.refs_2_), channel_id=1, source_target_pairs={{4,0},{5,1},{8,4},{9,5},{12,8},{13,9},{14,12},{15,13},{10,14},{11,... | collective-permute-start | bytes 2850824 | tf_op jit(solution)/shard_map/ppermute | solution.py:265
  33.5 1.6 %collective-permute-start.7 = (bf16[32,3584]{1,0:T(8,128)(2,1)S(1)}, bf16[32,3584]{1,0:T(8,128)(2,1)S(1)}, u32[]{:S(2)}, u32[]{:S(2)}) collective-permute-start(bf16[32,3584]{1,0:T(8,128)(2,1)S(1)} %get-tuple-element.70.refs_1_), channel_id=1, source_target_pairs={{0,1},{1,0},{2,3},{3,2},{4,5},{5,4},{6,7},{7,6},{8,9},{9,8},{10,11... | collective-permute-start | bytes 688136 | tf_op jit(solution)/shard_map/ppermute | solution.py:262
  33.6 3.9 %collective-permute-start.9 = (bf16[256,896]{1,0:T(8,128)(2,1)S(1)}, bf16[256,896]{1,0:T(8,128)(2,1)S(1)}, u32[]{:S(2)}, u32[]{:S(2)}) collective-permute-start(bf16[256,896]{1,0:T(8,128)(2,1)S(1)} %get-tuple-element.77), channel_id=1, source_target_pairs={{0,1},{1,0},{2,3},{3,2},{4,5},{5,4},{6,7},{7,6},{8,9},{9,8},{10,11... | collective-permute-start | bytes 1376264 | tf_op jit(solution)/shard_map/ppermute | solution.py:262
  34.1 3.5 %collective-permute-start.10 = (bf16[256,896]{1,0:T(8,128)(2,1)S(1)}, bf16[256,896]{1,0:T(8,128)(2,1)S(1)}, u32[]{:S(2)}, u32[]{:S(2)}) collective-permute-start(bf16[256,896]{1,0:T(8,128)(2,1)S(1)} %get-tuple-element.78), channel_id=1, source_target_pairs={{0,1},{1,0},{2,3},{3,2},{4,5},{5,4},{6,7},{7,6},{8,9},{9,8},{10,11... | collective-permute-start | bytes 1376264 | tf_op jit(solution)/shard_map/ppermute | solution.py:262
  35.1 1.6 %collective-permute-start.8 = (bf16[32,3584]{1,0:T(8,128)(2,1)S(1)}, bf16[32,3584]{1,0:T(8,128)(2,1)S(1)}, u32[]{:S(2)}, u32[]{:S(2)}) collective-permute-start(bf16[32,3584]{1,0:T(8,128)(2,1)S(1)} %get-tuple-element.71.refs_2_), channel_id=1, source_target_pairs={{0,1},{1,0},{2,3},{3,2},{4,5},{5,4},{6,7},{7,6},{8,9},{9,8},{10,11... | collective-permute-start | bytes 688136 | tf_op jit(solution)/shard_map/ppermute | solution.py:262
  51.0 20.7 %collective-permute-start.11 = (bf16[128,3712]{1,0:T(8,128)(2,1)S(1)}, bf16[128,3712]{1,0:T(8,128)(2,1)S(1)}, u32[]{:S(2)}, u32[]{:S(2)}) collective-permute-start(bf16[128,3712]{1,0:T(8,128)(2,1)S(1)} %collective-permute-done.5.refs_1_), channel_id=1, source_target_pairs={{0,4},{1,5},{4,8},{5,9},{8,12},{9,13},{12,14},{13,15},{14,10},{15,... | collective-permute-start | bytes 2850824 | tf_op jit(solution)/shard_map/ppermute | solution.py:265
  52.5 20.3 %collective-permute-start.12 = (bf16[128,3712]{1,0:T(8,128)(2,1)S(1)}, bf16[128,3712]{1,0:T(8,128)(2,1)S(1)}, u32[]{:S(2)}, u32[]{:S(2)}) collective-permute-start(bf16[128,3712]{1,0:T(8,128)(2,1)S(1)} %collective-permute-done.6.refs_2_), channel_id=1, source_target_pairs={{4,0},{5,1},{8,4},{9,5},{12,8},{13,9},{14,12},{15,13},{10,14},{11,... | collective-permute-start | bytes 2850824 | tf_op jit(solution)/shard_map/ppermute | solution.py:265
  55.6 1.6 %collective-permute-start.13 = (bf16[32,3584]{1,0:T(8,128)(2,1)S(1)}, bf16[32,3584]{1,0:T(8,128)(2,1)S(1)}, u32[]{:S(2)}, u32[]{:S(2)}) collective-permute-start(bf16[32,3584]{1,0:T(8,128)(2,1)S(1)} %get-tuple-element.84.refs_1_), channel_id=1, source_target_pairs={{0,1},{1,0},{2,3},{3,2},{4,5},{5,4},{6,7},{7,6},{8,9},{9,8},{10,11... | collective-permute-start | bytes 688136 | tf_op jit(solution)/shard_map/ppermute | solution.py:262
  55.7 3.9 %collective-permute-start.15 = (bf16[256,896]{1,0:T(8,128)(2,1)S(1)}, bf16[256,896]{1,0:T(8,128)(2,1)S(1)}, u32[]{:S(2)}, u32[]{:S(2)}) collective-permute-start(bf16[256,896]{1,0:T(8,128)(2,1)S(1)} %get-tuple-element.91), channel_id=1, source_target_pairs={{0,1},{1,0},{2,3},{3,2},{4,5},{5,4},{6,7},{7,6},{8,9},{9,8},{10,11... | collective-permute-start | bytes 1376264 | tf_op jit(solution)/shard_map/ppermute | solution.py:262
  56.2 3.5 %collective-permute-start.16 = (bf16[256,896]{1,0:T(8,128)(2,1)S(1)}, bf16[256,896]{1,0:T(8,128)(2,1)S(1)}, u32[]{:S(2)}, u32[]{:S(2)}) collective-permute-start(bf16[256,896]{1,0:T(8,128)(2,1)S(1)} %get-tuple-element.92), channel_id=1, source_target_pairs={{0,1},{1,0},{2,3},{3,2},{4,5},{5,4},{6,7},{7,6},{8,9},{9,8},{10,11... | collective-permute-start | bytes 1376264 | tf_op jit(solution)/shard_map/ppermute | solution.py:262
  57.1 1.6 %collective-permute-start.14 = (bf16[32,3584]{1,0:T(8,128)(2,1)S(1)}, bf16[32,3584]{1,0:T(8,128)(2,1)S(1)}, u32[]{:S(2)}, u32[]{:S(2)}) collective-permute-start(bf16[32,3584]{1,0:T(8,128)(2,1)S(1)} %get-tuple-element.85.refs_2_), channel_id=1, source_target_pairs={{0,1},{1,0},{2,3},{3,2},{4,5},{5,4},{6,7},{7,6},{8,9},{9,8},{10,11... | collective-permute-start | bytes 688136 | tf_op jit(solution)/shard_map/ppermute | solution.py:262
  72.8 9.2 %collective-permute-start.17 = (bf16[64,3712]{1,0:T(8,128)(2,1)S(1)}, bf16[64,3712]{1,0:T(8,128)(2,1)S(1)}, u32[]{:S(2)}, u32[]{:S(2)}) collective-permute-start(bf16[64,3712]{1,0:T(8,128)(2,1)S(1)} %slice.6), channel_id=1, source_target_pairs={{0,4},{1,5},{4,8},{5,9},{8,12},{9,13},{12,14},{13,15},{14,10},{15,... | collective-permute-start | bytes 1425416 | tf_op jit(solution)/shard_map/ppermute | solution.py:265
  74.5 8.9 %collective-permute-start.18 = (bf16[64,3712]{1,0:T(8,128)(2,1)S(1)}, bf16[64,3712]{1,0:T(8,128)(2,1)S(1)}, u32[]{:S(2)}, u32[]{:S(2)}) collective-permute-start(bf16[64,3712]{1,0:T(8,128)(2,1)S(1)} %slice.7), channel_id=1, source_target_pairs={{4,0},{5,1},{8,4},{9,5},{12,8},{13,9},{14,12},{15,13},{10,14},{11,... | collective-permute-start | bytes 1425416 | tf_op jit(solution)/shard_map/ppermute | solution.py:265
  77.5 1.6 %collective-permute-start.19 = (bf16[32,3584]{1,0:T(8,128)(2,1)S(1)}, bf16[32,3584]{1,0:T(8,128)(2,1)S(1)}, u32[]{:S(2)}, u32[]{:S(2)}) collective-permute-start(bf16[32,3584]{1,0:T(8,128)(2,1)S(1)} %get-tuple-element.98.refs_1_), channel_id=1, source_target_pairs={{0,1},{1,0},{2,3},{3,2},{4,5},{5,4},{6,7},{7,6},{8,9},{9,8},{10,11... | collective-permute-start | bytes 688136 | tf_op jit(solution)/shard_map/ppermute | solution.py:262
  77.6 3.9 %collective-permute-start.21 = (bf16[256,896]{1,0:T(8,128)(2,1)S(1)}, bf16[256,896]{1,0:T(8,128)(2,1)S(1)}, u32[]{:S(2)}, u32[]{:S(2)}) collective-permute-start(bf16[256,896]{1,0:T(8,128)(2,1)S(1)} %get-tuple-element.105), channel_id=1, source_target_pairs={{0,1},{1,0},{2,3},{3,2},{4,5},{5,4},{6,7},{7,6},{8,9},{9,8},{10,11... | collective-permute-start | bytes 1376264 | tf_op jit(solution)/shard_map/ppermute | solution.py:262
  78.1 3.5 %collective-permute-start.22 = (bf16[256,896]{1,0:T(8,128)(2,1)S(1)}, bf16[256,896]{1,0:T(8,128)(2,1)S(1)}, u32[]{:S(2)}, u32[]{:S(2)}) collective-permute-start(bf16[256,896]{1,0:T(8,128)(2,1)S(1)} %get-tuple-element.106), channel_id=1, source_target_pairs={{0,1},{1,0},{2,3},{3,2},{4,5},{5,4},{6,7},{7,6},{8,9},{9,8},{10,11... | collective-permute-start | bytes 1376264 | tf_op jit(solution)/shard_map/ppermute | solution.py:262
  79.1 1.6 %collective-permute-start.20 = (bf16[32,3584]{1,0:T(8,128)(2,1)S(1)}, bf16[32,3584]{1,0:T(8,128)(2,1)S(1)}, u32[]{:S(2)}, u32[]{:S(2)}) collective-permute-start(bf16[32,3584]{1,0:T(8,128)(2,1)S(1)} %get-tuple-element.99.refs_2_), channel_id=1, source_target_pairs={{0,1},{1,0},{2,3},{3,2},{4,5},{5,4},{6,7},{7,6},{8,9},{9,8},{10,11... | collective-permute-start | bytes 688136 | tf_op jit(solution)/shard_map/ppermute | solution.py:262
  83.4 1.8 %collective-permute-start.23 = (bf16[64,3712]{1,0:T(8,128)(2,1)S(1)}, bf16[64,3712]{1,0:T(8,128)(2,1)S(1)}, u32[]{:S(2)}, u32[]{:S(2)}) collective-permute-start(bf16[64,3712]{1,0:T(8,128)(2,1)S(1)} %collective-permute-done.17.refs_1_), channel_id=1, source_target_pairs={{0,1},{1,0},{2,3},{3,2},{4,5},{5,4},{6,7},{7,6},{8,9},{9,8},{10,11... | collective-permute-start | bytes 1425416 | tf_op jit(solution)/shard_map/ppermute | solution.py:262
  83.4 2.5 %collective-permute-start.24 = (bf16[64,3712]{1,0:T(8,128)(2,1)S(1)}, bf16[64,3712]{1,0:T(8,128)(2,1)S(1)}, u32[]{:S(2)}, u32[]{:S(2)}) collective-permute-start(bf16[64,3712]{1,0:T(8,128)(2,1)S(1)} %collective-permute-done.18.refs_2_), channel_id=1, source_target_pairs={{0,1},{1,0},{2,3},{3,2},{4,5},{5,4},{6,7},{7,6},{8,9},{9,8},{10,11... | collective-permute-start | bytes 1425416 | tf_op jit(solution)/shard_map/ppermute | solution.py:262

commit v11 on v10

--- a/solution.py
+++ b/solution.py
@@ -168,36 +168,65 @@
     )(scalars, *packs, *operands)
 
 
+def take_in(scalars, halves, at, rows, across, left, right):
+    piece = jnp.concatenate([half[...] for half in halves], axis=0)
+    place_rows(scalars[4], pack(scalars[0], piece), at, rows, across)
+    fetch_tile(scalars[1], halves, left)
+    fetch_tile(scalars[2], halves, right)
+    return product(left, right)
+
+
+def take_own_kernel(*refs):
+    scalars, halves, before, refs = refs[0], refs[1:3], refs[3:6], refs[8:]
+    tile, rows, across, left, right = refs
+    update = before[0][...] + product(before[1], before[2])
+    at = rows.shape[0] - 2 * CAP
+    tile[...] = update + take_in(scalars, halves, at, rows, across, left, right)
+
+
+def take_own(scalars, halves, sums, operands):
+    edge = sums[0].shape[0]
+    count = sum(half.shape[0] for half in halves)
+    return pl.pallas_call(
+        take_own_kernel,
+        out_shape=[jax.ShapeDtypeStruct(a.shape, a.dtype) for a in (sums[0], *operands)],
+        in_specs=[SMEM] + [VMEM] * 7,
+        out_specs=[VMEM] * 3,
+        scratch_shapes=[pltpu.VMEM((count, edge), BF16)] * 2,
+        input_output_aliases={3: 0, 6: 1, 7: 2},
+        cost_estimate=SMALL,
+        compiler_params=params(14),
+        name="take_own",
+    )(scalars, *halves, *sums, *operands)
+
+
 def finish_kernel(final, *refs):
-    scalars, halves, refs = refs[0], refs[1:5], refs[5:]
-    before, (hessian, tile, rows, across, *scratch) = refs[:3], refs[5:]
+    scalars, halves, before, (hessian, tile, rows, across, *scratch) = (
+        refs[0], refs[1:3], refs[3], refs[6:]
+    )
     staging, sums, left, right, sent = scratch
-    pieces = [
-        jnp.concatenate([halves[k][...], halves[k + 1][...]], axis=0) for k in range(0, 4, 2)
-    ]
-    packed = jnp.concatenate([pack(scalars[0], piece) for piece in pieces], axis=0)
-    place_rows(scalars[4], packed, rows.shape[0] - packed.shape[0], rows, across)
+    at = rows.shape[0] - CAP
     copies = []
+
+    def write(source, target):
+        copies.append(pltpu.make_async_copy(source, target, sent.at[len(copies)]))
+        copies[-1].start()
+
+    update = take_in(scalars, halves, at, rows, across, left, right)
+    sums[...] = (before[...] + update) * final
+    write(sums, tile.at[0])
     for n in range(staging.shape[0]):
         span = slice(n * STEP, (n + 1) * STEP)
         staging[n, :, :] = (
             jnp.dot(across[...], rows[:, span], preferred_element_type=F32) * INVERSE
         )
-        copies.append(pltpu.make_async_copy(staging.at[n], hessian.at[:, span], sent.at[n]))
-        copies[-1].start()
-    fetch_tile(scalars[1], halves, left)
-    fetch_tile(scalars[2], halves, right)
-    sums[...] = (
-        before[0][...] + product(before[1], before[2]) + product(left, right)
-    ) * final
-    copies.append(pltpu.make_async_copy(sums, tile.at[0], sent.at[len(copies)]))
-    copies[-1].start()
+        write(staging.at[n], hessian.at[:, span])
     for copy in copies:
         copy.wait()
 
 
 def finish(scalars, halves, before, operands, final):
-    edge = before[0].shape[0]
+    edge = before.shape[0]
     rows, across = operands
     slab, width = across.shape[0], rows.shape[1]
     count = sum(half.shape[0] for half in halves)
@@ -210,7 +239,7 @@
             jax.ShapeDtypeStruct(rows.shape, BF16),
             jax.ShapeDtypeStruct(across.shape, BF16),
         ],
-        in_specs=[SMEM] + [VMEM] * 9,
+        in_specs=[SMEM] + [VMEM] * 5,
         out_specs=[ANY, ANY, VMEM, VMEM],
         scratch_shapes=[
             pltpu.VMEM((blocks, slab, STEP), F32),
@@ -219,11 +248,11 @@
             pltpu.VMEM((count, edge), BF16),
             pltpu.SemaphoreType.DMA((blocks + 1,)),
         ],
-        input_output_aliases={8: 2, 9: 3},
+        input_output_aliases={4: 2, 5: 3},
         cost_estimate=SMALL,
         compiler_params=params(38),
         name="finish",
-    )(scalars, *halves, *before, rows, across)[:2]
+    )(scalars, *halves, before, rows, across)[:2]
 
 
 def ring_of(chips):
@@ -281,11 +310,14 @@
         packs = list(packed) + [swap(array) for array in packed]
         operands = prepare(scalars, packs, at, operands, total, slab)
         if step < rounds:
-            moved, operands, sums = lax.optimization_barrier((moved, operands, sums))
+            ahead_of, operands, sums = lax.optimization_barrier((moved[0], operands, sums))
+            back_of, operands, sums = lax.optimization_barrier((moved[1], operands, sums))
+            moved = [ahead_of, back_of]
         pieces = moved
     pieces, operands, sums = lax.optimization_barrier((pieces, operands, sums))
     others = [swap(piece) for piece in pieces]
-    return tuple(finish(scalars, pieces + others, sums, operands, 1.0 / (devices * tok_rows)))
+    tile, *operands = take_own(scalars, pieces, sums, operands)
+    return tuple(finish(scalars, others, tile, operands, 1.0 / (devices * tok_rows)))
 
 
 def solution(mesh):

time: 98.9 us -> 98.4 us (level)
  waiting for transfers between devices: 57 us -> 54.6 us
  Pallas kernels: 25.3 us -> 27.2 us
    pallas_call x0 -> x1, Pallas kernels: none -> 2.77 us  [take_own(): pl.pallas_call(take_own_kernel, out_shape=[jax.ShapeDtypeStruct(a.shape,...]
    ppermute x17, waiting for transfers between devices: 10.1 us -> 8.13 us  [swap(): return lax.ppermute(array, 'tok', pair)]
  transfers between devices with their start and end apart: 25 -> 25, of which waited for: 17 -> 13; matrix products, arithmetic and copies ran while one was open for 0% -> 0% of each run, Pallas kernels for 13% -> 15%
where the time goes in v11:
time: 98.4 us; the launch traced here: 98.2 us
  waiting for transfers between devices  54.6 us (55%)
  Pallas kernels  27.2 us (28%)
  starting transfers between devices  12.7 us (13%)
  local copies, waits for them, and re-layouts  2.7 us (3%)
  between operations  1 us (1%)
    ppermute x8, waiting for transfers between devices, advance(): lax.ppermute(array, 'tok', stream)  46.5 us
    pallas_call x1, Pallas kernels, finish(): pl.pallas_call(functools.partial(finish_kernel, final), out_shape=[jax.Sh...  11.8 us
    ppermute x8, starting transfers between devices, advance(): lax.ppermute(array, 'tok', stream)  9.21 us
    pallas_call x4, Pallas kernels, absorb(): pl.pallas_call(functools.partial(absorb_kernel, count, bool(before)), out...  9.2 us
    ppermute x17, waiting for transfers between devices, swap(): return lax.ppermute(array, 'tok', pair)  8.13 us
    ppermute x17, starting transfers between devices, swap(): return lax.ppermute(array, 'tok', pair)  3.5 us
    pallas_call x4, Pallas kernels, prepare(): pl.pallas_call(functools.partial(prepare_kernel, len(packs), at), out_sha...  3.21 us
    pallas_call x1, Pallas kernels, take_own(): pl.pallas_call(take_own_kernel, out_shape=[jax.ShapeDtypeStruct(a.shape,...  2.77 us
  transfers between devices with their start and end apart: 25, of which 13 were waited for; matrix products, arithmetic and copies ran while one was open for 0% of the time, Pallas kernels for 15%

profile of v11, /device:TPU:0, one launch (start us, length us, event | category | flops | bytes accessed | tf_op | source)
XLA Modules:
  0.0 98.2 jit_solution(1280566675205626321)
XLA Ops:
  0.6 1.2 %copy-done = bf16[128,3584]{1,0:T(8,128)(2,1)S(1)} copy-done((bf16[128,3584]{1,0:T(8,128)(2,1)S(1)}, bf16[128,3584]{1,0:T(8,128)(2,1)}, u32[]{:S(2)}) %copy-start) | copy-done | bytes 917528
  1.8 0.7 copy-done.1
  2.5 0.7 copy-done.2
  3.2 0.2 make_message.1.refs_1_
  3.4 3.1 %collective-permute-start = (bf16[128,3712]{1,0:T(8,128)(2,1)S(1)}, bf16[128,3712]{1,0:T(8,128)(2,1)S(1)}, u32[]{:S(2)}, u32[]{:S(2)}) collective-permute-start(bf16[128,3712]{1,0:T(8,128)(2,1)S(1)} %make_message.1.refs_1_), channel_id=1, source_target_pairs={{0,4},{1,5},{4,8},{5,9},{8,12},{9,13},{12,14},{13,15},{14,10},{15,... | collective-permute-start | bytes 2850824 | tf_op jit(solution)/shard_map/ppermute | solution.py:294
  6.5 0.0 collective-permute-start.5
  6.5 0.1 stack.23.refs_0_
  6.6 1.5 %absorb.4 = (f32[896,896]{1,0:T(8,128)S(1)}, bf16[128,896]{1,0:T(8,128)(2,1)S(1)}, bf16[128,896]{1,0:T(8,128)(2,1)S(1)}, bf16[32,3584]{1,0:T(8,128)(2,1)S(1)}) custom-call(s32[5]{0:T(128)S(1)} %stack.23.refs_0_, bf16[128,3712]{1,0:T(8,128)(2,1)S(1)} %make_message.1.refs_1_), custom_call_target="tpu_custom_call" | custom-call | flops 1 | bytes 1 | tf_op jit(solution)/shard_map/absorb/pallas_call | solution.py:122
  8.0 0.1 collective-permute-start.1
  8.1 0.5 collective-permute-start.2
  8.6 0.1 collective-permute-start.3
  8.7 0.9 collective-permute-done.1.refs_2_
  9.6 0.8 prepare_rows.4
  10.4 0.0 collective-permute-done.2.refs_4_
  10.4 0.0 collective-permute-done.3.refs_5_
  10.4 17.1 %collective-permute-done.refs_1_ = bf16[128,3712]{1,0:T(8,128)(2,1)S(1)} collective-permute-done((bf16[128,3712]{1,0:T(8,128)(2,1)S(1)}, bf16[128,3712]{1,0:T(8,128)(2,1)S(1)}, u32[]{:S(2)}, u32[]{:S(2)}) %collective-permute-start) | collective-permute-done | bytes 950304 | tf_op jit(solution)/shard_map/ppermute | solution.py:294
  27.5 1.8 %collective-permute-start.4 = (bf16[128,3712]{1,0:T(8,128)(2,1)S(1)}, bf16[128,3712]{1,0:T(8,128)(2,1)S(1)}, u32[]{:S(2)}, u32[]{:S(2)}) collective-permute-start(bf16[128,3712]{1,0:T(8,128)(2,1)S(1)} %collective-permute-done.refs_1_), channel_id=1, source_target_pairs={{0,4},{1,5},{4,8},{5,9},{8,12},{9,13},{12,14},{13,15},{14,10},{15,... | collective-permute-start | bytes 2850824 | tf_op jit(solution)/shard_map/ppermute | solution.py:294
  29.3 0.0 collective-permute-done.5.refs_2_
  29.3 0.2 collective-permute-start.11
  29.5 2.6 %absorb.5 = (f32[896,896]{1,0:T(8,128)S(1)}, bf16[256,896]{1,0:T(8,128)(2,1)S(1)}, bf16[256,896]{1,0:T(8,128)(2,1)S(1)}, bf16[32,3584]{1,0:T(8,128)(2,1)S(1)}, bf16[32,3584]{1,0:T(8,128)(2,1)S(1)}) custom-call(s32[5]{0:T(128)S(1)} %stack.23.refs_0_, bf16[128,3712]{1,0:T(8,128)(2,1)S(1)} %collective-permute-done.refs_1_, ...), custom_call_target="tpu_custom_call", output_to_operand_aliasing={{0}: (3, {})} | custom-call | flops 1 | bytes 1 | tf_op jit(solution)/shard_map/absorb/pallas_call | solution.py:122
  32.1 0.1 collective-permute-start.6
  32.1 0.5 collective-permute-start.8
  32.6 0.1 collective-permute-start.9
  32.7 0.9 collective-permute-done.6.refs_3_
  33.6 0.1 collective-permute-start.7
  33.7 1.5 %collective-permute-done.7.refs_4_ = bf16[32,3584]{1,0:T(8,128)(2,1)S(1)} collective-permute-done((bf16[32,3584]{1,0:T(8,128)(2,1)S(1)}, bf16[32,3584]{1,0:T(8,128)(2,1)S(1)}, u32[]{:S(2)}, u32[]{:S(2)}) %collective-permute-start.7) | collective-permute-done | bytes 229408 | tf_op jit(solution)/shard_map/ppermute | solution.py:291
  35.2 0.8 prepare_rows.5
  36.1 0.0 collective-permute-done.8.refs_4_
  36.1 0.0 collective-permute-done.9.refs_5_
  36.1 13.6 %collective-permute-done.4.refs_1_ = bf16[128,3712]{1,0:T(8,128)(2,1)S(1)} collective-permute-done((bf16[128,3712]{1,0:T(8,128)(2,1)S(1)}, bf16[128,3712]{1,0:T(8,128)(2,1)S(1)}, u32[]{:S(2)}, u32[]{:S(2)}) %collective-permute-start.4) | collective-permute-done | bytes 950304 | tf_op jit(solution)/shard_map/ppermute | solution.py:294
  49.7 1.5 %collective-permute-start.10 = (bf16[128,3712]{1,0:T(8,128)(2,1)S(1)}, bf16[128,3712]{1,0:T(8,128)(2,1)S(1)}, u32[]{:S(2)}, u32[]{:S(2)}) collective-permute-start(bf16[128,3712]{1,0:T(8,128)(2,1)S(1)} %collective-permute-done.4.refs_1_), channel_id=1, source_target_pairs={{0,4},{1,5},{4,8},{5,9},{8,12},{9,13},{12,14},{13,15},{14,10},{15,... | collective-permute-start | bytes 2850824 | tf_op jit(solution)/shard_map/ppermute | solution.py:294
  51.2 0.0 collective-permute-done.11.refs_2_
  51.2 0.5 collective-permute-start.17
  51.7 2.6 %absorb.6 = (f32[896,896]{1,0:T(8,128)S(1)}, bf16[256,896]{1,0:T(8,128)(2,1)S(1)}, bf16[256,896]{1,0:T(8,128)(2,1)S(1)}, bf16[32,3584]{1,0:T(8,128)(2,1)S(1)}, bf16[32,3584]{1,0:T(8,128)(2,1)S(1)}) custom-call(s32[5]{0:T(128)S(1)} %stack.23.refs_0_, bf16[128,3712]{1,0:T(8,128)(2,1)S(1)} %collective-permute-done.4.refs_1_, ...), custom_call_target="tpu_custom_call", output_to_operand_aliasing={{0}: (3, {})} | custom-call | flops 1 | bytes 1 | tf_op jit(solution)/shard_map/absorb/pallas_call | solution.py:122
  54.3 0.1 collective-permute-start.12
  54.4 0.5 collective-permute-start.14
  54.9 0.1 collective-permute-start.15
  55.0 0.9 collective-permute-done.12.refs_3_
  55.9 0.1 collective-permute-start.13
  56.0 1.5 %collective-permute-done.13.refs_4_ = bf16[32,3584]{1,0:T(8,128)(2,1)S(1)} collective-permute-done((bf16[32,3584]{1,0:T(8,128)(2,1)S(1)}, bf16[32,3584]{1,0:T(8,128)(2,1)S(1)}, u32[]{:S(2)}, u32[]{:S(2)}) %collective-permute-start.13) | collective-permute-done | bytes 229408 | tf_op jit(solution)/shard_map/ppermute | solution.py:291
  57.5 0.8 prepare_rows.6
  58.3 0.0 collective-permute-done.14.refs_4_
  58.4 0.0 collective-permute-done.15.refs_5_
  58.4 12.7 %collective-permute-done.10.refs_1_ = bf16[128,3712]{1,0:T(8,128)(2,1)S(1)} collective-permute-done((bf16[128,3712]{1,0:T(8,128)(2,1)S(1)}, bf16[128,3712]{1,0:T(8,128)(2,1)S(1)}, u32[]{:S(2)}, u32[]{:S(2)}) %collective-permute-start.10) | collective-permute-done | bytes 950304 | tf_op jit(solution)/shard_map/ppermute | solution.py:294
  71.0 0.9 collective-permute-done.17.refs_2_
  72.0 1.6 %collective-permute-start.16 = (bf16[64,3712]{1,0:T(8,128)(2,1)S(1)}, bf16[64,3712]{1,0:T(8,128)(2,1)S(1)}, u32[]{:S(2)}, u32[]{:S(2)}) collective-permute-start(bf16[64,3712]{1,0:T(8,128)(2,1)S(1)} %slice.6), channel_id=1, source_target_pairs={{0,4},{1,5},{4,8},{5,9},{8,12},{9,13},{12,14},{13,15},{14,10},{15,... | collective-permute-start | bytes 1425416 | tf_op jit(solution)/shard_map/ppermute | solution.py:294
  73.6 0.4 collective-permute-start.18
  74.1 2.6 %absorb.7 = (f32[896,896]{1,0:T(8,128)S(1)}, bf16[256,896]{1,0:T(8,128)(2,1)S(1)}, bf16[256,896]{1,0:T(8,128)(2,1)S(1)}, bf16[32,3584]{1,0:T(8,128)(2,1)S(1)}, bf16[32,3584]{1,0:T(8,128)(2,1)S(1)}) custom-call(s32[5]{0:T(128)S(1)} %stack.23.refs_0_, bf16[128,3712]{1,0:T(8,128)(2,1)S(1)} %collective-permute-done.10.refs_1_, ...), custom_call_target="tpu_custom_call", output_to_operand_aliasing={{0}: (3, {})} | custom-call | flops 1 | bytes 1 | tf_op jit(solution)/shard_map/absorb/pallas_call | solution.py:122
  76.7 0.1 collective-permute-start.19
  76.7 0.5 collective-permute-start.21
  77.2 0.1 collective-permute-start.22
  77.3 0.9 collective-permute-done.19.refs_3_
  78.2 0.1 collective-permute-start.20
  78.4 1.5 %collective-permute-done.20.refs_4_ = bf16[32,3584]{1,0:T(8,128)(2,1)S(1)} collective-permute-done((bf16[32,3584]{1,0:T(8,128)(2,1)S(1)}, bf16[32,3584]{1,0:T(8,128)(2,1)S(1)}, u32[]{:S(2)}, u32[]{:S(2)}) %collective-permute-start.20) | collective-permute-done | bytes 229408 | tf_op jit(solution)/shard_map/ppermute | solution.py:291
  79.9 0.8 prepare_rows.7
  80.7 0.0 collective-permute-done.21.refs_4_
  80.7 1.0 collective-permute-done.16.refs_1_
  81.7 1.3 %collective-permute-done.18.refs_2_ = bf16[64,3712]{1,0:T(8,128)(2,1)S(1)} collective-permute-done((bf16[64,3712]{1,0:T(8,128)(2,1)S(1)}, bf16[64,3712]{1,0:T(8,128)(2,1)S(1)}, u32[]{:S(2)}, u32[]{:S(2)}) %collective-permute-start.18) | collective-permute-done | bytes 475168 | tf_op jit(solution)/shard_map/ppermute | solution.py:294
  83.0 0.0 collective-permute-start.23
  83.0 0.5 collective-permute-start.24
  83.5 2.8 %take_own.1 = (f32[896,896]{1,0:T(8,128)S(1)}, bf16[512,3584]{1,0:T(8,128)(2,1)S(1)}, bf16[1792,512]{1,0:T(8,128)(2,1)S(1)}) custom-call(s32[5]{0:T(128)S(1)} %stack.23.refs_0_, bf16[64,3712]{1,0:T(8,128)(2,1)S(1)} %collective-permute-done.16.refs_1_, ...), custom_call_target="tpu_custom_call", output_to_operand_aliasing={{0}: (3, {}), {1}: (6, {}), {2}: (7, {})} | custom-call | flops 1 | bytes 1 | tf_op jit(solution)/shard_map/take_own/pallas_call | solution.py:190
  86.2 0.0 collective-permute-done.23.refs_1_
  86.3 0.0 collective-permute-done.24.refs_2_
  86.3 11.8 %finish.1 = (f32[1792,3584]{1,0:T(8,128)}, f32[1,896,896]{2,1,0:T(8,128)}, bf16[512,3584]{1,0:T(8,128)(2,1)S(1)}, bf16[1792,512]{1,0:T(8,128)(2,1)S(1)}) custom-call(s32[5]{0:T(128)S(1)} %stack.23.refs_0_, bf16[64,3712]{1,0:T(8,128)(2,1)S(1)} %collective-permute-done.23.refs_1_, ...), custom_call_target="tpu_custom_call", output_to_operand_aliasing={{2}: (4, {}), {3}: (5, {})} | custom-call | flops 1 | bytes 1 | tf_op jit(solution)/shard_map/finish/pallas_call | solution.py:234
  (6 shorter events, 0.1 us)
Async XLA Ops:
  0.6 1.2 %copy-start = (bf16[128,3584]{1,0:T(8,128)(2,1)S(1)}, bf16[128,3584]{1,0:T(8,128)(2,1)}, u32[]{:S(2)}) copy-start(bf16[128,3584]{1,0:T(8,128)(2,1)} %tokens.1) | copy-start | bytes 2752516
  1.8 0.7 copy-start.1
  2.5 0.7 copy-start.2
  3.4 24.1 %collective-permute-start = (bf16[128,3712]{1,0:T(8,128)(2,1)S(1)}, bf16[128,3712]{1,0:T(8,128)(2,1)S(1)}, u32[]{:S(2)}, u32[]{:S(2)}) collective-permute-start(bf16[128,3712]{1,0:T(8,128)(2,1)S(1)} %make_message.1.refs_1_), channel_id=1, source_target_pairs={{0,4},{1,5},{4,8},{5,9},{8,12},{9,13},{12,14},{13,15},{14,10},{15,... | collective-permute-start | bytes 2850824 | tf_op jit(solution)/shard_map/ppermute | solution.py:294
  6.5 22.8 %collective-permute-start.5 = (bf16[128,3712]{1,0:T(8,128)(2,1)S(1)}, bf16[128,3712]{1,0:T(8,128)(2,1)S(1)}, u32[]{:S(2)}, u32[]{:S(2)}) collective-permute-start(bf16[128,3712]{1,0:T(8,128)(2,1)S(1)} %make_message.1.refs_1_), channel_id=1, source_target_pairs={{4,0},{5,1},{8,4},{9,5},{12,8},{13,9},{14,12},{15,13},{10,14},{11,... | collective-permute-start | bytes 2850824 | tf_op jit(solution)/shard_map/ppermute | solution.py:294
  8.0 1.6 %collective-permute-start.1 = (bf16[32,3584]{1,0:T(8,128)(2,1)S(1)}, bf16[32,3584]{1,0:T(8,128)(2,1)S(1)}, u32[]{:S(2)}, u32[]{:S(2)}) collective-permute-start(bf16[32,3584]{1,0:T(8,128)(2,1)S(1)} %get-tuple-element.77.refs_1_), channel_id=1, source_target_pairs={{0,1},{1,0},{2,3},{3,2},{4,5},{5,4},{6,7},{7,6},{8,9},{9,8},{10,11... | collective-permute-start | bytes 688136 | tf_op jit(solution)/shard_map/ppermute | solution.py:291
  8.1 2.2 %collective-permute-start.2 = (bf16[128,896]{1,0:T(8,128)(2,1)S(1)}, bf16[128,896]{1,0:T(8,128)(2,1)S(1)}, u32[]{:S(2)}, u32[]{:S(2)}) collective-permute-start(bf16[128,896]{1,0:T(8,128)(2,1)S(1)} %get-tuple-element.81), channel_id=1, source_target_pairs={{0,1},{1,0},{2,3},{3,2},{4,5},{5,4},{6,7},{7,6},{8,9},{9,8},{10,11... | collective-permute-start | bytes 688136 | tf_op jit(solution)/shard_map/ppermute | solution.py:291
  8.6 1.8 %collective-permute-start.3 = (bf16[128,896]{1,0:T(8,128)(2,1)S(1)}, bf16[128,896]{1,0:T(8,128)(2,1)S(1)}, u32[]{:S(2)}, u32[]{:S(2)}) collective-permute-start(bf16[128,896]{1,0:T(8,128)(2,1)S(1)} %get-tuple-element.82), channel_id=1, source_target_pairs={{0,1},{1,0},{2,3},{3,2},{4,5},{5,4},{6,7},{7,6},{8,9},{9,8},{10,11... | collective-permute-start | bytes 688136 | tf_op jit(solution)/shard_map/ppermute | solution.py:291
  27.5 22.2 %collective-permute-start.4 = (bf16[128,3712]{1,0:T(8,128)(2,1)S(1)}, bf16[128,3712]{1,0:T(8,128)(2,1)S(1)}, u32[]{:S(2)}, u32[]{:S(2)}) collective-permute-start(bf16[128,3712]{1,0:T(8,128)(2,1)S(1)} %collective-permute-done.refs_1_), channel_id=1, source_target_pairs={{0,4},{1,5},{4,8},{5,9},{8,12},{9,13},{12,14},{13,15},{14,10},{15,... | collective-permute-start | bytes 2850824 | tf_op jit(solution)/shard_map/ppermute | solution.py:294
  29.3 21.9 %collective-permute-start.11 = (bf16[128,3712]{1,0:T(8,128)(2,1)S(1)}, bf16[128,3712]{1,0:T(8,128)(2,1)S(1)}, u32[]{:S(2)}, u32[]{:S(2)}) collective-permute-start(bf16[128,3712]{1,0:T(8,128)(2,1)S(1)} %collective-permute-done.5.refs_2_), channel_id=1, source_target_pairs={{4,0},{5,1},{8,4},{9,5},{12,8},{13,9},{14,12},{15,13},{10,14},{11,... | collective-permute-start | bytes 2850824 | tf_op jit(solution)/shard_map/ppermute | solution.py:294
  32.1 1.6 %collective-permute-start.6 = (bf16[32,3584]{1,0:T(8,128)(2,1)S(1)}, bf16[32,3584]{1,0:T(8,128)(2,1)S(1)}, u32[]{:S(2)}, u32[]{:S(2)}) collective-permute-start(bf16[32,3584]{1,0:T(8,128)(2,1)S(1)} %get-tuple-element.93.refs_1_), channel_id=1, source_target_pairs={{0,1},{1,0},{2,3},{3,2},{4,5},{5,4},{6,7},{7,6},{8,9},{9,8},{10,11... | collective-permute-start | bytes 688136 | tf_op jit(solution)/shard_map/ppermute | solution.py:291
  32.1 3.9 %collective-permute-start.8 = (bf16[256,896]{1,0:T(8,128)(2,1)S(1)}, bf16[256,896]{1,0:T(8,128)(2,1)S(1)}, u32[]{:S(2)}, u32[]{:S(2)}) collective-permute-start(bf16[256,896]{1,0:T(8,128)(2,1)S(1)} %get-tuple-element.100), channel_id=1, source_target_pairs={{0,1},{1,0},{2,3},{3,2},{4,5},{5,4},{6,7},{7,6},{8,9},{9,8},{10,11... | collective-permute-start | bytes 1376264 | tf_op jit(solution)/shard_map/ppermute | solution.py:291
  32.6 3.5 %collective-permute-start.9 = (bf16[256,896]{1,0:T(8,128)(2,1)S(1)}, bf16[256,896]{1,0:T(8,128)(2,1)S(1)}, u32[]{:S(2)}, u32[]{:S(2)}) collective-permute-start(bf16[256,896]{1,0:T(8,128)(2,1)S(1)} %get-tuple-element.101), channel_id=1, source_target_pairs={{0,1},{1,0},{2,3},{3,2},{4,5},{5,4},{6,7},{7,6},{8,9},{9,8},{10,11... | collective-permute-start | bytes 1376264 | tf_op jit(solution)/shard_map/ppermute | solution.py:291
  33.6 1.6 %collective-permute-start.7 = (bf16[32,3584]{1,0:T(8,128)(2,1)S(1)}, bf16[32,3584]{1,0:T(8,128)(2,1)S(1)}, u32[]{:S(2)}, u32[]{:S(2)}) collective-permute-start(bf16[32,3584]{1,0:T(8,128)(2,1)S(1)} %get-tuple-element.94.refs_2_), channel_id=1, source_target_pairs={{0,1},{1,0},{2,3},{3,2},{4,5},{5,4},{6,7},{7,6},{8,9},{9,8},{10,11... | collective-permute-start | bytes 688136 | tf_op jit(solution)/shard_map/ppermute | solution.py:291
  49.7 21.3 %collective-permute-start.10 = (bf16[128,3712]{1,0:T(8,128)(2,1)S(1)}, bf16[128,3712]{1,0:T(8,128)(2,1)S(1)}, u32[]{:S(2)}, u32[]{:S(2)}) collective-permute-start(bf16[128,3712]{1,0:T(8,128)(2,1)S(1)} %collective-permute-done.4.refs_1_), channel_id=1, source_target_pairs={{0,4},{1,5},{4,8},{5,9},{8,12},{9,13},{12,14},{13,15},{14,10},{15,... | collective-permute-start | bytes 2850824 | tf_op jit(solution)/shard_map/ppermute | solution.py:294
  51.2 20.7 %collective-permute-start.17 = (bf16[128,3712]{1,0:T(8,128)(2,1)S(1)}, bf16[128,3712]{1,0:T(8,128)(2,1)S(1)}, u32[]{:S(2)}, u32[]{:S(2)}) collective-permute-start(bf16[128,3712]{1,0:T(8,128)(2,1)S(1)} %collective-permute-done.11.refs_2_), channel_id=1, source_target_pairs={{4,0},{5,1},{8,4},{9,5},{12,8},{13,9},{14,12},{15,13},{10,14},{11,... | collective-permute-start | bytes 2850824 | tf_op jit(solution)/shard_map/ppermute | solution.py:294
  54.3 1.6 %collective-permute-start.12 = (bf16[32,3584]{1,0:T(8,128)(2,1)S(1)}, bf16[32,3584]{1,0:T(8,128)(2,1)S(1)}, u32[]{:S(2)}, u32[]{:S(2)}) collective-permute-start(bf16[32,3584]{1,0:T(8,128)(2,1)S(1)} %get-tuple-element.112.refs_1_), channel_id=1, source_target_pairs={{0,1},{1,0},{2,3},{3,2},{4,5},{5,4},{6,7},{7,6},{8,9},{9,8},{10,11... | collective-permute-start | bytes 688136 | tf_op jit(solution)/shard_map/ppermute | solution.py:291
  54.4 3.9 %collective-permute-start.14 = (bf16[256,896]{1,0:T(8,128)(2,1)S(1)}, bf16[256,896]{1,0:T(8,128)(2,1)S(1)}, u32[]{:S(2)}, u32[]{:S(2)}) collective-permute-start(bf16[256,896]{1,0:T(8,128)(2,1)S(1)} %get-tuple-element.119), channel_id=1, source_target_pairs={{0,1},{1,0},{2,3},{3,2},{4,5},{5,4},{6,7},{7,6},{8,9},{9,8},{10,11... | collective-permute-start | bytes 1376264 | tf_op jit(solution)/shard_map/ppermute | solution.py:291
  54.9 3.5 %collective-permute-start.15 = (bf16[256,896]{1,0:T(8,128)(2,1)S(1)}, bf16[256,896]{1,0:T(8,128)(2,1)S(1)}, u32[]{:S(2)}, u32[]{:S(2)}) collective-permute-start(bf16[256,896]{1,0:T(8,128)(2,1)S(1)} %get-tuple-element.120), channel_id=1, source_target_pairs={{0,1},{1,0},{2,3},{3,2},{4,5},{5,4},{6,7},{7,6},{8,9},{9,8},{10,11... | collective-permute-start | bytes 1376264 | tf_op jit(solution)/shard_map/ppermute | solution.py:291
  55.9 1.6 %collective-permute-start.13 = (bf16[32,3584]{1,0:T(8,128)(2,1)S(1)}, bf16[32,3584]{1,0:T(8,128)(2,1)S(1)}, u32[]{:S(2)}, u32[]{:S(2)}) collective-permute-start(bf16[32,3584]{1,0:T(8,128)(2,1)S(1)} %get-tuple-element.113.refs_2_), channel_id=1, source_target_pairs={{0,1},{1,0},{2,3},{3,2},{4,5},{5,4},{6,7},{7,6},{8,9},{9,8},{10,11... | collective-permute-start | bytes 688136 | tf_op jit(solution)/shard_map/ppermute | solution.py:291
  72.0 9.7 %collective-permute-start.16 = (bf16[64,3712]{1,0:T(8,128)(2,1)S(1)}, bf16[64,3712]{1,0:T(8,128)(2,1)S(1)}, u32[]{:S(2)}, u32[]{:S(2)}) collective-permute-start(bf16[64,3712]{1,0:T(8,128)(2,1)S(1)} %slice.6), channel_id=1, source_target_pairs={{0,4},{1,5},{4,8},{5,9},{8,12},{9,13},{12,14},{13,15},{14,10},{15,... | collective-permute-start | bytes 1425416 | tf_op jit(solution)/shard_map/ppermute | solution.py:294
  73.6 9.3 %collective-permute-start.18 = (bf16[64,3712]{1,0:T(8,128)(2,1)S(1)}, bf16[64,3712]{1,0:T(8,128)(2,1)S(1)}, u32[]{:S(2)}, u32[]{:S(2)}) collective-permute-start(bf16[64,3712]{1,0:T(8,128)(2,1)S(1)} %slice.7), channel_id=1, source_target_pairs={{4,0},{5,1},{8,4},{9,5},{12,8},{13,9},{14,12},{15,13},{10,14},{11,... | collective-permute-start | bytes 1425416 | tf_op jit(solution)/shard_map/ppermute | solution.py:294
  76.7 1.6 %collective-permute-start.19 = (bf16[32,3584]{1,0:T(8,128)(2,1)S(1)}, bf16[32,3584]{1,0:T(8,128)(2,1)S(1)}, u32[]{:S(2)}, u32[]{:S(2)}) collective-permute-start(bf16[32,3584]{1,0:T(8,128)(2,1)S(1)} %get-tuple-element.131.refs_1_), channel_id=1, source_target_pairs={{0,1},{1,0},{2,3},{3,2},{4,5},{5,4},{6,7},{7,6},{8,9},{9,8},{10,11... | collective-permute-start | bytes 688136 | tf_op jit(solution)/shard_map/ppermute | solution.py:291
  76.7 3.9 %collective-permute-start.21 = (bf16[256,896]{1,0:T(8,128)(2,1)S(1)}, bf16[256,896]{1,0:T(8,128)(2,1)S(1)}, u32[]{:S(2)}, u32[]{:S(2)}) collective-permute-start(bf16[256,896]{1,0:T(8,128)(2,1)S(1)} %get-tuple-element.138), channel_id=1, source_target_pairs={{0,1},{1,0},{2,3},{3,2},{4,5},{5,4},{6,7},{7,6},{8,9},{9,8},{10,11... | collective-permute-start | bytes 1376264 | tf_op jit(solution)/shard_map/ppermute | solution.py:291
  77.2 3.5 %collective-permute-start.22 = (bf16[256,896]{1,0:T(8,128)(2,1)S(1)}, bf16[256,896]{1,0:T(8,128)(2,1)S(1)}, u32[]{:S(2)}, u32[]{:S(2)}) collective-permute-start(bf16[256,896]{1,0:T(8,128)(2,1)S(1)} %get-tuple-element.139), channel_id=1, source_target_pairs={{0,1},{1,0},{2,3},{3,2},{4,5},{5,4},{6,7},{7,6},{8,9},{9,8},{10,11... | collective-permute-start | bytes 1376264 | tf_op jit(solution)/shard_map/ppermute | solution.py:291
  78.2 1.6 %collective-permute-start.20 = (bf16[32,3584]{1,0:T(8,128)(2,1)S(1)}, bf16[32,3584]{1,0:T(8,128)(2,1)S(1)}, u32[]{:S(2)}, u32[]{:S(2)}) collective-permute-start(bf16[32,3584]{1,0:T(8,128)(2,1)S(1)} %get-tuple-element.132.refs_2_), channel_id=1, source_target_pairs={{0,1},{1,0},{2,3},{3,2},{4,5},{5,4},{6,7},{7,6},{8,9},{9,8},{10,11... | collective-permute-start | bytes 688136 | tf_op jit(solution)/shard_map/ppermute | solution.py:291
  83.0 3.3 %collective-permute-start.23 = (bf16[64,3712]{1,0:T(8,128)(2,1)S(1)}, bf16[64,3712]{1,0:T(8,128)(2,1)S(1)}, u32[]{:S(2)}, u32[]{:S(2)}) collective-permute-start(bf16[64,3712]{1,0:T(8,128)(2,1)S(1)} %collective-permute-done.16.refs_1_), channel_id=1, source_target_pairs={{0,1},{1,0},{2,3},{3,2},{4,5},{5,4},{6,7},{7,6},{8,9},{9,8},{10,11... | collective-permute-start | bytes 1425416 | tf_op jit(solution)/shard_map/ppermute | solution.py:291
  83.0 3.3 %collective-permute-start.24 = (bf16[64,3712]{1,0:T(8,128)(2,1)S(1)}, bf16[64,3712]{1,0:T(8,128)(2,1)S(1)}, u32[]{:S(2)}, u32[]{:S(2)}) collective-permute-start(bf16[64,3712]{1,0:T(8,128)(2,1)S(1)} %collective-permute-done.18.refs_2_), channel_id=1, source_target_pairs={{0,1},{1,0},{2,3},{3,2},{4,5},{5,4},{6,7},{7,6},{8,9},{9,8},{10,11... | collective-permute-start | bytes 1425416 | tf_op jit(solution)/shard_map/ppermute | solution.py:291

commit v12 on v11

--- a/solution.py
+++ b/solution.py
@@ -11,8 +11,10 @@
 EXP = 8
 CAP = 32
 CORES = 2
-TABLE = 128
+LANES = 128
+TABLE = 32
 STEP = 512
+SPLITS = 7
 VMEM = pl.BlockSpec(memory_space=pltpu.VMEM)
 SMEM = pl.BlockSpec(memory_space=pltpu.SMEM)
 ANY = pl.BlockSpec(memory_space=pl.ANY)
@@ -27,10 +29,10 @@
     return pltpu.CompilerParams(vmem_limit_bytes=mib * 2**20)
 
 
-def message_kernel(tokens, ids, weights, out, arrived):
+def message_kernel(tokens, ids, weights, out):
     rows, width = tokens.shape
-    copy = pltpu.make_async_copy(tokens, out.at[:, :width], arrived)
-    copy.start()
+    for b in range(width // LANES):
+        out[b * rows : (b + 1) * rows, :] = tokens[:, b * LANES : (b + 1) * LANES]
     row_at = lax.broadcasted_iota(jnp.int32, (TABLE, rows), 0)
     roots = jnp.zeros((TABLE, rows), F32)
     for e in range(EXP):
@@ -40,60 +42,78 @@
     middle = (roots - high).astype(BF16).astype(F32)
     low = roots - high - middle
     terms = jnp.where(row_at < EXP, high, jnp.where(row_at < 2 * EXP, middle, low))
-    out[:, width:] = jnp.where(row_at < 3 * EXP, terms, 0.0).T.astype(BF16)
-    copy.wait()
+    out[rows * width // LANES :, :] = jnp.where(row_at < 3 * EXP, terms, 0.0).astype(BF16)
 
 
 def make_message(tokens, ids, weights):
     rows, width = tokens.shape
     return pl.pallas_call(
         message_kernel,
-        out_shape=jax.ShapeDtypeStruct((rows, width + TABLE), BF16),
-        in_specs=[ANY, VMEM, VMEM],
+        out_shape=jax.ShapeDtypeStruct((rows * width // LANES + TABLE, LANES), BF16),
+        in_specs=[VMEM] * 3,
         out_specs=VMEM,
-        scratch_shapes=[pltpu.SemaphoreType.DMA],
         cost_estimate=SMALL,
         compiler_params=params(8),
         name="make_message",
     )(tokens, ids.T, weights.T)
 
 
-def choose(expert, table):
-    rows = table.shape[0]
-    row_at = lax.broadcasted_iota(jnp.int32, (TABLE, rows), 0)
+def block_of(piece, index):
+    for array in piece:
+        inside = array.shape[0] // LANES
+        if index < inside:
+            return array.at[index * LANES : (index + 1) * LANES]
+        index -= inside
+
+
+def choose(expert, piece):
+    last = piece[-1]
+    table = last[last.shape[0] - TABLE :, :].astype(F32)
+    row_at = lax.broadcasted_iota(jnp.int32, (TABLE, LANES), 0)
     ours = jnp.logical_and(row_at % EXP == expert, row_at < 3 * EXP)
-    root = jnp.sum(jnp.where(ours, table.astype(F32).T, 0.0), axis=0, keepdims=True)
-    root = jnp.broadcast_to(root, (CAP, rows))
+    root = jnp.sum(jnp.where(ours, table, 0.0), axis=0, keepdims=True)
+    root = jnp.broadcast_to(root, (CAP, LANES))
     member = root > 0.0
-    from_at = lax.broadcasted_iota(jnp.int32, (rows, rows), 0)
-    to_at = lax.broadcasted_iota(jnp.int32, (rows, rows), 1)
+    from_at = lax.broadcasted_iota(jnp.int32, (LANES, LANES), 0)
+    to_at = lax.broadcasted_iota(jnp.int32, (LANES, LANES), 1)
     upto = (from_at <= to_at).astype(F32).astype(BF16)
     counted = jnp.dot(member.astype(F32).astype(BF16), upto, preferred_element_type=F32)
     place = counted.astype(jnp.int32) - 1
-    slot_at = lax.broadcasted_iota(jnp.int32, (CAP, rows), 0)
+    slot_at = lax.broadcasted_iota(jnp.int32, (CAP, LANES), 0)
     select = jnp.logical_and(member, place == slot_at)
     scale = jnp.sum(jnp.where(select, root, 0.0), axis=1, keepdims=True)
     return select.astype(F32).astype(BF16), scale
 
 
 def pack(expert, piece):
-    width = piece.shape[1] - TABLE
-    select, scale = choose(expert, piece[:, width:])
-    picked = jnp.dot(select, piece[:, :width], preferred_element_type=F32)
-    return (picked * scale).astype(BF16)
+    select, scale = choose(expert, piece)
+    blocks = sum(array.shape[0] // LANES for array in piece)
+    groups = []
+    for b in range(0, blocks, 4):
+        some = jnp.concatenate(
+            [block_of(piece, k)[...] for k in range(b, min(b + 4, blocks))], axis=1
+        )
+        picked = jnp.dot(select, some, preferred_element_type=F32)
+        groups.append((picked * scale).astype(BF16))
+    return jnp.concatenate(groups, axis=1)
 
 
 def fetch_tile(index, pieces, scratch):
     edge = scratch.shape[1]
-    for b in range((pieces[0].shape[1] - TABLE) // edge):
+    blocks = sum(array.shape[0] // LANES for array in pieces[0])
+    for b in range(blocks * LANES // edge):
 
         @pl.when(index == b)
         def _(b=b):
-            row = 0
-            for piece in pieces:
-                rows = piece.shape[0]
-                scratch[row : row + rows, :] = piece[:, b * edge : (b + 1) * edge]
-                row += rows
+            for k, piece in enumerate(pieces):
+                at = b * edge
+                while at < (b + 1) * edge:
+                    first = at % LANES
+                    count = min(LANES - first, (b + 1) * edge - at)
+                    scratch[k * LANES : (k + 1) * LANES, at - b * edge : at - b * edge + count] = (
+                        block_of(piece, at // LANES)[:, first : first + count]
+                    )
+                    at += count
 
 
 def product(left, right):
@@ -102,7 +122,8 @@
 
 def absorb_kernel(count, started, *refs):
     scalars, refs = refs[0], refs[1:]
-    pieces, before, refs = refs[:count], refs[count : count + 3 * started], refs[count + 3 * started :]
+    pieces, refs = [[ref] for ref in refs[:count]], refs[count:]
+    before, refs = refs[: 3 * started], refs[3 * started :]
     tile, left, theirs, *packs, mine = refs
     for slot, which in enumerate((left, mine, theirs), start=1):
         fetch_tile(scalars[slot], pieces, which)
@@ -115,8 +136,7 @@
 
 
 def absorb(scalars, pieces, before, edge):
-    rows, width = pieces[0].shape
-    width -= TABLE
+    rows, width = LANES, pieces[0].shape[0] - TABLE
     count = len(pieces)
     columns = jax.ShapeDtypeStruct((count * rows, edge), BF16)
     out = pl.pallas_call(
@@ -169,10 +189,9 @@
 
 
 def take_in(scalars, halves, at, rows, across, left, right):
-    piece = jnp.concatenate([half[...] for half in halves], axis=0)
-    place_rows(scalars[4], pack(scalars[0], piece), at, rows, across)
-    fetch_tile(scalars[1], halves, left)
-    fetch_tile(scalars[2], halves, right)
+    place_rows(scalars[4], pack(scalars[0], halves), at, rows, across)
+    fetch_tile(scalars[1], [halves], left)
+    fetch_tile(scalars[2], [halves], right)
     return product(left, right)
 
 
@@ -186,13 +205,12 @@
 
 def take_own(scalars, halves, sums, operands):
     edge = sums[0].shape[0]
-    count = sum(half.shape[0] for half in halves)
     return pl.pallas_call(
         take_own_kernel,
         out_shape=[jax.ShapeDtypeStruct(a.shape, a.dtype) for a in (sums[0], *operands)],
         in_specs=[SMEM] + [VMEM] * 7,
         out_specs=[VMEM] * 3,
-        scratch_shapes=[pltpu.VMEM((count, edge), BF16)] * 2,
+        scratch_shapes=[pltpu.VMEM((LANES, edge), BF16)] * 2,
         input_output_aliases={3: 0, 6: 1, 7: 2},
         cost_estimate=SMALL,
         compiler_params=params(14),
@@ -215,12 +233,15 @@
     update = take_in(scalars, halves, at, rows, across, left, right)
     sums[...] = (before[...] + update) * final
     write(sums, tile.at[0])
-    for n in range(staging.shape[0]):
-        span = slice(n * STEP, (n + 1) * STEP)
-        staging[n, :, :] = (
-            jnp.dot(across[...], rows[:, span], preferred_element_type=F32) * INVERSE
-        )
-        write(staging.at[n], hessian.at[:, span])
+    height = staging.shape[1]
+    for m in range(SPLITS):
+        span = slice(m * height, (m + 1) * height)
+        for n in range(0, rows.shape[1], STEP):
+            staging[m, :, n : n + STEP] = (
+                jnp.dot(across[span, :], rows[:, n : n + STEP], preferred_element_type=F32)
+                * INVERSE
+            )
+        write(staging.at[m], hessian.at[span, :])
     for copy in copies:
         copy.wait()
 
@@ -229,8 +250,6 @@
     edge = before.shape[0]
     rows, across = operands
     slab, width = across.shape[0], rows.shape[1]
-    count = sum(half.shape[0] for half in halves)
-    blocks = width // STEP
     return pl.pallas_call(
         functools.partial(finish_kernel, final),
         out_shape=[
@@ -242,11 +261,11 @@
         in_specs=[SMEM] + [VMEM] * 5,
         out_specs=[ANY, ANY, VMEM, VMEM],
         scratch_shapes=[
-            pltpu.VMEM((blocks, slab, STEP), F32),
+            pltpu.VMEM((SPLITS, slab // SPLITS, width), F32),
             pltpu.VMEM((edge, edge), F32),
-            pltpu.VMEM((count, edge), BF16),
-            pltpu.VMEM((count, edge), BF16),
-            pltpu.SemaphoreType.DMA((blocks + 1,)),
+            pltpu.VMEM((LANES, edge), BF16),
+            pltpu.VMEM((LANES, edge), BF16),
+            pltpu.SemaphoreType.DMA((SPLITS + 1,)),
         ],
         input_output_aliases={4: 2, 5: 3},
         cost_estimate=SMALL,
@@ -298,11 +317,11 @@
 
     pieces = [make_message(tokens, route_ids, route_weights)]
     operands, sums = [], []
-    half = tok_rows // 2
+    half = tok_rows * (width // LANES // 2)
     for step in range(1, rounds + 1):
         held = pieces * CORES if step == 1 else pieces
         if step == rounds:
-            held = [held[0][:half], held[1][half:]]
+            held = [held[0][: half + TABLE], held[1][half:]]
         moved = advance(held)
         tile, columns, packed = absorb(scalars, pieces, sums, edge)
         sums = [tile] + [swap(array) for array in columns]

time: 98.4 us -> 96.8 us (0.984)
  waiting for transfers between devices: 54.6 us -> 52.2 us
    ppermute x8, waiting for transfers between devices: 46.5 us -> 44.1 us  [advance(): lax.ppermute(array, 'tok', stream)]
  transfers between devices with their start and end apart: 25 -> 25, of which waited for: 13 -> 13; matrix products, arithmetic and copies ran while one was open for 0% -> 0% of each run, Pallas kernels for 15% -> 16%
where the time goes in v12:
time: 96.8 us; the launch traced here: 96.6 us
  waiting for transfers between devices  52.2 us (54%)
  Pallas kernels  27.9 us (29%)
  starting transfers between devices  12.7 us (13%)
  local copies, waits for them, and re-layouts  2.69 us (3%)
  between operations  1.01 us (1%)
    ppermute x8, waiting for transfers between devices, advance(): lax.ppermute(array, 'tok', stream)  44.1 us
    pallas_call x1, Pallas kernels, finish(): pl.pallas_call(functools.partial(finish_kernel, final), out_shape=[jax.Sh...  12 us
    pallas_call x4, Pallas kernels, absorb(): pl.pallas_call(functools.partial(absorb_kernel, count, bool(before)), out...  9.83 us
    ppermute x8, starting transfers between devices, advance(): lax.ppermute(array, 'tok', stream)  9.21 us
    ppermute x17, waiting for transfers between devices, swap(): return lax.ppermute(array, 'tok', pair)  8.13 us
    ppermute x17, starting transfers between devices, swap(): return lax.ppermute(array, 'tok', pair)  3.5 us
    pallas_call x4, Pallas kernels, prepare(): pl.pallas_call(functools.partial(prepare_kernel, len(packs), at), out_sha...  3.21 us
    pallas_call x1, Pallas kernels, take_own(): pl.pallas_call(take_own_kernel, out_shape=[jax.ShapeDtypeStruct(a.shape,...  2.66 us
  transfers between devices with their start and end apart: 25, of which 13 were waited for; matrix products, arithmetic and copies ran while one was open for 0% of the time, Pallas kernels for 16%

profile of v12, /device:TPU:0, one launch (start us, length us, event | category | flops | bytes accessed | tf_op | source)
XLA Modules:
  0.0 96.6 jit_solution(547907999644717657)
XLA Ops:
  0.6 1.2 %copy-done = bf16[128,3584]{1,0:T(8,128)(2,1)S(1)} copy-done((bf16[128,3584]{1,0:T(8,128)(2,1)S(1)}, bf16[128,3584]{1,0:T(8,128)(2,1)}, u32[]{:S(2)}) %copy-start) | copy-done | bytes 917528
  1.8 0.7 copy-done.1
  2.5 0.7 copy-done.2
  3.2 0.2 make_message.1.refs_1_
  3.4 3.1 %collective-permute-start = (bf16[3616,128]{1,0:T(8,128)(2,1)S(1)}, bf16[3616,128]{1,0:T(8,128)(2,1)S(1)}, u32[]{:S(2)}, u32[]{:S(2)}) collective-permute-start(bf16[3616,128]{1,0:T(8,128)(2,1)S(1)} %make_message.1.refs_1_), channel_id=1, source_target_pairs={{0,4},{1,5},{4,8},{5,9},{8,12},{9,13},{12,14},{13,15},{14,10},{15,... | collective-permute-start | bytes 2777096 | tf_op jit(solution)/shard_map/ppermute | solution.py:313
  6.5 0.0 collective-permute-start.5
  6.5 0.1 stack.23.refs_0_
  6.5 1.5 %absorb.4 = (f32[896,896]{1,0:T(8,128)S(1)}, bf16[128,896]{1,0:T(8,128)(2,1)S(1)}, bf16[128,896]{1,0:T(8,128)(2,1)S(1)}, bf16[32,3584]{1,0:T(8,128)(2,1)S(1)}) custom-call(s32[5]{0:T(128)S(1)} %stack.23.refs_0_, bf16[3616,128]{1,0:T(8,128)(2,1)S(1)} %make_message.1.refs_1_), custom_call_target="tpu_custom_call" | custom-call | flops 1 | bytes 1 | tf_op jit(solution)/shard_map/absorb/pallas_call | solution.py:142
  8.1 0.1 collective-permute-start.1
  8.2 0.5 collective-permute-start.2
  8.7 0.1 collective-permute-start.3
  8.7 0.9 collective-permute-done.1.refs_2_
  9.6 0.8 prepare_rows.4
  10.4 0.0 collective-permute-done.2.refs_4_
  10.4 0.0 collective-permute-done.3.refs_5_
  10.4 16.5 %collective-permute-done.refs_1_ = bf16[3616,128]{1,0:T(8,128)(2,1)S(1)} collective-permute-done((bf16[3616,128]{1,0:T(8,128)(2,1)S(1)}, bf16[3616,128]{1,0:T(8,128)(2,1)S(1)}, u32[]{:S(2)}, u32[]{:S(2)}) %collective-permute-start) | collective-permute-done | bytes 925728 | tf_op jit(solution)/shard_map/ppermute | solution.py:313
  26.9 1.8 %collective-permute-start.4 = (bf16[3616,128]{1,0:T(8,128)(2,1)S(1)}, bf16[3616,128]{1,0:T(8,128)(2,1)S(1)}, u32[]{:S(2)}, u32[]{:S(2)}) collective-permute-start(bf16[3616,128]{1,0:T(8,128)(2,1)S(1)} %collective-permute-done.refs_1_), channel_id=1, source_target_pairs={{0,4},{1,5},{4,8},{5,9},{8,12},{9,13},{12,14},{13,15},{14,10},{15,... | collective-permute-start | bytes 2777096 | tf_op jit(solution)/shard_map/ppermute | solution.py:313
  28.7 0.0 collective-permute-done.5.refs_2_
  28.7 0.2 collective-permute-start.11
  29.0 2.7 %absorb.5 = (f32[896,896]{1,0:T(8,128)S(1)}, bf16[256,896]{1,0:T(8,128)(2,1)S(1)}, bf16[256,896]{1,0:T(8,128)(2,1)S(1)}, bf16[32,3584]{1,0:T(8,128)(2,1)S(1)}, bf16[32,3584]{1,0:T(8,128)(2,1)S(1)}) custom-call(s32[5]{0:T(128)S(1)} %stack.23.refs_0_, bf16[3616,128]{1,0:T(8,128)(2,1)S(1)} %collective-permute-done.refs_1_, ...), custom_call_target="tpu_custom_call", output_to_operand_aliasing={{0}: (3, {})} | custom-call | flops 1 | bytes 1 | tf_op jit(solution)/shard_map/absorb/pallas_call | solution.py:142
  31.6 0.1 collective-permute-start.6
  31.7 0.5 collective-permute-start.8
  32.2 0.1 collective-permute-start.9
  32.3 0.9 collective-permute-done.6.refs_3_
  33.2 0.1 collective-permute-start.7
  33.3 1.5 %collective-permute-done.7.refs_4_ = bf16[32,3584]{1,0:T(8,128)(2,1)S(1)} collective-permute-done((bf16[32,3584]{1,0:T(8,128)(2,1)S(1)}, bf16[32,3584]{1,0:T(8,128)(2,1)S(1)}, u32[]{:S(2)}, u32[]{:S(2)}) %collective-permute-start.7) | collective-permute-done | bytes 229408 | tf_op jit(solution)/shard_map/ppermute | solution.py:310
  34.8 0.8 prepare_rows.5
  35.6 0.0 collective-permute-done.8.refs_4_
  35.6 0.0 collective-permute-done.9.refs_5_
  35.7 13.0 %collective-permute-done.4.refs_1_ = bf16[3616,128]{1,0:T(8,128)(2,1)S(1)} collective-permute-done((bf16[3616,128]{1,0:T(8,128)(2,1)S(1)}, bf16[3616,128]{1,0:T(8,128)(2,1)S(1)}, u32[]{:S(2)}, u32[]{:S(2)}) %collective-permute-start.4) | collective-permute-done | bytes 925728 | tf_op jit(solution)/shard_map/ppermute | solution.py:313
  48.6 1.5 %collective-permute-start.10 = (bf16[3616,128]{1,0:T(8,128)(2,1)S(1)}, bf16[3616,128]{1,0:T(8,128)(2,1)S(1)}, u32[]{:S(2)}, u32[]{:S(2)}) collective-permute-start(bf16[3616,128]{1,0:T(8,128)(2,1)S(1)} %collective-permute-done.4.refs_1_), channel_id=1, source_target_pairs={{0,4},{1,5},{4,8},{5,9},{8,12},{9,13},{12,14},{13,15},{14,10},{15,... | collective-permute-start | bytes 2777096 | tf_op jit(solution)/shard_map/ppermute | solution.py:313
  50.1 0.0 collective-permute-done.11.refs_2_
  50.1 0.5 collective-permute-start.17
  50.7 2.7 %absorb.6 = (f32[896,896]{1,0:T(8,128)S(1)}, bf16[256,896]{1,0:T(8,128)(2,1)S(1)}, bf16[256,896]{1,0:T(8,128)(2,1)S(1)}, bf16[32,3584]{1,0:T(8,128)(2,1)S(1)}, bf16[32,3584]{1,0:T(8,128)(2,1)S(1)}) custom-call(s32[5]{0:T(128)S(1)} %stack.23.refs_0_, bf16[3616,128]{1,0:T(8,128)(2,1)S(1)} %collective-permute-done.4.refs_1_, ...), custom_call_target="tpu_custom_call", output_to_operand_aliasing={{0}: (3, {})} | custom-call | flops 1 | bytes 1 | tf_op jit(solution)/shard_map/absorb/pallas_call | solution.py:142
  53.4 0.1 collective-permute-start.12
  53.5 0.5 collective-permute-start.14
  54.0 0.1 collective-permute-start.15
  54.1 0.9 collective-permute-done.12.refs_3_
  55.0 0.1 collective-permute-start.13
  55.1 1.5 %collective-permute-done.13.refs_4_ = bf16[32,3584]{1,0:T(8,128)(2,1)S(1)} collective-permute-done((bf16[32,3584]{1,0:T(8,128)(2,1)S(1)}, bf16[32,3584]{1,0:T(8,128)(2,1)S(1)}, u32[]{:S(2)}, u32[]{:S(2)}) %collective-permute-start.13) | collective-permute-done | bytes 229408 | tf_op jit(solution)/shard_map/ppermute | solution.py:310
  56.6 0.8 prepare_rows.6
  57.4 0.0 collective-permute-done.14.refs_4_
  57.4 12.0 %collective-permute-done.10.refs_1_ = bf16[3616,128]{1,0:T(8,128)(2,1)S(1)} collective-permute-done((bf16[3616,128]{1,0:T(8,128)(2,1)S(1)}, bf16[3616,128]{1,0:T(8,128)(2,1)S(1)}, u32[]{:S(2)}, u32[]{:S(2)}) %collective-permute-start.10) | collective-permute-done | bytes 925728 | tf_op jit(solution)/shard_map/ppermute | solution.py:313
  69.4 0.9 collective-permute-done.17.refs_2_
  70.4 1.6 %collective-permute-start.16 = (bf16[1824,128]{1,0:T(8,128)(2,1)S(1)}, bf16[1824,128]{1,0:T(8,128)(2,1)S(1)}, u32[]{:S(2)}, u32[]{:S(2)}) collective-permute-start(bf16[1824,128]{1,0:T(8,128)(2,1)S(1)} %slice.6), channel_id=1, source_target_pairs={{0,4},{1,5},{4,8},{5,9},{8,12},{9,13},{12,14},{13,15},{14,10},{15,... | collective-permute-start | bytes 1400840 | tf_op jit(solution)/shard_map/ppermute | solution.py:313
  72.0 0.4 collective-permute-start.18
  72.5 2.9 %absorb.7 = (f32[896,896]{1,0:T(8,128)S(1)}, bf16[256,896]{1,0:T(8,128)(2,1)S(1)}, bf16[256,896]{1,0:T(8,128)(2,1)S(1)}, bf16[32,3584]{1,0:T(8,128)(2,1)S(1)}, bf16[32,3584]{1,0:T(8,128)(2,1)S(1)}) custom-call(s32[5]{0:T(128)S(1)} %stack.23.refs_0_, bf16[3616,128]{1,0:T(8,128)(2,1)S(1)} %collective-permute-done.10.refs_1_, ...), custom_call_target="tpu_custom_call", output_to_operand_aliasing={{0}: (3, {})} | custom-call | flops 1 | bytes 1 | tf_op jit(solution)/shard_map/absorb/pallas_call | solution.py:142
  75.4 0.1 collective-permute-start.19
  75.5 0.5 collective-permute-start.21
  76.0 0.1 collective-permute-start.22
  76.0 0.9 collective-permute-done.19.refs_3_
  76.9 0.1 collective-permute-start.20
  77.1 1.5 %collective-permute-done.20.refs_4_ = bf16[32,3584]{1,0:T(8,128)(2,1)S(1)} collective-permute-done((bf16[32,3584]{1,0:T(8,128)(2,1)S(1)}, bf16[32,3584]{1,0:T(8,128)(2,1)S(1)}, u32[]{:S(2)}, u32[]{:S(2)}) %collective-permute-start.20) | collective-permute-done | bytes 229408 | tf_op jit(solution)/shard_map/ppermute | solution.py:310
  78.6 0.8 prepare_rows.7
  79.4 0.0 collective-permute-done.21.refs_4_
  79.4 0.0 collective-permute-done.22.refs_5_
  79.4 0.5 collective-permute-done.16.refs_1_
  79.9 1.3 %collective-permute-done.18.refs_2_ = bf16[1824,128]{1,0:T(8,128)(2,1)S(1)} collective-permute-done((bf16[1824,128]{1,0:T(8,128)(2,1)S(1)}, bf16[1824,128]{1,0:T(8,128)(2,1)S(1)}, u32[]{:S(2)}, u32[]{:S(2)}) %collective-permute-start.18) | collective-permute-done | bytes 466976 | tf_op jit(solution)/shard_map/ppermute | solution.py:313
  81.2 0.0 collective-permute-start.23
  81.2 0.5 collective-permute-start.24
  81.7 2.7 %take_own.1 = (f32[896,896]{1,0:T(8,128)S(1)}, bf16[512,3584]{1,0:T(8,128)(2,1)S(1)}, bf16[1792,512]{1,0:T(8,128)(2,1)S(1)}) custom-call(s32[5]{0:T(128)S(1)} %stack.23.refs_0_, bf16[1824,128]{1,0:T(8,128)(2,1)S(1)} %collective-permute-done.16.refs_1_, ...), custom_call_target="tpu_custom_call", output_to_operand_aliasing={{0}: (3, {}), {1}: (6, {}), {2}: (7, {})} | custom-call | flops 1 | bytes 1 | tf_op jit(solution)/shard_map/take_own/pallas_call | solution.py:208
  84.4 0.0 collective-permute-done.23.refs_1_
  84.4 0.0 collective-permute-done.24.refs_2_
  84.4 12.0 %finish.1 = (f32[1792,3584]{1,0:T(8,128)}, f32[1,896,896]{2,1,0:T(8,128)}, bf16[512,3584]{1,0:T(8,128)(2,1)S(1)}, bf16[1792,512]{1,0:T(8,128)(2,1)S(1)}) custom-call(s32[5]{0:T(128)S(1)} %stack.23.refs_0_, bf16[1824,128]{1,0:T(8,128)(2,1)S(1)} %collective-permute-done.23.refs_1_, ...), custom_call_target="tpu_custom_call", output_to_operand_aliasing={{2}: (4, {}), {3}: (5, {})} | custom-call | flops 1 | bytes 1 | tf_op jit(solution)/shard_map/finish/pallas_call | solution.py:253
  (6 shorter events, 0.1 us)
Async XLA Ops:
  0.6 1.2 %copy-start = (bf16[128,3584]{1,0:T(8,128)(2,1)S(1)}, bf16[128,3584]{1,0:T(8,128)(2,1)}, u32[]{:S(2)}) copy-start(bf16[128,3584]{1,0:T(8,128)(2,1)} %tokens.1) | copy-start | bytes 2752516
  1.8 0.7 copy-start.1
  2.5 0.7 copy-start.2
  3.4 23.5 %collective-permute-start = (bf16[3616,128]{1,0:T(8,128)(2,1)S(1)}, bf16[3616,128]{1,0:T(8,128)(2,1)S(1)}, u32[]{:S(2)}, u32[]{:S(2)}) collective-permute-start(bf16[3616,128]{1,0:T(8,128)(2,1)S(1)} %make_message.1.refs_1_), channel_id=1, source_target_pairs={{0,4},{1,5},{4,8},{5,9},{8,12},{9,13},{12,14},{13,15},{14,10},{15,... | collective-permute-start | bytes 2777096 | tf_op jit(solution)/shard_map/ppermute | solution.py:313
  6.5 22.3 %collective-permute-start.5 = (bf16[3616,128]{1,0:T(8,128)(2,1)S(1)}, bf16[3616,128]{1,0:T(8,128)(2,1)S(1)}, u32[]{:S(2)}, u32[]{:S(2)}) collective-permute-start(bf16[3616,128]{1,0:T(8,128)(2,1)S(1)} %make_message.1.refs_1_), channel_id=1, source_target_pairs={{4,0},{5,1},{8,4},{9,5},{12,8},{13,9},{14,12},{15,13},{10,14},{11,... | collective-permute-start | bytes 2777096 | tf_op jit(solution)/shard_map/ppermute | solution.py:313
  8.1 1.6 %collective-permute-start.1 = (bf16[32,3584]{1,0:T(8,128)(2,1)S(1)}, bf16[32,3584]{1,0:T(8,128)(2,1)S(1)}, u32[]{:S(2)}, u32[]{:S(2)}) collective-permute-start(bf16[32,3584]{1,0:T(8,128)(2,1)S(1)} %get-tuple-element.77.refs_1_), channel_id=1, source_target_pairs={{0,1},{1,0},{2,3},{3,2},{4,5},{5,4},{6,7},{7,6},{8,9},{9,8},{10,11... | collective-permute-start | bytes 688136 | tf_op jit(solution)/shard_map/ppermute | solution.py:310
  8.2 2.2 %collective-permute-start.2 = (bf16[128,896]{1,0:T(8,128)(2,1)S(1)}, bf16[128,896]{1,0:T(8,128)(2,1)S(1)}, u32[]{:S(2)}, u32[]{:S(2)}) collective-permute-start(bf16[128,896]{1,0:T(8,128)(2,1)S(1)} %get-tuple-element.81), channel_id=1, source_target_pairs={{0,1},{1,0},{2,3},{3,2},{4,5},{5,4},{6,7},{7,6},{8,9},{9,8},{10,11... | collective-permute-start | bytes 688136 | tf_op jit(solution)/shard_map/ppermute | solution.py:310
  8.7 1.8 %collective-permute-start.3 = (bf16[128,896]{1,0:T(8,128)(2,1)S(1)}, bf16[128,896]{1,0:T(8,128)(2,1)S(1)}, u32[]{:S(2)}, u32[]{:S(2)}) collective-permute-start(bf16[128,896]{1,0:T(8,128)(2,1)S(1)} %get-tuple-element.82), channel_id=1, source_target_pairs={{0,1},{1,0},{2,3},{3,2},{4,5},{5,4},{6,7},{7,6},{8,9},{9,8},{10,11... | collective-permute-start | bytes 688136 | tf_op jit(solution)/shard_map/ppermute | solution.py:310
  26.9 21.7 %collective-permute-start.4 = (bf16[3616,128]{1,0:T(8,128)(2,1)S(1)}, bf16[3616,128]{1,0:T(8,128)(2,1)S(1)}, u32[]{:S(2)}, u32[]{:S(2)}) collective-permute-start(bf16[3616,128]{1,0:T(8,128)(2,1)S(1)} %collective-permute-done.refs_1_), channel_id=1, source_target_pairs={{0,4},{1,5},{4,8},{5,9},{8,12},{9,13},{12,14},{13,15},{14,10},{15,... | collective-permute-start | bytes 2777096 | tf_op jit(solution)/shard_map/ppermute | solution.py:313
  28.7 21.4 %collective-permute-start.11 = (bf16[3616,128]{1,0:T(8,128)(2,1)S(1)}, bf16[3616,128]{1,0:T(8,128)(2,1)S(1)}, u32[]{:S(2)}, u32[]{:S(2)}) collective-permute-start(bf16[3616,128]{1,0:T(8,128)(2,1)S(1)} %collective-permute-done.5.refs_2_), channel_id=1, source_target_pairs={{4,0},{5,1},{8,4},{9,5},{12,8},{13,9},{14,12},{15,13},{10,14},{11,... | collective-permute-start | bytes 2777096 | tf_op jit(solution)/shard_map/ppermute | solution.py:313
  31.6 1.6 %collective-permute-start.6 = (bf16[32,3584]{1,0:T(8,128)(2,1)S(1)}, bf16[32,3584]{1,0:T(8,128)(2,1)S(1)}, u32[]{:S(2)}, u32[]{:S(2)}) collective-permute-start(bf16[32,3584]{1,0:T(8,128)(2,1)S(1)} %get-tuple-element.93.refs_1_), channel_id=1, source_target_pairs={{0,1},{1,0},{2,3},{3,2},{4,5},{5,4},{6,7},{7,6},{8,9},{9,8},{10,11... | collective-permute-start | bytes 688136 | tf_op jit(solution)/shard_map/ppermute | solution.py:310
  31.7 3.9 %collective-permute-start.8 = (bf16[256,896]{1,0:T(8,128)(2,1)S(1)}, bf16[256,896]{1,0:T(8,128)(2,1)S(1)}, u32[]{:S(2)}, u32[]{:S(2)}) collective-permute-start(bf16[256,896]{1,0:T(8,128)(2,1)S(1)} %get-tuple-element.100), channel_id=1, source_target_pairs={{0,1},{1,0},{2,3},{3,2},{4,5},{5,4},{6,7},{7,6},{8,9},{9,8},{10,11... | collective-permute-start | bytes 1376264 | tf_op jit(solution)/shard_map/ppermute | solution.py:310
  32.2 3.5 %collective-permute-start.9 = (bf16[256,896]{1,0:T(8,128)(2,1)S(1)}, bf16[256,896]{1,0:T(8,128)(2,1)S(1)}, u32[]{:S(2)}, u32[]{:S(2)}) collective-permute-start(bf16[256,896]{1,0:T(8,128)(2,1)S(1)} %get-tuple-element.101), channel_id=1, source_target_pairs={{0,1},{1,0},{2,3},{3,2},{4,5},{5,4},{6,7},{7,6},{8,9},{9,8},{10,11... | collective-permute-start | bytes 1376264 | tf_op jit(solution)/shard_map/ppermute | solution.py:310
  33.2 1.6 %collective-permute-start.7 = (bf16[32,3584]{1,0:T(8,128)(2,1)S(1)}, bf16[32,3584]{1,0:T(8,128)(2,1)S(1)}, u32[]{:S(2)}, u32[]{:S(2)}) collective-permute-start(bf16[32,3584]{1,0:T(8,128)(2,1)S(1)} %get-tuple-element.94.refs_2_), channel_id=1, source_target_pairs={{0,1},{1,0},{2,3},{3,2},{4,5},{5,4},{6,7},{7,6},{8,9},{9,8},{10,11... | collective-permute-start | bytes 688136 | tf_op jit(solution)/shard_map/ppermute | solution.py:310
  48.6 20.8 %collective-permute-start.10 = (bf16[3616,128]{1,0:T(8,128)(2,1)S(1)}, bf16[3616,128]{1,0:T(8,128)(2,1)S(1)}, u32[]{:S(2)}, u32[]{:S(2)}) collective-permute-start(bf16[3616,128]{1,0:T(8,128)(2,1)S(1)} %collective-permute-done.4.refs_1_), channel_id=1, source_target_pairs={{0,4},{1,5},{4,8},{5,9},{8,12},{9,13},{12,14},{13,15},{14,10},{15,... | collective-permute-start | bytes 2777096 | tf_op jit(solution)/shard_map/ppermute | solution.py:313
  50.1 20.2 %collective-permute-start.17 = (bf16[3616,128]{1,0:T(8,128)(2,1)S(1)}, bf16[3616,128]{1,0:T(8,128)(2,1)S(1)}, u32[]{:S(2)}, u32[]{:S(2)}) collective-permute-start(bf16[3616,128]{1,0:T(8,128)(2,1)S(1)} %collective-permute-done.11.refs_2_), channel_id=1, source_target_pairs={{4,0},{5,1},{8,4},{9,5},{12,8},{13,9},{14,12},{15,13},{10,14},{11,... | collective-permute-start | bytes 2777096 | tf_op jit(solution)/shard_map/ppermute | solution.py:313
  53.4 1.6 %collective-permute-start.12 = (bf16[32,3584]{1,0:T(8,128)(2,1)S(1)}, bf16[32,3584]{1,0:T(8,128)(2,1)S(1)}, u32[]{:S(2)}, u32[]{:S(2)}) collective-permute-start(bf16[32,3584]{1,0:T(8,128)(2,1)S(1)} %get-tuple-element.112.refs_1_), channel_id=1, source_target_pairs={{0,1},{1,0},{2,3},{3,2},{4,5},{5,4},{6,7},{7,6},{8,9},{9,8},{10,11... | collective-permute-start | bytes 688136 | tf_op jit(solution)/shard_map/ppermute | solution.py:310
  53.5 3.9 %collective-permute-start.14 = (bf16[256,896]{1,0:T(8,128)(2,1)S(1)}, bf16[256,896]{1,0:T(8,128)(2,1)S(1)}, u32[]{:S(2)}, u32[]{:S(2)}) collective-permute-start(bf16[256,896]{1,0:T(8,128)(2,1)S(1)} %get-tuple-element.119), channel_id=1, source_target_pairs={{0,1},{1,0},{2,3},{3,2},{4,5},{5,4},{6,7},{7,6},{8,9},{9,8},{10,11... | collective-permute-start | bytes 1376264 | tf_op jit(solution)/shard_map/ppermute | solution.py:310
  54.0 3.5 %collective-permute-start.15 = (bf16[256,896]{1,0:T(8,128)(2,1)S(1)}, bf16[256,896]{1,0:T(8,128)(2,1)S(1)}, u32[]{:S(2)}, u32[]{:S(2)}) collective-permute-start(bf16[256,896]{1,0:T(8,128)(2,1)S(1)} %get-tuple-element.120), channel_id=1, source_target_pairs={{0,1},{1,0},{2,3},{3,2},{4,5},{5,4},{6,7},{7,6},{8,9},{9,8},{10,11... | collective-permute-start | bytes 1376264 | tf_op jit(solution)/shard_map/ppermute | solution.py:310
  55.0 1.6 %collective-permute-start.13 = (bf16[32,3584]{1,0:T(8,128)(2,1)S(1)}, bf16[32,3584]{1,0:T(8,128)(2,1)S(1)}, u32[]{:S(2)}, u32[]{:S(2)}) collective-permute-start(bf16[32,3584]{1,0:T(8,128)(2,1)S(1)} %get-tuple-element.113.refs_2_), channel_id=1, source_target_pairs={{0,1},{1,0},{2,3},{3,2},{4,5},{5,4},{6,7},{7,6},{8,9},{9,8},{10,11... | collective-permute-start | bytes 688136 | tf_op jit(solution)/shard_map/ppermute | solution.py:310
  70.4 9.5 %collective-permute-start.16 = (bf16[1824,128]{1,0:T(8,128)(2,1)S(1)}, bf16[1824,128]{1,0:T(8,128)(2,1)S(1)}, u32[]{:S(2)}, u32[]{:S(2)}) collective-permute-start(bf16[1824,128]{1,0:T(8,128)(2,1)S(1)} %slice.6), channel_id=1, source_target_pairs={{0,4},{1,5},{4,8},{5,9},{8,12},{9,13},{12,14},{13,15},{14,10},{15,... | collective-permute-start | bytes 1400840 | tf_op jit(solution)/shard_map/ppermute | solution.py:313
  72.0 9.2 %collective-permute-start.18 = (bf16[1824,128]{1,0:T(8,128)(2,1)S(1)}, bf16[1824,128]{1,0:T(8,128)(2,1)S(1)}, u32[]{:S(2)}, u32[]{:S(2)}) collective-permute-start(bf16[1824,128]{1,0:T(8,128)(2,1)S(1)} %slice.7), channel_id=1, source_target_pairs={{4,0},{5,1},{8,4},{9,5},{12,8},{13,9},{14,12},{15,13},{10,14},{11,... | collective-permute-start | bytes 1400840 | tf_op jit(solution)/shard_map/ppermute | solution.py:313
  75.4 1.6 %collective-permute-start.19 = (bf16[32,3584]{1,0:T(8,128)(2,1)S(1)}, bf16[32,3584]{1,0:T(8,128)(2,1)S(1)}, u32[]{:S(2)}, u32[]{:S(2)}) collective-permute-start(bf16[32,3584]{1,0:T(8,128)(2,1)S(1)} %get-tuple-element.131.refs_1_), channel_id=1, source_target_pairs={{0,1},{1,0},{2,3},{3,2},{4,5},{5,4},{6,7},{7,6},{8,9},{9,8},{10,11... | collective-permute-start | bytes 688136 | tf_op jit(solution)/shard_map/ppermute | solution.py:310
  75.5 3.9 %collective-permute-start.21 = (bf16[256,896]{1,0:T(8,128)(2,1)S(1)}, bf16[256,896]{1,0:T(8,128)(2,1)S(1)}, u32[]{:S(2)}, u32[]{:S(2)}) collective-permute-start(bf16[256,896]{1,0:T(8,128)(2,1)S(1)} %get-tuple-element.138), channel_id=1, source_target_pairs={{0,1},{1,0},{2,3},{3,2},{4,5},{5,4},{6,7},{7,6},{8,9},{9,8},{10,11... | collective-permute-start | bytes 1376264 | tf_op jit(solution)/shard_map/ppermute | solution.py:310
  76.0 3.5 %collective-permute-start.22 = (bf16[256,896]{1,0:T(8,128)(2,1)S(1)}, bf16[256,896]{1,0:T(8,128)(2,1)S(1)}, u32[]{:S(2)}, u32[]{:S(2)}) collective-permute-start(bf16[256,896]{1,0:T(8,128)(2,1)S(1)} %get-tuple-element.139), channel_id=1, source_target_pairs={{0,1},{1,0},{2,3},{3,2},{4,5},{5,4},{6,7},{7,6},{8,9},{9,8},{10,11... | collective-permute-start | bytes 1376264 | tf_op jit(solution)/shard_map/ppermute | solution.py:310
  76.9 1.6 %collective-permute-start.20 = (bf16[32,3584]{1,0:T(8,128)(2,1)S(1)}, bf16[32,3584]{1,0:T(8,128)(2,1)S(1)}, u32[]{:S(2)}, u32[]{:S(2)}) collective-permute-start(bf16[32,3584]{1,0:T(8,128)(2,1)S(1)} %get-tuple-element.132.refs_2_), channel_id=1, source_target_pairs={{0,1},{1,0},{2,3},{3,2},{4,5},{5,4},{6,7},{7,6},{8,9},{9,8},{10,11... | collective-permute-start | bytes 688136 | tf_op jit(solution)/shard_map/ppermute | solution.py:310
  81.2 3.2 %collective-permute-start.23 = (bf16[1824,128]{1,0:T(8,128)(2,1)S(1)}, bf16[1824,128]{1,0:T(8,128)(2,1)S(1)}, u32[]{:S(2)}, u32[]{:S(2)}) collective-permute-start(bf16[1824,128]{1,0:T(8,128)(2,1)S(1)} %collective-permute-done.16.refs_1_), channel_id=1, source_target_pairs={{0,1},{1,0},{2,3},{3,2},{4,5},{5,4},{6,7},{7,6},{8,9},{9,8},{10,11... | collective-permute-start | bytes 1400840 | tf_op jit(solution)/shard_map/ppermute | solution.py:310
  81.2 3.2 %collective-permute-start.24 = (bf16[1824,128]{1,0:T(8,128)(2,1)S(1)}, bf16[1824,128]{1,0:T(8,128)(2,1)S(1)}, u32[]{:S(2)}, u32[]{:S(2)}) collective-permute-start(bf16[1824,128]{1,0:T(8,128)(2,1)S(1)} %collective-permute-done.18.refs_2_), channel_id=1, source_target_pairs={{0,1},{1,0},{2,3},{3,2},{4,5},{5,4},{6,7},{7,6},{8,9},{9,8},{10,11... | collective-permute-start | bytes 1400840 | tf_op jit(solution)/shard_map/ppermute | solution.py:310

commit v13 on v12

--- a/solution.py
+++ b/solution.py
@@ -29,15 +29,14 @@
     return pltpu.CompilerParams(vmem_limit_bytes=mib * 2**20)
 
 
-def message_kernel(tokens, ids, weights, out):
+def message_kernel(tokens, weights, out):
     rows, width = tokens.shape
     for b in range(width // LANES):
         out[b * rows : (b + 1) * rows, :] = tokens[:, b * LANES : (b + 1) * LANES]
     row_at = lax.broadcasted_iota(jnp.int32, (TABLE, rows), 0)
     roots = jnp.zeros((TABLE, rows), F32)
     for e in range(EXP):
-        weight = jnp.sum(jnp.where(ids[...] == e, weights[...], 0.0), axis=0, keepdims=True)
-        roots = jnp.where(row_at % EXP == e, jnp.sqrt(weight), roots)
+        roots = jnp.where(row_at % EXP == e, jnp.sqrt(weights[e : e + 1, :]), roots)
     high = roots.astype(BF16).astype(F32)
     middle = (roots - high).astype(BF16).astype(F32)
     low = roots - high - middle
@@ -47,15 +46,17 @@
 
 def make_message(tokens, ids, weights):
     rows, width = tokens.shape
+    hits = ids[:, :, None] == jnp.arange(EXP, dtype=jnp.int32)[None, None, :]
+    table = jnp.sum(jnp.where(hits, weights[:, :, None], 0.0), axis=1)
     return pl.pallas_call(
         message_kernel,
         out_shape=jax.ShapeDtypeStruct((rows * width // LANES + TABLE, LANES), BF16),
-        in_specs=[VMEM] * 3,
+        in_specs=[VMEM] * 2,
         out_specs=VMEM,
         cost_estimate=SMALL,
         compiler_params=params(8),
         name="make_message",
-    )(tokens, ids.T, weights.T)
+    )(tokens, table.T)
 
 
 def block_of(piece, index):
@@ -195,27 +196,43 @@
     return product(left, right)
 
 
+def settle_kernel(before, left, right, tile):
+    tile[...] = before[...] + product(left, right)
+
+
+def settle(sums):
+    return pl.pallas_call(
+        settle_kernel,
+        out_shape=jax.ShapeDtypeStruct(sums[0].shape, F32),
+        in_specs=[VMEM] * 3,
+        out_specs=VMEM,
+        input_output_aliases={0: 0},
+        cost_estimate=SMALL,
+        compiler_params=params(14),
+        name="settle",
+    )(*sums)
+
+
 def take_own_kernel(*refs):
-    scalars, halves, before, refs = refs[0], refs[1:3], refs[3:6], refs[8:]
+    scalars, halves, before, refs = refs[0], refs[1:3], refs[3], refs[6:]
     tile, rows, across, left, right = refs
-    update = before[0][...] + product(before[1], before[2])
     at = rows.shape[0] - 2 * CAP
-    tile[...] = update + take_in(scalars, halves, at, rows, across, left, right)
-
-
-def take_own(scalars, halves, sums, operands):
-    edge = sums[0].shape[0]
+    tile[...] = before[...] + take_in(scalars, halves, at, rows, across, left, right)
+
+
+def take_own(scalars, halves, tile, operands):
+    edge = tile.shape[0]
     return pl.pallas_call(
         take_own_kernel,
-        out_shape=[jax.ShapeDtypeStruct(a.shape, a.dtype) for a in (sums[0], *operands)],
-        in_specs=[SMEM] + [VMEM] * 7,
+        out_shape=[jax.ShapeDtypeStruct(a.shape, a.dtype) for a in (tile, *operands)],
+        in_specs=[SMEM] + [VMEM] * 5,
         out_specs=[VMEM] * 3,
         scratch_shapes=[pltpu.VMEM((LANES, edge), BF16)] * 2,
-        input_output_aliases={3: 0, 6: 1, 7: 2},
+        input_output_aliases={3: 0, 4: 1, 5: 2},
         cost_estimate=SMALL,
         compiler_params=params(14),
         name="take_own",
-    )(scalars, *halves, *sums, *operands)
+    )(scalars, *halves, tile, *operands)
 
 
 def finish_kernel(final, *refs):
@@ -333,9 +350,9 @@
             back_of, operands, sums = lax.optimization_barrier((moved[1], operands, sums))
             moved = [ahead_of, back_of]
         pieces = moved
-    pieces, operands, sums = lax.optimization_barrier((pieces, operands, sums))
+    pieces, operands, tile = lax.optimization_barrier((pieces, operands, settle(sums)))
     others = [swap(piece) for piece in pieces]
-    tile, *operands = take_own(scalars, pieces, sums, operands)
+    tile, *operands = take_own(scalars, pieces, tile, operands)
     return tuple(finish(scalars, others, tile, operands, 1.0 / (devices * tok_rows)))
 
 

time: 96.8 us -> 95.7 us (0.989)
  local copies, waits for them, and re-layouts: 2.69 us -> 1.32 us
    unnamed x6 -> x2, local copies, waits for them, and re-layouts: 2.54 us -> 1.17 us
  transfers between devices with their start and end apart: 25 -> 25, of which waited for: 13 -> 12; matrix products, arithmetic and copies ran while one was open for 0% -> 0% of each run, Pallas kernels for 16% -> 17%
where the time goes in v13:
time: 95.7 us; the launch traced here: 95.5 us
  waiting for transfers between devices  51.5 us (54%)
  Pallas kernels  28.2 us (29%)
  starting transfers between devices  12.7 us (13%)
  local copies, waits for them, and re-layouts  1.32 us (1%)
  between operations  1.02 us (1%)
    ppermute x8, waiting for transfers between devices, advance(): lax.ppermute(array, 'tok', stream)  43.4 us
    pallas_call x1, Pallas kernels, finish(): pl.pallas_call(functools.partial(finish_kernel, final), out_shape=[jax.Sh...  12 us
    pallas_call x4, Pallas kernels, absorb(): pl.pallas_call(functools.partial(absorb_kernel, count, bool(before)), out...  9.82 us
    ppermute x8, starting transfers between devices, advance(): lax.ppermute(array, 'tok', stream)  9.21 us
    ppermute x17, waiting for transfers between devices, swap(): return lax.ppermute(array, 'tok', pair)  8.13 us
    ppermute x17, starting transfers between devices, swap(): return lax.ppermute(array, 'tok', pair)  3.5 us
    pallas_call x4, Pallas kernels, prepare(): pl.pallas_call(functools.partial(prepare_kernel, len(packs), at), out_sha...  3.21 us
    pallas_call x1, Pallas kernels, take_own(): pl.pallas_call(take_own_kernel, out_shape=[jax.ShapeDtypeStruct(a.shape,...  2.28 us
  transfers between devices with their start and end apart: 25, of which 12 were waited for; matrix products, arithmetic and copies ran while one was open for 0% of the time, Pallas kernels for 17%

profile of v13, /device:TPU:0, one launch (start us, length us, event | category | flops | bytes accessed | tf_op | source)
XLA Modules:
  0.0 95.5 jit_solution(14215714637282996851)
XLA Ops:
  0.6 0.7 select_reduce_fusion
  1.3 0.0 copy-start
  1.4 1.2 %copy-done = bf16[128,3584]{1,0:T(8,128)(2,1)S(1)} copy-done((bf16[128,3584]{1,0:T(8,128)(2,1)S(1)}, bf16[128,3584]{1,0:T(8,128)(2,1)}, u32[]{:S(2)}) %copy-start) | copy-done | bytes 917528
  2.5 0.2 make_message.1.refs_1_
  2.7 3.1 %collective-permute-start = (bf16[3616,128]{1,0:T(8,128)(2,1)S(1)}, bf16[3616,128]{1,0:T(8,128)(2,1)S(1)}, u32[]{:S(2)}, u32[]{:S(2)}) collective-permute-start(bf16[3616,128]{1,0:T(8,128)(2,1)S(1)} %make_message.1.refs_1_), channel_id=1, source_target_pairs={{0,4},{1,5},{4,8},{5,9},{8,12},{9,13},{12,14},{13,15},{14,10},{15,... | collective-permute-start | bytes 2777096 | tf_op jit(solution)/shard_map/ppermute | solution.py:330
  5.8 0.0 collective-permute-start.5
  5.8 0.1 stack.23.refs_0_
  5.9 1.5 %absorb.4 = (f32[896,896]{1,0:T(8,128)S(1)}, bf16[128,896]{1,0:T(8,128)(2,1)S(1)}, bf16[128,896]{1,0:T(8,128)(2,1)S(1)}, bf16[32,3584]{1,0:T(8,128)(2,1)S(1)}) custom-call(s32[5]{0:T(128)S(1)} %stack.23.refs_0_, bf16[3616,128]{1,0:T(8,128)(2,1)S(1)} %make_message.1.refs_1_), custom_call_target="tpu_custom_call" | custom-call | flops 1 | bytes 1 | tf_op jit(solution)/shard_map/absorb/pallas_call | solution.py:143
  7.4 0.1 collective-permute-start.1
  7.5 0.5 collective-permute-start.2
  8.0 0.1 collective-permute-start.3
  8.1 0.9 collective-permute-done.1.refs_2_
  9.0 0.8 prepare_rows.4
  9.8 0.0 collective-permute-done.2.refs_4_
  9.8 0.0 collective-permute-done.3.refs_5_
  9.8 16.5 %collective-permute-done.refs_1_ = bf16[3616,128]{1,0:T(8,128)(2,1)S(1)} collective-permute-done((bf16[3616,128]{1,0:T(8,128)(2,1)S(1)}, bf16[3616,128]{1,0:T(8,128)(2,1)S(1)}, u32[]{:S(2)}, u32[]{:S(2)}) %collective-permute-start) | collective-permute-done | bytes 925728 | tf_op jit(solution)/shard_map/ppermute | solution.py:330
  26.3 1.8 %collective-permute-start.4 = (bf16[3616,128]{1,0:T(8,128)(2,1)S(1)}, bf16[3616,128]{1,0:T(8,128)(2,1)S(1)}, u32[]{:S(2)}, u32[]{:S(2)}) collective-permute-start(bf16[3616,128]{1,0:T(8,128)(2,1)S(1)} %collective-permute-done.refs_1_), channel_id=1, source_target_pairs={{0,4},{1,5},{4,8},{5,9},{8,12},{9,13},{12,14},{13,15},{14,10},{15,... | collective-permute-start | bytes 2777096 | tf_op jit(solution)/shard_map/ppermute | solution.py:330
  28.1 0.0 collective-permute-done.5.refs_2_
  28.1 0.2 collective-permute-start.11
  28.3 2.7 %absorb.5 = (f32[896,896]{1,0:T(8,128)S(1)}, bf16[256,896]{1,0:T(8,128)(2,1)S(1)}, bf16[256,896]{1,0:T(8,128)(2,1)S(1)}, bf16[32,3584]{1,0:T(8,128)(2,1)S(1)}, bf16[32,3584]{1,0:T(8,128)(2,1)S(1)}) custom-call(s32[5]{0:T(128)S(1)} %stack.23.refs_0_, bf16[3616,128]{1,0:T(8,128)(2,1)S(1)} %collective-permute-done.refs_1_, ...), custom_call_target="tpu_custom_call", output_to_operand_aliasing={{0}: (3, {})} | custom-call | flops 1 | bytes 1 | tf_op jit(solution)/shard_map/absorb/pallas_call | solution.py:143
  30.9 0.1 collective-permute-start.6
  31.0 0.5 collective-permute-start.8
  31.5 0.1 collective-permute-start.9
  31.6 0.9 collective-permute-done.6.refs_3_
  32.5 0.1 collective-permute-start.7
  32.6 1.5 %collective-permute-done.7.refs_4_ = bf16[32,3584]{1,0:T(8,128)(2,1)S(1)} collective-permute-done((bf16[32,3584]{1,0:T(8,128)(2,1)S(1)}, bf16[32,3584]{1,0:T(8,128)(2,1)S(1)}, u32[]{:S(2)}, u32[]{:S(2)}) %collective-permute-start.7) | collective-permute-done | bytes 229408 | tf_op jit(solution)/shard_map/ppermute | solution.py:327
  34.1 0.8 prepare_rows.5
  35.0 0.0 collective-permute-done.8.refs_4_
  35.0 0.0 collective-permute-done.9.refs_5_
  35.0 13.0 %collective-permute-done.4.refs_1_ = bf16[3616,128]{1,0:T(8,128)(2,1)S(1)} collective-permute-done((bf16[3616,128]{1,0:T(8,128)(2,1)S(1)}, bf16[3616,128]{1,0:T(8,128)(2,1)S(1)}, u32[]{:S(2)}, u32[]{:S(2)}) %collective-permute-start.4) | collective-permute-done | bytes 925728 | tf_op jit(solution)/shard_map/ppermute | solution.py:330
  48.0 1.5 %collective-permute-start.10 = (bf16[3616,128]{1,0:T(8,128)(2,1)S(1)}, bf16[3616,128]{1,0:T(8,128)(2,1)S(1)}, u32[]{:S(2)}, u32[]{:S(2)}) collective-permute-start(bf16[3616,128]{1,0:T(8,128)(2,1)S(1)} %collective-permute-done.4.refs_1_), channel_id=1, source_target_pairs={{0,4},{1,5},{4,8},{5,9},{8,12},{9,13},{12,14},{13,15},{14,10},{15,... | collective-permute-start | bytes 2777096 | tf_op jit(solution)/shard_map/ppermute | solution.py:330
  49.5 0.5 collective-permute-start.17
  50.0 2.7 %absorb.6 = (f32[896,896]{1,0:T(8,128)S(1)}, bf16[256,896]{1,0:T(8,128)(2,1)S(1)}, bf16[256,896]{1,0:T(8,128)(2,1)S(1)}, bf16[32,3584]{1,0:T(8,128)(2,1)S(1)}, bf16[32,3584]{1,0:T(8,128)(2,1)S(1)}) custom-call(s32[5]{0:T(128)S(1)} %stack.23.refs_0_, bf16[3616,128]{1,0:T(8,128)(2,1)S(1)} %collective-permute-done.4.refs_1_, ...), custom_call_target="tpu_custom_call", output_to_operand_aliasing={{0}: (3, {})} | custom-call | flops 1 | bytes 1 | tf_op jit(solution)/shard_map/absorb/pallas_call | solution.py:143
  52.7 0.1 collective-permute-start.12
  52.8 0.5 collective-permute-start.14
  53.3 0.1 collective-permute-start.15
  53.4 0.9 collective-permute-done.12.refs_3_
  54.3 0.1 collective-permute-start.13
  54.4 1.5 %collective-permute-done.13.refs_4_ = bf16[32,3584]{1,0:T(8,128)(2,1)S(1)} collective-permute-done((bf16[32,3584]{1,0:T(8,128)(2,1)S(1)}, bf16[32,3584]{1,0:T(8,128)(2,1)S(1)}, u32[]{:S(2)}, u32[]{:S(2)}) %collective-permute-start.13) | collective-permute-done | bytes 229408 | tf_op jit(solution)/shard_map/ppermute | solution.py:327
  55.9 0.8 prepare_rows.6
  56.8 0.0 collective-permute-done.14.refs_4_
  56.8 0.0 collective-permute-done.15.refs_5_
  56.8 12.0 %collective-permute-done.10.refs_1_ = bf16[3616,128]{1,0:T(8,128)(2,1)S(1)} collective-permute-done((bf16[3616,128]{1,0:T(8,128)(2,1)S(1)}, bf16[3616,128]{1,0:T(8,128)(2,1)S(1)}, u32[]{:S(2)}, u32[]{:S(2)}) %collective-permute-start.10) | collective-permute-done | bytes 925728 | tf_op jit(solution)/shard_map/ppermute | solution.py:330
  68.8 0.9 collective-permute-done.17.refs_2_
  69.7 1.6 %collective-permute-start.16 = (bf16[1824,128]{1,0:T(8,128)(2,1)S(1)}, bf16[1824,128]{1,0:T(8,128)(2,1)S(1)}, u32[]{:S(2)}, u32[]{:S(2)}) collective-permute-start(bf16[1824,128]{1,0:T(8,128)(2,1)S(1)} %slice.6), channel_id=1, source_target_pairs={{0,4},{1,5},{4,8},{5,9},{8,12},{9,13},{12,14},{13,15},{14,10},{15,... | collective-permute-start | bytes 1400840 | tf_op jit(solution)/shard_map/ppermute | solution.py:330
  71.4 0.4 collective-permute-start.18
  71.8 2.9 %absorb.7 = (f32[896,896]{1,0:T(8,128)S(1)}, bf16[256,896]{1,0:T(8,128)(2,1)S(1)}, bf16[256,896]{1,0:T(8,128)(2,1)S(1)}, bf16[32,3584]{1,0:T(8,128)(2,1)S(1)}, bf16[32,3584]{1,0:T(8,128)(2,1)S(1)}) custom-call(s32[5]{0:T(128)S(1)} %stack.23.refs_0_, bf16[3616,128]{1,0:T(8,128)(2,1)S(1)} %collective-permute-done.10.refs_1_, ...), custom_call_target="tpu_custom_call", output_to_operand_aliasing={{0}: (3, {})} | custom-call | flops 1 | bytes 1 | tf_op jit(solution)/shard_map/absorb/pallas_call | solution.py:143
  74.7 0.1 collective-permute-start.19
  74.8 0.5 collective-permute-start.21
  75.3 0.1 collective-permute-start.22
  75.4 0.9 collective-permute-done.19.refs_3_
  76.3 0.1 collective-permute-start.20
  76.4 1.5 %collective-permute-done.20.refs_4_ = bf16[32,3584]{1,0:T(8,128)(2,1)S(1)} collective-permute-done((bf16[32,3584]{1,0:T(8,128)(2,1)S(1)}, bf16[32,3584]{1,0:T(8,128)(2,1)S(1)}, u32[]{:S(2)}, u32[]{:S(2)}) %collective-permute-start.20) | collective-permute-done | bytes 229408 | tf_op jit(solution)/shard_map/ppermute | solution.py:327
  77.9 0.8 prepare_rows.7
  78.7 0.0 collective-permute-done.21.left
  78.7 0.0 collective-permute-done.22.right
  78.8 0.7 settle.1.refs_3_
  79.5 0.0 collective-permute-done.16.refs_1_
  79.5 1.0 %collective-permute-done.18.refs_2_ = bf16[1824,128]{1,0:T(8,128)(2,1)S(1)} collective-permute-done((bf16[1824,128]{1,0:T(8,128)(2,1)S(1)}, bf16[1824,128]{1,0:T(8,128)(2,1)S(1)}, u32[]{:S(2)}, u32[]{:S(2)}) %collective-permute-start.18) | collective-permute-done | bytes 466976 | tf_op jit(solution)/shard_map/ppermute | solution.py:330
  80.5 0.5 collective-permute-start.24
  81.0 2.3 %take_own.1 = (f32[896,896]{1,0:T(8,128)S(1)}, bf16[512,3584]{1,0:T(8,128)(2,1)S(1)}, bf16[1792,512]{1,0:T(8,128)(2,1)S(1)}) custom-call(s32[5]{0:T(128)S(1)} %stack.23.refs_0_, bf16[1824,128]{1,0:T(8,128)(2,1)S(1)} %collective-permute-done.16.refs_1_, ...), custom_call_target="tpu_custom_call", output_to_operand_aliasing={{0}: (3, {}), {1}: (4, {}), {2}: (5, {})} | custom-call | flops 1 | bytes 1 | tf_op jit(solution)/shard_map/take_own/pallas_call | solution.py:225
  83.3 0.0 collective-permute-done.23.refs_1_
  83.3 0.0 collective-permute-done.24.refs_2_
  83.3 12.0 %finish.1 = (f32[1792,3584]{1,0:T(8,128)}, f32[1,896,896]{2,1,0:T(8,128)}, bf16[512,3584]{1,0:T(8,128)(2,1)S(1)}, bf16[1792,512]{1,0:T(8,128)(2,1)S(1)}) custom-call(s32[5]{0:T(128)S(1)} %stack.23.refs_0_, bf16[1824,128]{1,0:T(8,128)(2,1)S(1)} %collective-permute-done.23.refs_1_, ...), custom_call_target="tpu_custom_call", output_to_operand_aliasing={{2}: (4, {}), {3}: (5, {})} | custom-call | flops 1 | bytes 1 | tf_op jit(solution)/shard_map/finish/pallas_call | solution.py:270
  (4 shorter events, 0.1 us)
Async XLA Ops:
  1.3 1.2 %copy-start = (bf16[128,3584]{1,0:T(8,128)(2,1)S(1)}, bf16[128,3584]{1,0:T(8,128)(2,1)}, u32[]{:S(2)}) copy-start(bf16[128,3584]{1,0:T(8,128)(2,1)} %tokens.1) | copy-start | bytes 2752516
  2.7 23.5 %collective-permute-start = (bf16[3616,128]{1,0:T(8,128)(2,1)S(1)}, bf16[3616,128]{1,0:T(8,128)(2,1)S(1)}, u32[]{:S(2)}, u32[]{:S(2)}) collective-permute-start(bf16[3616,128]{1,0:T(8,128)(2,1)S(1)} %make_message.1.refs_1_), channel_id=1, source_target_pairs={{0,4},{1,5},{4,8},{5,9},{8,12},{9,13},{12,14},{13,15},{14,10},{15,... | collective-permute-start | bytes 2777096 | tf_op jit(solution)/shard_map/ppermute | solution.py:330
  5.8 22.3 %collective-permute-start.5 = (bf16[3616,128]{1,0:T(8,128)(2,1)S(1)}, bf16[3616,128]{1,0:T(8,128)(2,1)S(1)}, u32[]{:S(2)}, u32[]{:S(2)}) collective-permute-start(bf16[3616,128]{1,0:T(8,128)(2,1)S(1)} %make_message.1.refs_1_), channel_id=1, source_target_pairs={{4,0},{5,1},{8,4},{9,5},{12,8},{13,9},{14,12},{15,13},{10,14},{11,... | collective-permute-start | bytes 2777096 | tf_op jit(solution)/shard_map/ppermute | solution.py:330
  7.4 1.6 %collective-permute-start.1 = (bf16[32,3584]{1,0:T(8,128)(2,1)S(1)}, bf16[32,3584]{1,0:T(8,128)(2,1)S(1)}, u32[]{:S(2)}, u32[]{:S(2)}) collective-permute-start(bf16[32,3584]{1,0:T(8,128)(2,1)S(1)} %get-tuple-element.75.refs_1_), channel_id=1, source_target_pairs={{0,1},{1,0},{2,3},{3,2},{4,5},{5,4},{6,7},{7,6},{8,9},{9,8},{10,11... | collective-permute-start | bytes 688136 | tf_op jit(solution)/shard_map/ppermute | solution.py:327
  7.5 2.2 %collective-permute-start.2 = (bf16[128,896]{1,0:T(8,128)(2,1)S(1)}, bf16[128,896]{1,0:T(8,128)(2,1)S(1)}, u32[]{:S(2)}, u32[]{:S(2)}) collective-permute-start(bf16[128,896]{1,0:T(8,128)(2,1)S(1)} %get-tuple-element.79), channel_id=1, source_target_pairs={{0,1},{1,0},{2,3},{3,2},{4,5},{5,4},{6,7},{7,6},{8,9},{9,8},{10,11... | collective-permute-start | bytes 688136 | tf_op jit(solution)/shard_map/ppermute | solution.py:327
  8.0 1.8 %collective-permute-start.3 = (bf16[128,896]{1,0:T(8,128)(2,1)S(1)}, bf16[128,896]{1,0:T(8,128)(2,1)S(1)}, u32[]{:S(2)}, u32[]{:S(2)}) collective-permute-start(bf16[128,896]{1,0:T(8,128)(2,1)S(1)} %get-tuple-element.80), channel_id=1, source_target_pairs={{0,1},{1,0},{2,3},{3,2},{4,5},{5,4},{6,7},{7,6},{8,9},{9,8},{10,11... | collective-permute-start | bytes 688136 | tf_op jit(solution)/shard_map/ppermute | solution.py:327
  26.3 21.7 %collective-permute-start.4 = (bf16[3616,128]{1,0:T(8,128)(2,1)S(1)}, bf16[3616,128]{1,0:T(8,128)(2,1)S(1)}, u32[]{:S(2)}, u32[]{:S(2)}) collective-permute-start(bf16[3616,128]{1,0:T(8,128)(2,1)S(1)} %collective-permute-done.refs_1_), channel_id=1, source_target_pairs={{0,4},{1,5},{4,8},{5,9},{8,12},{9,13},{12,14},{13,15},{14,10},{15,... | collective-permute-start | bytes 2777096 | tf_op jit(solution)/shard_map/ppermute | solution.py:330
  28.1 21.4 %collective-permute-start.11 = (bf16[3616,128]{1,0:T(8,128)(2,1)S(1)}, bf16[3616,128]{1,0:T(8,128)(2,1)S(1)}, u32[]{:S(2)}, u32[]{:S(2)}) collective-permute-start(bf16[3616,128]{1,0:T(8,128)(2,1)S(1)} %collective-permute-done.5.refs_2_), channel_id=1, source_target_pairs={{4,0},{5,1},{8,4},{9,5},{12,8},{13,9},{14,12},{15,13},{10,14},{11,... | collective-permute-start | bytes 2777096 | tf_op jit(solution)/shard_map/ppermute | solution.py:330
  30.9 1.6 %collective-permute-start.6 = (bf16[32,3584]{1,0:T(8,128)(2,1)S(1)}, bf16[32,3584]{1,0:T(8,128)(2,1)S(1)}, u32[]{:S(2)}, u32[]{:S(2)}) collective-permute-start(bf16[32,3584]{1,0:T(8,128)(2,1)S(1)} %get-tuple-element.91.refs_1_), channel_id=1, source_target_pairs={{0,1},{1,0},{2,3},{3,2},{4,5},{5,4},{6,7},{7,6},{8,9},{9,8},{10,11... | collective-permute-start | bytes 688136 | tf_op jit(solution)/shard_map/ppermute | solution.py:327
  31.0 3.9 %collective-permute-start.8 = (bf16[256,896]{1,0:T(8,128)(2,1)S(1)}, bf16[256,896]{1,0:T(8,128)(2,1)S(1)}, u32[]{:S(2)}, u32[]{:S(2)}) collective-permute-start(bf16[256,896]{1,0:T(8,128)(2,1)S(1)} %get-tuple-element.98), channel_id=1, source_target_pairs={{0,1},{1,0},{2,3},{3,2},{4,5},{5,4},{6,7},{7,6},{8,9},{9,8},{10,11... | collective-permute-start | bytes 1376264 | tf_op jit(solution)/shard_map/ppermute | solution.py:327
  31.5 3.5 %collective-permute-start.9 = (bf16[256,896]{1,0:T(8,128)(2,1)S(1)}, bf16[256,896]{1,0:T(8,128)(2,1)S(1)}, u32[]{:S(2)}, u32[]{:S(2)}) collective-permute-start(bf16[256,896]{1,0:T(8,128)(2,1)S(1)} %get-tuple-element.99), channel_id=1, source_target_pairs={{0,1},{1,0},{2,3},{3,2},{4,5},{5,4},{6,7},{7,6},{8,9},{9,8},{10,11... | collective-permute-start | bytes 1376264 | tf_op jit(solution)/shard_map/ppermute | solution.py:327
  32.5 1.6 %collective-permute-start.7 = (bf16[32,3584]{1,0:T(8,128)(2,1)S(1)}, bf16[32,3584]{1,0:T(8,128)(2,1)S(1)}, u32[]{:S(2)}, u32[]{:S(2)}) collective-permute-start(bf16[32,3584]{1,0:T(8,128)(2,1)S(1)} %get-tuple-element.92.refs_2_), channel_id=1, source_target_pairs={{0,1},{1,0},{2,3},{3,2},{4,5},{5,4},{6,7},{7,6},{8,9},{9,8},{10,11... | collective-permute-start | bytes 688136 | tf_op jit(solution)/shard_map/ppermute | solution.py:327
  48.0 20.8 %collective-permute-start.10 = (bf16[3616,128]{1,0:T(8,128)(2,1)S(1)}, bf16[3616,128]{1,0:T(8,128)(2,1)S(1)}, u32[]{:S(2)}, u32[]{:S(2)}) collective-permute-start(bf16[3616,128]{1,0:T(8,128)(2,1)S(1)} %collective-permute-done.4.refs_1_), channel_id=1, source_target_pairs={{0,4},{1,5},{4,8},{5,9},{8,12},{9,13},{12,14},{13,15},{14,10},{15,... | collective-permute-start | bytes 2777096 | tf_op jit(solution)/shard_map/ppermute | solution.py:330
  49.5 20.2 %collective-permute-start.17 = (bf16[3616,128]{1,0:T(8,128)(2,1)S(1)}, bf16[3616,128]{1,0:T(8,128)(2,1)S(1)}, u32[]{:S(2)}, u32[]{:S(2)}) collective-permute-start(bf16[3616,128]{1,0:T(8,128)(2,1)S(1)} %collective-permute-done.11.refs_2_), channel_id=1, source_target_pairs={{4,0},{5,1},{8,4},{9,5},{12,8},{13,9},{14,12},{15,13},{10,14},{11,... | collective-permute-start | bytes 2777096 | tf_op jit(solution)/shard_map/ppermute | solution.py:330
  52.7 1.6 %collective-permute-start.12 = (bf16[32,3584]{1,0:T(8,128)(2,1)S(1)}, bf16[32,3584]{1,0:T(8,128)(2,1)S(1)}, u32[]{:S(2)}, u32[]{:S(2)}) collective-permute-start(bf16[32,3584]{1,0:T(8,128)(2,1)S(1)} %get-tuple-element.110.refs_1_), channel_id=1, source_target_pairs={{0,1},{1,0},{2,3},{3,2},{4,5},{5,4},{6,7},{7,6},{8,9},{9,8},{10,11... | collective-permute-start | bytes 688136 | tf_op jit(solution)/shard_map/ppermute | solution.py:327
  52.8 3.9 %collective-permute-start.14 = (bf16[256,896]{1,0:T(8,128)(2,1)S(1)}, bf16[256,896]{1,0:T(8,128)(2,1)S(1)}, u32[]{:S(2)}, u32[]{:S(2)}) collective-permute-start(bf16[256,896]{1,0:T(8,128)(2,1)S(1)} %get-tuple-element.117), channel_id=1, source_target_pairs={{0,1},{1,0},{2,3},{3,2},{4,5},{5,4},{6,7},{7,6},{8,9},{9,8},{10,11... | collective-permute-start | bytes 1376264 | tf_op jit(solution)/shard_map/ppermute | solution.py:327
  53.3 3.5 %collective-permute-start.15 = (bf16[256,896]{1,0:T(8,128)(2,1)S(1)}, bf16[256,896]{1,0:T(8,128)(2,1)S(1)}, u32[]{:S(2)}, u32[]{:S(2)}) collective-permute-start(bf16[256,896]{1,0:T(8,128)(2,1)S(1)} %get-tuple-element.118), channel_id=1, source_target_pairs={{0,1},{1,0},{2,3},{3,2},{4,5},{5,4},{6,7},{7,6},{8,9},{9,8},{10,11... | collective-permute-start | bytes 1376264 | tf_op jit(solution)/shard_map/ppermute | solution.py:327
  54.3 1.6 %collective-permute-start.13 = (bf16[32,3584]{1,0:T(8,128)(2,1)S(1)}, bf16[32,3584]{1,0:T(8,128)(2,1)S(1)}, u32[]{:S(2)}, u32[]{:S(2)}) collective-permute-start(bf16[32,3584]{1,0:T(8,128)(2,1)S(1)} %get-tuple-element.111.refs_2_), channel_id=1, source_target_pairs={{0,1},{1,0},{2,3},{3,2},{4,5},{5,4},{6,7},{7,6},{8,9},{9,8},{10,11... | collective-permute-start | bytes 688136 | tf_op jit(solution)/shard_map/ppermute | solution.py:327
  69.7 9.8 %collective-permute-start.16 = (bf16[1824,128]{1,0:T(8,128)(2,1)S(1)}, bf16[1824,128]{1,0:T(8,128)(2,1)S(1)}, u32[]{:S(2)}, u32[]{:S(2)}) collective-permute-start(bf16[1824,128]{1,0:T(8,128)(2,1)S(1)} %slice.6), channel_id=1, source_target_pairs={{0,4},{1,5},{4,8},{5,9},{8,12},{9,13},{12,14},{13,15},{14,10},{15,... | collective-permute-start | bytes 1400840 | tf_op jit(solution)/shard_map/ppermute | solution.py:330
  71.4 9.2 %collective-permute-start.18 = (bf16[1824,128]{1,0:T(8,128)(2,1)S(1)}, bf16[1824,128]{1,0:T(8,128)(2,1)S(1)}, u32[]{:S(2)}, u32[]{:S(2)}) collective-permute-start(bf16[1824,128]{1,0:T(8,128)(2,1)S(1)} %slice.7), channel_id=1, source_target_pairs={{4,0},{5,1},{8,4},{9,5},{12,8},{13,9},{14,12},{15,13},{10,14},{11,... | collective-permute-start | bytes 1400840 | tf_op jit(solution)/shard_map/ppermute | solution.py:330
  74.7 1.6 %collective-permute-start.19 = (bf16[32,3584]{1,0:T(8,128)(2,1)S(1)}, bf16[32,3584]{1,0:T(8,128)(2,1)S(1)}, u32[]{:S(2)}, u32[]{:S(2)}) collective-permute-start(bf16[32,3584]{1,0:T(8,128)(2,1)S(1)} %get-tuple-element.129.refs_1_), channel_id=1, source_target_pairs={{0,1},{1,0},{2,3},{3,2},{4,5},{5,4},{6,7},{7,6},{8,9},{9,8},{10,11... | collective-permute-start | bytes 688136 | tf_op jit(solution)/shard_map/ppermute | solution.py:327
  74.8 3.9 %collective-permute-start.21 = (bf16[256,896]{1,0:T(8,128)(2,1)S(1)}, bf16[256,896]{1,0:T(8,128)(2,1)S(1)}, u32[]{:S(2)}, u32[]{:S(2)}) collective-permute-start(bf16[256,896]{1,0:T(8,128)(2,1)S(1)} %get-tuple-element.136), channel_id=1, source_target_pairs={{0,1},{1,0},{2,3},{3,2},{4,5},{5,4},{6,7},{7,6},{8,9},{9,8},{10,11... | collective-permute-start | bytes 1376264 | tf_op jit(solution)/shard_map/ppermute | solution.py:327
  75.3 3.5 %collective-permute-start.22 = (bf16[256,896]{1,0:T(8,128)(2,1)S(1)}, bf16[256,896]{1,0:T(8,128)(2,1)S(1)}, u32[]{:S(2)}, u32[]{:S(2)}) collective-permute-start(bf16[256,896]{1,0:T(8,128)(2,1)S(1)} %get-tuple-element.137), channel_id=1, source_target_pairs={{0,1},{1,0},{2,3},{3,2},{4,5},{5,4},{6,7},{7,6},{8,9},{9,8},{10,11... | collective-permute-start | bytes 1376264 | tf_op jit(solution)/shard_map/ppermute | solution.py:327
  76.3 1.6 %collective-permute-start.20 = (bf16[32,3584]{1,0:T(8,128)(2,1)S(1)}, bf16[32,3584]{1,0:T(8,128)(2,1)S(1)}, u32[]{:S(2)}, u32[]{:S(2)}) collective-permute-start(bf16[32,3584]{1,0:T(8,128)(2,1)S(1)} %get-tuple-element.130.refs_2_), channel_id=1, source_target_pairs={{0,1},{1,0},{2,3},{3,2},{4,5},{5,4},{6,7},{7,6},{8,9},{9,8},{10,11... | collective-permute-start | bytes 688136 | tf_op jit(solution)/shard_map/ppermute | solution.py:327
  80.5 2.8 %collective-permute-start.23 = (bf16[1824,128]{1,0:T(8,128)(2,1)S(1)}, bf16[1824,128]{1,0:T(8,128)(2,1)S(1)}, u32[]{:S(2)}, u32[]{:S(2)}) collective-permute-start(bf16[1824,128]{1,0:T(8,128)(2,1)S(1)} %collective-permute-done.16.refs_1_), channel_id=1, source_target_pairs={{0,1},{1,0},{2,3},{3,2},{4,5},{5,4},{6,7},{7,6},{8,9},{9,8},{10,11... | collective-permute-start | bytes 1400840 | tf_op jit(solution)/shard_map/ppermute | solution.py:327
  80.5 2.8 %collective-permute-start.24 = (bf16[1824,128]{1,0:T(8,128)(2,1)S(1)}, bf16[1824,128]{1,0:T(8,128)(2,1)S(1)}, u32[]{:S(2)}, u32[]{:S(2)}) collective-permute-start(bf16[1824,128]{1,0:T(8,128)(2,1)S(1)} %collective-permute-done.18.refs_2_), channel_id=1, source_target_pairs={{0,1},{1,0},{2,3},{3,2},{4,5},{5,4},{6,7},{7,6},{8,9},{9,8},{10,11... | collective-permute-start | bytes 1400840 | tf_op jit(solution)/shard_map/ppermute | solution.py:327

commit v14 on v13

--- a/solution.py
+++ b/solution.py
@@ -245,7 +245,7 @@
 
     def write(source, target):
         copies.append(pltpu.make_async_copy(source, target, sent.at[len(copies)]))
-        copies[-1].start()
+        copies[-1].start(priority=len(copies) % 2)
 
     update = take_in(scalars, halves, at, rows, across, left, right)
     sums[...] = (before[...] + update) * final

time: 95.7 us -> 95.7 us (level)
  no operation moved by 1% of the time
where the time goes in v14:
time: 95.7 us; the launch traced here: 95.5 us
  waiting for transfers between devices  51.5 us (54%)
  Pallas kernels  28.2 us (29%)
  starting transfers between devices  12.7 us (13%)
  local copies, waits for them, and re-layouts  1.32 us (1%)
  between operations  1.02 us (1%)
    ppermute x8, waiting for transfers between devices, advance(): lax.ppermute(array, 'tok', stream)  43.4 us
    pallas_call x1, Pallas kernels, finish(): pl.pallas_call(functools.partial(finish_kernel, final), out_shape=[jax.Sh...  12 us
    pallas_call x4, Pallas kernels, absorb(): pl.pallas_call(functools.partial(absorb_kernel, count, bool(before)), out...  9.82 us
    ppermute x8, starting transfers between devices, advance(): lax.ppermute(array, 'tok', stream)  9.21 us
    ppermute x17, waiting for transfers between devices, swap(): return lax.ppermute(array, 'tok', pair)  8.13 us
    ppermute x17, starting transfers between devices, swap(): return lax.ppermute(array, 'tok', pair)  3.5 us
    pallas_call x4, Pallas kernels, prepare(): pl.pallas_call(functools.partial(prepare_kernel, len(packs), at), out_sha...  3.21 us
    pallas_call x1, Pallas kernels, take_own(): pl.pallas_call(take_own_kernel, out_shape=[jax.ShapeDtypeStruct(a.shape,...  2.28 us
  transfers between devices with their start and end apart: 25, of which 12 were waited for; matrix products, arithmetic and copies ran while one was open for 0% of the time, Pallas kernels for 17%

profile of v14, /device:TPU:0, one launch (start us, length us, event | category | flops | bytes accessed | tf_op | source)
XLA Modules:
  0.0 95.5 jit_solution(4177897574292547870)
XLA Ops:
  0.6 0.7 select_reduce_fusion
  1.3 0.0 copy-start
  1.4 1.2 %copy-done = bf16[128,3584]{1,0:T(8,128)(2,1)S(1)} copy-done((bf16[128,3584]{1,0:T(8,128)(2,1)S(1)}, bf16[128,3584]{1,0:T(8,128)(2,1)}, u32[]{:S(2)}) %copy-start) | copy-done | bytes 917528
  2.5 0.2 make_message.1.refs_1_
  2.7 3.1 %collective-permute-start = (bf16[3616,128]{1,0:T(8,128)(2,1)S(1)}, bf16[3616,128]{1,0:T(8,128)(2,1)S(1)}, u32[]{:S(2)}, u32[]{:S(2)}) collective-permute-start(bf16[3616,128]{1,0:T(8,128)(2,1)S(1)} %make_message.1.refs_1_), channel_id=1, source_target_pairs={{0,4},{1,5},{4,8},{5,9},{8,12},{9,13},{12,14},{13,15},{14,10},{15,... | collective-permute-start | bytes 2777096 | tf_op jit(solution)/shard_map/ppermute | solution.py:330
  5.8 0.0 collective-permute-start.5
  5.8 0.1 stack.23.refs_0_
  5.9 1.5 %absorb.4 = (f32[896,896]{1,0:T(8,128)S(1)}, bf16[128,896]{1,0:T(8,128)(2,1)S(1)}, bf16[128,896]{1,0:T(8,128)(2,1)S(1)}, bf16[32,3584]{1,0:T(8,128)(2,1)S(1)}) custom-call(s32[5]{0:T(128)S(1)} %stack.23.refs_0_, bf16[3616,128]{1,0:T(8,128)(2,1)S(1)} %make_message.1.refs_1_), custom_call_target="tpu_custom_call" | custom-call | flops 1 | bytes 1 | tf_op jit(solution)/shard_map/absorb/pallas_call | solution.py:143
  7.4 0.1 collective-permute-start.1
  7.5 0.5 collective-permute-start.2
  8.0 0.1 collective-permute-start.3
  8.1 0.9 collective-permute-done.1.refs_2_
  9.0 0.8 prepare_rows.4
  9.8 0.0 collective-permute-done.2.refs_4_
  9.8 0.0 collective-permute-done.3.refs_5_
  9.8 16.5 %collective-permute-done.refs_1_ = bf16[3616,128]{1,0:T(8,128)(2,1)S(1)} collective-permute-done((bf16[3616,128]{1,0:T(8,128)(2,1)S(1)}, bf16[3616,128]{1,0:T(8,128)(2,1)S(1)}, u32[]{:S(2)}, u32[]{:S(2)}) %collective-permute-start) | collective-permute-done | bytes 925728 | tf_op jit(solution)/shard_map/ppermute | solution.py:330
  26.3 1.8 %collective-permute-start.4 = (bf16[3616,128]{1,0:T(8,128)(2,1)S(1)}, bf16[3616,128]{1,0:T(8,128)(2,1)S(1)}, u32[]{:S(2)}, u32[]{:S(2)}) collective-permute-start(bf16[3616,128]{1,0:T(8,128)(2,1)S(1)} %collective-permute-done.refs_1_), channel_id=1, source_target_pairs={{0,4},{1,5},{4,8},{5,9},{8,12},{9,13},{12,14},{13,15},{14,10},{15,... | collective-permute-start | bytes 2777096 | tf_op jit(solution)/shard_map/ppermute | solution.py:330
  28.1 0.0 collective-permute-done.5.refs_2_
  28.1 0.2 collective-permute-start.11
  28.3 2.7 %absorb.5 = (f32[896,896]{1,0:T(8,128)S(1)}, bf16[256,896]{1,0:T(8,128)(2,1)S(1)}, bf16[256,896]{1,0:T(8,128)(2,1)S(1)}, bf16[32,3584]{1,0:T(8,128)(2,1)S(1)}, bf16[32,3584]{1,0:T(8,128)(2,1)S(1)}) custom-call(s32[5]{0:T(128)S(1)} %stack.23.refs_0_, bf16[3616,128]{1,0:T(8,128)(2,1)S(1)} %collective-permute-done.refs_1_, ...), custom_call_target="tpu_custom_call", output_to_operand_aliasing={{0}: (3, {})} | custom-call | flops 1 | bytes 1 | tf_op jit(solution)/shard_map/absorb/pallas_call | solution.py:143
  30.9 0.1 collective-permute-start.6
  31.0 0.5 collective-permute-start.8
  31.5 0.1 collective-permute-start.9
  31.6 0.9 collective-permute-done.6.refs_3_
  32.5 0.1 collective-permute-start.7
  32.6 1.5 %collective-permute-done.7.refs_4_ = bf16[32,3584]{1,0:T(8,128)(2,1)S(1)} collective-permute-done((bf16[32,3584]{1,0:T(8,128)(2,1)S(1)}, bf16[32,3584]{1,0:T(8,128)(2,1)S(1)}, u32[]{:S(2)}, u32[]{:S(2)}) %collective-permute-start.7) | collective-permute-done | bytes 229408 | tf_op jit(solution)/shard_map/ppermute | solution.py:327
  34.1 0.8 prepare_rows.5
  35.0 0.0 collective-permute-done.8.refs_4_
  35.0 0.0 collective-permute-done.9.refs_5_
  35.0 13.0 %collective-permute-done.4.refs_1_ = bf16[3616,128]{1,0:T(8,128)(2,1)S(1)} collective-permute-done((bf16[3616,128]{1,0:T(8,128)(2,1)S(1)}, bf16[3616,128]{1,0:T(8,128)(2,1)S(1)}, u32[]{:S(2)}, u32[]{:S(2)}) %collective-permute-start.4) | collective-permute-done | bytes 925728 | tf_op jit(solution)/shard_map/ppermute | solution.py:330
  48.0 1.5 %collective-permute-start.10 = (bf16[3616,128]{1,0:T(8,128)(2,1)S(1)}, bf16[3616,128]{1,0:T(8,128)(2,1)S(1)}, u32[]{:S(2)}, u32[]{:S(2)}) collective-permute-start(bf16[3616,128]{1,0:T(8,128)(2,1)S(1)} %collective-permute-done.4.refs_1_), channel_id=1, source_target_pairs={{0,4},{1,5},{4,8},{5,9},{8,12},{9,13},{12,14},{13,15},{14,10},{15,... | collective-permute-start | bytes 2777096 | tf_op jit(solution)/shard_map/ppermute | solution.py:330
  49.5 0.5 collective-permute-start.17
  50.0 2.7 %absorb.6 = (f32[896,896]{1,0:T(8,128)S(1)}, bf16[256,896]{1,0:T(8,128)(2,1)S(1)}, bf16[256,896]{1,0:T(8,128)(2,1)S(1)}, bf16[32,3584]{1,0:T(8,128)(2,1)S(1)}, bf16[32,3584]{1,0:T(8,128)(2,1)S(1)}) custom-call(s32[5]{0:T(128)S(1)} %stack.23.refs_0_, bf16[3616,128]{1,0:T(8,128)(2,1)S(1)} %collective-permute-done.4.refs_1_, ...), custom_call_target="tpu_custom_call", output_to_operand_aliasing={{0}: (3, {})} | custom-call | flops 1 | bytes 1 | tf_op jit(solution)/shard_map/absorb/pallas_call | solution.py:143
  52.7 0.1 collective-permute-start.12
  52.8 0.5 collective-permute-start.14
  53.3 0.1 collective-permute-start.15
  53.4 0.9 collective-permute-done.12.refs_3_
  54.3 0.1 collective-permute-start.13
  54.4 1.5 %collective-permute-done.13.refs_4_ = bf16[32,3584]{1,0:T(8,128)(2,1)S(1)} collective-permute-done((bf16[32,3584]{1,0:T(8,128)(2,1)S(1)}, bf16[32,3584]{1,0:T(8,128)(2,1)S(1)}, u32[]{:S(2)}, u32[]{:S(2)}) %collective-permute-start.13) | collective-permute-done | bytes 229408 | tf_op jit(solution)/shard_map/ppermute | solution.py:327
  55.9 0.8 prepare_rows.6
  56.8 0.0 collective-permute-done.14.refs_4_
  56.8 0.0 collective-permute-done.15.refs_5_
  56.8 12.0 %collective-permute-done.10.refs_1_ = bf16[3616,128]{1,0:T(8,128)(2,1)S(1)} collective-permute-done((bf16[3616,128]{1,0:T(8,128)(2,1)S(1)}, bf16[3616,128]{1,0:T(8,128)(2,1)S(1)}, u32[]{:S(2)}, u32[]{:S(2)}) %collective-permute-start.10) | collective-permute-done | bytes 925728 | tf_op jit(solution)/shard_map/ppermute | solution.py:330
  68.8 0.9 collective-permute-done.17.refs_2_
  69.7 1.6 %collective-permute-start.16 = (bf16[1824,128]{1,0:T(8,128)(2,1)S(1)}, bf16[1824,128]{1,0:T(8,128)(2,1)S(1)}, u32[]{:S(2)}, u32[]{:S(2)}) collective-permute-start(bf16[1824,128]{1,0:T(8,128)(2,1)S(1)} %slice.6), channel_id=1, source_target_pairs={{0,4},{1,5},{4,8},{5,9},{8,12},{9,13},{12,14},{13,15},{14,10},{15,... | collective-permute-start | bytes 1400840 | tf_op jit(solution)/shard_map/ppermute | solution.py:330
  71.4 0.4 collective-permute-start.18
  71.8 2.9 %absorb.7 = (f32[896,896]{1,0:T(8,128)S(1)}, bf16[256,896]{1,0:T(8,128)(2,1)S(1)}, bf16[256,896]{1,0:T(8,128)(2,1)S(1)}, bf16[32,3584]{1,0:T(8,128)(2,1)S(1)}, bf16[32,3584]{1,0:T(8,128)(2,1)S(1)}) custom-call(s32[5]{0:T(128)S(1)} %stack.23.refs_0_, bf16[3616,128]{1,0:T(8,128)(2,1)S(1)} %collective-permute-done.10.refs_1_, ...), custom_call_target="tpu_custom_call", output_to_operand_aliasing={{0}: (3, {})} | custom-call | flops 1 | bytes 1 | tf_op jit(solution)/shard_map/absorb/pallas_call | solution.py:143
  74.7 0.1 collective-permute-start.19
  74.8 0.5 collective-permute-start.21
  75.3 0.1 collective-permute-start.22
  75.4 0.9 collective-permute-done.19.refs_3_
  76.3 0.1 collective-permute-start.20
  76.4 1.5 %collective-permute-done.20.refs_4_ = bf16[32,3584]{1,0:T(8,128)(2,1)S(1)} collective-permute-done((bf16[32,3584]{1,0:T(8,128)(2,1)S(1)}, bf16[32,3584]{1,0:T(8,128)(2,1)S(1)}, u32[]{:S(2)}, u32[]{:S(2)}) %collective-permute-start.20) | collective-permute-done | bytes 229408 | tf_op jit(solution)/shard_map/ppermute | solution.py:327
  77.9 0.8 prepare_rows.7
  78.7 0.0 collective-permute-done.21.left
  78.7 0.0 collective-permute-done.22.right
  78.8 0.7 settle.1.refs_3_
  79.5 0.0 collective-permute-done.16.refs_1_
  79.5 1.0 %collective-permute-done.18.refs_2_ = bf16[1824,128]{1,0:T(8,128)(2,1)S(1)} collective-permute-done((bf16[1824,128]{1,0:T(8,128)(2,1)S(1)}, bf16[1824,128]{1,0:T(8,128)(2,1)S(1)}, u32[]{:S(2)}, u32[]{:S(2)}) %collective-permute-start.18) | collective-permute-done | bytes 466976 | tf_op jit(solution)/shard_map/ppermute | solution.py:330
  80.5 0.5 collective-permute-start.24
  81.0 2.3 %take_own.1 = (f32[896,896]{1,0:T(8,128)S(1)}, bf16[512,3584]{1,0:T(8,128)(2,1)S(1)}, bf16[1792,512]{1,0:T(8,128)(2,1)S(1)}) custom-call(s32[5]{0:T(128)S(1)} %stack.23.refs_0_, bf16[1824,128]{1,0:T(8,128)(2,1)S(1)} %collective-permute-done.16.refs_1_, ...), custom_call_target="tpu_custom_call", output_to_operand_aliasing={{0}: (3, {}), {1}: (4, {}), {2}: (5, {})} | custom-call | flops 1 | bytes 1 | tf_op jit(solution)/shard_map/take_own/pallas_call | solution.py:225
  83.3 0.0 collective-permute-done.23.refs_1_
  83.3 0.0 collective-permute-done.24.refs_2_
  83.3 12.0 %finish.1 = (f32[1792,3584]{1,0:T(8,128)}, f32[1,896,896]{2,1,0:T(8,128)}, bf16[512,3584]{1,0:T(8,128)(2,1)S(1)}, bf16[1792,512]{1,0:T(8,128)(2,1)S(1)}) custom-call(s32[5]{0:T(128)S(1)} %stack.23.refs_0_, bf16[1824,128]{1,0:T(8,128)(2,1)S(1)} %collective-permute-done.23.refs_1_, ...), custom_call_target="tpu_custom_call", output_to_operand_aliasing={{2}: (4, {}), {3}: (5, {})} | custom-call | flops 1 | bytes 1 | tf_op jit(solution)/shard_map/finish/pallas_call | solution.py:270
  (4 shorter events, 0.1 us)
Async XLA Ops:
  1.3 1.2 %copy-start = (bf16[128,3584]{1,0:T(8,128)(2,1)S(1)}, bf16[128,3584]{1,0:T(8,128)(2,1)}, u32[]{:S(2)}) copy-start(bf16[128,3584]{1,0:T(8,128)(2,1)} %tokens.1) | copy-start | bytes 2752516
  2.7 23.5 %collective-permute-start = (bf16[3616,128]{1,0:T(8,128)(2,1)S(1)}, bf16[3616,128]{1,0:T(8,128)(2,1)S(1)}, u32[]{:S(2)}, u32[]{:S(2)}) collective-permute-start(bf16[3616,128]{1,0:T(8,128)(2,1)S(1)} %make_message.1.refs_1_), channel_id=1, source_target_pairs={{0,4},{1,5},{4,8},{5,9},{8,12},{9,13},{12,14},{13,15},{14,10},{15,... | collective-permute-start | bytes 2777096 | tf_op jit(solution)/shard_map/ppermute | solution.py:330
  5.8 22.3 %collective-permute-start.5 = (bf16[3616,128]{1,0:T(8,128)(2,1)S(1)}, bf16[3616,128]{1,0:T(8,128)(2,1)S(1)}, u32[]{:S(2)}, u32[]{:S(2)}) collective-permute-start(bf16[3616,128]{1,0:T(8,128)(2,1)S(1)} %make_message.1.refs_1_), channel_id=1, source_target_pairs={{4,0},{5,1},{8,4},{9,5},{12,8},{13,9},{14,12},{15,13},{10,14},{11,... | collective-permute-start | bytes 2777096 | tf_op jit(solution)/shard_map/ppermute | solution.py:330
  7.4 1.6 %collective-permute-start.1 = (bf16[32,3584]{1,0:T(8,128)(2,1)S(1)}, bf16[32,3584]{1,0:T(8,128)(2,1)S(1)}, u32[]{:S(2)}, u32[]{:S(2)}) collective-permute-start(bf16[32,3584]{1,0:T(8,128)(2,1)S(1)} %get-tuple-element.75.refs_1_), channel_id=1, source_target_pairs={{0,1},{1,0},{2,3},{3,2},{4,5},{5,4},{6,7},{7,6},{8,9},{9,8},{10,11... | collective-permute-start | bytes 688136 | tf_op jit(solution)/shard_map/ppermute | solution.py:327
  7.5 2.2 %collective-permute-start.2 = (bf16[128,896]{1,0:T(8,128)(2,1)S(1)}, bf16[128,896]{1,0:T(8,128)(2,1)S(1)}, u32[]{:S(2)}, u32[]{:S(2)}) collective-permute-start(bf16[128,896]{1,0:T(8,128)(2,1)S(1)} %get-tuple-element.79), channel_id=1, source_target_pairs={{0,1},{1,0},{2,3},{3,2},{4,5},{5,4},{6,7},{7,6},{8,9},{9,8},{10,11... | collective-permute-start | bytes 688136 | tf_op jit(solution)/shard_map/ppermute | solution.py:327
  8.0 1.8 %collective-permute-start.3 = (bf16[128,896]{1,0:T(8,128)(2,1)S(1)}, bf16[128,896]{1,0:T(8,128)(2,1)S(1)}, u32[]{:S(2)}, u32[]{:S(2)}) collective-permute-start(bf16[128,896]{1,0:T(8,128)(2,1)S(1)} %get-tuple-element.80), channel_id=1, source_target_pairs={{0,1},{1,0},{2,3},{3,2},{4,5},{5,4},{6,7},{7,6},{8,9},{9,8},{10,11... | collective-permute-start | bytes 688136 | tf_op jit(solution)/shard_map/ppermute | solution.py:327
  26.3 21.7 %collective-permute-start.4 = (bf16[3616,128]{1,0:T(8,128)(2,1)S(1)}, bf16[3616,128]{1,0:T(8,128)(2,1)S(1)}, u32[]{:S(2)}, u32[]{:S(2)}) collective-permute-start(bf16[3616,128]{1,0:T(8,128)(2,1)S(1)} %collective-permute-done.refs_1_), channel_id=1, source_target_pairs={{0,4},{1,5},{4,8},{5,9},{8,12},{9,13},{12,14},{13,15},{14,10},{15,... | collective-permute-start | bytes 2777096 | tf_op jit(solution)/shard_map/ppermute | solution.py:330
  28.1 21.4 %collective-permute-start.11 = (bf16[3616,128]{1,0:T(8,128)(2,1)S(1)}, bf16[3616,128]{1,0:T(8,128)(2,1)S(1)}, u32[]{:S(2)}, u32[]{:S(2)}) collective-permute-start(bf16[3616,128]{1,0:T(8,128)(2,1)S(1)} %collective-permute-done.5.refs_2_), channel_id=1, source_target_pairs={{4,0},{5,1},{8,4},{9,5},{12,8},{13,9},{14,12},{15,13},{10,14},{11,... | collective-permute-start | bytes 2777096 | tf_op jit(solution)/shard_map/ppermute | solution.py:330
  30.9 1.6 %collective-permute-start.6 = (bf16[32,3584]{1,0:T(8,128)(2,1)S(1)}, bf16[32,3584]{1,0:T(8,128)(2,1)S(1)}, u32[]{:S(2)}, u32[]{:S(2)}) collective-permute-start(bf16[32,3584]{1,0:T(8,128)(2,1)S(1)} %get-tuple-element.91.refs_1_), channel_id=1, source_target_pairs={{0,1},{1,0},{2,3},{3,2},{4,5},{5,4},{6,7},{7,6},{8,9},{9,8},{10,11... | collective-permute-start | bytes 688136 | tf_op jit(solution)/shard_map/ppermute | solution.py:327
  31.0 3.9 %collective-permute-start.8 = (bf16[256,896]{1,0:T(8,128)(2,1)S(1)}, bf16[256,896]{1,0:T(8,128)(2,1)S(1)}, u32[]{:S(2)}, u32[]{:S(2)}) collective-permute-start(bf16[256,896]{1,0:T(8,128)(2,1)S(1)} %get-tuple-element.98), channel_id=1, source_target_pairs={{0,1},{1,0},{2,3},{3,2},{4,5},{5,4},{6,7},{7,6},{8,9},{9,8},{10,11... | collective-permute-start | bytes 1376264 | tf_op jit(solution)/shard_map/ppermute | solution.py:327
  31.5 3.5 %collective-permute-start.9 = (bf16[256,896]{1,0:T(8,128)(2,1)S(1)}, bf16[256,896]{1,0:T(8,128)(2,1)S(1)}, u32[]{:S(2)}, u32[]{:S(2)}) collective-permute-start(bf16[256,896]{1,0:T(8,128)(2,1)S(1)} %get-tuple-element.99), channel_id=1, source_target_pairs={{0,1},{1,0},{2,3},{3,2},{4,5},{5,4},{6,7},{7,6},{8,9},{9,8},{10,11... | collective-permute-start | bytes 1376264 | tf_op jit(solution)/shard_map/ppermute | solution.py:327
  32.5 1.6 %collective-permute-start.7 = (bf16[32,3584]{1,0:T(8,128)(2,1)S(1)}, bf16[32,3584]{1,0:T(8,128)(2,1)S(1)}, u32[]{:S(2)}, u32[]{:S(2)}) collective-permute-start(bf16[32,3584]{1,0:T(8,128)(2,1)S(1)} %get-tuple-element.92.refs_2_), channel_id=1, source_target_pairs={{0,1},{1,0},{2,3},{3,2},{4,5},{5,4},{6,7},{7,6},{8,9},{9,8},{10,11... | collective-permute-start | bytes 688136 | tf_op jit(solution)/shard_map/ppermute | solution.py:327
  48.0 20.8 %collective-permute-start.10 = (bf16[3616,128]{1,0:T(8,128)(2,1)S(1)}, bf16[3616,128]{1,0:T(8,128)(2,1)S(1)}, u32[]{:S(2)}, u32[]{:S(2)}) collective-permute-start(bf16[3616,128]{1,0:T(8,128)(2,1)S(1)} %collective-permute-done.4.refs_1_), channel_id=1, source_target_pairs={{0,4},{1,5},{4,8},{5,9},{8,12},{9,13},{12,14},{13,15},{14,10},{15,... | collective-permute-start | bytes 2777096 | tf_op jit(solution)/shard_map/ppermute | solution.py:330
  49.5 20.2 %collective-permute-start.17 = (bf16[3616,128]{1,0:T(8,128)(2,1)S(1)}, bf16[3616,128]{1,0:T(8,128)(2,1)S(1)}, u32[]{:S(2)}, u32[]{:S(2)}) collective-permute-start(bf16[3616,128]{1,0:T(8,128)(2,1)S(1)} %collective-permute-done.11.refs_2_), channel_id=1, source_target_pairs={{4,0},{5,1},{8,4},{9,5},{12,8},{13,9},{14,12},{15,13},{10,14},{11,... | collective-permute-start | bytes 2777096 | tf_op jit(solution)/shard_map/ppermute | solution.py:330
  52.7 1.6 %collective-permute-start.12 = (bf16[32,3584]{1,0:T(8,128)(2,1)S(1)}, bf16[32,3584]{1,0:T(8,128)(2,1)S(1)}, u32[]{:S(2)}, u32[]{:S(2)}) collective-permute-start(bf16[32,3584]{1,0:T(8,128)(2,1)S(1)} %get-tuple-element.110.refs_1_), channel_id=1, source_target_pairs={{0,1},{1,0},{2,3},{3,2},{4,5},{5,4},{6,7},{7,6},{8,9},{9,8},{10,11... | collective-permute-start | bytes 688136 | tf_op jit(solution)/shard_map/ppermute | solution.py:327
  52.8 3.9 %collective-permute-start.14 = (bf16[256,896]{1,0:T(8,128)(2,1)S(1)}, bf16[256,896]{1,0:T(8,128)(2,1)S(1)}, u32[]{:S(2)}, u32[]{:S(2)}) collective-permute-start(bf16[256,896]{1,0:T(8,128)(2,1)S(1)} %get-tuple-element.117), channel_id=1, source_target_pairs={{0,1},{1,0},{2,3},{3,2},{4,5},{5,4},{6,7},{7,6},{8,9},{9,8},{10,11... | collective-permute-start | bytes 1376264 | tf_op jit(solution)/shard_map/ppermute | solution.py:327
  53.3 3.5 %collective-permute-start.15 = (bf16[256,896]{1,0:T(8,128)(2,1)S(1)}, bf16[256,896]{1,0:T(8,128)(2,1)S(1)}, u32[]{:S(2)}, u32[]{:S(2)}) collective-permute-start(bf16[256,896]{1,0:T(8,128)(2,1)S(1)} %get-tuple-element.118), channel_id=1, source_target_pairs={{0,1},{1,0},{2,3},{3,2},{4,5},{5,4},{6,7},{7,6},{8,9},{9,8},{10,11... | collective-permute-start | bytes 1376264 | tf_op jit(solution)/shard_map/ppermute | solution.py:327
  54.3 1.6 %collective-permute-start.13 = (bf16[32,3584]{1,0:T(8,128)(2,1)S(1)}, bf16[32,3584]{1,0:T(8,128)(2,1)S(1)}, u32[]{:S(2)}, u32[]{:S(2)}) collective-permute-start(bf16[32,3584]{1,0:T(8,128)(2,1)S(1)} %get-tuple-element.111.refs_2_), channel_id=1, source_target_pairs={{0,1},{1,0},{2,3},{3,2},{4,5},{5,4},{6,7},{7,6},{8,9},{9,8},{10,11... | collective-permute-start | bytes 688136 | tf_op jit(solution)/shard_map/ppermute | solution.py:327
  69.7 9.8 %collective-permute-start.16 = (bf16[1824,128]{1,0:T(8,128)(2,1)S(1)}, bf16[1824,128]{1,0:T(8,128)(2,1)S(1)}, u32[]{:S(2)}, u32[]{:S(2)}) collective-permute-start(bf16[1824,128]{1,0:T(8,128)(2,1)S(1)} %slice.6), channel_id=1, source_target_pairs={{0,4},{1,5},{4,8},{5,9},{8,12},{9,13},{12,14},{13,15},{14,10},{15,... | collective-permute-start | bytes 1400840 | tf_op jit(solution)/shard_map/ppermute | solution.py:330
  71.4 9.2 %collective-permute-start.18 = (bf16[1824,128]{1,0:T(8,128)(2,1)S(1)}, bf16[1824,128]{1,0:T(8,128)(2,1)S(1)}, u32[]{:S(2)}, u32[]{:S(2)}) collective-permute-start(bf16[1824,128]{1,0:T(8,128)(2,1)S(1)} %slice.7), channel_id=1, source_target_pairs={{4,0},{5,1},{8,4},{9,5},{12,8},{13,9},{14,12},{15,13},{10,14},{11,... | collective-permute-start | bytes 1400840 | tf_op jit(solution)/shard_map/ppermute | solution.py:330
  74.7 1.6 %collective-permute-start.19 = (bf16[32,3584]{1,0:T(8,128)(2,1)S(1)}, bf16[32,3584]{1,0:T(8,128)(2,1)S(1)}, u32[]{:S(2)}, u32[]{:S(2)}) collective-permute-start(bf16[32,3584]{1,0:T(8,128)(2,1)S(1)} %get-tuple-element.129.refs_1_), channel_id=1, source_target_pairs={{0,1},{1,0},{2,3},{3,2},{4,5},{5,4},{6,7},{7,6},{8,9},{9,8},{10,11... | collective-permute-start | bytes 688136 | tf_op jit(solution)/shard_map/ppermute | solution.py:327
  74.8 3.9 %collective-permute-start.21 = (bf16[256,896]{1,0:T(8,128)(2,1)S(1)}, bf16[256,896]{1,0:T(8,128)(2,1)S(1)}, u32[]{:S(2)}, u32[]{:S(2)}) collective-permute-start(bf16[256,896]{1,0:T(8,128)(2,1)S(1)} %get-tuple-element.136), channel_id=1, source_target_pairs={{0,1},{1,0},{2,3},{3,2},{4,5},{5,4},{6,7},{7,6},{8,9},{9,8},{10,11... | collective-permute-start | bytes 1376264 | tf_op jit(solution)/shard_map/ppermute | solution.py:327
  75.3 3.5 %collective-permute-start.22 = (bf16[256,896]{1,0:T(8,128)(2,1)S(1)}, bf16[256,896]{1,0:T(8,128)(2,1)S(1)}, u32[]{:S(2)}, u32[]{:S(2)}) collective-permute-start(bf16[256,896]{1,0:T(8,128)(2,1)S(1)} %get-tuple-element.137), channel_id=1, source_target_pairs={{0,1},{1,0},{2,3},{3,2},{4,5},{5,4},{6,7},{7,6},{8,9},{9,8},{10,11... | collective-permute-start | bytes 1376264 | tf_op jit(solution)/shard_map/ppermute | solution.py:327
  76.3 1.6 %collective-permute-start.20 = (bf16[32,3584]{1,0:T(8,128)(2,1)S(1)}, bf16[32,3584]{1,0:T(8,128)(2,1)S(1)}, u32[]{:S(2)}, u32[]{:S(2)}) collective-permute-start(bf16[32,3584]{1,0:T(8,128)(2,1)S(1)} %get-tuple-element.130.refs_2_), channel_id=1, source_target_pairs={{0,1},{1,0},{2,3},{3,2},{4,5},{5,4},{6,7},{7,6},{8,9},{9,8},{10,11... | collective-permute-start | bytes 688136 | tf_op jit(solution)/shard_map/ppermute | solution.py:327
  80.5 2.8 %collective-permute-start.23 = (bf16[1824,128]{1,0:T(8,128)(2,1)S(1)}, bf16[1824,128]{1,0:T(8,128)(2,1)S(1)}, u32[]{:S(2)}, u32[]{:S(2)}) collective-permute-start(bf16[1824,128]{1,0:T(8,128)(2,1)S(1)} %collective-permute-done.16.refs_1_), channel_id=1, source_target_pairs={{0,1},{1,0},{2,3},{3,2},{4,5},{5,4},{6,7},{7,6},{8,9},{9,8},{10,11... | collective-permute-start | bytes 1400840 | tf_op jit(solution)/shard_map/ppermute | solution.py:327
  80.5 2.8 %collective-permute-start.24 = (bf16[1824,128]{1,0:T(8,128)(2,1)S(1)}, bf16[1824,128]{1,0:T(8,128)(2,1)S(1)}, u32[]{:S(2)}, u32[]{:S(2)}) collective-permute-start(bf16[1824,128]{1,0:T(8,128)(2,1)S(1)} %collective-permute-done.18.refs_2_), channel_id=1, source_target_pairs={{0,1},{1,0},{2,3},{3,2},{4,5},{5,4},{6,7},{7,6},{8,9},{9,8},{10,11... | collective-permute-start | bytes 1400840 | tf_op jit(solution)/shard_map/ppermute | solution.py:327

commit v15 on v13

--- a/solution.py
+++ b/solution.py
@@ -13,7 +13,6 @@
 CORES = 2
 LANES = 128
 TABLE = 32
-STEP = 512
 SPLITS = 7
 VMEM = pl.BlockSpec(memory_space=pltpu.VMEM)
 SMEM = pl.BlockSpec(memory_space=pltpu.SMEM)
@@ -163,7 +162,8 @@
 
         @pl.when(slab_at == s)
         def _():
-            across[:, at : at + count] = packed[:, s * slab : (s + 1) * slab].T
+            turned = packed[:, s * slab : (s + 1) * slab].T
+            across[:, at : at + count] = (turned.astype(F32) * INVERSE).astype(BF16)
 
 
 def prepare_kernel(count, at, *refs):
@@ -253,11 +253,7 @@
     height = staging.shape[1]
     for m in range(SPLITS):
         span = slice(m * height, (m + 1) * height)
-        for n in range(0, rows.shape[1], STEP):
-            staging[m, :, n : n + STEP] = (
-                jnp.dot(across[span, :], rows[:, n : n + STEP], preferred_element_type=F32)
-                * INVERSE
-            )
+        staging[m, :, :] = jnp.dot(across[span, :], rows[...], preferred_element_type=F32)
         write(staging.at[m], hessian.at[span, :])
     for copy in copies:
         copy.wait()

time: 95.7 us -> 95.7 us (level)
  no operation moved by 1% of the time
where the time goes in v15:
time: 95.7 us; the launch traced here: 95.5 us
  waiting for transfers between devices  51.5 us (54%)
  Pallas kernels  28.2 us (29%)
  starting transfers between devices  12.7 us (13%)
  local copies, waits for them, and re-layouts  1.32 us (1%)
  between operations  1.02 us (1%)
    ppermute x8, waiting for transfers between devices, advance(): lax.ppermute(array, 'tok', stream)  43.4 us
    pallas_call x1, Pallas kernels, finish(): pl.pallas_call(functools.partial(finish_kernel, final), out_shape=[jax.Sh...  12 us
    pallas_call x4, Pallas kernels, absorb(): pl.pallas_call(functools.partial(absorb_kernel, count, bool(before)), out...  9.82 us
    ppermute x8, starting transfers between devices, advance(): lax.ppermute(array, 'tok', stream)  9.21 us
    ppermute x17, waiting for transfers between devices, swap(): return lax.ppermute(array, 'tok', pair)  8.13 us
    ppermute x17, starting transfers between devices, swap(): return lax.ppermute(array, 'tok', pair)  3.5 us
    pallas_call x4, Pallas kernels, prepare(): pl.pallas_call(functools.partial(prepare_kernel, len(packs), at), out_sha...  3.21 us
    pallas_call x1, Pallas kernels, take_own(): pl.pallas_call(take_own_kernel, out_shape=[jax.ShapeDtypeStruct(a.shape,...  2.28 us
  transfers between devices with their start and end apart: 25, of which 12 were waited for; matrix products, arithmetic and copies ran while one was open for 0% of the time, Pallas kernels for 17%

profile of v15, /device:TPU:0, one launch (start us, length us, event | category | flops | bytes accessed | tf_op | source)
XLA Modules:
  0.0 95.5 jit_solution(266953764787476479)
XLA Ops:
  0.6 0.7 select_reduce_fusion
  1.3 0.0 copy-start
  1.4 1.2 %copy-done = bf16[128,3584]{1,0:T(8,128)(2,1)S(1)} copy-done((bf16[128,3584]{1,0:T(8,128)(2,1)S(1)}, bf16[128,3584]{1,0:T(8,128)(2,1)}, u32[]{:S(2)}) %copy-start) | copy-done | bytes 917528
  2.5 0.2 make_message.1.refs_1_
  2.7 3.1 %collective-permute-start = (bf16[3616,128]{1,0:T(8,128)(2,1)S(1)}, bf16[3616,128]{1,0:T(8,128)(2,1)S(1)}, u32[]{:S(2)}, u32[]{:S(2)}) collective-permute-start(bf16[3616,128]{1,0:T(8,128)(2,1)S(1)} %make_message.1.refs_1_), channel_id=1, source_target_pairs={{0,4},{1,5},{4,8},{5,9},{8,12},{9,13},{12,14},{13,15},{14,10},{15,... | collective-permute-start | bytes 2777096 | tf_op jit(solution)/shard_map/ppermute | solution.py:326
  5.8 0.0 collective-permute-start.5
  5.8 0.1 stack.23.refs_0_
  5.9 1.5 %absorb.4 = (f32[896,896]{1,0:T(8,128)S(1)}, bf16[128,896]{1,0:T(8,128)(2,1)S(1)}, bf16[128,896]{1,0:T(8,128)(2,1)S(1)}, bf16[32,3584]{1,0:T(8,128)(2,1)S(1)}) custom-call(s32[5]{0:T(128)S(1)} %stack.23.refs_0_, bf16[3616,128]{1,0:T(8,128)(2,1)S(1)} %make_message.1.refs_1_), custom_call_target="tpu_custom_call" | custom-call | flops 1 | bytes 1 | tf_op jit(solution)/shard_map/absorb/pallas_call | solution.py:142
  7.4 0.1 collective-permute-start.1
  7.5 0.5 collective-permute-start.2
  8.0 0.1 collective-permute-start.3
  8.1 0.9 collective-permute-done.1.refs_2_
  9.0 0.8 prepare_rows.4
  9.8 0.0 collective-permute-done.2.refs_4_
  9.8 0.0 collective-permute-done.3.refs_5_
  9.8 16.5 %collective-permute-done.refs_1_ = bf16[3616,128]{1,0:T(8,128)(2,1)S(1)} collective-permute-done((bf16[3616,128]{1,0:T(8,128)(2,1)S(1)}, bf16[3616,128]{1,0:T(8,128)(2,1)S(1)}, u32[]{:S(2)}, u32[]{:S(2)}) %collective-permute-start) | collective-permute-done | bytes 925728 | tf_op jit(solution)/shard_map/ppermute | solution.py:326
  26.3 1.8 %collective-permute-start.4 = (bf16[3616,128]{1,0:T(8,128)(2,1)S(1)}, bf16[3616,128]{1,0:T(8,128)(2,1)S(1)}, u32[]{:S(2)}, u32[]{:S(2)}) collective-permute-start(bf16[3616,128]{1,0:T(8,128)(2,1)S(1)} %collective-permute-done.refs_1_), channel_id=1, source_target_pairs={{0,4},{1,5},{4,8},{5,9},{8,12},{9,13},{12,14},{13,15},{14,10},{15,... | collective-permute-start | bytes 2777096 | tf_op jit(solution)/shard_map/ppermute | solution.py:326
  28.1 0.0 collective-permute-done.5.refs_2_
  28.1 0.2 collective-permute-start.11
  28.3 2.7 %absorb.5 = (f32[896,896]{1,0:T(8,128)S(1)}, bf16[256,896]{1,0:T(8,128)(2,1)S(1)}, bf16[256,896]{1,0:T(8,128)(2,1)S(1)}, bf16[32,3584]{1,0:T(8,128)(2,1)S(1)}, bf16[32,3584]{1,0:T(8,128)(2,1)S(1)}) custom-call(s32[5]{0:T(128)S(1)} %stack.23.refs_0_, bf16[3616,128]{1,0:T(8,128)(2,1)S(1)} %collective-permute-done.refs_1_, ...), custom_call_target="tpu_custom_call", output_to_operand_aliasing={{0}: (3, {})} | custom-call | flops 1 | bytes 1 | tf_op jit(solution)/shard_map/absorb/pallas_call | solution.py:142
  30.9 0.1 collective-permute-start.6
  31.0 0.5 collective-permute-start.8
  31.5 0.1 collective-permute-start.9
  31.6 0.9 collective-permute-done.6.refs_3_
  32.5 0.1 collective-permute-start.7
  32.6 1.5 %collective-permute-done.7.refs_4_ = bf16[32,3584]{1,0:T(8,128)(2,1)S(1)} collective-permute-done((bf16[32,3584]{1,0:T(8,128)(2,1)S(1)}, bf16[32,3584]{1,0:T(8,128)(2,1)S(1)}, u32[]{:S(2)}, u32[]{:S(2)}) %collective-permute-start.7) | collective-permute-done | bytes 229408 | tf_op jit(solution)/shard_map/ppermute | solution.py:323
  34.1 0.8 prepare_rows.5
  35.0 0.0 collective-permute-done.8.refs_4_
  35.0 0.0 collective-permute-done.9.refs_5_
  35.0 13.0 %collective-permute-done.4.refs_1_ = bf16[3616,128]{1,0:T(8,128)(2,1)S(1)} collective-permute-done((bf16[3616,128]{1,0:T(8,128)(2,1)S(1)}, bf16[3616,128]{1,0:T(8,128)(2,1)S(1)}, u32[]{:S(2)}, u32[]{:S(2)}) %collective-permute-start.4) | collective-permute-done | bytes 925728 | tf_op jit(solution)/shard_map/ppermute | solution.py:326
  48.0 1.5 %collective-permute-start.10 = (bf16[3616,128]{1,0:T(8,128)(2,1)S(1)}, bf16[3616,128]{1,0:T(8,128)(2,1)S(1)}, u32[]{:S(2)}, u32[]{:S(2)}) collective-permute-start(bf16[3616,128]{1,0:T(8,128)(2,1)S(1)} %collective-permute-done.4.refs_1_), channel_id=1, source_target_pairs={{0,4},{1,5},{4,8},{5,9},{8,12},{9,13},{12,14},{13,15},{14,10},{15,... | collective-permute-start | bytes 2777096 | tf_op jit(solution)/shard_map/ppermute | solution.py:326
  49.5 0.0 collective-permute-done.11.refs_2_
  49.5 0.5 collective-permute-start.17
  50.0 2.7 %absorb.6 = (f32[896,896]{1,0:T(8,128)S(1)}, bf16[256,896]{1,0:T(8,128)(2,1)S(1)}, bf16[256,896]{1,0:T(8,128)(2,1)S(1)}, bf16[32,3584]{1,0:T(8,128)(2,1)S(1)}, bf16[32,3584]{1,0:T(8,128)(2,1)S(1)}) custom-call(s32[5]{0:T(128)S(1)} %stack.23.refs_0_, bf16[3616,128]{1,0:T(8,128)(2,1)S(1)} %collective-permute-done.4.refs_1_, ...), custom_call_target="tpu_custom_call", output_to_operand_aliasing={{0}: (3, {})} | custom-call | flops 1 | bytes 1 | tf_op jit(solution)/shard_map/absorb/pallas_call | solution.py:142
  52.7 0.1 collective-permute-start.12
  52.8 0.5 collective-permute-start.14
  53.3 0.1 collective-permute-start.15
  53.4 0.9 collective-permute-done.12.refs_3_
  54.3 0.1 collective-permute-start.13
  54.4 1.5 %collective-permute-done.13.refs_4_ = bf16[32,3584]{1,0:T(8,128)(2,1)S(1)} collective-permute-done((bf16[32,3584]{1,0:T(8,128)(2,1)S(1)}, bf16[32,3584]{1,0:T(8,128)(2,1)S(1)}, u32[]{:S(2)}, u32[]{:S(2)}) %collective-permute-start.13) | collective-permute-done | bytes 229408 | tf_op jit(solution)/shard_map/ppermute | solution.py:323
  55.9 0.8 prepare_rows.6
  56.8 0.0 collective-permute-done.14.refs_4_
  56.8 0.0 collective-permute-done.15.refs_5_
  56.8 12.0 %collective-permute-done.10.refs_1_ = bf16[3616,128]{1,0:T(8,128)(2,1)S(1)} collective-permute-done((bf16[3616,128]{1,0:T(8,128)(2,1)S(1)}, bf16[3616,128]{1,0:T(8,128)(2,1)S(1)}, u32[]{:S(2)}, u32[]{:S(2)}) %collective-permute-start.10) | collective-permute-done | bytes 925728 | tf_op jit(solution)/shard_map/ppermute | solution.py:326
  68.8 0.9 collective-permute-done.17.refs_2_
  69.7 1.6 %collective-permute-start.16 = (bf16[1824,128]{1,0:T(8,128)(2,1)S(1)}, bf16[1824,128]{1,0:T(8,128)(2,1)S(1)}, u32[]{:S(2)}, u32[]{:S(2)}) collective-permute-start(bf16[1824,128]{1,0:T(8,128)(2,1)S(1)} %slice.6), channel_id=1, source_target_pairs={{0,4},{1,5},{4,8},{5,9},{8,12},{9,13},{12,14},{13,15},{14,10},{15,... | collective-permute-start | bytes 1400840 | tf_op jit(solution)/shard_map/ppermute | solution.py:326
  71.4 0.4 collective-permute-start.18
  71.8 2.9 %absorb.7 = (f32[896,896]{1,0:T(8,128)S(1)}, bf16[256,896]{1,0:T(8,128)(2,1)S(1)}, bf16[256,896]{1,0:T(8,128)(2,1)S(1)}, bf16[32,3584]{1,0:T(8,128)(2,1)S(1)}, bf16[32,3584]{1,0:T(8,128)(2,1)S(1)}) custom-call(s32[5]{0:T(128)S(1)} %stack.23.refs_0_, bf16[3616,128]{1,0:T(8,128)(2,1)S(1)} %collective-permute-done.10.refs_1_, ...), custom_call_target="tpu_custom_call", output_to_operand_aliasing={{0}: (3, {})} | custom-call | flops 1 | bytes 1 | tf_op jit(solution)/shard_map/absorb/pallas_call | solution.py:142
  74.7 0.1 collective-permute-start.19
  74.8 0.5 collective-permute-start.21
  75.3 0.1 collective-permute-start.22
  75.4 0.9 collective-permute-done.19.refs_3_
  76.3 0.1 collective-permute-start.20
  76.4 1.5 %collective-permute-done.20.refs_4_ = bf16[32,3584]{1,0:T(8,128)(2,1)S(1)} collective-permute-done((bf16[32,3584]{1,0:T(8,128)(2,1)S(1)}, bf16[32,3584]{1,0:T(8,128)(2,1)S(1)}, u32[]{:S(2)}, u32[]{:S(2)}) %collective-permute-start.20) | collective-permute-done | bytes 229408 | tf_op jit(solution)/shard_map/ppermute | solution.py:323
  77.9 0.8 prepare_rows.7
  78.7 0.0 collective-permute-done.21.left
  78.8 0.7 settle.1.refs_3_
  79.5 0.0 collective-permute-done.16.refs_1_
  79.5 1.0 %collective-permute-done.18.refs_2_ = bf16[1824,128]{1,0:T(8,128)(2,1)S(1)} collective-permute-done((bf16[1824,128]{1,0:T(8,128)(2,1)S(1)}, bf16[1824,128]{1,0:T(8,128)(2,1)S(1)}, u32[]{:S(2)}, u32[]{:S(2)}) %collective-permute-start.18) | collective-permute-done | bytes 466976 | tf_op jit(solution)/shard_map/ppermute | solution.py:326
  80.5 0.5 collective-permute-start.24
  81.0 2.3 %take_own.1 = (f32[896,896]{1,0:T(8,128)S(1)}, bf16[512,3584]{1,0:T(8,128)(2,1)S(1)}, bf16[1792,512]{1,0:T(8,128)(2,1)S(1)}) custom-call(s32[5]{0:T(128)S(1)} %stack.23.refs_0_, bf16[1824,128]{1,0:T(8,128)(2,1)S(1)} %collective-permute-done.16.refs_1_, ...), custom_call_target="tpu_custom_call", output_to_operand_aliasing={{0}: (3, {}), {1}: (4, {}), {2}: (5, {})} | custom-call | flops 1 | bytes 1 | tf_op jit(solution)/shard_map/take_own/pallas_call | solution.py:225
  83.3 0.0 collective-permute-done.23.refs_1_
  83.3 0.0 collective-permute-done.24.refs_2_
  83.3 12.0 %finish.1 = (f32[1792,3584]{1,0:T(8,128)}, f32[1,896,896]{2,1,0:T(8,128)}, bf16[512,3584]{1,0:T(8,128)(2,1)S(1)}, bf16[1792,512]{1,0:T(8,128)(2,1)S(1)}) custom-call(s32[5]{0:T(128)S(1)} %stack.23.refs_0_, bf16[1824,128]{1,0:T(8,128)(2,1)S(1)} %collective-permute-done.23.refs_1_, ...), custom_call_target="tpu_custom_call", output_to_operand_aliasing={{2}: (4, {}), {3}: (5, {})} | custom-call | flops 1 | bytes 1 | tf_op jit(solution)/shard_map/finish/pallas_call | solution.py:266
  (4 shorter events, 0.1 us)
Async XLA Ops:
  1.3 1.2 %copy-start = (bf16[128,3584]{1,0:T(8,128)(2,1)S(1)}, bf16[128,3584]{1,0:T(8,128)(2,1)}, u32[]{:S(2)}) copy-start(bf16[128,3584]{1,0:T(8,128)(2,1)} %tokens.1) | copy-start | bytes 2752516
  2.7 23.5 %collective-permute-start = (bf16[3616,128]{1,0:T(8,128)(2,1)S(1)}, bf16[3616,128]{1,0:T(8,128)(2,1)S(1)}, u32[]{:S(2)}, u32[]{:S(2)}) collective-permute-start(bf16[3616,128]{1,0:T(8,128)(2,1)S(1)} %make_message.1.refs_1_), channel_id=1, source_target_pairs={{0,4},{1,5},{4,8},{5,9},{8,12},{9,13},{12,14},{13,15},{14,10},{15,... | collective-permute-start | bytes 2777096 | tf_op jit(solution)/shard_map/ppermute | solution.py:326
  5.8 22.3 %collective-permute-start.5 = (bf16[3616,128]{1,0:T(8,128)(2,1)S(1)}, bf16[3616,128]{1,0:T(8,128)(2,1)S(1)}, u32[]{:S(2)}, u32[]{:S(2)}) collective-permute-start(bf16[3616,128]{1,0:T(8,128)(2,1)S(1)} %make_message.1.refs_1_), channel_id=1, source_target_pairs={{4,0},{5,1},{8,4},{9,5},{12,8},{13,9},{14,12},{15,13},{10,14},{11,... | collective-permute-start | bytes 2777096 | tf_op jit(solution)/shard_map/ppermute | solution.py:326
  7.4 1.6 %collective-permute-start.1 = (bf16[32,3584]{1,0:T(8,128)(2,1)S(1)}, bf16[32,3584]{1,0:T(8,128)(2,1)S(1)}, u32[]{:S(2)}, u32[]{:S(2)}) collective-permute-start(bf16[32,3584]{1,0:T(8,128)(2,1)S(1)} %get-tuple-element.75.refs_1_), channel_id=1, source_target_pairs={{0,1},{1,0},{2,3},{3,2},{4,5},{5,4},{6,7},{7,6},{8,9},{9,8},{10,11... | collective-permute-start | bytes 688136 | tf_op jit(solution)/shard_map/ppermute | solution.py:323
  7.5 2.3 %collective-permute-start.2 = (bf16[128,896]{1,0:T(8,128)(2,1)S(1)}, bf16[128,896]{1,0:T(8,128)(2,1)S(1)}, u32[]{:S(2)}, u32[]{:S(2)}) collective-permute-start(bf16[128,896]{1,0:T(8,128)(2,1)S(1)} %get-tuple-element.79), channel_id=1, source_target_pairs={{0,1},{1,0},{2,3},{3,2},{4,5},{5,4},{6,7},{7,6},{8,9},{9,8},{10,11... | collective-permute-start | bytes 688136 | tf_op jit(solution)/shard_map/ppermute | solution.py:323
  8.0 1.8 %collective-permute-start.3 = (bf16[128,896]{1,0:T(8,128)(2,1)S(1)}, bf16[128,896]{1,0:T(8,128)(2,1)S(1)}, u32[]{:S(2)}, u32[]{:S(2)}) collective-permute-start(bf16[128,896]{1,0:T(8,128)(2,1)S(1)} %get-tuple-element.80), channel_id=1, source_target_pairs={{0,1},{1,0},{2,3},{3,2},{4,5},{5,4},{6,7},{7,6},{8,9},{9,8},{10,11... | collective-permute-start | bytes 688136 | tf_op jit(solution)/shard_map/ppermute | solution.py:323
  26.3 21.7 %collective-permute-start.4 = (bf16[3616,128]{1,0:T(8,128)(2,1)S(1)}, bf16[3616,128]{1,0:T(8,128)(2,1)S(1)}, u32[]{:S(2)}, u32[]{:S(2)}) collective-permute-start(bf16[3616,128]{1,0:T(8,128)(2,1)S(1)} %collective-permute-done.refs_1_), channel_id=1, source_target_pairs={{0,4},{1,5},{4,8},{5,9},{8,12},{9,13},{12,14},{13,15},{14,10},{15,... | collective-permute-start | bytes 2777096 | tf_op jit(solution)/shard_map/ppermute | solution.py:326
  28.1 21.4 %collective-permute-start.11 = (bf16[3616,128]{1,0:T(8,128)(2,1)S(1)}, bf16[3616,128]{1,0:T(8,128)(2,1)S(1)}, u32[]{:S(2)}, u32[]{:S(2)}) collective-permute-start(bf16[3616,128]{1,0:T(8,128)(2,1)S(1)} %collective-permute-done.5.refs_2_), channel_id=1, source_target_pairs={{4,0},{5,1},{8,4},{9,5},{12,8},{13,9},{14,12},{15,13},{10,14},{11,... | collective-permute-start | bytes 2777096 | tf_op jit(solution)/shard_map/ppermute | solution.py:326
  30.9 1.6 %collective-permute-start.6 = (bf16[32,3584]{1,0:T(8,128)(2,1)S(1)}, bf16[32,3584]{1,0:T(8,128)(2,1)S(1)}, u32[]{:S(2)}, u32[]{:S(2)}) collective-permute-start(bf16[32,3584]{1,0:T(8,128)(2,1)S(1)} %get-tuple-element.91.refs_1_), channel_id=1, source_target_pairs={{0,1},{1,0},{2,3},{3,2},{4,5},{5,4},{6,7},{7,6},{8,9},{9,8},{10,11... | collective-permute-start | bytes 688136 | tf_op jit(solution)/shard_map/ppermute | solution.py:323
  31.0 3.9 %collective-permute-start.8 = (bf16[256,896]{1,0:T(8,128)(2,1)S(1)}, bf16[256,896]{1,0:T(8,128)(2,1)S(1)}, u32[]{:S(2)}, u32[]{:S(2)}) collective-permute-start(bf16[256,896]{1,0:T(8,128)(2,1)S(1)} %get-tuple-element.98), channel_id=1, source_target_pairs={{0,1},{1,0},{2,3},{3,2},{4,5},{5,4},{6,7},{7,6},{8,9},{9,8},{10,11... | collective-permute-start | bytes 1376264 | tf_op jit(solution)/shard_map/ppermute | solution.py:323
  31.5 3.5 %collective-permute-start.9 = (bf16[256,896]{1,0:T(8,128)(2,1)S(1)}, bf16[256,896]{1,0:T(8,128)(2,1)S(1)}, u32[]{:S(2)}, u32[]{:S(2)}) collective-permute-start(bf16[256,896]{1,0:T(8,128)(2,1)S(1)} %get-tuple-element.99), channel_id=1, source_target_pairs={{0,1},{1,0},{2,3},{3,2},{4,5},{5,4},{6,7},{7,6},{8,9},{9,8},{10,11... | collective-permute-start | bytes 1376264 | tf_op jit(solution)/shard_map/ppermute | solution.py:323
  32.5 1.6 %collective-permute-start.7 = (bf16[32,3584]{1,0:T(8,128)(2,1)S(1)}, bf16[32,3584]{1,0:T(8,128)(2,1)S(1)}, u32[]{:S(2)}, u32[]{:S(2)}) collective-permute-start(bf16[32,3584]{1,0:T(8,128)(2,1)S(1)} %get-tuple-element.92.refs_2_), channel_id=1, source_target_pairs={{0,1},{1,0},{2,3},{3,2},{4,5},{5,4},{6,7},{7,6},{8,9},{9,8},{10,11... | collective-permute-start | bytes 688136 | tf_op jit(solution)/shard_map/ppermute | solution.py:323
  48.0 20.8 %collective-permute-start.10 = (bf16[3616,128]{1,0:T(8,128)(2,1)S(1)}, bf16[3616,128]{1,0:T(8,128)(2,1)S(1)}, u32[]{:S(2)}, u32[]{:S(2)}) collective-permute-start(bf16[3616,128]{1,0:T(8,128)(2,1)S(1)} %collective-permute-done.4.refs_1_), channel_id=1, source_target_pairs={{0,4},{1,5},{4,8},{5,9},{8,12},{9,13},{12,14},{13,15},{14,10},{15,... | collective-permute-start | bytes 2777096 | tf_op jit(solution)/shard_map/ppermute | solution.py:326
  49.5 20.2 %collective-permute-start.17 = (bf16[3616,128]{1,0:T(8,128)(2,1)S(1)}, bf16[3616,128]{1,0:T(8,128)(2,1)S(1)}, u32[]{:S(2)}, u32[]{:S(2)}) collective-permute-start(bf16[3616,128]{1,0:T(8,128)(2,1)S(1)} %collective-permute-done.11.refs_2_), channel_id=1, source_target_pairs={{4,0},{5,1},{8,4},{9,5},{12,8},{13,9},{14,12},{15,13},{10,14},{11,... | collective-permute-start | bytes 2777096 | tf_op jit(solution)/shard_map/ppermute | solution.py:326
  52.7 1.6 %collective-permute-start.12 = (bf16[32,3584]{1,0:T(8,128)(2,1)S(1)}, bf16[32,3584]{1,0:T(8,128)(2,1)S(1)}, u32[]{:S(2)}, u32[]{:S(2)}) collective-permute-start(bf16[32,3584]{1,0:T(8,128)(2,1)S(1)} %get-tuple-element.110.refs_1_), channel_id=1, source_target_pairs={{0,1},{1,0},{2,3},{3,2},{4,5},{5,4},{6,7},{7,6},{8,9},{9,8},{10,11... | collective-permute-start | bytes 688136 | tf_op jit(solution)/shard_map/ppermute | solution.py:323
  52.8 3.9 %collective-permute-start.14 = (bf16[256,896]{1,0:T(8,128)(2,1)S(1)}, bf16[256,896]{1,0:T(8,128)(2,1)S(1)}, u32[]{:S(2)}, u32[]{:S(2)}) collective-permute-start(bf16[256,896]{1,0:T(8,128)(2,1)S(1)} %get-tuple-element.117), channel_id=1, source_target_pairs={{0,1},{1,0},{2,3},{3,2},{4,5},{5,4},{6,7},{7,6},{8,9},{9,8},{10,11... | collective-permute-start | bytes 1376264 | tf_op jit(solution)/shard_map/ppermute | solution.py:323
  53.3 3.5 %collective-permute-start.15 = (bf16[256,896]{1,0:T(8,128)(2,1)S(1)}, bf16[256,896]{1,0:T(8,128)(2,1)S(1)}, u32[]{:S(2)}, u32[]{:S(2)}) collective-permute-start(bf16[256,896]{1,0:T(8,128)(2,1)S(1)} %get-tuple-element.118), channel_id=1, source_target_pairs={{0,1},{1,0},{2,3},{3,2},{4,5},{5,4},{6,7},{7,6},{8,9},{9,8},{10,11... | collective-permute-start | bytes 1376264 | tf_op jit(solution)/shard_map/ppermute | solution.py:323
  54.3 1.6 %collective-permute-start.13 = (bf16[32,3584]{1,0:T(8,128)(2,1)S(1)}, bf16[32,3584]{1,0:T(8,128)(2,1)S(1)}, u32[]{:S(2)}, u32[]{:S(2)}) collective-permute-start(bf16[32,3584]{1,0:T(8,128)(2,1)S(1)} %get-tuple-element.111.refs_2_), channel_id=1, source_target_pairs={{0,1},{1,0},{2,3},{3,2},{4,5},{5,4},{6,7},{7,6},{8,9},{9,8},{10,11... | collective-permute-start | bytes 688136 | tf_op jit(solution)/shard_map/ppermute | solution.py:323
  69.7 9.8 %collective-permute-start.16 = (bf16[1824,128]{1,0:T(8,128)(2,1)S(1)}, bf16[1824,128]{1,0:T(8,128)(2,1)S(1)}, u32[]{:S(2)}, u32[]{:S(2)}) collective-permute-start(bf16[1824,128]{1,0:T(8,128)(2,1)S(1)} %slice.6), channel_id=1, source_target_pairs={{0,4},{1,5},{4,8},{5,9},{8,12},{9,13},{12,14},{13,15},{14,10},{15,... | collective-permute-start | bytes 1400840 | tf_op jit(solution)/shard_map/ppermute | solution.py:326
  71.4 9.2 %collective-permute-start.18 = (bf16[1824,128]{1,0:T(8,128)(2,1)S(1)}, bf16[1824,128]{1,0:T(8,128)(2,1)S(1)}, u32[]{:S(2)}, u32[]{:S(2)}) collective-permute-start(bf16[1824,128]{1,0:T(8,128)(2,1)S(1)} %slice.7), channel_id=1, source_target_pairs={{4,0},{5,1},{8,4},{9,5},{12,8},{13,9},{14,12},{15,13},{10,14},{11,... | collective-permute-start | bytes 1400840 | tf_op jit(solution)/shard_map/ppermute | solution.py:326
  74.7 1.6 %collective-permute-start.19 = (bf16[32,3584]{1,0:T(8,128)(2,1)S(1)}, bf16[32,3584]{1,0:T(8,128)(2,1)S(1)}, u32[]{:S(2)}, u32[]{:S(2)}) collective-permute-start(bf16[32,3584]{1,0:T(8,128)(2,1)S(1)} %get-tuple-element.129.refs_1_), channel_id=1, source_target_pairs={{0,1},{1,0},{2,3},{3,2},{4,5},{5,4},{6,7},{7,6},{8,9},{9,8},{10,11... | collective-permute-start | bytes 688136 | tf_op jit(solution)/shard_map/ppermute | solution.py:323
  74.8 3.9 %collective-permute-start.21 = (bf16[256,896]{1,0:T(8,128)(2,1)S(1)}, bf16[256,896]{1,0:T(8,128)(2,1)S(1)}, u32[]{:S(2)}, u32[]{:S(2)}) collective-permute-start(bf16[256,896]{1,0:T(8,128)(2,1)S(1)} %get-tuple-element.136), channel_id=1, source_target_pairs={{0,1},{1,0},{2,3},{3,2},{4,5},{5,4},{6,7},{7,6},{8,9},{9,8},{10,11... | collective-permute-start | bytes 1376264 | tf_op jit(solution)/shard_map/ppermute | solution.py:323
  75.3 3.5 %collective-permute-start.22 = (bf16[256,896]{1,0:T(8,128)(2,1)S(1)}, bf16[256,896]{1,0:T(8,128)(2,1)S(1)}, u32[]{:S(2)}, u32[]{:S(2)}) collective-permute-start(bf16[256,896]{1,0:T(8,128)(2,1)S(1)} %get-tuple-element.137), channel_id=1, source_target_pairs={{0,1},{1,0},{2,3},{3,2},{4,5},{5,4},{6,7},{7,6},{8,9},{9,8},{10,11... | collective-permute-start | bytes 1376264 | tf_op jit(solution)/shard_map/ppermute | solution.py:323
  76.3 1.6 %collective-permute-start.20 = (bf16[32,3584]{1,0:T(8,128)(2,1)S(1)}, bf16[32,3584]{1,0:T(8,128)(2,1)S(1)}, u32[]{:S(2)}, u32[]{:S(2)}) collective-permute-start(bf16[32,3584]{1,0:T(8,128)(2,1)S(1)} %get-tuple-element.130.refs_2_), channel_id=1, source_target_pairs={{0,1},{1,0},{2,3},{3,2},{4,5},{5,4},{6,7},{7,6},{8,9},{9,8},{10,11... | collective-permute-start | bytes 688136 | tf_op jit(solution)/shard_map/ppermute | solution.py:323
  80.5 2.8 %collective-permute-start.23 = (bf16[1824,128]{1,0:T(8,128)(2,1)S(1)}, bf16[1824,128]{1,0:T(8,128)(2,1)S(1)}, u32[]{:S(2)}, u32[]{:S(2)}) collective-permute-start(bf16[1824,128]{1,0:T(8,128)(2,1)S(1)} %collective-permute-done.16.refs_1_), channel_id=1, source_target_pairs={{0,1},{1,0},{2,3},{3,2},{4,5},{5,4},{6,7},{7,6},{8,9},{9,8},{10,11... | collective-permute-start | bytes 1400840 | tf_op jit(solution)/shard_map/ppermute | solution.py:323
  80.5 2.8 %collective-permute-start.24 = (bf16[1824,128]{1,0:T(8,128)(2,1)S(1)}, bf16[1824,128]{1,0:T(8,128)(2,1)S(1)}, u32[]{:S(2)}, u32[]{:S(2)}) collective-permute-start(bf16[1824,128]{1,0:T(8,128)(2,1)S(1)} %collective-permute-done.18.refs_2_), channel_id=1, source_target_pairs={{0,1},{1,0},{2,3},{3,2},{4,5},{5,4},{6,7},{7,6},{8,9},{9,8},{10,11... | collective-permute-start | bytes 1400840 | tf_op jit(solution)/shard_map/ppermute | solution.py:323

commit v16 on v13

--- a/solution.py
+++ b/solution.py
@@ -350,7 +350,9 @@
             back_of, operands, sums = lax.optimization_barrier((moved[1], operands, sums))
             moved = [ahead_of, back_of]
         pieces = moved
-    pieces, operands, tile = lax.optimization_barrier((pieces, operands, settle(sums)))
+    tile, pieces = settle(sums), list(pieces)
+    for k in range(len(pieces)):
+        pieces[k], operands, tile = lax.optimization_barrier((pieces[k], operands, tile))
     others = [swap(piece) for piece in pieces]
     tile, *operands = take_own(scalars, pieces, tile, operands)
     return tuple(finish(scalars, others, tile, operands, 1.0 / (devices * tok_rows)))

time: 95.7 us -> 94.4 us (0.986)
  no operation moved by 1% of the time
where the time goes in v16:
time: 94.4 us; the launch traced here: 94.2 us
  waiting for transfers between devices  50.6 us (54%)
  Pallas kernels  28.2 us (30%)
  starting transfers between devices  12.3 us (13%)
  local copies, waits for them, and re-layouts  1.32 us (1%)
  between operations  1.01 us (1%)
    ppermute x8, waiting for transfers between devices, advance(): lax.ppermute(array, 'tok', stream)  42.4 us
    pallas_call x1, Pallas kernels, finish(): pl.pallas_call(functools.partial(finish_kernel, final), out_shape=[jax.Sh...  12 us
    pallas_call x4, Pallas kernels, absorb(): pl.pallas_call(functools.partial(absorb_kernel, count, bool(before)), out...  9.82 us
    ppermute x8, starting transfers between devices, advance(): lax.ppermute(array, 'tok', stream)  9.27 us
    ppermute x17, waiting for transfers between devices, swap(): return lax.ppermute(array, 'tok', pair)  8.13 us
    pallas_call x4, Pallas kernels, prepare(): pl.pallas_call(functools.partial(prepare_kernel, len(packs), at), out_sha...  3.21 us
    ppermute x17, starting transfers between devices, swap(): return lax.ppermute(array, 'tok', pair)  3.02 us
    pallas_call x1, Pallas kernels, take_own(): pl.pallas_call(take_own_kernel, out_shape=[jax.ShapeDtypeStruct(a.shape,...  2.28 us
  transfers between devices with their start and end apart: 25, of which 12 were waited for; matrix products, arithmetic and copies ran while one was open for 0% of the time, Pallas kernels for 17%

profile of v16, /device:TPU:0, one launch (start us, length us, event | category | flops | bytes accessed | tf_op | source)
XLA Modules:
  0.0 94.2 jit_solution(17727284001175201374)
XLA Ops:
  0.6 0.7 select_reduce_fusion
  1.3 0.0 copy-start
  1.4 1.2 %copy-done = bf16[128,3584]{1,0:T(8,128)(2,1)S(1)} copy-done((bf16[128,3584]{1,0:T(8,128)(2,1)S(1)}, bf16[128,3584]{1,0:T(8,128)(2,1)}, u32[]{:S(2)}) %copy-start) | copy-done | bytes 917528
  2.5 0.2 make_message.1.refs_1_
  2.7 3.1 %collective-permute-start = (bf16[3616,128]{1,0:T(8,128)(2,1)S(1)}, bf16[3616,128]{1,0:T(8,128)(2,1)S(1)}, u32[]{:S(2)}, u32[]{:S(2)}) collective-permute-start(bf16[3616,128]{1,0:T(8,128)(2,1)S(1)} %make_message.1.refs_1_), channel_id=1, source_target_pairs={{0,4},{1,5},{4,8},{5,9},{8,12},{9,13},{12,14},{13,15},{14,10},{15,... | collective-permute-start | bytes 2777096 | tf_op jit(solution)/shard_map/ppermute | solution.py:330
  5.8 0.0 collective-permute-start.5
  5.8 0.1 stack.23.refs_0_
  5.9 1.5 %absorb.4 = (f32[896,896]{1,0:T(8,128)S(1)}, bf16[128,896]{1,0:T(8,128)(2,1)S(1)}, bf16[128,896]{1,0:T(8,128)(2,1)S(1)}, bf16[32,3584]{1,0:T(8,128)(2,1)S(1)}) custom-call(s32[5]{0:T(128)S(1)} %stack.23.refs_0_, bf16[3616,128]{1,0:T(8,128)(2,1)S(1)} %make_message.1.refs_1_), custom_call_target="tpu_custom_call" | custom-call | flops 1 | bytes 1 | tf_op jit(solution)/shard_map/absorb/pallas_call | solution.py:143
  7.4 0.1 collective-permute-start.1
  7.5 0.5 collective-permute-start.2
  8.0 0.1 collective-permute-start.3
  8.1 0.9 collective-permute-done.1.refs_2_
  9.0 0.8 prepare_rows.4
  9.8 0.0 collective-permute-done.2.refs_4_
  9.8 0.0 collective-permute-done.3.refs_5_
  9.8 16.5 %collective-permute-done.refs_1_ = bf16[3616,128]{1,0:T(8,128)(2,1)S(1)} collective-permute-done((bf16[3616,128]{1,0:T(8,128)(2,1)S(1)}, bf16[3616,128]{1,0:T(8,128)(2,1)S(1)}, u32[]{:S(2)}, u32[]{:S(2)}) %collective-permute-start) | collective-permute-done | bytes 925728 | tf_op jit(solution)/shard_map/ppermute | solution.py:330
  26.3 1.8 %collective-permute-start.4 = (bf16[3616,128]{1,0:T(8,128)(2,1)S(1)}, bf16[3616,128]{1,0:T(8,128)(2,1)S(1)}, u32[]{:S(2)}, u32[]{:S(2)}) collective-permute-start(bf16[3616,128]{1,0:T(8,128)(2,1)S(1)} %collective-permute-done.refs_1_), channel_id=1, source_target_pairs={{0,4},{1,5},{4,8},{5,9},{8,12},{9,13},{12,14},{13,15},{14,10},{15,... | collective-permute-start | bytes 2777096 | tf_op jit(solution)/shard_map/ppermute | solution.py:330
  28.1 0.0 collective-permute-done.5.refs_2_
  28.1 0.2 collective-permute-start.11
  28.3 2.7 %absorb.5 = (f32[896,896]{1,0:T(8,128)S(1)}, bf16[256,896]{1,0:T(8,128)(2,1)S(1)}, bf16[256,896]{1,0:T(8,128)(2,1)S(1)}, bf16[32,3584]{1,0:T(8,128)(2,1)S(1)}, bf16[32,3584]{1,0:T(8,128)(2,1)S(1)}) custom-call(s32[5]{0:T(128)S(1)} %stack.23.refs_0_, bf16[3616,128]{1,0:T(8,128)(2,1)S(1)} %collective-permute-done.refs_1_, ...), custom_call_target="tpu_custom_call", output_to_operand_aliasing={{0}: (3, {})} | custom-call | flops 1 | bytes 1 | tf_op jit(solution)/shard_map/absorb/pallas_call | solution.py:143
  30.9 0.1 collective-permute-start.6
  31.0 0.5 collective-permute-start.8
  31.5 0.1 collective-permute-start.9
  31.6 0.9 collective-permute-done.6.refs_3_
  32.5 0.1 collective-permute-start.7
  32.6 1.5 %collective-permute-done.7.refs_4_ = bf16[32,3584]{1,0:T(8,128)(2,1)S(1)} collective-permute-done((bf16[32,3584]{1,0:T(8,128)(2,1)S(1)}, bf16[32,3584]{1,0:T(8,128)(2,1)S(1)}, u32[]{:S(2)}, u32[]{:S(2)}) %collective-permute-start.7) | collective-permute-done | bytes 229408 | tf_op jit(solution)/shard_map/ppermute | solution.py:327
  34.1 0.8 prepare_rows.5
  35.0 0.0 collective-permute-done.8.refs_4_
  35.0 0.0 collective-permute-done.9.refs_5_
  35.0 13.0 %collective-permute-done.4.refs_1_ = bf16[3616,128]{1,0:T(8,128)(2,1)S(1)} collective-permute-done((bf16[3616,128]{1,0:T(8,128)(2,1)S(1)}, bf16[3616,128]{1,0:T(8,128)(2,1)S(1)}, u32[]{:S(2)}, u32[]{:S(2)}) %collective-permute-start.4) | collective-permute-done | bytes 925728 | tf_op jit(solution)/shard_map/ppermute | solution.py:330
  48.0 1.5 %collective-permute-start.10 = (bf16[3616,128]{1,0:T(8,128)(2,1)S(1)}, bf16[3616,128]{1,0:T(8,128)(2,1)S(1)}, u32[]{:S(2)}, u32[]{:S(2)}) collective-permute-start(bf16[3616,128]{1,0:T(8,128)(2,1)S(1)} %collective-permute-done.4.refs_1_), channel_id=1, source_target_pairs={{0,4},{1,5},{4,8},{5,9},{8,12},{9,13},{12,14},{13,15},{14,10},{15,... | collective-permute-start | bytes 2777096 | tf_op jit(solution)/shard_map/ppermute | solution.py:330
  49.5 0.0 collective-permute-done.11.refs_2_
  49.5 0.5 collective-permute-start.17
  50.0 2.7 %absorb.6 = (f32[896,896]{1,0:T(8,128)S(1)}, bf16[256,896]{1,0:T(8,128)(2,1)S(1)}, bf16[256,896]{1,0:T(8,128)(2,1)S(1)}, bf16[32,3584]{1,0:T(8,128)(2,1)S(1)}, bf16[32,3584]{1,0:T(8,128)(2,1)S(1)}) custom-call(s32[5]{0:T(128)S(1)} %stack.23.refs_0_, bf16[3616,128]{1,0:T(8,128)(2,1)S(1)} %collective-permute-done.4.refs_1_, ...), custom_call_target="tpu_custom_call", output_to_operand_aliasing={{0}: (3, {})} | custom-call | flops 1 | bytes 1 | tf_op jit(solution)/shard_map/absorb/pallas_call | solution.py:143
  52.7 0.1 collective-permute-start.12
  52.8 0.5 collective-permute-start.14
  53.3 0.1 collective-permute-start.15
  53.4 0.9 collective-permute-done.12.refs_3_
  54.3 0.1 collective-permute-start.13
  54.4 1.5 %collective-permute-done.13.refs_4_ = bf16[32,3584]{1,0:T(8,128)(2,1)S(1)} collective-permute-done((bf16[32,3584]{1,0:T(8,128)(2,1)S(1)}, bf16[32,3584]{1,0:T(8,128)(2,1)S(1)}, u32[]{:S(2)}, u32[]{:S(2)}) %collective-permute-start.13) | collective-permute-done | bytes 229408 | tf_op jit(solution)/shard_map/ppermute | solution.py:327
  55.9 0.8 prepare_rows.6
  56.8 0.0 collective-permute-done.14.refs_4_
  56.8 0.0 collective-permute-done.15.refs_5_
  56.8 12.0 %collective-permute-done.10.refs_1_ = bf16[3616,128]{1,0:T(8,128)(2,1)S(1)} collective-permute-done((bf16[3616,128]{1,0:T(8,128)(2,1)S(1)}, bf16[3616,128]{1,0:T(8,128)(2,1)S(1)}, u32[]{:S(2)}, u32[]{:S(2)}) %collective-permute-start.10) | collective-permute-done | bytes 925728 | tf_op jit(solution)/shard_map/ppermute | solution.py:330
  68.8 1.3 %collective-permute-start.16 = (bf16[1824,128]{1,0:T(8,128)(2,1)S(1)}, bf16[1824,128]{1,0:T(8,128)(2,1)S(1)}, u32[]{:S(2)}, u32[]{:S(2)}) collective-permute-start(bf16[1824,128]{1,0:T(8,128)(2,1)S(1)} %slice.6), channel_id=1, source_target_pairs={{0,4},{1,5},{4,8},{5,9},{8,12},{9,13},{12,14},{13,15},{14,10},{15,... | collective-permute-start | bytes 1400840 | tf_op jit(solution)/shard_map/ppermute | solution.py:330
  70.1 0.0 collective-permute-done.17.refs_2_
  70.2 0.8 collective-permute-start.23
  71.0 2.9 %absorb.7 = (f32[896,896]{1,0:T(8,128)S(1)}, bf16[256,896]{1,0:T(8,128)(2,1)S(1)}, bf16[256,896]{1,0:T(8,128)(2,1)S(1)}, bf16[32,3584]{1,0:T(8,128)(2,1)S(1)}, bf16[32,3584]{1,0:T(8,128)(2,1)S(1)}) custom-call(s32[5]{0:T(128)S(1)} %stack.23.refs_0_, bf16[3616,128]{1,0:T(8,128)(2,1)S(1)} %collective-permute-done.10.refs_1_, ...), custom_call_target="tpu_custom_call", output_to_operand_aliasing={{0}: (3, {})} | custom-call | flops 1 | bytes 1 | tf_op jit(solution)/shard_map/absorb/pallas_call | solution.py:143
  73.9 0.1 collective-permute-start.18
  74.0 0.5 collective-permute-start.20
  74.5 0.1 collective-permute-start.21
  74.5 0.9 collective-permute-done.18.refs_3_
  75.4 0.1 collective-permute-start.19
  75.6 1.5 %collective-permute-done.19.refs_4_ = bf16[32,3584]{1,0:T(8,128)(2,1)S(1)} collective-permute-done((bf16[32,3584]{1,0:T(8,128)(2,1)S(1)}, bf16[32,3584]{1,0:T(8,128)(2,1)S(1)}, u32[]{:S(2)}, u32[]{:S(2)}) %collective-permute-start.19) | collective-permute-done | bytes 229408 | tf_op jit(solution)/shard_map/ppermute | solution.py:327
  77.1 0.8 prepare_rows.7
  77.9 0.0 collective-permute-done.20.left
  77.9 0.7 settle.1.refs_3_
  78.7 0.2 collective-permute-done.16.refs_1_
  78.9 0.0 collective-permute-start.22
  78.9 0.7 collective-permute-done.23.refs_2_
  79.7 0.0 collective-permute-start.24
  79.7 2.3 %take_own.1 = (f32[896,896]{1,0:T(8,128)S(1)}, bf16[512,3584]{1,0:T(8,128)(2,1)S(1)}, bf16[1792,512]{1,0:T(8,128)(2,1)S(1)}) custom-call(s32[5]{0:T(128)S(1)} %stack.23.refs_0_, bf16[1824,128]{1,0:T(8,128)(2,1)S(1)} %collective-permute-done.16.refs_1_, ...), custom_call_target="tpu_custom_call", output_to_operand_aliasing={{0}: (3, {}), {1}: (4, {}), {2}: (5, {})} | custom-call | flops 1 | bytes 1 | tf_op jit(solution)/shard_map/take_own/pallas_call | solution.py:225
  82.0 0.0 collective-permute-done.24.refs_2_
  82.0 12.0 %finish.1 = (f32[1792,3584]{1,0:T(8,128)}, f32[1,896,896]{2,1,0:T(8,128)}, bf16[512,3584]{1,0:T(8,128)(2,1)S(1)}, bf16[1792,512]{1,0:T(8,128)(2,1)S(1)}) custom-call(s32[5]{0:T(128)S(1)} %stack.23.refs_0_, bf16[1824,128]{1,0:T(8,128)(2,1)S(1)} %collective-permute-done.22.refs_1_, ...), custom_call_target="tpu_custom_call", output_to_operand_aliasing={{2}: (4, {}), {3}: (5, {})} | custom-call | flops 1 | bytes 1 | tf_op jit(solution)/shard_map/finish/pallas_call | solution.py:270
  (4 shorter events, 0.1 us)
Async XLA Ops:
  1.3 1.2 %copy-start = (bf16[128,3584]{1,0:T(8,128)(2,1)S(1)}, bf16[128,3584]{1,0:T(8,128)(2,1)}, u32[]{:S(2)}) copy-start(bf16[128,3584]{1,0:T(8,128)(2,1)} %tokens.1) | copy-start | bytes 2752516
  2.7 23.5 %collective-permute-start = (bf16[3616,128]{1,0:T(8,128)(2,1)S(1)}, bf16[3616,128]{1,0:T(8,128)(2,1)S(1)}, u32[]{:S(2)}, u32[]{:S(2)}) collective-permute-start(bf16[3616,128]{1,0:T(8,128)(2,1)S(1)} %make_message.1.refs_1_), channel_id=1, source_target_pairs={{0,4},{1,5},{4,8},{5,9},{8,12},{9,13},{12,14},{13,15},{14,10},{15,... | collective-permute-start | bytes 2777096 | tf_op jit(solution)/shard_map/ppermute | solution.py:330
  5.8 22.3 %collective-permute-start.5 = (bf16[3616,128]{1,0:T(8,128)(2,1)S(1)}, bf16[3616,128]{1,0:T(8,128)(2,1)S(1)}, u32[]{:S(2)}, u32[]{:S(2)}) collective-permute-start(bf16[3616,128]{1,0:T(8,128)(2,1)S(1)} %make_message.1.refs_1_), channel_id=1, source_target_pairs={{4,0},{5,1},{8,4},{9,5},{12,8},{13,9},{14,12},{15,13},{10,14},{11,... | collective-permute-start | bytes 2777096 | tf_op jit(solution)/shard_map/ppermute | solution.py:330
  7.4 1.6 %collective-permute-start.1 = (bf16[32,3584]{1,0:T(8,128)(2,1)S(1)}, bf16[32,3584]{1,0:T(8,128)(2,1)S(1)}, u32[]{:S(2)}, u32[]{:S(2)}) collective-permute-start(bf16[32,3584]{1,0:T(8,128)(2,1)S(1)} %get-tuple-element.78.refs_1_), channel_id=1, source_target_pairs={{0,1},{1,0},{2,3},{3,2},{4,5},{5,4},{6,7},{7,6},{8,9},{9,8},{10,11... | collective-permute-start | bytes 688136 | tf_op jit(solution)/shard_map/ppermute | solution.py:327
  7.5 2.2 %collective-permute-start.2 = (bf16[128,896]{1,0:T(8,128)(2,1)S(1)}, bf16[128,896]{1,0:T(8,128)(2,1)S(1)}, u32[]{:S(2)}, u32[]{:S(2)}) collective-permute-start(bf16[128,896]{1,0:T(8,128)(2,1)S(1)} %get-tuple-element.82), channel_id=1, source_target_pairs={{0,1},{1,0},{2,3},{3,2},{4,5},{5,4},{6,7},{7,6},{8,9},{9,8},{10,11... | collective-permute-start | bytes 688136 | tf_op jit(solution)/shard_map/ppermute | solution.py:327
  8.0 1.8 %collective-permute-start.3 = (bf16[128,896]{1,0:T(8,128)(2,1)S(1)}, bf16[128,896]{1,0:T(8,128)(2,1)S(1)}, u32[]{:S(2)}, u32[]{:S(2)}) collective-permute-start(bf16[128,896]{1,0:T(8,128)(2,1)S(1)} %get-tuple-element.83), channel_id=1, source_target_pairs={{0,1},{1,0},{2,3},{3,2},{4,5},{5,4},{6,7},{7,6},{8,9},{9,8},{10,11... | collective-permute-start | bytes 688136 | tf_op jit(solution)/shard_map/ppermute | solution.py:327
  26.3 21.7 %collective-permute-start.4 = (bf16[3616,128]{1,0:T(8,128)(2,1)S(1)}, bf16[3616,128]{1,0:T(8,128)(2,1)S(1)}, u32[]{:S(2)}, u32[]{:S(2)}) collective-permute-start(bf16[3616,128]{1,0:T(8,128)(2,1)S(1)} %collective-permute-done.refs_1_), channel_id=1, source_target_pairs={{0,4},{1,5},{4,8},{5,9},{8,12},{9,13},{12,14},{13,15},{14,10},{15,... | collective-permute-start | bytes 2777096 | tf_op jit(solution)/shard_map/ppermute | solution.py:330
  28.1 21.4 %collective-permute-start.11 = (bf16[3616,128]{1,0:T(8,128)(2,1)S(1)}, bf16[3616,128]{1,0:T(8,128)(2,1)S(1)}, u32[]{:S(2)}, u32[]{:S(2)}) collective-permute-start(bf16[3616,128]{1,0:T(8,128)(2,1)S(1)} %collective-permute-done.5.refs_2_), channel_id=1, source_target_pairs={{4,0},{5,1},{8,4},{9,5},{12,8},{13,9},{14,12},{15,13},{10,14},{11,... | collective-permute-start | bytes 2777096 | tf_op jit(solution)/shard_map/ppermute | solution.py:330
  30.9 1.6 %collective-permute-start.6 = (bf16[32,3584]{1,0:T(8,128)(2,1)S(1)}, bf16[32,3584]{1,0:T(8,128)(2,1)S(1)}, u32[]{:S(2)}, u32[]{:S(2)}) collective-permute-start(bf16[32,3584]{1,0:T(8,128)(2,1)S(1)} %get-tuple-element.94.refs_1_), channel_id=1, source_target_pairs={{0,1},{1,0},{2,3},{3,2},{4,5},{5,4},{6,7},{7,6},{8,9},{9,8},{10,11... | collective-permute-start | bytes 688136 | tf_op jit(solution)/shard_map/ppermute | solution.py:327
  31.0 3.9 %collective-permute-start.8 = (bf16[256,896]{1,0:T(8,128)(2,1)S(1)}, bf16[256,896]{1,0:T(8,128)(2,1)S(1)}, u32[]{:S(2)}, u32[]{:S(2)}) collective-permute-start(bf16[256,896]{1,0:T(8,128)(2,1)S(1)} %get-tuple-element.101), channel_id=1, source_target_pairs={{0,1},{1,0},{2,3},{3,2},{4,5},{5,4},{6,7},{7,6},{8,9},{9,8},{10,11... | collective-permute-start | bytes 1376264 | tf_op jit(solution)/shard_map/ppermute | solution.py:327
  31.5 3.5 %collective-permute-start.9 = (bf16[256,896]{1,0:T(8,128)(2,1)S(1)}, bf16[256,896]{1,0:T(8,128)(2,1)S(1)}, u32[]{:S(2)}, u32[]{:S(2)}) collective-permute-start(bf16[256,896]{1,0:T(8,128)(2,1)S(1)} %get-tuple-element.102), channel_id=1, source_target_pairs={{0,1},{1,0},{2,3},{3,2},{4,5},{5,4},{6,7},{7,6},{8,9},{9,8},{10,11... | collective-permute-start | bytes 1376264 | tf_op jit(solution)/shard_map/ppermute | solution.py:327
  32.5 1.6 %collective-permute-start.7 = (bf16[32,3584]{1,0:T(8,128)(2,1)S(1)}, bf16[32,3584]{1,0:T(8,128)(2,1)S(1)}, u32[]{:S(2)}, u32[]{:S(2)}) collective-permute-start(bf16[32,3584]{1,0:T(8,128)(2,1)S(1)} %get-tuple-element.95.refs_2_), channel_id=1, source_target_pairs={{0,1},{1,0},{2,3},{3,2},{4,5},{5,4},{6,7},{7,6},{8,9},{9,8},{10,11... | collective-permute-start | bytes 688136 | tf_op jit(solution)/shard_map/ppermute | solution.py:327
  48.0 20.8 %collective-permute-start.10 = (bf16[3616,128]{1,0:T(8,128)(2,1)S(1)}, bf16[3616,128]{1,0:T(8,128)(2,1)S(1)}, u32[]{:S(2)}, u32[]{:S(2)}) collective-permute-start(bf16[3616,128]{1,0:T(8,128)(2,1)S(1)} %collective-permute-done.4.refs_1_), channel_id=1, source_target_pairs={{0,4},{1,5},{4,8},{5,9},{8,12},{9,13},{12,14},{13,15},{14,10},{15,... | collective-permute-start | bytes 2777096 | tf_op jit(solution)/shard_map/ppermute | solution.py:330
  49.5 20.7 %collective-permute-start.17 = (bf16[3616,128]{1,0:T(8,128)(2,1)S(1)}, bf16[3616,128]{1,0:T(8,128)(2,1)S(1)}, u32[]{:S(2)}, u32[]{:S(2)}) collective-permute-start(bf16[3616,128]{1,0:T(8,128)(2,1)S(1)} %collective-permute-done.11.refs_2_), channel_id=1, source_target_pairs={{4,0},{5,1},{8,4},{9,5},{12,8},{13,9},{14,12},{15,13},{10,14},{11,... | collective-permute-start | bytes 2777096 | tf_op jit(solution)/shard_map/ppermute | solution.py:330
  52.7 1.6 %collective-permute-start.12 = (bf16[32,3584]{1,0:T(8,128)(2,1)S(1)}, bf16[32,3584]{1,0:T(8,128)(2,1)S(1)}, u32[]{:S(2)}, u32[]{:S(2)}) collective-permute-start(bf16[32,3584]{1,0:T(8,128)(2,1)S(1)} %get-tuple-element.113.refs_1_), channel_id=1, source_target_pairs={{0,1},{1,0},{2,3},{3,2},{4,5},{5,4},{6,7},{7,6},{8,9},{9,8},{10,11... | collective-permute-start | bytes 688136 | tf_op jit(solution)/shard_map/ppermute | solution.py:327
  52.8 3.9 %collective-permute-start.14 = (bf16[256,896]{1,0:T(8,128)(2,1)S(1)}, bf16[256,896]{1,0:T(8,128)(2,1)S(1)}, u32[]{:S(2)}, u32[]{:S(2)}) collective-permute-start(bf16[256,896]{1,0:T(8,128)(2,1)S(1)} %get-tuple-element.120), channel_id=1, source_target_pairs={{0,1},{1,0},{2,3},{3,2},{4,5},{5,4},{6,7},{7,6},{8,9},{9,8},{10,11... | collective-permute-start | bytes 1376264 | tf_op jit(solution)/shard_map/ppermute | solution.py:327
  53.3 3.5 %collective-permute-start.15 = (bf16[256,896]{1,0:T(8,128)(2,1)S(1)}, bf16[256,896]{1,0:T(8,128)(2,1)S(1)}, u32[]{:S(2)}, u32[]{:S(2)}) collective-permute-start(bf16[256,896]{1,0:T(8,128)(2,1)S(1)} %get-tuple-element.121), channel_id=1, source_target_pairs={{0,1},{1,0},{2,3},{3,2},{4,5},{5,4},{6,7},{7,6},{8,9},{9,8},{10,11... | collective-permute-start | bytes 1376264 | tf_op jit(solution)/shard_map/ppermute | solution.py:327
  54.3 1.6 %collective-permute-start.13 = (bf16[32,3584]{1,0:T(8,128)(2,1)S(1)}, bf16[32,3584]{1,0:T(8,128)(2,1)S(1)}, u32[]{:S(2)}, u32[]{:S(2)}) collective-permute-start(bf16[32,3584]{1,0:T(8,128)(2,1)S(1)} %get-tuple-element.114.refs_2_), channel_id=1, source_target_pairs={{0,1},{1,0},{2,3},{3,2},{4,5},{5,4},{6,7},{7,6},{8,9},{9,8},{10,11... | collective-permute-start | bytes 688136 | tf_op jit(solution)/shard_map/ppermute | solution.py:327
  68.8 10.1 %collective-permute-start.16 = (bf16[1824,128]{1,0:T(8,128)(2,1)S(1)}, bf16[1824,128]{1,0:T(8,128)(2,1)S(1)}, u32[]{:S(2)}, u32[]{:S(2)}) collective-permute-start(bf16[1824,128]{1,0:T(8,128)(2,1)S(1)} %slice.6), channel_id=1, source_target_pairs={{0,4},{1,5},{4,8},{5,9},{8,12},{9,13},{12,14},{13,15},{14,10},{15,... | collective-permute-start | bytes 1400840 | tf_op jit(solution)/shard_map/ppermute | solution.py:330
  70.2 9.5 %collective-permute-start.23 = (bf16[1824,128]{1,0:T(8,128)(2,1)S(1)}, bf16[1824,128]{1,0:T(8,128)(2,1)S(1)}, u32[]{:S(2)}, u32[]{:S(2)}) collective-permute-start(bf16[1824,128]{1,0:T(8,128)(2,1)S(1)} %slice.7), channel_id=1, source_target_pairs={{4,0},{5,1},{8,4},{9,5},{12,8},{13,9},{14,12},{15,13},{10,14},{11,... | collective-permute-start | bytes 1400840 | tf_op jit(solution)/shard_map/ppermute | solution.py:330
  73.9 1.6 %collective-permute-start.18 = (bf16[32,3584]{1,0:T(8,128)(2,1)S(1)}, bf16[32,3584]{1,0:T(8,128)(2,1)S(1)}, u32[]{:S(2)}, u32[]{:S(2)}) collective-permute-start(bf16[32,3584]{1,0:T(8,128)(2,1)S(1)} %get-tuple-element.132.refs_1_), channel_id=1, source_target_pairs={{0,1},{1,0},{2,3},{3,2},{4,5},{5,4},{6,7},{7,6},{8,9},{9,8},{10,11... | collective-permute-start | bytes 688136 | tf_op jit(solution)/shard_map/ppermute | solution.py:327
  74.0 3.9 %collective-permute-start.20 = (bf16[256,896]{1,0:T(8,128)(2,1)S(1)}, bf16[256,896]{1,0:T(8,128)(2,1)S(1)}, u32[]{:S(2)}, u32[]{:S(2)}) collective-permute-start(bf16[256,896]{1,0:T(8,128)(2,1)S(1)} %get-tuple-element.139), channel_id=1, source_target_pairs={{0,1},{1,0},{2,3},{3,2},{4,5},{5,4},{6,7},{7,6},{8,9},{9,8},{10,11... | collective-permute-start | bytes 1376264 | tf_op jit(solution)/shard_map/ppermute | solution.py:327
  74.5 3.5 %collective-permute-start.21 = (bf16[256,896]{1,0:T(8,128)(2,1)S(1)}, bf16[256,896]{1,0:T(8,128)(2,1)S(1)}, u32[]{:S(2)}, u32[]{:S(2)}) collective-permute-start(bf16[256,896]{1,0:T(8,128)(2,1)S(1)} %get-tuple-element.140), channel_id=1, source_target_pairs={{0,1},{1,0},{2,3},{3,2},{4,5},{5,4},{6,7},{7,6},{8,9},{9,8},{10,11... | collective-permute-start | bytes 1376264 | tf_op jit(solution)/shard_map/ppermute | solution.py:327
  75.4 1.6 %collective-permute-start.19 = (bf16[32,3584]{1,0:T(8,128)(2,1)S(1)}, bf16[32,3584]{1,0:T(8,128)(2,1)S(1)}, u32[]{:S(2)}, u32[]{:S(2)}) collective-permute-start(bf16[32,3584]{1,0:T(8,128)(2,1)S(1)} %get-tuple-element.133.refs_2_), channel_id=1, source_target_pairs={{0,1},{1,0},{2,3},{3,2},{4,5},{5,4},{6,7},{7,6},{8,9},{9,8},{10,11... | collective-permute-start | bytes 688136 | tf_op jit(solution)/shard_map/ppermute | solution.py:327
  78.9 3.1 %collective-permute-start.22 = (bf16[1824,128]{1,0:T(8,128)(2,1)S(1)}, bf16[1824,128]{1,0:T(8,128)(2,1)S(1)}, u32[]{:S(2)}, u32[]{:S(2)}) collective-permute-start(bf16[1824,128]{1,0:T(8,128)(2,1)S(1)} %collective-permute-done.16.refs_1_), channel_id=1, source_target_pairs={{0,1},{1,0},{2,3},{3,2},{4,5},{5,4},{6,7},{7,6},{8,9},{9,8},{10,11... | collective-permute-start | bytes 1400840 | tf_op jit(solution)/shard_map/ppermute | solution.py:327
  79.7 2.3 %collective-permute-start.24 = (bf16[1824,128]{1,0:T(8,128)(2,1)S(1)}, bf16[1824,128]{1,0:T(8,128)(2,1)S(1)}, u32[]{:S(2)}, u32[]{:S(2)}) collective-permute-start(bf16[1824,128]{1,0:T(8,128)(2,1)S(1)} %collective-permute-done.23.refs_2_), channel_id=1, source_target_pairs={{0,1},{1,0},{2,3},{3,2},{4,5},{5,4},{6,7},{7,6},{8,9},{9,8},{10,11... | collective-permute-start | bytes 1400840 | tf_op jit(solution)/shard_map/ppermute | solution.py:327

commit v17 on v16

--- a/solution.py
+++ b/solution.py
@@ -189,13 +189,6 @@
     )(scalars, *packs, *operands)
 
 
-def take_in(scalars, halves, at, rows, across, left, right):
-    place_rows(scalars[4], pack(scalars[0], halves), at, rows, across)
-    fetch_tile(scalars[1], [halves], left)
-    fetch_tile(scalars[2], [halves], right)
-    return product(left, right)
-
-
 def settle_kernel(before, left, right, tile):
     tile[...] = before[...] + product(left, right)
 
@@ -214,42 +207,39 @@
 
 
 def take_own_kernel(*refs):
-    scalars, halves, before, refs = refs[0], refs[1:3], refs[3], refs[6:]
-    tile, rows, across, left, right = refs
-    at = rows.shape[0] - 2 * CAP
-    tile[...] = before[...] + take_in(scalars, halves, at, rows, across, left, right)
-
-
-def take_own(scalars, halves, tile, operands):
-    edge = tile.shape[0]
+    scalars, piece, (rows, across) = refs[0], refs[1:3], refs[5:]
+    place_rows(scalars[4], pack(scalars[0], piece), rows.shape[0] - 2 * CAP, rows, across)
+
+
+def take_own(scalars, piece, operands):
     return pl.pallas_call(
         take_own_kernel,
-        out_shape=[jax.ShapeDtypeStruct(a.shape, a.dtype) for a in (tile, *operands)],
-        in_specs=[SMEM] + [VMEM] * 5,
-        out_specs=[VMEM] * 3,
-        scratch_shapes=[pltpu.VMEM((LANES, edge), BF16)] * 2,
-        input_output_aliases={3: 0, 4: 1, 5: 2},
+        out_shape=[jax.ShapeDtypeStruct(a.shape, a.dtype) for a in operands],
+        in_specs=[SMEM] + [VMEM] * 4,
+        out_specs=[VMEM] * 2,
+        input_output_aliases={3: 0, 4: 1},
         cost_estimate=SMALL,
         compiler_params=params(14),
         name="take_own",
-    )(scalars, *halves, tile, *operands)
+    )(scalars, *piece, *operands)
 
 
 def finish_kernel(final, *refs):
-    scalars, halves, before, (hessian, tile, rows, across, *scratch) = (
-        refs[0], refs[1:3], refs[3], refs[6:]
+    scalars, own, other, before, (hessian, tile, rows, across, *scratch) = (
+        refs[0], refs[1:3], refs[3:5], refs[5], refs[8:]
     )
     staging, sums, left, right, sent = scratch
-    at = rows.shape[0] - CAP
     copies = []
 
     def write(source, target):
         copies.append(pltpu.make_async_copy(source, target, sent.at[len(copies)]))
         copies[-1].start()
 
-    update = take_in(scalars, halves, at, rows, across, left, right)
-    sums[...] = (before[...] + update) * final
+    fetch_tile(scalars[1], [own, other], left)
+    fetch_tile(scalars[2], [own, other], right)
+    sums[...] = (before[...] + product(left, right)) * final
     write(sums, tile.at[0])
+    place_rows(scalars[4], pack(scalars[0], other), rows.shape[0] - CAP, rows, across)
     height = staging.shape[1]
     for m in range(SPLITS):
         span = slice(m * height, (m + 1) * height)
@@ -263,7 +253,7 @@
         copy.wait()
 
 
-def finish(scalars, halves, before, operands, final):
+def finish(scalars, own, other, before, operands, final):
     edge = before.shape[0]
     rows, across = operands
     slab, width = across.shape[0], rows.shape[1]
@@ -275,20 +265,20 @@
             jax.ShapeDtypeStruct(rows.shape, BF16),
             jax.ShapeDtypeStruct(across.shape, BF16),
         ],
-        in_specs=[SMEM] + [VMEM] * 5,
+        in_specs=[SMEM] + [VMEM] * 7,
         out_specs=[ANY, ANY, VMEM, VMEM],
         scratch_shapes=[
             pltpu.VMEM((SPLITS, slab // SPLITS, width), F32),
             pltpu.VMEM((edge, edge), F32),
-            pltpu.VMEM((LANES, edge), BF16),
-            pltpu.VMEM((LANES, edge), BF16),
+            pltpu.VMEM((2 * LANES, edge), BF16),
+            pltpu.VMEM((2 * LANES, edge), BF16),
             pltpu.SemaphoreType.DMA((SPLITS + 1,)),
         ],
-        input_output_aliases={4: 2, 5: 3},
+        input_output_aliases={6: 2, 7: 3},
         cost_estimate=SMALL,
         compiler_params=params(38),
         name="finish",
-    )(scalars, *halves, before, rows, across)[:2]
+    )(scalars, *own, *other, before, rows, across)[:2]
 
 
 def ring_of(chips):
@@ -354,8 +344,8 @@
     for k in range(len(pieces)):
         pieces[k], operands, tile = lax.optimization_barrier((pieces[k], operands, tile))
     others = [swap(piece) for piece in pieces]
-    tile, *operands = take_own(scalars, pieces, tile, operands)
-    return tuple(finish(scalars, others, tile, operands, 1.0 / (devices * tok_rows)))
+    operands = take_own(scalars, pieces, operands)
+    return tuple(finish(scalars, pieces, others, tile, operands, 1.0 / (devices * tok_rows)))
 
 
 def solution(mesh):

time: 94.4 us -> 93.8 us (level)
  transfers between devices with their start and end apart: 25 -> 25, of which waited for: 12 -> 13; matrix products, arithmetic and copies ran while one was open for 0% -> 0% of each run, Pallas kernels for 17% -> 16%
where the time goes in v17:
time: 93.8 us; the launch traced here: 93.6 us
  waiting for transfers between devices  51 us (54%)
  Pallas kernels  27.3 us (29%)
  starting transfers between devices  12.3 us (13%)
  local copies, waits for them, and re-layouts  1.32 us (1%)
  between operations  0.99 us (1%)
    ppermute x8, waiting for transfers between devices, advance(): lax.ppermute(array, 'tok', stream)  42.4 us
    pallas_call x1, Pallas kernels, finish(): pl.pallas_call(functools.partial(finish_kernel, final), out_shape=[jax.Sh...  11.9 us
    pallas_call x4, Pallas kernels, absorb(): pl.pallas_call(functools.partial(absorb_kernel, count, bool(before)), out...  9.83 us
    ppermute x8, starting transfers between devices, advance(): lax.ppermute(array, 'tok', stream)  9.27 us
    ppermute x17, waiting for transfers between devices, swap(): return lax.ppermute(array, 'tok', pair)  8.58 us
    pallas_call x4, Pallas kernels, prepare(): pl.pallas_call(functools.partial(prepare_kernel, len(packs), at), out_sha...  3.21 us
    ppermute x17, starting transfers between devices, swap(): return lax.ppermute(array, 'tok', pair)  3.02 us
  transfers between devices with their start and end apart: 25, of which 13 were waited for; matrix products, arithmetic and copies ran while one was open for 0% of the time, Pallas kernels for 16%

profile of v17, /device:TPU:0, one launch (start us, length us, event | category | flops | bytes accessed | tf_op | source)
XLA Modules:
  0.0 93.6 jit_solution(8900283520896909843)
XLA Ops:
  0.6 0.7 select_reduce_fusion
  1.3 0.0 copy-start
  1.4 1.2 %copy-done = bf16[128,3584]{1,0:T(8,128)(2,1)S(1)} copy-done((bf16[128,3584]{1,0:T(8,128)(2,1)S(1)}, bf16[128,3584]{1,0:T(8,128)(2,1)}, u32[]{:S(2)}) %copy-start) | copy-done | bytes 917528
  2.5 0.2 make_message.1.refs_1_
  2.7 3.1 %collective-permute-start = (bf16[3616,128]{1,0:T(8,128)(2,1)S(1)}, bf16[3616,128]{1,0:T(8,128)(2,1)S(1)}, u32[]{:S(2)}, u32[]{:S(2)}) collective-permute-start(bf16[3616,128]{1,0:T(8,128)(2,1)S(1)} %make_message.1.refs_1_), channel_id=1, source_target_pairs={{0,4},{1,5},{4,8},{5,9},{8,12},{9,13},{12,14},{13,15},{14,10},{15,... | collective-permute-start | bytes 2777096 | tf_op jit(solution)/shard_map/ppermute | solution.py:320
  5.8 0.0 collective-permute-start.5
  5.8 0.1 stack.23.refs_0_
  5.9 1.5 %absorb.4 = (f32[896,896]{1,0:T(8,128)S(1)}, bf16[128,896]{1,0:T(8,128)(2,1)S(1)}, bf16[128,896]{1,0:T(8,128)(2,1)S(1)}, bf16[32,3584]{1,0:T(8,128)(2,1)S(1)}) custom-call(s32[5]{0:T(128)S(1)} %stack.23.refs_0_, bf16[3616,128]{1,0:T(8,128)(2,1)S(1)} %make_message.1.refs_1_), custom_call_target="tpu_custom_call" | custom-call | flops 1 | bytes 1 | tf_op jit(solution)/shard_map/absorb/pallas_call | solution.py:143
  7.4 0.1 collective-permute-start.1
  7.5 0.5 collective-permute-start.2
  8.0 0.1 collective-permute-start.3
  8.1 0.9 collective-permute-done.1.refs_2_
  9.0 0.8 prepare_rows.4
  9.8 0.0 collective-permute-done.2.refs_4_
  9.8 0.0 collective-permute-done.3.refs_5_
  9.8 16.5 %collective-permute-done.refs_1_ = bf16[3616,128]{1,0:T(8,128)(2,1)S(1)} collective-permute-done((bf16[3616,128]{1,0:T(8,128)(2,1)S(1)}, bf16[3616,128]{1,0:T(8,128)(2,1)S(1)}, u32[]{:S(2)}, u32[]{:S(2)}) %collective-permute-start) | collective-permute-done | bytes 925728 | tf_op jit(solution)/shard_map/ppermute | solution.py:320
  26.3 1.8 %collective-permute-start.4 = (bf16[3616,128]{1,0:T(8,128)(2,1)S(1)}, bf16[3616,128]{1,0:T(8,128)(2,1)S(1)}, u32[]{:S(2)}, u32[]{:S(2)}) collective-permute-start(bf16[3616,128]{1,0:T(8,128)(2,1)S(1)} %collective-permute-done.refs_1_), channel_id=1, source_target_pairs={{0,4},{1,5},{4,8},{5,9},{8,12},{9,13},{12,14},{13,15},{14,10},{15,... | collective-permute-start | bytes 2777096 | tf_op jit(solution)/shard_map/ppermute | solution.py:320
  28.1 0.0 collective-permute-done.5.refs_2_
  28.1 0.2 collective-permute-start.11
  28.3 2.7 %absorb.5 = (f32[896,896]{1,0:T(8,128)S(1)}, bf16[256,896]{1,0:T(8,128)(2,1)S(1)}, bf16[256,896]{1,0:T(8,128)(2,1)S(1)}, bf16[32,3584]{1,0:T(8,128)(2,1)S(1)}, bf16[32,3584]{1,0:T(8,128)(2,1)S(1)}) custom-call(s32[5]{0:T(128)S(1)} %stack.23.refs_0_, bf16[3616,128]{1,0:T(8,128)(2,1)S(1)} %collective-permute-done.refs_1_, ...), custom_call_target="tpu_custom_call", output_to_operand_aliasing={{0}: (3, {})} | custom-call | flops 1 | bytes 1 | tf_op jit(solution)/shard_map/absorb/pallas_call | solution.py:143
  31.0 0.1 collective-permute-start.6
  31.0 0.5 collective-permute-start.8
  31.5 0.1 collective-permute-start.9
  31.6 0.9 collective-permute-done.6.refs_3_
  32.5 0.1 collective-permute-start.7
  32.6 1.5 %collective-permute-done.7.refs_4_ = bf16[32,3584]{1,0:T(8,128)(2,1)S(1)} collective-permute-done((bf16[32,3584]{1,0:T(8,128)(2,1)S(1)}, bf16[32,3584]{1,0:T(8,128)(2,1)S(1)}, u32[]{:S(2)}, u32[]{:S(2)}) %collective-permute-start.7) | collective-permute-done | bytes 229408 | tf_op jit(solution)/shard_map/ppermute | solution.py:317
  34.1 0.8 prepare_rows.5
  35.0 0.0 collective-permute-done.8.refs_4_
  35.0 0.0 collective-permute-done.9.refs_5_
  35.0 13.0 %collective-permute-done.4.refs_1_ = bf16[3616,128]{1,0:T(8,128)(2,1)S(1)} collective-permute-done((bf16[3616,128]{1,0:T(8,128)(2,1)S(1)}, bf16[3616,128]{1,0:T(8,128)(2,1)S(1)}, u32[]{:S(2)}, u32[]{:S(2)}) %collective-permute-start.4) | collective-permute-done | bytes 925728 | tf_op jit(solution)/shard_map/ppermute | solution.py:320
  48.0 1.5 %collective-permute-start.10 = (bf16[3616,128]{1,0:T(8,128)(2,1)S(1)}, bf16[3616,128]{1,0:T(8,128)(2,1)S(1)}, u32[]{:S(2)}, u32[]{:S(2)}) collective-permute-start(bf16[3616,128]{1,0:T(8,128)(2,1)S(1)} %collective-permute-done.4.refs_1_), channel_id=1, source_target_pairs={{0,4},{1,5},{4,8},{5,9},{8,12},{9,13},{12,14},{13,15},{14,10},{15,... | collective-permute-start | bytes 2777096 | tf_op jit(solution)/shard_map/ppermute | solution.py:320
  49.5 0.0 collective-permute-done.11.refs_2_
  49.5 0.5 collective-permute-start.17
  50.0 2.7 %absorb.6 = (f32[896,896]{1,0:T(8,128)S(1)}, bf16[256,896]{1,0:T(8,128)(2,1)S(1)}, bf16[256,896]{1,0:T(8,128)(2,1)S(1)}, bf16[32,3584]{1,0:T(8,128)(2,1)S(1)}, bf16[32,3584]{1,0:T(8,128)(2,1)S(1)}) custom-call(s32[5]{0:T(128)S(1)} %stack.23.refs_0_, bf16[3616,128]{1,0:T(8,128)(2,1)S(1)} %collective-permute-done.4.refs_1_, ...), custom_call_target="tpu_custom_call", output_to_operand_aliasing={{0}: (3, {})} | custom-call | flops 1 | bytes 1 | tf_op jit(solution)/shard_map/absorb/pallas_call | solution.py:143
  52.7 0.1 collective-permute-start.12
  52.8 0.5 collective-permute-start.14
  53.3 0.1 collective-permute-start.15
  53.4 0.9 collective-permute-done.12.refs_3_
  54.3 0.1 collective-permute-start.13
  54.4 1.5 %collective-permute-done.13.refs_4_ = bf16[32,3584]{1,0:T(8,128)(2,1)S(1)} collective-permute-done((bf16[32,3584]{1,0:T(8,128)(2,1)S(1)}, bf16[32,3584]{1,0:T(8,128)(2,1)S(1)}, u32[]{:S(2)}, u32[]{:S(2)}) %collective-permute-start.13) | collective-permute-done | bytes 229408 | tf_op jit(solution)/shard_map/ppermute | solution.py:317
  55.9 0.8 prepare_rows.6
  56.8 0.0 collective-permute-done.14.refs_4_
  56.8 0.0 collective-permute-done.15.refs_5_
  56.8 12.0 %collective-permute-done.10.refs_1_ = bf16[3616,128]{1,0:T(8,128)(2,1)S(1)} collective-permute-done((bf16[3616,128]{1,0:T(8,128)(2,1)S(1)}, bf16[3616,128]{1,0:T(8,128)(2,1)S(1)}, u32[]{:S(2)}, u32[]{:S(2)}) %collective-permute-start.10) | collective-permute-done | bytes 925728 | tf_op jit(solution)/shard_map/ppermute | solution.py:320
  68.8 1.3 %collective-permute-start.16 = (bf16[1824,128]{1,0:T(8,128)(2,1)S(1)}, bf16[1824,128]{1,0:T(8,128)(2,1)S(1)}, u32[]{:S(2)}, u32[]{:S(2)}) collective-permute-start(bf16[1824,128]{1,0:T(8,128)(2,1)S(1)} %slice.6), channel_id=1, source_target_pairs={{0,4},{1,5},{4,8},{5,9},{8,12},{9,13},{12,14},{13,15},{14,10},{15,... | collective-permute-start | bytes 1400840 | tf_op jit(solution)/shard_map/ppermute | solution.py:320
  70.2 0.8 collective-permute-start.22
  71.0 2.9 %absorb.7 = (f32[896,896]{1,0:T(8,128)S(1)}, bf16[256,896]{1,0:T(8,128)(2,1)S(1)}, bf16[256,896]{1,0:T(8,128)(2,1)S(1)}, bf16[32,3584]{1,0:T(8,128)(2,1)S(1)}, bf16[32,3584]{1,0:T(8,128)(2,1)S(1)}) custom-call(s32[5]{0:T(128)S(1)} %stack.23.refs_0_, bf16[3616,128]{1,0:T(8,128)(2,1)S(1)} %collective-permute-done.10.refs_1_, ...), custom_call_target="tpu_custom_call", output_to_operand_aliasing={{0}: (3, {})} | custom-call | flops 1 | bytes 1 | tf_op jit(solution)/shard_map/absorb/pallas_call | solution.py:143
  73.9 0.1 collective-permute-start.18
  74.0 0.5 collective-permute-start.20
  74.5 0.1 collective-permute-start.21
  74.5 0.9 collective-permute-done.18.refs_3_
  75.4 0.1 collective-permute-start.19
  75.6 1.5 %collective-permute-done.19.refs_4_ = bf16[32,3584]{1,0:T(8,128)(2,1)S(1)} collective-permute-done((bf16[32,3584]{1,0:T(8,128)(2,1)S(1)}, bf16[32,3584]{1,0:T(8,128)(2,1)S(1)}, u32[]{:S(2)}, u32[]{:S(2)}) %collective-permute-start.19) | collective-permute-done | bytes 229408 | tf_op jit(solution)/shard_map/ppermute | solution.py:317
  77.1 0.8 prepare_rows.7
  77.9 0.0 collective-permute-done.20.left
  77.9 0.0 collective-permute-done.21.right
  77.9 0.7 settle.1.refs_5_
  78.7 0.2 collective-permute-done.16.refs_1_
  78.9 0.0 collective-permute-start.23
  78.9 0.7 collective-permute-done.22.refs_2_
  79.7 0.0 collective-permute-start.24
  79.7 1.4 %take_own.1 = (bf16[512,3584]{1,0:T(8,128)(2,1)S(1)}, bf16[1792,512]{1,0:T(8,128)(2,1)S(1)}) custom-call(s32[5]{0:T(128)S(1)} %stack.23.refs_0_, bf16[1824,128]{1,0:T(8,128)(2,1)S(1)} %collective-permute-done.16.refs_1_, bf16[1824,128]{1,0:T(8,128)(2,1)S(1)} %collective-permute-done.22.refs_2_, ...), custom_call_target="tpu_custom_call", output_to_operand_aliasing={{0}: (3, {}), {1}: (4, {})} | custom-call | flops 1 | bytes 1 | tf_op jit(solution)/shard_map/take_own/pallas_call | solution.py:215
  81.0 0.5 collective-permute-done.24.refs_4_
  81.5 11.9 %finish.1 = (f32[1792,3584]{1,0:T(8,128)}, f32[1,896,896]{2,1,0:T(8,128)}, bf16[512,3584]{1,0:T(8,128)(2,1)S(1)}, bf16[1792,512]{1,0:T(8,128)(2,1)S(1)}) custom-call(s32[5]{0:T(128)S(1)} %stack.23.refs_0_, bf16[1824,128]{1,0:T(8,128)(2,1)S(1)} %collective-permute-done.16.refs_1_, ...), custom_call_target="tpu_custom_call", output_to_operand_aliasing={{2}: (6, {}), {3}: (7, {})} | custom-call | flops 1 | bytes 1 | tf_op jit(solution)/shard_map/finish/pallas_call | solution.py:260
  (4 shorter events, 0.1 us)
Async XLA Ops:
  1.3 1.2 %copy-start = (bf16[128,3584]{1,0:T(8,128)(2,1)S(1)}, bf16[128,3584]{1,0:T(8,128)(2,1)}, u32[]{:S(2)}) copy-start(bf16[128,3584]{1,0:T(8,128)(2,1)} %tokens.1) | copy-start | bytes 2752516
  2.7 23.5 %collective-permute-start = (bf16[3616,128]{1,0:T(8,128)(2,1)S(1)}, bf16[3616,128]{1,0:T(8,128)(2,1)S(1)}, u32[]{:S(2)}, u32[]{:S(2)}) collective-permute-start(bf16[3616,128]{1,0:T(8,128)(2,1)S(1)} %make_message.1.refs_1_), channel_id=1, source_target_pairs={{0,4},{1,5},{4,8},{5,9},{8,12},{9,13},{12,14},{13,15},{14,10},{15,... | collective-permute-start | bytes 2777096 | tf_op jit(solution)/shard_map/ppermute | solution.py:320
  5.8 22.3 %collective-permute-start.5 = (bf16[3616,128]{1,0:T(8,128)(2,1)S(1)}, bf16[3616,128]{1,0:T(8,128)(2,1)S(1)}, u32[]{:S(2)}, u32[]{:S(2)}) collective-permute-start(bf16[3616,128]{1,0:T(8,128)(2,1)S(1)} %make_message.1.refs_1_), channel_id=1, source_target_pairs={{4,0},{5,1},{8,4},{9,5},{12,8},{13,9},{14,12},{15,13},{10,14},{11,... | collective-permute-start | bytes 2777096 | tf_op jit(solution)/shard_map/ppermute | solution.py:320
  7.4 1.6 %collective-permute-start.1 = (bf16[32,3584]{1,0:T(8,128)(2,1)S(1)}, bf16[32,3584]{1,0:T(8,128)(2,1)S(1)}, u32[]{:S(2)}, u32[]{:S(2)}) collective-permute-start(bf16[32,3584]{1,0:T(8,128)(2,1)S(1)} %get-tuple-element.77.refs_1_), channel_id=1, source_target_pairs={{0,1},{1,0},{2,3},{3,2},{4,5},{5,4},{6,7},{7,6},{8,9},{9,8},{10,11... | collective-permute-start | bytes 688136 | tf_op jit(solution)/shard_map/ppermute | solution.py:317
  7.5 2.2 %collective-permute-start.2 = (bf16[128,896]{1,0:T(8,128)(2,1)S(1)}, bf16[128,896]{1,0:T(8,128)(2,1)S(1)}, u32[]{:S(2)}, u32[]{:S(2)}) collective-permute-start(bf16[128,896]{1,0:T(8,128)(2,1)S(1)} %get-tuple-element.81), channel_id=1, source_target_pairs={{0,1},{1,0},{2,3},{3,2},{4,5},{5,4},{6,7},{7,6},{8,9},{9,8},{10,11... | collective-permute-start | bytes 688136 | tf_op jit(solution)/shard_map/ppermute | solution.py:317
  8.0 1.8 %collective-permute-start.3 = (bf16[128,896]{1,0:T(8,128)(2,1)S(1)}, bf16[128,896]{1,0:T(8,128)(2,1)S(1)}, u32[]{:S(2)}, u32[]{:S(2)}) collective-permute-start(bf16[128,896]{1,0:T(8,128)(2,1)S(1)} %get-tuple-element.82), channel_id=1, source_target_pairs={{0,1},{1,0},{2,3},{3,2},{4,5},{5,4},{6,7},{7,6},{8,9},{9,8},{10,11... | collective-permute-start | bytes 688136 | tf_op jit(solution)/shard_map/ppermute | solution.py:317
  26.3 21.7 %collective-permute-start.4 = (bf16[3616,128]{1,0:T(8,128)(2,1)S(1)}, bf16[3616,128]{1,0:T(8,128)(2,1)S(1)}, u32[]{:S(2)}, u32[]{:S(2)}) collective-permute-start(bf16[3616,128]{1,0:T(8,128)(2,1)S(1)} %collective-permute-done.refs_1_), channel_id=1, source_target_pairs={{0,4},{1,5},{4,8},{5,9},{8,12},{9,13},{12,14},{13,15},{14,10},{15,... | collective-permute-start | bytes 2777096 | tf_op jit(solution)/shard_map/ppermute | solution.py:320
  28.1 21.4 %collective-permute-start.11 = (bf16[3616,128]{1,0:T(8,128)(2,1)S(1)}, bf16[3616,128]{1,0:T(8,128)(2,1)S(1)}, u32[]{:S(2)}, u32[]{:S(2)}) collective-permute-start(bf16[3616,128]{1,0:T(8,128)(2,1)S(1)} %collective-permute-done.5.refs_2_), channel_id=1, source_target_pairs={{4,0},{5,1},{8,4},{9,5},{12,8},{13,9},{14,12},{15,13},{10,14},{11,... | collective-permute-start | bytes 2777096 | tf_op jit(solution)/shard_map/ppermute | solution.py:320
  31.0 1.6 %collective-permute-start.6 = (bf16[32,3584]{1,0:T(8,128)(2,1)S(1)}, bf16[32,3584]{1,0:T(8,128)(2,1)S(1)}, u32[]{:S(2)}, u32[]{:S(2)}) collective-permute-start(bf16[32,3584]{1,0:T(8,128)(2,1)S(1)} %get-tuple-element.93.refs_1_), channel_id=1, source_target_pairs={{0,1},{1,0},{2,3},{3,2},{4,5},{5,4},{6,7},{7,6},{8,9},{9,8},{10,11... | collective-permute-start | bytes 688136 | tf_op jit(solution)/shard_map/ppermute | solution.py:317
  31.0 3.9 %collective-permute-start.8 = (bf16[256,896]{1,0:T(8,128)(2,1)S(1)}, bf16[256,896]{1,0:T(8,128)(2,1)S(1)}, u32[]{:S(2)}, u32[]{:S(2)}) collective-permute-start(bf16[256,896]{1,0:T(8,128)(2,1)S(1)} %get-tuple-element.100), channel_id=1, source_target_pairs={{0,1},{1,0},{2,3},{3,2},{4,5},{5,4},{6,7},{7,6},{8,9},{9,8},{10,11... | collective-permute-start | bytes 1376264 | tf_op jit(solution)/shard_map/ppermute | solution.py:317
  31.5 3.5 %collective-permute-start.9 = (bf16[256,896]{1,0:T(8,128)(2,1)S(1)}, bf16[256,896]{1,0:T(8,128)(2,1)S(1)}, u32[]{:S(2)}, u32[]{:S(2)}) collective-permute-start(bf16[256,896]{1,0:T(8,128)(2,1)S(1)} %get-tuple-element.101), channel_id=1, source_target_pairs={{0,1},{1,0},{2,3},{3,2},{4,5},{5,4},{6,7},{7,6},{8,9},{9,8},{10,11... | collective-permute-start | bytes 1376264 | tf_op jit(solution)/shard_map/ppermute | solution.py:317
  32.5 1.6 %collective-permute-start.7 = (bf16[32,3584]{1,0:T(8,128)(2,1)S(1)}, bf16[32,3584]{1,0:T(8,128)(2,1)S(1)}, u32[]{:S(2)}, u32[]{:S(2)}) collective-permute-start(bf16[32,3584]{1,0:T(8,128)(2,1)S(1)} %get-tuple-element.94.refs_2_), channel_id=1, source_target_pairs={{0,1},{1,0},{2,3},{3,2},{4,5},{5,4},{6,7},{7,6},{8,9},{9,8},{10,11... | collective-permute-start | bytes 688136 | tf_op jit(solution)/shard_map/ppermute | solution.py:317
  48.0 20.8 %collective-permute-start.10 = (bf16[3616,128]{1,0:T(8,128)(2,1)S(1)}, bf16[3616,128]{1,0:T(8,128)(2,1)S(1)}, u32[]{:S(2)}, u32[]{:S(2)}) collective-permute-start(bf16[3616,128]{1,0:T(8,128)(2,1)S(1)} %collective-permute-done.4.refs_1_), channel_id=1, source_target_pairs={{0,4},{1,5},{4,8},{5,9},{8,12},{9,13},{12,14},{13,15},{14,10},{15,... | collective-permute-start | bytes 2777096 | tf_op jit(solution)/shard_map/ppermute | solution.py:320
  49.5 20.7 %collective-permute-start.17 = (bf16[3616,128]{1,0:T(8,128)(2,1)S(1)}, bf16[3616,128]{1,0:T(8,128)(2,1)S(1)}, u32[]{:S(2)}, u32[]{:S(2)}) collective-permute-start(bf16[3616,128]{1,0:T(8,128)(2,1)S(1)} %collective-permute-done.11.refs_2_), channel_id=1, source_target_pairs={{4,0},{5,1},{8,4},{9,5},{12,8},{13,9},{14,12},{15,13},{10,14},{11,... | collective-permute-start | bytes 2777096 | tf_op jit(solution)/shard_map/ppermute | solution.py:320
  52.7 1.6 %collective-permute-start.12 = (bf16[32,3584]{1,0:T(8,128)(2,1)S(1)}, bf16[32,3584]{1,0:T(8,128)(2,1)S(1)}, u32[]{:S(2)}, u32[]{:S(2)}) collective-permute-start(bf16[32,3584]{1,0:T(8,128)(2,1)S(1)} %get-tuple-element.112.refs_1_), channel_id=1, source_target_pairs={{0,1},{1,0},{2,3},{3,2},{4,5},{5,4},{6,7},{7,6},{8,9},{9,8},{10,11... | collective-permute-start | bytes 688136 | tf_op jit(solution)/shard_map/ppermute | solution.py:317
  52.8 3.9 %collective-permute-start.14 = (bf16[256,896]{1,0:T(8,128)(2,1)S(1)}, bf16[256,896]{1,0:T(8,128)(2,1)S(1)}, u32[]{:S(2)}, u32[]{:S(2)}) collective-permute-start(bf16[256,896]{1,0:T(8,128)(2,1)S(1)} %get-tuple-element.119), channel_id=1, source_target_pairs={{0,1},{1,0},{2,3},{3,2},{4,5},{5,4},{6,7},{7,6},{8,9},{9,8},{10,11... | collective-permute-start | bytes 1376264 | tf_op jit(solution)/shard_map/ppermute | solution.py:317
  53.3 3.5 %collective-permute-start.15 = (bf16[256,896]{1,0:T(8,128)(2,1)S(1)}, bf16[256,896]{1,0:T(8,128)(2,1)S(1)}, u32[]{:S(2)}, u32[]{:S(2)}) collective-permute-start(bf16[256,896]{1,0:T(8,128)(2,1)S(1)} %get-tuple-element.120), channel_id=1, source_target_pairs={{0,1},{1,0},{2,3},{3,2},{4,5},{5,4},{6,7},{7,6},{8,9},{9,8},{10,11... | collective-permute-start | bytes 1376264 | tf_op jit(solution)/shard_map/ppermute | solution.py:317
  54.3 1.6 %collective-permute-start.13 = (bf16[32,3584]{1,0:T(8,128)(2,1)S(1)}, bf16[32,3584]{1,0:T(8,128)(2,1)S(1)}, u32[]{:S(2)}, u32[]{:S(2)}) collective-permute-start(bf16[32,3584]{1,0:T(8,128)(2,1)S(1)} %get-tuple-element.113.refs_2_), channel_id=1, source_target_pairs={{0,1},{1,0},{2,3},{3,2},{4,5},{5,4},{6,7},{7,6},{8,9},{9,8},{10,11... | collective-permute-start | bytes 688136 | tf_op jit(solution)/shard_map/ppermute | solution.py:317
  68.8 10.1 %collective-permute-start.16 = (bf16[1824,128]{1,0:T(8,128)(2,1)S(1)}, bf16[1824,128]{1,0:T(8,128)(2,1)S(1)}, u32[]{:S(2)}, u32[]{:S(2)}) collective-permute-start(bf16[1824,128]{1,0:T(8,128)(2,1)S(1)} %slice.6), channel_id=1, source_target_pairs={{0,4},{1,5},{4,8},{5,9},{8,12},{9,13},{12,14},{13,15},{14,10},{15,... | collective-permute-start | bytes 1400840 | tf_op jit(solution)/shard_map/ppermute | solution.py:320
  70.2 9.5 %collective-permute-start.22 = (bf16[1824,128]{1,0:T(8,128)(2,1)S(1)}, bf16[1824,128]{1,0:T(8,128)(2,1)S(1)}, u32[]{:S(2)}, u32[]{:S(2)}) collective-permute-start(bf16[1824,128]{1,0:T(8,128)(2,1)S(1)} %slice.7), channel_id=1, source_target_pairs={{4,0},{5,1},{8,4},{9,5},{12,8},{13,9},{14,12},{15,13},{10,14},{11,... | collective-permute-start | bytes 1400840 | tf_op jit(solution)/shard_map/ppermute | solution.py:320
  73.9 1.6 %collective-permute-start.18 = (bf16[32,3584]{1,0:T(8,128)(2,1)S(1)}, bf16[32,3584]{1,0:T(8,128)(2,1)S(1)}, u32[]{:S(2)}, u32[]{:S(2)}) collective-permute-start(bf16[32,3584]{1,0:T(8,128)(2,1)S(1)} %get-tuple-element.131.refs_1_), channel_id=1, source_target_pairs={{0,1},{1,0},{2,3},{3,2},{4,5},{5,4},{6,7},{7,6},{8,9},{9,8},{10,11... | collective-permute-start | bytes 688136 | tf_op jit(solution)/shard_map/ppermute | solution.py:317
  74.0 3.9 %collective-permute-start.20 = (bf16[256,896]{1,0:T(8,128)(2,1)S(1)}, bf16[256,896]{1,0:T(8,128)(2,1)S(1)}, u32[]{:S(2)}, u32[]{:S(2)}) collective-permute-start(bf16[256,896]{1,0:T(8,128)(2,1)S(1)} %get-tuple-element.138), channel_id=1, source_target_pairs={{0,1},{1,0},{2,3},{3,2},{4,5},{5,4},{6,7},{7,6},{8,9},{9,8},{10,11... | collective-permute-start | bytes 1376264 | tf_op jit(solution)/shard_map/ppermute | solution.py:317
  74.5 3.5 %collective-permute-start.21 = (bf16[256,896]{1,0:T(8,128)(2,1)S(1)}, bf16[256,896]{1,0:T(8,128)(2,1)S(1)}, u32[]{:S(2)}, u32[]{:S(2)}) collective-permute-start(bf16[256,896]{1,0:T(8,128)(2,1)S(1)} %get-tuple-element.139), channel_id=1, source_target_pairs={{0,1},{1,0},{2,3},{3,2},{4,5},{5,4},{6,7},{7,6},{8,9},{9,8},{10,11... | collective-permute-start | bytes 1376264 | tf_op jit(solution)/shard_map/ppermute | solution.py:317
  75.4 1.6 %collective-permute-start.19 = (bf16[32,3584]{1,0:T(8,128)(2,1)S(1)}, bf16[32,3584]{1,0:T(8,128)(2,1)S(1)}, u32[]{:S(2)}, u32[]{:S(2)}) collective-permute-start(bf16[32,3584]{1,0:T(8,128)(2,1)S(1)} %get-tuple-element.132.refs_2_), channel_id=1, source_target_pairs={{0,1},{1,0},{2,3},{3,2},{4,5},{5,4},{6,7},{7,6},{8,9},{9,8},{10,11... | collective-permute-start | bytes 688136 | tf_op jit(solution)/shard_map/ppermute | solution.py:317
  78.9 2.1 %collective-permute-start.23 = (bf16[1824,128]{1,0:T(8,128)(2,1)S(1)}, bf16[1824,128]{1,0:T(8,128)(2,1)S(1)}, u32[]{:S(2)}, u32[]{:S(2)}) collective-permute-start(bf16[1824,128]{1,0:T(8,128)(2,1)S(1)} %collective-permute-done.16.refs_1_), channel_id=1, source_target_pairs={{0,1},{1,0},{2,3},{3,2},{4,5},{5,4},{6,7},{7,6},{8,9},{9,8},{10,11... | collective-permute-start | bytes 1400840 | tf_op jit(solution)/shard_map/ppermute | solution.py:317
  79.7 1.8 %collective-permute-start.24 = (bf16[1824,128]{1,0:T(8,128)(2,1)S(1)}, bf16[1824,128]{1,0:T(8,128)(2,1)S(1)}, u32[]{:S(2)}, u32[]{:S(2)}) collective-permute-start(bf16[1824,128]{1,0:T(8,128)(2,1)S(1)} %collective-permute-done.22.refs_2_), channel_id=1, source_target_pairs={{0,1},{1,0},{2,3},{3,2},{4,5},{5,4},{6,7},{7,6},{8,9},{9,8},{10,11... | collective-permute-start | bytes 1400840 | tf_op jit(solution)/shard_map/ppermute | solution.py:317

commit v18 on v17

--- a/solution.py
+++ b/solution.py
@@ -14,7 +14,7 @@
 LANES = 128
 TABLE = 32
 STEP = 512
-SPLITS = 7
+SPLITS = 14
 VMEM = pl.BlockSpec(memory_space=pltpu.VMEM)
 SMEM = pl.BlockSpec(memory_space=pltpu.SMEM)
 ANY = pl.BlockSpec(memory_space=pl.ANY)

time: 93.8 us -> 93.4 us (level)
  no operation moved by 1% of the time
where the time goes in v18:
time: 93.4 us; the launch traced here: 93.2 us
  waiting for transfers between devices  51 us (55%)
  Pallas kernels  26.9 us (29%)
  starting transfers between devices  12.3 us (13%)
  local copies, waits for them, and re-layouts  1.32 us (1%)
  between operations  1.01 us (1%)
    ppermute x8, waiting for transfers between devices, advance(): lax.ppermute(array, 'tok', stream)  42.4 us
    pallas_call x1, Pallas kernels, finish(): pl.pallas_call(functools.partial(finish_kernel, final), out_shape=[jax.Sh...  11.5 us
    pallas_call x4, Pallas kernels, absorb(): pl.pallas_call(functools.partial(absorb_kernel, count, bool(before)), out...  9.83 us
    ppermute x8, starting transfers between devices, advance(): lax.ppermute(array, 'tok', stream)  9.27 us
    ppermute x17, waiting for transfers between devices, swap(): return lax.ppermute(array, 'tok', pair)  8.58 us
    pallas_call x4, Pallas kernels, prepare(): pl.pallas_call(functools.partial(prepare_kernel, len(packs), at), out_sha...  3.21 us
    ppermute x17, starting transfers between devices, swap(): return lax.ppermute(array, 'tok', pair)  3.02 us
  transfers between devices with their start and end apart: 25, of which 13 were waited for; matrix products, arithmetic and copies ran while one was open for 0% of the time, Pallas kernels for 16%

profile of v18, /device:TPU:0, one launch (start us, length us, event | category | flops | bytes accessed | tf_op | source)
XLA Modules:
  0.0 93.2 jit_solution(13000620843010829718)
XLA Ops:
  0.6 0.7 select_reduce_fusion
  1.3 0.0 copy-start
  1.4 1.2 %copy-done = bf16[128,3584]{1,0:T(8,128)(2,1)S(1)} copy-done((bf16[128,3584]{1,0:T(8,128)(2,1)S(1)}, bf16[128,3584]{1,0:T(8,128)(2,1)}, u32[]{:S(2)}) %copy-start) | copy-done | bytes 917528
  2.5 0.2 make_message.1.refs_1_
  2.7 3.1 %collective-permute-start = (bf16[3616,128]{1,0:T(8,128)(2,1)S(1)}, bf16[3616,128]{1,0:T(8,128)(2,1)S(1)}, u32[]{:S(2)}, u32[]{:S(2)}) collective-permute-start(bf16[3616,128]{1,0:T(8,128)(2,1)S(1)} %make_message.1.refs_1_), channel_id=1, source_target_pairs={{0,4},{1,5},{4,8},{5,9},{8,12},{9,13},{12,14},{13,15},{14,10},{15,... | collective-permute-start | bytes 2777096 | tf_op jit(solution)/shard_map/ppermute | solution.py:320
  5.8 0.0 collective-permute-start.5
  5.8 0.1 stack.23.refs_0_
  5.9 1.5 %absorb.4 = (f32[896,896]{1,0:T(8,128)S(1)}, bf16[128,896]{1,0:T(8,128)(2,1)S(1)}, bf16[128,896]{1,0:T(8,128)(2,1)S(1)}, bf16[32,3584]{1,0:T(8,128)(2,1)S(1)}) custom-call(s32[5]{0:T(128)S(1)} %stack.23.refs_0_, bf16[3616,128]{1,0:T(8,128)(2,1)S(1)} %make_message.1.refs_1_), custom_call_target="tpu_custom_call" | custom-call | flops 1 | bytes 1 | tf_op jit(solution)/shard_map/absorb/pallas_call | solution.py:143
  7.4 0.1 collective-permute-start.1
  7.5 0.5 collective-permute-start.2
  8.0 0.1 collective-permute-start.3
  8.1 0.9 collective-permute-done.1.refs_2_
  9.0 0.8 prepare_rows.4
  9.8 0.0 collective-permute-done.2.refs_4_
  9.8 0.0 collective-permute-done.3.refs_5_
  9.8 16.5 %collective-permute-done.refs_1_ = bf16[3616,128]{1,0:T(8,128)(2,1)S(1)} collective-permute-done((bf16[3616,128]{1,0:T(8,128)(2,1)S(1)}, bf16[3616,128]{1,0:T(8,128)(2,1)S(1)}, u32[]{:S(2)}, u32[]{:S(2)}) %collective-permute-start) | collective-permute-done | bytes 925728 | tf_op jit(solution)/shard_map/ppermute | solution.py:320
  26.3 1.8 %collective-permute-start.4 = (bf16[3616,128]{1,0:T(8,128)(2,1)S(1)}, bf16[3616,128]{1,0:T(8,128)(2,1)S(1)}, u32[]{:S(2)}, u32[]{:S(2)}) collective-permute-start(bf16[3616,128]{1,0:T(8,128)(2,1)S(1)} %collective-permute-done.refs_1_), channel_id=1, source_target_pairs={{0,4},{1,5},{4,8},{5,9},{8,12},{9,13},{12,14},{13,15},{14,10},{15,... | collective-permute-start | bytes 2777096 | tf_op jit(solution)/shard_map/ppermute | solution.py:320
  28.1 0.0 collective-permute-done.5.refs_2_
  28.1 0.2 collective-permute-start.11
  28.3 2.7 %absorb.5 = (f32[896,896]{1,0:T(8,128)S(1)}, bf16[256,896]{1,0:T(8,128)(2,1)S(1)}, bf16[256,896]{1,0:T(8,128)(2,1)S(1)}, bf16[32,3584]{1,0:T(8,128)(2,1)S(1)}, bf16[32,3584]{1,0:T(8,128)(2,1)S(1)}) custom-call(s32[5]{0:T(128)S(1)} %stack.23.refs_0_, bf16[3616,128]{1,0:T(8,128)(2,1)S(1)} %collective-permute-done.refs_1_, ...), custom_call_target="tpu_custom_call", output_to_operand_aliasing={{0}: (3, {})} | custom-call | flops 1 | bytes 1 | tf_op jit(solution)/shard_map/absorb/pallas_call | solution.py:143
  31.0 0.1 collective-permute-start.6
  31.0 0.5 collective-permute-start.8
  31.5 0.1 collective-permute-start.9
  31.6 0.9 collective-permute-done.6.refs_3_
  32.5 0.1 collective-permute-start.7
  32.6 1.5 %collective-permute-done.7.refs_4_ = bf16[32,3584]{1,0:T(8,128)(2,1)S(1)} collective-permute-done((bf16[32,3584]{1,0:T(8,128)(2,1)S(1)}, bf16[32,3584]{1,0:T(8,128)(2,1)S(1)}, u32[]{:S(2)}, u32[]{:S(2)}) %collective-permute-start.7) | collective-permute-done | bytes 229408 | tf_op jit(solution)/shard_map/ppermute | solution.py:317
  34.1 0.8 prepare_rows.5
  35.0 0.0 collective-permute-done.8.refs_4_
  35.0 13.0 %collective-permute-done.4.refs_1_ = bf16[3616,128]{1,0:T(8,128)(2,1)S(1)} collective-permute-done((bf16[3616,128]{1,0:T(8,128)(2,1)S(1)}, bf16[3616,128]{1,0:T(8,128)(2,1)S(1)}, u32[]{:S(2)}, u32[]{:S(2)}) %collective-permute-start.4) | collective-permute-done | bytes 925728 | tf_op jit(solution)/shard_map/ppermute | solution.py:320
  48.0 1.5 %collective-permute-start.10 = (bf16[3616,128]{1,0:T(8,128)(2,1)S(1)}, bf16[3616,128]{1,0:T(8,128)(2,1)S(1)}, u32[]{:S(2)}, u32[]{:S(2)}) collective-permute-start(bf16[3616,128]{1,0:T(8,128)(2,1)S(1)} %collective-permute-done.4.refs_1_), channel_id=1, source_target_pairs={{0,4},{1,5},{4,8},{5,9},{8,12},{9,13},{12,14},{13,15},{14,10},{15,... | collective-permute-start | bytes 2777096 | tf_op jit(solution)/shard_map/ppermute | solution.py:320
  49.5 0.0 collective-permute-done.11.refs_2_
  49.5 0.5 collective-permute-start.17
  50.0 2.7 %absorb.6 = (f32[896,896]{1,0:T(8,128)S(1)}, bf16[256,896]{1,0:T(8,128)(2,1)S(1)}, bf16[256,896]{1,0:T(8,128)(2,1)S(1)}, bf16[32,3584]{1,0:T(8,128)(2,1)S(1)}, bf16[32,3584]{1,0:T(8,128)(2,1)S(1)}) custom-call(s32[5]{0:T(128)S(1)} %stack.23.refs_0_, bf16[3616,128]{1,0:T(8,128)(2,1)S(1)} %collective-permute-done.4.refs_1_, ...), custom_call_target="tpu_custom_call", output_to_operand_aliasing={{0}: (3, {})} | custom-call | flops 1 | bytes 1 | tf_op jit(solution)/shard_map/absorb/pallas_call | solution.py:143
  52.7 0.1 collective-permute-start.12
  52.8 0.5 collective-permute-start.14
  53.3 0.1 collective-permute-start.15
  53.4 0.9 collective-permute-done.12.refs_3_
  54.3 0.1 collective-permute-start.13
  54.4 1.5 %collective-permute-done.13.refs_4_ = bf16[32,3584]{1,0:T(8,128)(2,1)S(1)} collective-permute-done((bf16[32,3584]{1,0:T(8,128)(2,1)S(1)}, bf16[32,3584]{1,0:T(8,128)(2,1)S(1)}, u32[]{:S(2)}, u32[]{:S(2)}) %collective-permute-start.13) | collective-permute-done | bytes 229408 | tf_op jit(solution)/shard_map/ppermute | solution.py:317
  55.9 0.8 prepare_rows.6
  56.8 0.0 collective-permute-done.14.refs_4_
  56.8 0.0 collective-permute-done.15.refs_5_
  56.8 12.0 %collective-permute-done.10.refs_1_ = bf16[3616,128]{1,0:T(8,128)(2,1)S(1)} collective-permute-done((bf16[3616,128]{1,0:T(8,128)(2,1)S(1)}, bf16[3616,128]{1,0:T(8,128)(2,1)S(1)}, u32[]{:S(2)}, u32[]{:S(2)}) %collective-permute-start.10) | collective-permute-done | bytes 925728 | tf_op jit(solution)/shard_map/ppermute | solution.py:320
  68.8 1.3 %collective-permute-start.16 = (bf16[1824,128]{1,0:T(8,128)(2,1)S(1)}, bf16[1824,128]{1,0:T(8,128)(2,1)S(1)}, u32[]{:S(2)}, u32[]{:S(2)}) collective-permute-start(bf16[1824,128]{1,0:T(8,128)(2,1)S(1)} %slice.6), channel_id=1, source_target_pairs={{0,4},{1,5},{4,8},{5,9},{8,12},{9,13},{12,14},{13,15},{14,10},{15,... | collective-permute-start | bytes 1400840 | tf_op jit(solution)/shard_map/ppermute | solution.py:320
  70.1 0.0 collective-permute-done.17.refs_2_
  70.2 0.8 collective-permute-start.22
  71.0 2.9 %absorb.7 = (f32[896,896]{1,0:T(8,128)S(1)}, bf16[256,896]{1,0:T(8,128)(2,1)S(1)}, bf16[256,896]{1,0:T(8,128)(2,1)S(1)}, bf16[32,3584]{1,0:T(8,128)(2,1)S(1)}, bf16[32,3584]{1,0:T(8,128)(2,1)S(1)}) custom-call(s32[5]{0:T(128)S(1)} %stack.23.refs_0_, bf16[3616,128]{1,0:T(8,128)(2,1)S(1)} %collective-permute-done.10.refs_1_, ...), custom_call_target="tpu_custom_call", output_to_operand_aliasing={{0}: (3, {})} | custom-call | flops 1 | bytes 1 | tf_op jit(solution)/shard_map/absorb/pallas_call | solution.py:143
  73.9 0.1 collective-permute-start.18
  74.0 0.5 collective-permute-start.20
  74.5 0.1 collective-permute-start.21
  74.5 0.9 collective-permute-done.18.refs_3_
  75.4 0.1 collective-permute-start.19
  75.6 1.5 %collective-permute-done.19.refs_4_ = bf16[32,3584]{1,0:T(8,128)(2,1)S(1)} collective-permute-done((bf16[32,3584]{1,0:T(8,128)(2,1)S(1)}, bf16[32,3584]{1,0:T(8,128)(2,1)S(1)}, u32[]{:S(2)}, u32[]{:S(2)}) %collective-permute-start.19) | collective-permute-done | bytes 229408 | tf_op jit(solution)/shard_map/ppermute | solution.py:317
  77.1 0.8 prepare_rows.7
  77.9 0.0 collective-permute-done.21.right
  77.9 0.7 settle.1.refs_5_
  78.7 0.2 collective-permute-done.16.refs_1_
  78.9 0.0 collective-permute-start.23
  78.9 0.7 collective-permute-done.22.refs_2_
  79.7 0.0 collective-permute-start.24
  79.7 1.4 %take_own.1 = (bf16[512,3584]{1,0:T(8,128)(2,1)S(1)}, bf16[1792,512]{1,0:T(8,128)(2,1)S(1)}) custom-call(s32[5]{0:T(128)S(1)} %stack.23.refs_0_, bf16[1824,128]{1,0:T(8,128)(2,1)S(1)} %collective-permute-done.16.refs_1_, bf16[1824,128]{1,0:T(8,128)(2,1)S(1)} %collective-permute-done.22.refs_2_, ...), custom_call_target="tpu_custom_call", output_to_operand_aliasing={{0}: (3, {}), {1}: (4, {})} | custom-call | flops 1 | bytes 1 | tf_op jit(solution)/shard_map/take_own/pallas_call | solution.py:215
  81.0 0.0 collective-permute-done.23.refs_3_
  81.0 0.5 collective-permute-done.24.refs_4_
  81.5 11.5 %finish.1 = (f32[1792,3584]{1,0:T(8,128)}, f32[1,896,896]{2,1,0:T(8,128)}, bf16[512,3584]{1,0:T(8,128)(2,1)S(1)}, bf16[1792,512]{1,0:T(8,128)(2,1)S(1)}) custom-call(s32[5]{0:T(128)S(1)} %stack.23.refs_0_, bf16[1824,128]{1,0:T(8,128)(2,1)S(1)} %collective-permute-done.16.refs_1_, ...), custom_call_target="tpu_custom_call", output_to_operand_aliasing={{2}: (6, {}), {3}: (7, {})} | custom-call | flops 1 | bytes 1 | tf_op jit(solution)/shard_map/finish/pallas_call | solution.py:260
  (4 shorter events, 0.1 us)
Async XLA Ops:
  1.3 1.2 %copy-start = (bf16[128,3584]{1,0:T(8,128)(2,1)S(1)}, bf16[128,3584]{1,0:T(8,128)(2,1)}, u32[]{:S(2)}) copy-start(bf16[128,3584]{1,0:T(8,128)(2,1)} %tokens.1) | copy-start | bytes 2752516
  2.7 23.5 %collective-permute-start = (bf16[3616,128]{1,0:T(8,128)(2,1)S(1)}, bf16[3616,128]{1,0:T(8,128)(2,1)S(1)}, u32[]{:S(2)}, u32[]{:S(2)}) collective-permute-start(bf16[3616,128]{1,0:T(8,128)(2,1)S(1)} %make_message.1.refs_1_), channel_id=1, source_target_pairs={{0,4},{1,5},{4,8},{5,9},{8,12},{9,13},{12,14},{13,15},{14,10},{15,... | collective-permute-start | bytes 2777096 | tf_op jit(solution)/shard_map/ppermute | solution.py:320
  5.8 22.3 %collective-permute-start.5 = (bf16[3616,128]{1,0:T(8,128)(2,1)S(1)}, bf16[3616,128]{1,0:T(8,128)(2,1)S(1)}, u32[]{:S(2)}, u32[]{:S(2)}) collective-permute-start(bf16[3616,128]{1,0:T(8,128)(2,1)S(1)} %make_message.1.refs_1_), channel_id=1, source_target_pairs={{4,0},{5,1},{8,4},{9,5},{12,8},{13,9},{14,12},{15,13},{10,14},{11,... | collective-permute-start | bytes 2777096 | tf_op jit(solution)/shard_map/ppermute | solution.py:320
  7.4 1.6 %collective-permute-start.1 = (bf16[32,3584]{1,0:T(8,128)(2,1)S(1)}, bf16[32,3584]{1,0:T(8,128)(2,1)S(1)}, u32[]{:S(2)}, u32[]{:S(2)}) collective-permute-start(bf16[32,3584]{1,0:T(8,128)(2,1)S(1)} %get-tuple-element.77.refs_1_), channel_id=1, source_target_pairs={{0,1},{1,0},{2,3},{3,2},{4,5},{5,4},{6,7},{7,6},{8,9},{9,8},{10,11... | collective-permute-start | bytes 688136 | tf_op jit(solution)/shard_map/ppermute | solution.py:317
  7.5 2.2 %collective-permute-start.2 = (bf16[128,896]{1,0:T(8,128)(2,1)S(1)}, bf16[128,896]{1,0:T(8,128)(2,1)S(1)}, u32[]{:S(2)}, u32[]{:S(2)}) collective-permute-start(bf16[128,896]{1,0:T(8,128)(2,1)S(1)} %get-tuple-element.81), channel_id=1, source_target_pairs={{0,1},{1,0},{2,3},{3,2},{4,5},{5,4},{6,7},{7,6},{8,9},{9,8},{10,11... | collective-permute-start | bytes 688136 | tf_op jit(solution)/shard_map/ppermute | solution.py:317
  8.0 1.8 %collective-permute-start.3 = (bf16[128,896]{1,0:T(8,128)(2,1)S(1)}, bf16[128,896]{1,0:T(8,128)(2,1)S(1)}, u32[]{:S(2)}, u32[]{:S(2)}) collective-permute-start(bf16[128,896]{1,0:T(8,128)(2,1)S(1)} %get-tuple-element.82), channel_id=1, source_target_pairs={{0,1},{1,0},{2,3},{3,2},{4,5},{5,4},{6,7},{7,6},{8,9},{9,8},{10,11... | collective-permute-start | bytes 688136 | tf_op jit(solution)/shard_map/ppermute | solution.py:317
  26.3 21.7 %collective-permute-start.4 = (bf16[3616,128]{1,0:T(8,128)(2,1)S(1)}, bf16[3616,128]{1,0:T(8,128)(2,1)S(1)}, u32[]{:S(2)}, u32[]{:S(2)}) collective-permute-start(bf16[3616,128]{1,0:T(8,128)(2,1)S(1)} %collective-permute-done.refs_1_), channel_id=1, source_target_pairs={{0,4},{1,5},{4,8},{5,9},{8,12},{9,13},{12,14},{13,15},{14,10},{15,... | collective-permute-start | bytes 2777096 | tf_op jit(solution)/shard_map/ppermute | solution.py:320
  28.1 21.4 %collective-permute-start.11 = (bf16[3616,128]{1,0:T(8,128)(2,1)S(1)}, bf16[3616,128]{1,0:T(8,128)(2,1)S(1)}, u32[]{:S(2)}, u32[]{:S(2)}) collective-permute-start(bf16[3616,128]{1,0:T(8,128)(2,1)S(1)} %collective-permute-done.5.refs_2_), channel_id=1, source_target_pairs={{4,0},{5,1},{8,4},{9,5},{12,8},{13,9},{14,12},{15,13},{10,14},{11,... | collective-permute-start | bytes 2777096 | tf_op jit(solution)/shard_map/ppermute | solution.py:320
  31.0 1.6 %collective-permute-start.6 = (bf16[32,3584]{1,0:T(8,128)(2,1)S(1)}, bf16[32,3584]{1,0:T(8,128)(2,1)S(1)}, u32[]{:S(2)}, u32[]{:S(2)}) collective-permute-start(bf16[32,3584]{1,0:T(8,128)(2,1)S(1)} %get-tuple-element.93.refs_1_), channel_id=1, source_target_pairs={{0,1},{1,0},{2,3},{3,2},{4,5},{5,4},{6,7},{7,6},{8,9},{9,8},{10,11... | collective-permute-start | bytes 688136 | tf_op jit(solution)/shard_map/ppermute | solution.py:317
  31.0 3.9 %collective-permute-start.8 = (bf16[256,896]{1,0:T(8,128)(2,1)S(1)}, bf16[256,896]{1,0:T(8,128)(2,1)S(1)}, u32[]{:S(2)}, u32[]{:S(2)}) collective-permute-start(bf16[256,896]{1,0:T(8,128)(2,1)S(1)} %get-tuple-element.100), channel_id=1, source_target_pairs={{0,1},{1,0},{2,3},{3,2},{4,5},{5,4},{6,7},{7,6},{8,9},{9,8},{10,11... | collective-permute-start | bytes 1376264 | tf_op jit(solution)/shard_map/ppermute | solution.py:317
  31.5 3.5 %collective-permute-start.9 = (bf16[256,896]{1,0:T(8,128)(2,1)S(1)}, bf16[256,896]{1,0:T(8,128)(2,1)S(1)}, u32[]{:S(2)}, u32[]{:S(2)}) collective-permute-start(bf16[256,896]{1,0:T(8,128)(2,1)S(1)} %get-tuple-element.101), channel_id=1, source_target_pairs={{0,1},{1,0},{2,3},{3,2},{4,5},{5,4},{6,7},{7,6},{8,9},{9,8},{10,11... | collective-permute-start | bytes 1376264 | tf_op jit(solution)/shard_map/ppermute | solution.py:317
  32.5 1.6 %collective-permute-start.7 = (bf16[32,3584]{1,0:T(8,128)(2,1)S(1)}, bf16[32,3584]{1,0:T(8,128)(2,1)S(1)}, u32[]{:S(2)}, u32[]{:S(2)}) collective-permute-start(bf16[32,3584]{1,0:T(8,128)(2,1)S(1)} %get-tuple-element.94.refs_2_), channel_id=1, source_target_pairs={{0,1},{1,0},{2,3},{3,2},{4,5},{5,4},{6,7},{7,6},{8,9},{9,8},{10,11... | collective-permute-start | bytes 688136 | tf_op jit(solution)/shard_map/ppermute | solution.py:317
  48.0 20.8 %collective-permute-start.10 = (bf16[3616,128]{1,0:T(8,128)(2,1)S(1)}, bf16[3616,128]{1,0:T(8,128)(2,1)S(1)}, u32[]{:S(2)}, u32[]{:S(2)}) collective-permute-start(bf16[3616,128]{1,0:T(8,128)(2,1)S(1)} %collective-permute-done.4.refs_1_), channel_id=1, source_target_pairs={{0,4},{1,5},{4,8},{5,9},{8,12},{9,13},{12,14},{13,15},{14,10},{15,... | collective-permute-start | bytes 2777096 | tf_op jit(solution)/shard_map/ppermute | solution.py:320
  49.5 20.7 %collective-permute-start.17 = (bf16[3616,128]{1,0:T(8,128)(2,1)S(1)}, bf16[3616,128]{1,0:T(8,128)(2,1)S(1)}, u32[]{:S(2)}, u32[]{:S(2)}) collective-permute-start(bf16[3616,128]{1,0:T(8,128)(2,1)S(1)} %collective-permute-done.11.refs_2_), channel_id=1, source_target_pairs={{4,0},{5,1},{8,4},{9,5},{12,8},{13,9},{14,12},{15,13},{10,14},{11,... | collective-permute-start | bytes 2777096 | tf_op jit(solution)/shard_map/ppermute | solution.py:320
  52.7 1.6 %collective-permute-start.12 = (bf16[32,3584]{1,0:T(8,128)(2,1)S(1)}, bf16[32,3584]{1,0:T(8,128)(2,1)S(1)}, u32[]{:S(2)}, u32[]{:S(2)}) collective-permute-start(bf16[32,3584]{1,0:T(8,128)(2,1)S(1)} %get-tuple-element.112.refs_1_), channel_id=1, source_target_pairs={{0,1},{1,0},{2,3},{3,2},{4,5},{5,4},{6,7},{7,6},{8,9},{9,8},{10,11... | collective-permute-start | bytes 688136 | tf_op jit(solution)/shard_map/ppermute | solution.py:317
  52.8 3.9 %collective-permute-start.14 = (bf16[256,896]{1,0:T(8,128)(2,1)S(1)}, bf16[256,896]{1,0:T(8,128)(2,1)S(1)}, u32[]{:S(2)}, u32[]{:S(2)}) collective-permute-start(bf16[256,896]{1,0:T(8,128)(2,1)S(1)} %get-tuple-element.119), channel_id=1, source_target_pairs={{0,1},{1,0},{2,3},{3,2},{4,5},{5,4},{6,7},{7,6},{8,9},{9,8},{10,11... | collective-permute-start | bytes 1376264 | tf_op jit(solution)/shard_map/ppermute | solution.py:317
  53.3 3.5 %collective-permute-start.15 = (bf16[256,896]{1,0:T(8,128)(2,1)S(1)}, bf16[256,896]{1,0:T(8,128)(2,1)S(1)}, u32[]{:S(2)}, u32[]{:S(2)}) collective-permute-start(bf16[256,896]{1,0:T(8,128)(2,1)S(1)} %get-tuple-element.120), channel_id=1, source_target_pairs={{0,1},{1,0},{2,3},{3,2},{4,5},{5,4},{6,7},{7,6},{8,9},{9,8},{10,11... | collective-permute-start | bytes 1376264 | tf_op jit(solution)/shard_map/ppermute | solution.py:317
  54.3 1.6 %collective-permute-start.13 = (bf16[32,3584]{1,0:T(8,128)(2,1)S(1)}, bf16[32,3584]{1,0:T(8,128)(2,1)S(1)}, u32[]{:S(2)}, u32[]{:S(2)}) collective-permute-start(bf16[32,3584]{1,0:T(8,128)(2,1)S(1)} %get-tuple-element.113.refs_2_), channel_id=1, source_target_pairs={{0,1},{1,0},{2,3},{3,2},{4,5},{5,4},{6,7},{7,6},{8,9},{9,8},{10,11... | collective-permute-start | bytes 688136 | tf_op jit(solution)/shard_map/ppermute | solution.py:317
  68.8 10.1 %collective-permute-start.16 = (bf16[1824,128]{1,0:T(8,128)(2,1)S(1)}, bf16[1824,128]{1,0:T(8,128)(2,1)S(1)}, u32[]{:S(2)}, u32[]{:S(2)}) collective-permute-start(bf16[1824,128]{1,0:T(8,128)(2,1)S(1)} %slice.6), channel_id=1, source_target_pairs={{0,4},{1,5},{4,8},{5,9},{8,12},{9,13},{12,14},{13,15},{14,10},{15,... | collective-permute-start | bytes 1400840 | tf_op jit(solution)/shard_map/ppermute | solution.py:320
  70.2 9.5 %collective-permute-start.22 = (bf16[1824,128]{1,0:T(8,128)(2,1)S(1)}, bf16[1824,128]{1,0:T(8,128)(2,1)S(1)}, u32[]{:S(2)}, u32[]{:S(2)}) collective-permute-start(bf16[1824,128]{1,0:T(8,128)(2,1)S(1)} %slice.7), channel_id=1, source_target_pairs={{4,0},{5,1},{8,4},{9,5},{12,8},{13,9},{14,12},{15,13},{10,14},{11,... | collective-permute-start | bytes 1400840 | tf_op jit(solution)/shard_map/ppermute | solution.py:320
  73.9 1.6 %collective-permute-start.18 = (bf16[32,3584]{1,0:T(8,128)(2,1)S(1)}, bf16[32,3584]{1,0:T(8,128)(2,1)S(1)}, u32[]{:S(2)}, u32[]{:S(2)}) collective-permute-start(bf16[32,3584]{1,0:T(8,128)(2,1)S(1)} %get-tuple-element.131.refs_1_), channel_id=1, source_target_pairs={{0,1},{1,0},{2,3},{3,2},{4,5},{5,4},{6,7},{7,6},{8,9},{9,8},{10,11... | collective-permute-start | bytes 688136 | tf_op jit(solution)/shard_map/ppermute | solution.py:317
  74.0 3.9 %collective-permute-start.20 = (bf16[256,896]{1,0:T(8,128)(2,1)S(1)}, bf16[256,896]{1,0:T(8,128)(2,1)S(1)}, u32[]{:S(2)}, u32[]{:S(2)}) collective-permute-start(bf16[256,896]{1,0:T(8,128)(2,1)S(1)} %get-tuple-element.138), channel_id=1, source_target_pairs={{0,1},{1,0},{2,3},{3,2},{4,5},{5,4},{6,7},{7,6},{8,9},{9,8},{10,11... | collective-permute-start | bytes 1376264 | tf_op jit(solution)/shard_map/ppermute | solution.py:317
  74.5 3.5 %collective-permute-start.21 = (bf16[256,896]{1,0:T(8,128)(2,1)S(1)}, bf16[256,896]{1,0:T(8,128)(2,1)S(1)}, u32[]{:S(2)}, u32[]{:S(2)}) collective-permute-start(bf16[256,896]{1,0:T(8,128)(2,1)S(1)} %get-tuple-element.139), channel_id=1, source_target_pairs={{0,1},{1,0},{2,3},{3,2},{4,5},{5,4},{6,7},{7,6},{8,9},{9,8},{10,11... | collective-permute-start | bytes 1376264 | tf_op jit(solution)/shard_map/ppermute | solution.py:317
  75.4 1.6 %collective-permute-start.19 = (bf16[32,3584]{1,0:T(8,128)(2,1)S(1)}, bf16[32,3584]{1,0:T(8,128)(2,1)S(1)}, u32[]{:S(2)}, u32[]{:S(2)}) collective-permute-start(bf16[32,3584]{1,0:T(8,128)(2,1)S(1)} %get-tuple-element.132.refs_2_), channel_id=1, source_target_pairs={{0,1},{1,0},{2,3},{3,2},{4,5},{5,4},{6,7},{7,6},{8,9},{9,8},{10,11... | collective-permute-start | bytes 688136 | tf_op jit(solution)/shard_map/ppermute | solution.py:317
  78.9 2.1 %collective-permute-start.23 = (bf16[1824,128]{1,0:T(8,128)(2,1)S(1)}, bf16[1824,128]{1,0:T(8,128)(2,1)S(1)}, u32[]{:S(2)}, u32[]{:S(2)}) collective-permute-start(bf16[1824,128]{1,0:T(8,128)(2,1)S(1)} %collective-permute-done.16.refs_1_), channel_id=1, source_target_pairs={{0,1},{1,0},{2,3},{3,2},{4,5},{5,4},{6,7},{7,6},{8,9},{9,8},{10,11... | collective-permute-start | bytes 1400840 | tf_op jit(solution)/shard_map/ppermute | solution.py:317
  79.7 1.8 %collective-permute-start.24 = (bf16[1824,128]{1,0:T(8,128)(2,1)S(1)}, bf16[1824,128]{1,0:T(8,128)(2,1)S(1)}, u32[]{:S(2)}, u32[]{:S(2)}) collective-permute-start(bf16[1824,128]{1,0:T(8,128)(2,1)S(1)} %collective-permute-done.22.refs_2_), channel_id=1, source_target_pairs={{0,1},{1,0},{2,3},{3,2},{4,5},{5,4},{6,7},{7,6},{8,9},{9,8},{10,11... | collective-permute-start | bytes 1400840 | tf_op jit(solution)/shard_map/ppermute | solution.py:317

commit v19 on v18

--- a/solution.py
+++ b/solution.py
@@ -125,15 +125,15 @@
     scalars, refs = refs[0], refs[1:]
     pieces, refs = [[ref] for ref in refs[:count]], refs[count:]
     before, refs = refs[: 3 * started], refs[3 * started :]
-    tile, left, theirs, *packs, mine = refs
+    tile, left, theirs, packs, mine = refs
     for slot, which in enumerate((left, mine, theirs), start=1):
         fetch_tile(scalars[slot], pieces, which)
     update = product(left, mine)
     if started:
         update = before[0][...] + update + product(before[1], before[2])
     tile[...] = update
-    for piece, packed in zip(pieces, packs):
-        packed[...] = pack(scalars[0], piece)
+    for k, piece in enumerate(pieces):
+        packs[k * CAP : (k + 1) * CAP, :] = pack(scalars[0], piece)
 
 
 def absorb(scalars, pieces, before, edge):
@@ -143,9 +143,9 @@
     out = pl.pallas_call(
         functools.partial(absorb_kernel, count, bool(before)),
         out_shape=[jax.ShapeDtypeStruct((edge, edge), F32), columns, columns]
-        + [jax.ShapeDtypeStruct((CAP, width), BF16)] * count,
+        + [jax.ShapeDtypeStruct((count * CAP, width), BF16)],
         in_specs=[SMEM] + [VMEM] * (count + len(before)),
-        out_specs=[VMEM] * (3 + count),
+        out_specs=[VMEM] * 4,
         scratch_shapes=[pltpu.VMEM((count * rows, edge), BF16)],
         cost_estimate=SMALL,
         input_output_aliases={1 + count: 0} if before else {},

time: 93.4 us -> 93.2 us (level)
    ppermute x8, waiting for transfers between devices: 42.4 us -> 44.8 us  [advance(): lax.ppermute(array, 'tok', stream)]
    ppermute x17 -> x14, waiting for transfers between devices: 8.58 us -> 6.66 us  [swap(): return lax.ppermute(array, 'tok', pair)]
    ppermute x17 -> x14, starting transfers between devices: 3.02 us -> 2.59 us  [swap(): return lax.ppermute(array, 'tok', pair)]
  transfers between devices with their start and end apart: 25 -> 22, of which waited for: 13 -> 13; matrix products, arithmetic and copies ran while one was open for 0% -> 0% of each run, Pallas kernels for 16% -> 16%
where the time goes in v19:
time: 93.2 us; the launch traced here: 93 us
  waiting for transfers between devices  51.5 us (55%)
  Pallas kernels  26.6 us (29%)
  starting transfers between devices  11.9 us (13%)
  local copies, waits for them, and re-layouts  1.32 us (1%)
  between operations  0.96 us (1%)
    ppermute x8, waiting for transfers between devices, advance(): lax.ppermute(array, 'tok', stream)  44.8 us
    pallas_call x1, Pallas kernels, finish(): pl.pallas_call(functools.partial(finish_kernel, final), out_shape=[jax.Sh...  11.3 us
    pallas_call x4, Pallas kernels, absorb(): pl.pallas_call(functools.partial(absorb_kernel, count, bool(before)), out...  9.83 us
    ppermute x8, starting transfers between devices, advance(): lax.ppermute(array, 'tok', stream)  9.27 us
    ppermute x14, waiting for transfers between devices, swap(): return lax.ppermute(array, 'tok', pair)  6.66 us
    pallas_call x4, Pallas kernels, prepare(): pl.pallas_call(functools.partial(prepare_kernel, len(packs), at), out_sha...  3.21 us
    ppermute x14, starting transfers between devices, swap(): return lax.ppermute(array, 'tok', pair)  2.59 us
  transfers between devices with their start and end apart: 22, of which 13 were waited for; matrix products, arithmetic and copies ran while one was open for 0% of the time, Pallas kernels for 16%

profile of v19, /device:TPU:0, one launch (start us, length us, event | category | flops | bytes accessed | tf_op | source)
XLA Modules:
  0.0 93.0 jit_solution(8500982947107214077)
XLA Ops:
  0.6 0.7 select_reduce_fusion
  1.3 0.0 copy-start
  1.4 1.2 %copy-done = bf16[128,3584]{1,0:T(8,128)(2,1)S(1)} copy-done((bf16[128,3584]{1,0:T(8,128)(2,1)S(1)}, bf16[128,3584]{1,0:T(8,128)(2,1)}, u32[]{:S(2)}) %copy-start) | copy-done | bytes 917528
  2.5 0.2 make_message.1.refs_1_
  2.7 3.1 %collective-permute-start = (bf16[3616,128]{1,0:T(8,128)(2,1)S(1)}, bf16[3616,128]{1,0:T(8,128)(2,1)S(1)}, u32[]{:S(2)}, u32[]{:S(2)}) collective-permute-start(bf16[3616,128]{1,0:T(8,128)(2,1)S(1)} %make_message.1.refs_1_), channel_id=1, source_target_pairs={{0,4},{1,5},{4,8},{5,9},{8,12},{9,13},{12,14},{13,15},{14,10},{15,... | collective-permute-start | bytes 2777096 | tf_op jit(solution)/shard_map/ppermute | solution.py:320
  5.8 0.0 collective-permute-start.5
  5.8 0.1 stack.23.refs_0_
  5.9 1.5 %absorb.4 = (f32[896,896]{1,0:T(8,128)S(1)}, bf16[128,896]{1,0:T(8,128)(2,1)S(1)}, bf16[128,896]{1,0:T(8,128)(2,1)S(1)}, bf16[32,3584]{1,0:T(8,128)(2,1)S(1)}) custom-call(s32[5]{0:T(128)S(1)} %stack.23.refs_0_, bf16[3616,128]{1,0:T(8,128)(2,1)S(1)} %make_message.1.refs_1_), custom_call_target="tpu_custom_call" | custom-call | flops 1 | bytes 1 | tf_op jit(solution)/shard_map/absorb/pallas_call | solution.py:143
  7.4 0.1 collective-permute-start.1
  7.5 0.5 collective-permute-start.2
  8.0 0.1 collective-permute-start.3
  8.1 0.9 collective-permute-done.1.refs_2_
  9.0 0.8 prepare_rows.4
  9.8 0.0 collective-permute-done.2.refs_4_
  9.8 0.0 collective-permute-done.3.refs_5_
  9.8 16.5 %collective-permute-done.refs_1_ = bf16[3616,128]{1,0:T(8,128)(2,1)S(1)} collective-permute-done((bf16[3616,128]{1,0:T(8,128)(2,1)S(1)}, bf16[3616,128]{1,0:T(8,128)(2,1)S(1)}, u32[]{:S(2)}, u32[]{:S(2)}) %collective-permute-start) | collective-permute-done | bytes 925728 | tf_op jit(solution)/shard_map/ppermute | solution.py:320
  26.3 1.8 %collective-permute-start.4 = (bf16[3616,128]{1,0:T(8,128)(2,1)S(1)}, bf16[3616,128]{1,0:T(8,128)(2,1)S(1)}, u32[]{:S(2)}, u32[]{:S(2)}) collective-permute-start(bf16[3616,128]{1,0:T(8,128)(2,1)S(1)} %collective-permute-done.refs_1_), channel_id=1, source_target_pairs={{0,4},{1,5},{4,8},{5,9},{8,12},{9,13},{12,14},{13,15},{14,10},{15,... | collective-permute-start | bytes 2777096 | tf_op jit(solution)/shard_map/ppermute | solution.py:320
  28.1 0.0 collective-permute-done.5.refs_2_
  28.1 0.2 collective-permute-start.10
  28.3 2.7 %absorb.5 = (f32[896,896]{1,0:T(8,128)S(1)}, bf16[256,896]{1,0:T(8,128)(2,1)S(1)}, bf16[256,896]{1,0:T(8,128)(2,1)S(1)}, bf16[64,3584]{1,0:T(8,128)(2,1)S(1)}) custom-call(s32[5]{0:T(128)S(1)} %stack.23.refs_0_, bf16[3616,128]{1,0:T(8,128)(2,1)S(1)} %collective-permute-done.refs_1_, ...), custom_call_target="tpu_custom_call", output_to_operand_aliasing={{0}: (3, {})} | custom-call | flops 1 | bytes 1 | tf_op jit(solution)/shard_map/absorb/pallas_call | solution.py:143
  31.0 0.1 collective-permute-start.6
  31.0 0.5 collective-permute-start.7
  31.5 0.1 collective-permute-start.8
  31.6 1.2 %collective-permute-done.6.refs_2_ = bf16[64,3584]{1,0:T(8,128)(2,1)S(1)} collective-permute-done((bf16[64,3584]{1,0:T(8,128)(2,1)S(1)}, bf16[64,3584]{1,0:T(8,128)(2,1)S(1)}, u32[]{:S(2)}, u32[]{:S(2)}) %collective-permute-start.6) | collective-permute-done | bytes 458784 | tf_op jit(solution)/shard_map/ppermute | solution.py:317
  32.8 0.8 prepare_rows.5
  33.7 0.0 collective-permute-done.7.refs_4_
  33.7 0.5 collective-permute-done.8.refs_5_
  34.1 13.8 %collective-permute-done.4.refs_1_ = bf16[3616,128]{1,0:T(8,128)(2,1)S(1)} collective-permute-done((bf16[3616,128]{1,0:T(8,128)(2,1)S(1)}, bf16[3616,128]{1,0:T(8,128)(2,1)S(1)}, u32[]{:S(2)}, u32[]{:S(2)}) %collective-permute-start.4) | collective-permute-done | bytes 925728 | tf_op jit(solution)/shard_map/ppermute | solution.py:320
  48.0 1.5 %collective-permute-start.9 = (bf16[3616,128]{1,0:T(8,128)(2,1)S(1)}, bf16[3616,128]{1,0:T(8,128)(2,1)S(1)}, u32[]{:S(2)}, u32[]{:S(2)}) collective-permute-start(bf16[3616,128]{1,0:T(8,128)(2,1)S(1)} %collective-permute-done.4.refs_1_), channel_id=1, source_target_pairs={{0,4},{1,5},{4,8},{5,9},{8,12},{9,13},{12,14},{13,15},{14,10},{15,... | collective-permute-start | bytes 2777096 | tf_op jit(solution)/shard_map/ppermute | solution.py:320
  49.5 0.0 collective-permute-done.10.refs_2_
  49.5 0.5 collective-permute-start.15
  50.0 2.7 %absorb.6 = (f32[896,896]{1,0:T(8,128)S(1)}, bf16[256,896]{1,0:T(8,128)(2,1)S(1)}, bf16[256,896]{1,0:T(8,128)(2,1)S(1)}, bf16[64,3584]{1,0:T(8,128)(2,1)S(1)}) custom-call(s32[5]{0:T(128)S(1)} %stack.23.refs_0_, bf16[3616,128]{1,0:T(8,128)(2,1)S(1)} %collective-permute-done.4.refs_1_, ...), custom_call_target="tpu_custom_call", output_to_operand_aliasing={{0}: (3, {})} | custom-call | flops 1 | bytes 1 | tf_op jit(solution)/shard_map/absorb/pallas_call | solution.py:143
  52.7 0.1 collective-permute-start.11
  52.8 0.5 collective-permute-start.12
  53.3 0.1 collective-permute-start.13
  53.4 1.2 %collective-permute-done.11.refs_2_ = bf16[64,3584]{1,0:T(8,128)(2,1)S(1)} collective-permute-done((bf16[64,3584]{1,0:T(8,128)(2,1)S(1)}, bf16[64,3584]{1,0:T(8,128)(2,1)S(1)}, u32[]{:S(2)}, u32[]{:S(2)}) %collective-permute-start.11) | collective-permute-done | bytes 458784 | tf_op jit(solution)/shard_map/ppermute | solution.py:317
  54.6 0.8 prepare_rows.6
  55.4 0.0 collective-permute-done.12.refs_4_
  55.5 0.5 collective-permute-done.13.refs_5_
  55.9 12.8 %collective-permute-done.9.refs_1_ = bf16[3616,128]{1,0:T(8,128)(2,1)S(1)} collective-permute-done((bf16[3616,128]{1,0:T(8,128)(2,1)S(1)}, bf16[3616,128]{1,0:T(8,128)(2,1)S(1)}, u32[]{:S(2)}, u32[]{:S(2)}) %collective-permute-start.9) | collective-permute-done | bytes 925728 | tf_op jit(solution)/shard_map/ppermute | solution.py:320
  68.8 1.3 %collective-permute-start.14 = (bf16[1824,128]{1,0:T(8,128)(2,1)S(1)}, bf16[1824,128]{1,0:T(8,128)(2,1)S(1)}, u32[]{:S(2)}, u32[]{:S(2)}) collective-permute-start(bf16[1824,128]{1,0:T(8,128)(2,1)S(1)} %slice.6), channel_id=1, source_target_pairs={{0,4},{1,5},{4,8},{5,9},{8,12},{9,13},{12,14},{13,15},{14,10},{15,... | collective-permute-start | bytes 1400840 | tf_op jit(solution)/shard_map/ppermute | solution.py:320
  70.1 0.0 collective-permute-done.15.refs_2_
  70.2 0.8 collective-permute-start.19
  71.0 2.9 %absorb.7 = (f32[896,896]{1,0:T(8,128)S(1)}, bf16[256,896]{1,0:T(8,128)(2,1)S(1)}, bf16[256,896]{1,0:T(8,128)(2,1)S(1)}, bf16[64,3584]{1,0:T(8,128)(2,1)S(1)}) custom-call(s32[5]{0:T(128)S(1)} %stack.23.refs_0_, bf16[3616,128]{1,0:T(8,128)(2,1)S(1)} %collective-permute-done.9.refs_1_, ...), custom_call_target="tpu_custom_call", output_to_operand_aliasing={{0}: (3, {})} | custom-call | flops 1 | bytes 1 | tf_op jit(solution)/shard_map/absorb/pallas_call | solution.py:143
  73.9 0.1 collective-permute-start.17
  74.0 0.5 collective-permute-start.18
  74.5 0.1 collective-permute-start.16
  74.5 1.2 %collective-permute-done.17.left = bf16[256,896]{1,0:T(8,128)(2,1)S(1)} collective-permute-done((bf16[256,896]{1,0:T(8,128)(2,1)S(1)}, bf16[256,896]{1,0:T(8,128)(2,1)S(1)}, u32[]{:S(2)}, u32[]{:S(2)}) %collective-permute-start.17) | collective-permute-done | bytes 458784 | tf_op jit(solution)/shard_map/ppermute | solution.py:317
  75.8 0.7 collective-permute-done.18.right
  76.4 0.7 settle.1.refs_5_
  77.2 0.0 collective-permute-done.16.refs_2_
  77.2 0.8 prepare_rows.7
  78.0 0.9 collective-permute-done.14.refs_1_
  78.9 0.0 collective-permute-start.20
  78.9 0.8 collective-permute-done.19.refs_2_
  79.7 0.0 collective-permute-start.21
  79.7 1.4 %take_own.1 = (bf16[512,3584]{1,0:T(8,128)(2,1)S(1)}, bf16[1792,512]{1,0:T(8,128)(2,1)S(1)}) custom-call(s32[5]{0:T(128)S(1)} %stack.23.refs_0_, bf16[1824,128]{1,0:T(8,128)(2,1)S(1)} %collective-permute-done.14.refs_1_, bf16[1824,128]{1,0:T(8,128)(2,1)S(1)} %collective-permute-done.19.refs_2_, ...), custom_call_target="tpu_custom_call", output_to_operand_aliasing={{0}: (3, {}), {1}: (4, {})} | custom-call | flops 1 | bytes 1 | tf_op jit(solution)/shard_map/take_own/pallas_call | solution.py:215
  81.0 0.0 collective-permute-done.20.refs_3_
  81.0 0.5 collective-permute-done.21.refs_4_
  81.5 11.3 %finish.1 = (f32[1792,3584]{1,0:T(8,128)}, f32[1,896,896]{2,1,0:T(8,128)}, bf16[512,3584]{1,0:T(8,128)(2,1)S(1)}, bf16[1792,512]{1,0:T(8,128)(2,1)S(1)}) custom-call(s32[5]{0:T(128)S(1)} %stack.23.refs_0_, bf16[1824,128]{1,0:T(8,128)(2,1)S(1)} %collective-permute-done.14.refs_1_, ...), custom_call_target="tpu_custom_call", output_to_operand_aliasing={{2}: (6, {}), {3}: (7, {})} | custom-call | flops 1 | bytes 1 | tf_op jit(solution)/shard_map/finish/pallas_call | solution.py:260
  (2 shorter events, 0.1 us)
Async XLA Ops:
  1.3 1.2 %copy-start = (bf16[128,3584]{1,0:T(8,128)(2,1)S(1)}, bf16[128,3584]{1,0:T(8,128)(2,1)}, u32[]{:S(2)}) copy-start(bf16[128,3584]{1,0:T(8,128)(2,1)} %tokens.1) | copy-start | bytes 2752516
  2.7 23.5 %collective-permute-start = (bf16[3616,128]{1,0:T(8,128)(2,1)S(1)}, bf16[3616,128]{1,0:T(8,128)(2,1)S(1)}, u32[]{:S(2)}, u32[]{:S(2)}) collective-permute-start(bf16[3616,128]{1,0:T(8,128)(2,1)S(1)} %make_message.1.refs_1_), channel_id=1, source_target_pairs={{0,4},{1,5},{4,8},{5,9},{8,12},{9,13},{12,14},{13,15},{14,10},{15,... | collective-permute-start | bytes 2777096 | tf_op jit(solution)/shard_map/ppermute | solution.py:320
  5.8 22.3 %collective-permute-start.5 = (bf16[3616,128]{1,0:T(8,128)(2,1)S(1)}, bf16[3616,128]{1,0:T(8,128)(2,1)S(1)}, u32[]{:S(2)}, u32[]{:S(2)}) collective-permute-start(bf16[3616,128]{1,0:T(8,128)(2,1)S(1)} %make_message.1.refs_1_), channel_id=1, source_target_pairs={{4,0},{5,1},{8,4},{9,5},{12,8},{13,9},{14,12},{15,13},{10,14},{11,... | collective-permute-start | bytes 2777096 | tf_op jit(solution)/shard_map/ppermute | solution.py:320
  7.4 1.6 %collective-permute-start.1 = (bf16[32,3584]{1,0:T(8,128)(2,1)S(1)}, bf16[32,3584]{1,0:T(8,128)(2,1)S(1)}, u32[]{:S(2)}, u32[]{:S(2)}) collective-permute-start(bf16[32,3584]{1,0:T(8,128)(2,1)S(1)} %get-tuple-element.74.refs_1_), channel_id=1, source_target_pairs={{0,1},{1,0},{2,3},{3,2},{4,5},{5,4},{6,7},{7,6},{8,9},{9,8},{10,11... | collective-permute-start | bytes 688136 | tf_op jit(solution)/shard_map/ppermute | solution.py:317
  7.5 2.2 %collective-permute-start.2 = (bf16[128,896]{1,0:T(8,128)(2,1)S(1)}, bf16[128,896]{1,0:T(8,128)(2,1)S(1)}, u32[]{:S(2)}, u32[]{:S(2)}) collective-permute-start(bf16[128,896]{1,0:T(8,128)(2,1)S(1)} %get-tuple-element.78), channel_id=1, source_target_pairs={{0,1},{1,0},{2,3},{3,2},{4,5},{5,4},{6,7},{7,6},{8,9},{9,8},{10,11... | collective-permute-start | bytes 688136 | tf_op jit(solution)/shard_map/ppermute | solution.py:317
  8.0 1.8 %collective-permute-start.3 = (bf16[128,896]{1,0:T(8,128)(2,1)S(1)}, bf16[128,896]{1,0:T(8,128)(2,1)S(1)}, u32[]{:S(2)}, u32[]{:S(2)}) collective-permute-start(bf16[128,896]{1,0:T(8,128)(2,1)S(1)} %get-tuple-element.79), channel_id=1, source_target_pairs={{0,1},{1,0},{2,3},{3,2},{4,5},{5,4},{6,7},{7,6},{8,9},{9,8},{10,11... | collective-permute-start | bytes 688136 | tf_op jit(solution)/shard_map/ppermute | solution.py:317
  26.3 21.7 %collective-permute-start.4 = (bf16[3616,128]{1,0:T(8,128)(2,1)S(1)}, bf16[3616,128]{1,0:T(8,128)(2,1)S(1)}, u32[]{:S(2)}, u32[]{:S(2)}) collective-permute-start(bf16[3616,128]{1,0:T(8,128)(2,1)S(1)} %collective-permute-done.refs_1_), channel_id=1, source_target_pairs={{0,4},{1,5},{4,8},{5,9},{8,12},{9,13},{12,14},{13,15},{14,10},{15,... | collective-permute-start | bytes 2777096 | tf_op jit(solution)/shard_map/ppermute | solution.py:320
  28.1 21.4 %collective-permute-start.10 = (bf16[3616,128]{1,0:T(8,128)(2,1)S(1)}, bf16[3616,128]{1,0:T(8,128)(2,1)S(1)}, u32[]{:S(2)}, u32[]{:S(2)}) collective-permute-start(bf16[3616,128]{1,0:T(8,128)(2,1)S(1)} %collective-permute-done.5.refs_2_), channel_id=1, source_target_pairs={{4,0},{5,1},{8,4},{9,5},{12,8},{13,9},{14,12},{15,13},{10,14},{11,... | collective-permute-start | bytes 2777096 | tf_op jit(solution)/shard_map/ppermute | solution.py:320
  31.0 1.9 %collective-permute-start.6 = (bf16[64,3584]{1,0:T(8,128)(2,1)S(1)}, bf16[64,3584]{1,0:T(8,128)(2,1)S(1)}, u32[]{:S(2)}, u32[]{:S(2)}) collective-permute-start(bf16[64,3584]{1,0:T(8,128)(2,1)S(1)} %get-tuple-element.90.refs_1_), channel_id=1, source_target_pairs={{0,1},{1,0},{2,3},{3,2},{4,5},{5,4},{6,7},{7,6},{8,9},{9,8},{10,11... | collective-permute-start | bytes 1376264 | tf_op jit(solution)/shard_map/ppermute | solution.py:317
  31.0 2.6 %collective-permute-start.7 = (bf16[256,896]{1,0:T(8,128)(2,1)S(1)}, bf16[256,896]{1,0:T(8,128)(2,1)S(1)}, u32[]{:S(2)}, u32[]{:S(2)}) collective-permute-start(bf16[256,896]{1,0:T(8,128)(2,1)S(1)} %get-tuple-element.96), channel_id=1, source_target_pairs={{0,1},{1,0},{2,3},{3,2},{4,5},{5,4},{6,7},{7,6},{8,9},{9,8},{10,11... | collective-permute-start | bytes 1376264 | tf_op jit(solution)/shard_map/ppermute | solution.py:317
  31.5 2.6 %collective-permute-start.8 = (bf16[256,896]{1,0:T(8,128)(2,1)S(1)}, bf16[256,896]{1,0:T(8,128)(2,1)S(1)}, u32[]{:S(2)}, u32[]{:S(2)}) collective-permute-start(bf16[256,896]{1,0:T(8,128)(2,1)S(1)} %get-tuple-element.97), channel_id=1, source_target_pairs={{0,1},{1,0},{2,3},{3,2},{4,5},{5,4},{6,7},{7,6},{8,9},{9,8},{10,11... | collective-permute-start | bytes 1376264 | tf_op jit(solution)/shard_map/ppermute | solution.py:317
  48.0 20.8 %collective-permute-start.9 = (bf16[3616,128]{1,0:T(8,128)(2,1)S(1)}, bf16[3616,128]{1,0:T(8,128)(2,1)S(1)}, u32[]{:S(2)}, u32[]{:S(2)}) collective-permute-start(bf16[3616,128]{1,0:T(8,128)(2,1)S(1)} %collective-permute-done.4.refs_1_), channel_id=1, source_target_pairs={{0,4},{1,5},{4,8},{5,9},{8,12},{9,13},{12,14},{13,15},{14,10},{15,... | collective-permute-start | bytes 2777096 | tf_op jit(solution)/shard_map/ppermute | solution.py:320
  49.5 20.7 %collective-permute-start.15 = (bf16[3616,128]{1,0:T(8,128)(2,1)S(1)}, bf16[3616,128]{1,0:T(8,128)(2,1)S(1)}, u32[]{:S(2)}, u32[]{:S(2)}) collective-permute-start(bf16[3616,128]{1,0:T(8,128)(2,1)S(1)} %collective-permute-done.10.refs_2_), channel_id=1, source_target_pairs={{4,0},{5,1},{8,4},{9,5},{12,8},{13,9},{14,12},{15,13},{10,14},{11,... | collective-permute-start | bytes 2777096 | tf_op jit(solution)/shard_map/ppermute | solution.py:320
  52.7 1.9 %collective-permute-start.11 = (bf16[64,3584]{1,0:T(8,128)(2,1)S(1)}, bf16[64,3584]{1,0:T(8,128)(2,1)S(1)}, u32[]{:S(2)}, u32[]{:S(2)}) collective-permute-start(bf16[64,3584]{1,0:T(8,128)(2,1)S(1)} %get-tuple-element.108.refs_1_), channel_id=1, source_target_pairs={{0,1},{1,0},{2,3},{3,2},{4,5},{5,4},{6,7},{7,6},{8,9},{9,8},{10,11... | collective-permute-start | bytes 1376264 | tf_op jit(solution)/shard_map/ppermute | solution.py:317
  52.8 2.6 %collective-permute-start.12 = (bf16[256,896]{1,0:T(8,128)(2,1)S(1)}, bf16[256,896]{1,0:T(8,128)(2,1)S(1)}, u32[]{:S(2)}, u32[]{:S(2)}) collective-permute-start(bf16[256,896]{1,0:T(8,128)(2,1)S(1)} %get-tuple-element.114), channel_id=1, source_target_pairs={{0,1},{1,0},{2,3},{3,2},{4,5},{5,4},{6,7},{7,6},{8,9},{9,8},{10,11... | collective-permute-start | bytes 1376264 | tf_op jit(solution)/shard_map/ppermute | solution.py:317
  53.3 2.6 %collective-permute-start.13 = (bf16[256,896]{1,0:T(8,128)(2,1)S(1)}, bf16[256,896]{1,0:T(8,128)(2,1)S(1)}, u32[]{:S(2)}, u32[]{:S(2)}) collective-permute-start(bf16[256,896]{1,0:T(8,128)(2,1)S(1)} %get-tuple-element.115), channel_id=1, source_target_pairs={{0,1},{1,0},{2,3},{3,2},{4,5},{5,4},{6,7},{7,6},{8,9},{9,8},{10,11... | collective-permute-start | bytes 1376264 | tf_op jit(solution)/shard_map/ppermute | solution.py:317
  68.8 10.1 %collective-permute-start.14 = (bf16[1824,128]{1,0:T(8,128)(2,1)S(1)}, bf16[1824,128]{1,0:T(8,128)(2,1)S(1)}, u32[]{:S(2)}, u32[]{:S(2)}) collective-permute-start(bf16[1824,128]{1,0:T(8,128)(2,1)S(1)} %slice.6), channel_id=1, source_target_pairs={{0,4},{1,5},{4,8},{5,9},{8,12},{9,13},{12,14},{13,15},{14,10},{15,... | collective-permute-start | bytes 1400840 | tf_op jit(solution)/shard_map/ppermute | solution.py:320
  70.2 9.5 %collective-permute-start.19 = (bf16[1824,128]{1,0:T(8,128)(2,1)S(1)}, bf16[1824,128]{1,0:T(8,128)(2,1)S(1)}, u32[]{:S(2)}, u32[]{:S(2)}) collective-permute-start(bf16[1824,128]{1,0:T(8,128)(2,1)S(1)} %slice.7), channel_id=1, source_target_pairs={{4,0},{5,1},{8,4},{9,5},{12,8},{13,9},{14,12},{15,13},{10,14},{11,... | collective-permute-start | bytes 1400840 | tf_op jit(solution)/shard_map/ppermute | solution.py:320
  73.9 1.9 %collective-permute-start.17 = (bf16[256,896]{1,0:T(8,128)(2,1)S(1)}, bf16[256,896]{1,0:T(8,128)(2,1)S(1)}, u32[]{:S(2)}, u32[]{:S(2)}) collective-permute-start(bf16[256,896]{1,0:T(8,128)(2,1)S(1)} %get-tuple-element.132), channel_id=1, source_target_pairs={{0,1},{1,0},{2,3},{3,2},{4,5},{5,4},{6,7},{7,6},{8,9},{9,8},{10,11... | collective-permute-start | bytes 1376264 | tf_op jit(solution)/shard_map/ppermute | solution.py:317
  74.0 2.5 %collective-permute-start.18 = (bf16[256,896]{1,0:T(8,128)(2,1)S(1)}, bf16[256,896]{1,0:T(8,128)(2,1)S(1)}, u32[]{:S(2)}, u32[]{:S(2)}) collective-permute-start(bf16[256,896]{1,0:T(8,128)(2,1)S(1)} %get-tuple-element.133), channel_id=1, source_target_pairs={{0,1},{1,0},{2,3},{3,2},{4,5},{5,4},{6,7},{7,6},{8,9},{9,8},{10,11... | collective-permute-start | bytes 1376264 | tf_op jit(solution)/shard_map/ppermute | solution.py:317
  74.5 2.7 %collective-permute-start.16 = (bf16[64,3584]{1,0:T(8,128)(2,1)S(1)}, bf16[64,3584]{1,0:T(8,128)(2,1)S(1)}, u32[]{:S(2)}, u32[]{:S(2)}) collective-permute-start(bf16[64,3584]{1,0:T(8,128)(2,1)S(1)} %get-tuple-element.126.refs_1_), channel_id=1, source_target_pairs={{0,1},{1,0},{2,3},{3,2},{4,5},{5,4},{6,7},{7,6},{8,9},{9,8},{10,11... | collective-permute-start | bytes 1376264 | tf_op jit(solution)/shard_map/ppermute | solution.py:317
  78.9 2.1 %collective-permute-start.20 = (bf16[1824,128]{1,0:T(8,128)(2,1)S(1)}, bf16[1824,128]{1,0:T(8,128)(2,1)S(1)}, u32[]{:S(2)}, u32[]{:S(2)}) collective-permute-start(bf16[1824,128]{1,0:T(8,128)(2,1)S(1)} %collective-permute-done.14.refs_1_), channel_id=1, source_target_pairs={{0,1},{1,0},{2,3},{3,2},{4,5},{5,4},{6,7},{7,6},{8,9},{9,8},{10,11... | collective-permute-start | bytes 1400840 | tf_op jit(solution)/shard_map/ppermute | solution.py:317
  79.7 1.8 %collective-permute-start.21 = (bf16[1824,128]{1,0:T(8,128)(2,1)S(1)}, bf16[1824,128]{1,0:T(8,128)(2,1)S(1)}, u32[]{:S(2)}, u32[]{:S(2)}) collective-permute-start(bf16[1824,128]{1,0:T(8,128)(2,1)S(1)} %collective-permute-done.19.refs_2_), channel_id=1, source_target_pairs={{0,1},{1,0},{2,3},{3,2},{4,5},{5,4},{6,7},{7,6},{8,9},{9,8},{10,11... | collective-permute-start | bytes 1400840 | tf_op jit(solution)/shard_map/ppermute | solution.py:317
